TPU v7x, 32 devices: a whole 2x2x4 slice. The times are simulated.
32 devices in a mesh: seq: 16 (over z, x, core), batch: 2 (over y).
Axes of the slice: x: 2, y: 2, z: 4, core: 2. Of those that a mesh axis runs over, the one named last changes fastest.
Arguments:
- tokens: bfloat16 [4, 2048, 2048], P('batch', 'seq'), may hold values from -6 to 6
- cotangent: bfloat16 [4, 2048, 2048], P('batch', 'seq'), may hold values from -6 to 6
- doc_lengths: int32 [4, 4], P('batch'), may hold values from 1 to 1920, 2048 in all within a row
- w_branch: bfloat16 [2048, 2560], P(('seq', 'batch')), may hold values from -0.125 to 0.125
- w_input: bfloat16 [2048, 2560], P(('seq', 'batch')), may hold values from -0.125 to 0.125
- w_output: bfloat16 [2048, 2560], P(('seq', 'batch')), may hold values from -0.25 to 0.25
- w_gate: bfloat16 [2048, 6144], P(('seq', 'batch')), may hold values from -0.125 to 0.125
- w_up: bfloat16 [2048, 6144], P(('seq', 'batch')), may hold values from -0.125 to 0.125
- w_down: bfloat16 [2048, 6144], P(('seq', 'batch')), may hold values from -0.109375 to 0.109375
- gate_weight: bfloat16 [2560, 320], P(('seq', 'batch')), may hold values from -0.5 to 0.5
- gate_bias: bfloat16 [2, 2560], P(None, ('seq', 'batch')), may hold values from -4 to 4
- conv_weight: bfloat16 [4, 2560], P(None, ('seq', 'batch')), may hold values from -3 to 3
- conv_bias: bfloat16 [2560], P(('seq', 'batch')), may hold values from -3 to 3
- lru_param: bfloat16 [2560], P(('seq', 'batch')), may hold values from -14 to -4
- mixer_gain: bfloat16 [2048], P(('seq', 'batch')), may hold values from 0.099609375 to 1.8984375
- mlp_gain: bfloat16 [2048], P(('seq', 'batch')), may hold values from 0.099609375 to 1.8984375
Outputs:
- block_output: bfloat16 [4, 2048, 2048], P('batch', 'seq')
- input_grad: float32 [4, 2048, 2048], P('batch', 'seq')
- w_branch_grad: float32 [2048, 2560], P(('seq', 'batch'))
- w_input_grad: float32 [2048, 2560], P(('seq', 'batch'))
- w_output_grad: float32 [2048, 2560], P(('seq', 'batch'))
- w_gate_grad: float32 [2048, 6144], P(('seq', 'batch'))
- w_up_grad: float32 [2048, 6144], P(('seq', 'batch'))
- w_down_grad: float32 [2048, 6144], P(('seq', 'batch'))
- gate_weight_grad: float32 [2560, 320], P(('seq', 'batch'))
- gate_bias_grad: float32 [2, 2560], P(None, ('seq', 'batch'))
- conv_weight_grad: float32 [4, 2560], P(None, ('seq', 'batch'))
- conv_bias_grad: float32 [2560], P(('seq', 'batch'))
- lru_param_grad: float32 [2560], P(('seq', 'batch'))
- mixer_gain_grad: float32 [2048], P(('seq', 'batch'))
- mlp_gain_grad: float32 [2048], P(('seq', 'batch'))
Inputs may be any that keep to these rules, and one draw needn't show every extreme that they name: `doc_lengths`: each row's 4 lengths add up to 2048; the longest is 1920.
All inputs are finite; a program needn't handle non-finite values.
Results may differ from a plain program's by a relative error of at most 0.0091.
Values may be sent and summed in bfloat16 or wider, within the bound.
A program may use at most 448 MiB of HBM per device.

v0:
```python
import jax
import jax.numpy as jnp
from jax import lax
from jax.sharding import PartitionSpec as P

HEADS = 16
WIDTH = 160


norm_eps = 1e-06
rows_contract = (((0,), (0,)), ((), ()))
last_contract = (((1,), (1,)), ((), ()))


def from_behind(value, axis, steps):
    count = lax.axis_size(axis)
    initial, last = (max(0, -steps), min(count, count - steps))
    return lax.ppermute(value, axis, [(source, source + steps) for source in range(initial, last)])


def rms_norm(values, gain_row):
    inverse = lax.rsqrt(jnp.mean(values * values, axis=-1, keepdims=True) + norm_eps)
    return values * inverse * gain_row


def link(earlier, latter):
    return (earlier[0] * latter[0], latter[0] * earlier[1] + latter[1])


def gated_pair(gate_pre, up_pre):
    return jax.nn.gelu(gate_pre) * up_pre


def mixing(states, branch):
    return states * jax.nn.gelu(branch)


def outer_rows(left_side, right_side):
    return lax.dot_general(left_side, right_side, rows_contract, preferred_element_type=jnp.float32)


def times_back(left_side, weight):
    return lax.dot_general(left_side, weight, last_contract, preferred_element_type=jnp.float32)


def shards(
    tokens,
    cotangent,
    doc_lengths,
    w_branch,
    w_input,
    w_output,
    w_gate,
    w_up,
    w_down,
    gate_weight,
    gate_bias,
    conv_weight,
    conv_bias,
    lru_param,
    mixer_gain,
    mlp_gain,
):
    row_count, group_len, model_width = tokens.shape
    token_count = row_count * group_len
    gathered = (
        lax.all_gather(w_branch, ("seq", "batch"), axis=0, tiled=True),
        lax.all_gather(w_input, ("seq", "batch"), axis=0, tiled=True),
        lax.all_gather(w_output, ("seq", "batch"), axis=0, tiled=True),
        lax.all_gather(w_gate, ("seq", "batch"), axis=0, tiled=True),
        lax.all_gather(w_up, ("seq", "batch"), axis=0, tiled=True),
        lax.all_gather(w_down, ("seq", "batch"), axis=0, tiled=True),
        lax.all_gather(gate_weight, ("seq", "batch"), axis=0, tiled=True),
        lax.all_gather(gate_bias, ("seq", "batch"), axis=1, tiled=True),
        lax.all_gather(conv_weight, ("seq", "batch"), axis=1, tiled=True),
        lax.all_gather(conv_bias, ("seq", "batch"), axis=0, tiled=True),
        lax.all_gather(lru_param, ("seq", "batch"), axis=0, tiled=True),
        lax.all_gather(mixer_gain, ("seq", "batch"), axis=0, tiled=True),
        lax.all_gather(mlp_gain, ("seq", "batch"), axis=0, tiled=True),
    )
    (
        branch_full,
        input_full,
        output_full,
        gate_full,
        up_full,
        down_full,
        heads_full,
        bias_full,
        taps_full,
        shift_full,
        decay_full,
        mixer_full,
        mlp_full,
    ) = gathered
    gate_shift = bias_full.astype(jnp.float32)
    conv_taps = taps_full.astype(jnp.float32)
    conv_shift = shift_full.astype(jnp.float32)
    lru_values = decay_full.astype(jnp.float32)
    mixer_scale = mixer_full.astype(jnp.float32)
    mlp_scale = mlp_full.astype(jnp.float32)
    lru_width = branch_full.shape[1]
    tap_count = conv_taps.shape[0]
    rim_width = tap_count - 1
    first_place = lax.axis_index("seq") * group_len
    places = first_place + jnp.arange(group_len, dtype=jnp.int32)
    starts = jnp.cumsum(doc_lengths, axis=1, dtype=jnp.int32) - doc_lengths
    reached = places[None, :, None] >= starts[:, None, :]
    begins = jnp.max(jnp.where(reached, starts[:, None, :], 0), axis=2)
    offsets = places[None, :] - begins
    resets = (offsets == 0)[..., None]
    rows_in = tokens.reshape(token_count, model_width).astype(jnp.float32)
    normed_value, first_pull = jax.vjp(rms_norm, rows_in, mixer_scale)
    normed = normed_value.astype(jnp.bfloat16)
    branch = jnp.dot(normed, branch_full, preferred_element_type=jnp.float32)
    inner_b = jnp.dot(normed, input_full, preferred_element_type=jnp.float32).astype(jnp.bfloat16)
    inner_rows = inner_b.reshape(row_count, group_len, lru_width)
    received = from_behind(inner_rows[:, group_len - rim_width :, :], "seq", 1)
    extended = jnp.concatenate([received, inner_rows], axis=1).astype(jnp.float32)
    conv_out = jnp.broadcast_to(conv_shift, (row_count, group_len, lru_width))
    for lag_index in range(tap_count):
        window = extended[:, rim_width - lag_index : rim_width - lag_index + group_len, :]
        conv_out = conv_out + jnp.where(
            (offsets >= lag_index)[..., None], conv_taps[lag_index] * window, 0.0
        )
    head_rows = conv_out.astype(jnp.bfloat16).reshape(token_count, HEADS, WIDTH)
    blocks = heads_full.reshape(HEADS, WIDTH, 2 * WIDTH)
    head_pre = jnp.einsum("thi,hij->thj", head_rows, blocks, preferred_element_type=jnp.float32)
    rate_pre = head_pre[..., :WIDTH].reshape(row_count, group_len, lru_width) + gate_shift[0]
    keep_pre = head_pre[..., WIDTH:].reshape(row_count, group_len, lru_width) + gate_shift[1]

    def recurrence_inputs(conv_in, rate_in, keep_in, param_in):
        rate_gate = jax.nn.sigmoid(rate_in)
        keep_gate = jax.nn.sigmoid(keep_in)
        log_decay = -8.0 * rate_gate * jax.nn.softplus(param_in)
        decays = jnp.where(resets, 0.0, jnp.exp(log_decay))
        scales = jnp.where(resets, 1.0, jnp.sqrt(-jnp.expm1(2.0 * log_decay)))
        return (decays, conv_in * keep_gate * scales)

    (decays, driven), recurrence_pull = jax.vjp(
        recurrence_inputs, conv_out, rate_pre, keep_pre, lru_values
    )
    cum_decay, local_states = lax.associative_scan(link, (decays, driven), axis=1)
    group_decay = cum_decay[:, -1, :]
    group_state = local_states[:, -1, :]

    def carry_state(step_index, incoming):
        return from_behind(group_decay * incoming + group_state, "seq", 1)

    entering = lax.fori_loop(0, lax.axis_size("seq") - 1, carry_state, jnp.zeros_like(group_state))
    states = local_states + cum_decay * entering[:, None, :]
    branch_rows = branch.reshape(row_count, group_len, lru_width)
    mixed_value, mixing_pull = jax.vjp(mixing, states, branch_rows)
    mixed_b = mixed_value.reshape(token_count, lru_width).astype(jnp.bfloat16)
    middle = rows_in + times_back(mixed_b, output_full)
    second_value, second_pull = jax.vjp(rms_norm, middle, mlp_scale)
    second_normed = second_value.astype(jnp.bfloat16)
    gate_pre = jnp.dot(second_normed, gate_full, preferred_element_type=jnp.float32)
    up_pre = jnp.dot(second_normed, up_full, preferred_element_type=jnp.float32)
    hidden_value, hidden_pull = jax.vjp(gated_pair, gate_pre, up_pre)
    hidden = hidden_value.astype(jnp.bfloat16)
    block_output = (
        (middle + times_back(hidden, down_full))
        .astype(jnp.bfloat16)
        .reshape(row_count, group_len, model_width)
    )
    grad_mlp = cotangent.reshape(token_count, model_width)
    grad_out = grad_mlp.astype(jnp.float32)
    grad_hidden = jnp.dot(grad_mlp, down_full, preferred_element_type=jnp.float32)
    grad_gate_value, grad_up_value = hidden_pull(grad_hidden)
    grad_gate = grad_gate_value.astype(jnp.bfloat16)
    grad_up = grad_up_value.astype(jnp.bfloat16)
    grad_second = times_back(grad_gate, gate_full) + times_back(grad_up, up_full)
    grad_middle_norm, mlp_gain_term = second_pull(grad_second)
    grad_middle = grad_out + grad_middle_norm
    grad_att = grad_middle.astype(jnp.bfloat16)
    grad_mixed = jnp.dot(grad_att, output_full, preferred_element_type=jnp.float32).reshape(
        row_count, group_len, lru_width
    )
    grad_state, grad_branch_value = mixing_pull(grad_mixed)
    grad_branch = grad_branch_value.reshape(token_count, lru_width).astype(jnp.bfloat16)
    following = jnp.concatenate([decays[:, 1:, :], jnp.ones_like(decays[:, :1, :])], axis=1)
    tail_decay, local_adjoint = lax.associative_scan(
        link, (following, grad_state), reverse=True, axis=1
    )
    first_pass = decays[:, 0, :] * local_adjoint[:, 0, :]

    def carry_adjoint(step_index, incoming):
        return from_behind(group_decay * incoming + first_pass, "seq", -1)

    arriving = lax.fori_loop(0, lax.axis_size("seq") - 1, carry_adjoint, jnp.zeros_like(first_pass))
    adjoint = local_adjoint + tail_decay * arriving[:, None, :]
    previous = jnp.concatenate([entering[:, None, :], states[:, :-1, :]], axis=1)
    grad_conv_own, grad_rate_value, grad_keep_value, lru_term = recurrence_pull(
        (adjoint * previous, adjoint)
    )
    grad_rate = grad_rate_value.astype(jnp.bfloat16)
    grad_keep = grad_keep_value.astype(jnp.bfloat16)
    bias_term = jnp.stack(
        [
            jnp.sum(grad_rate, axis=(0, 1), dtype=jnp.float32),
            jnp.sum(grad_keep, axis=(0, 1), dtype=jnp.float32),
        ]
    )
    grad_pre = jnp.concatenate(
        [
            grad_rate.reshape(token_count, HEADS, WIDTH),
            grad_keep.reshape(token_count, HEADS, WIDTH),
        ],
        axis=2,
    )
    grad_heads = jnp.einsum(
        "thj,hij->thi", grad_pre, blocks, preferred_element_type=jnp.float32
    ).reshape(row_count, group_len, lru_width)
    heads_term = jnp.einsum(
        "thi,thj->hij", head_rows, grad_pre, preferred_element_type=jnp.float32
    ).reshape(lru_width, 2 * WIDTH)
    grad_conv = grad_conv_own + grad_heads
    spread = jnp.zeros((row_count, group_len + rim_width, lru_width), jnp.float32)
    tap_terms = []
    for lag_index in range(tap_count):
        masked = jnp.where((offsets >= lag_index)[..., None], grad_conv, 0.0)
        lower = rim_width - lag_index
        spread = spread.at[:, lower : lower + group_len, :].add(conv_taps[lag_index] * masked)
        tap_terms.append(jnp.sum(masked * extended[:, lower : lower + group_len, :], axis=(0, 1)))
    taps_term = jnp.stack(tap_terms)
    shift_term = jnp.sum(grad_conv, axis=(0, 1))
    returned = from_behind(spread[:, :rim_width, :].astype(jnp.bfloat16), "seq", -1).astype(
        jnp.float32
    )
    grad_inner = spread[:, rim_width:, :].at[:, group_len - rim_width :, :].add(returned)
    grad_inner_b = grad_inner.reshape(token_count, lru_width).astype(jnp.bfloat16)
    grad_normed = times_back(grad_branch, branch_full) + times_back(grad_inner_b, input_full)
    grad_in_norm, mixer_term = first_pull(grad_normed)
    input_grad = (grad_middle + grad_in_norm).reshape(row_count, group_len, model_width)
    small_sums = (
        lax.psum_scatter(mixer_term, ("seq", "batch"), scatter_dimension=0, tiled=True),
        lax.psum_scatter(mlp_gain_term, ("seq", "batch"), scatter_dimension=0, tiled=True),
        lax.psum_scatter(taps_term, ("seq", "batch"), scatter_dimension=1, tiled=True),
        lax.psum_scatter(shift_term, ("seq", "batch"), scatter_dimension=0, tiled=True),
        lax.psum_scatter(bias_term, ("seq", "batch"), scatter_dimension=1, tiled=True),
        lax.psum_scatter(lru_term, ("seq", "batch"), scatter_dimension=0, tiled=True),
        lax.psum_scatter(heads_term, ("seq", "batch"), scatter_dimension=0, tiled=True),
    )
    (
        mixer_gain_grad,
        mlp_gain_grad,
        conv_weight_grad,
        conv_bias_grad,
        gate_bias_grad,
        lru_param_grad,
        gate_weight_grad,
    ) = small_sums
    joined = lax.psum_scatter(
        jnp.concatenate(
            [
                jnp.concatenate(
                    [
                        outer_rows(normed, grad_branch),
                        outer_rows(normed, grad_inner_b),
                        outer_rows(grad_att, mixed_b),
                    ],
                    axis=1,
                ),
                jnp.concatenate(
                    [
                        outer_rows(second_normed, grad_gate),
                        outer_rows(second_normed, grad_up),
                        outer_rows(grad_mlp, hidden),
                    ],
                    axis=1,
                ),
            ],
            axis=1,
        ),
        ("seq", "batch"),
        scatter_dimension=0,
        tiled=True,
    )
    mixer_sums = joined[:, : 3 * lru_width]
    mlp_sums = joined[:, 3 * lru_width :]
    ff_width = gate_full.shape[1]
    return (
        block_output,
        input_grad,
        mixer_sums[:, :lru_width],
        mixer_sums[:, lru_width : 2 * lru_width],
        mixer_sums[:, 2 * lru_width :],
        mlp_sums[:, :ff_width],
        mlp_sums[:, ff_width : 2 * ff_width],
        mlp_sums[:, 2 * ff_width :],
        gate_weight_grad,
        gate_bias_grad,
        conv_weight_grad,
        conv_bias_grad,
        lru_param_grad,
        mixer_gain_grad,
        mlp_gain_grad,
    )


def solution(mesh):
    placed = (
        P("batch", "seq", None),
        P("batch", "seq", None),
        P("batch", None),
        P(("seq", "batch"), None),
        P(("seq", "batch"), None),
        P(("seq", "batch"), None),
        P(("seq", "batch"), None),
        P(("seq", "batch"), None),
        P(("seq", "batch"), None),
        P(("seq", "batch"), None),
        P(None, ("seq", "batch")),
        P(None, ("seq", "batch")),
        P(("seq", "batch")),
        P(("seq", "batch")),
        P(("seq", "batch")),
        P(("seq", "batch")),
    )
    return jax.shard_map(
        shards,
        mesh=mesh,
        in_specs=placed,
        out_specs=(
            P("batch", "seq", None),
            P("batch", "seq", None),
            P(("seq", "batch"), None),
            P(("seq", "batch"), None),
            P(("seq", "batch"), None),
            P(("seq", "batch"), None),
            P(("seq", "batch"), None),
            P(("seq", "batch"), None),
            P(("seq", "batch"), None),
            P(None, ("seq", "batch")),
            P(None, ("seq", "batch")),
            P(("seq", "batch")),
            P(("seq", "batch")),
            P(("seq", "batch")),
            P(("seq", "batch")),
        ),
        check_vma=False,
    )
```

profile of v0, /device:TPU:0, one launch (start us, length us, event | category | flops | bytes accessed | tf_op | source)
XLA Modules:
  0.0 3188.2 jit_solution(17217232219913065727)
XLA Ops:
  13.2 43.1 %all-reduce.68 = (bf16[2560]{0:T(1024)(128)(2,1)S(1)}, bf16[2048]{0:T(1024)(128)(2,1)S(1)}, bf16[2560]{0:T(1024)(128)(2,1)S(1)}, bf16[2048]{0:T(1024)(128)(2,1)S(1)}) all-reduce(bf16[2560]{0:T(1024)(128)(2,1)S(1)} %dynamic-update-slice.17, ...), channel_id=1, replica_groups=mesh['seq'=16,'batch'=2] {'seq','batch'}, use_global_device_ids=true, to_apply=%add.61 | all-reduce | flops 9216 | bytes 36864
  56.4 66.1 %all-gather.1 = bf16[32,80,2]{1,2,0:T(2,128)(2,1)S(1)} all-gather(bf16[1,80,2]{1,2,0:T(2,128)(2,1)S(1)} %bitcast.180), channel_id=1, replica_groups=mesh['seq'=16,'batch'=2] {'seq','batch'}, dimensions={0}, use_global_device_ids=true | all-gather | bytes 10560 | tf_op jit(solution)/shard_map/all_gather | solution.py:74
  122.6 63.5 %all-gather = bf16[32,80,4]{1,2,0:T(4,128)(2,1)S(1)} all-gather(bf16[1,80,4]{1,2,0:T(4,128)(2,1)S(1)} %bitcast.179), channel_id=1, replica_groups=mesh['seq'=16,'batch'=2] {'seq','batch'}, dimensions={0}, use_global_device_ids=true | all-gather | bytes 21120 | tf_op jit(solution)/shard_map/all_gather | solution.py:75
  188.2 7.2 convolution_convert_fusion
  218.3 5.2 copy.77
  227.8 5.2 copy.78
  233.0 6.5 fusion.36
  241.0 5.9 slice.697
  246.9 5.6 slice.651
  252.5 5.6 slice.650
  259.6 5.6 slice.653
  265.2 5.6 slice.649
  298.9 5.9 slice.648
  308.4 5.6 slice.724
  314.0 5.6 slice.717
  319.6 5.6 slice.715
  353.0 5.8 pad.212
  370.7 5.8 pad.198
  377.7 5.8 pad.197
  384.5 79.3 %while.25 = (s32[]{:T(128)}, f32[2,2560]{1,0:T(2,128)S(1)}, f32[2,2560]{1,0:T(2,128)S(1)}, f32[2,2560]{1,0:T(2,128)S(1)}, s32[]{:T(128)}) while((s32[]{:T(128)}, f32[2,2560]{1,0:T(2,128)S(1)}, f32[2,2560]{1,0:T(2,128)S(1)}, f32[2,2560]{1,0:T(2,128)S(1)}, s32[]{:T(128)}) %tuple.168), condition=%wide.region_4.5_spmd, body=%wide.region_3.4_spmd.sunk | while | flops 10242 | bytes 163941 | solution.py:150
  391.7 4.9 collective-permute-start
  445.6 4.7 collective-permute-start
  451.2 5.6 collective-permute-start
  457.6 5.3 collective-permute-start
  464.4 10.9 slice.725
  475.3 10.8 slice.716
  486.1 6.6 slice.718
  492.7 11.9 multiply_convert_fusion.2
  504.6 6.4 multiply_reduce_fusion.7
  511.3 15.2 fusion.90
  526.4 123.9 %all-gather.18.cloned.1.call-done = bf16[2048,6144]{1,0:T(8,128)(2,1)} async-done(((bf16[64,6144]{1,0:T(8,128)(2,1)}), bf16[2048,6144]{1,0:T(8,128)(2,1)}) %all-gather.18.cloned.1.call-update) | async-done | bytes 25165840 | tf_op jit(solution)/shard_map/all_gather | solution.py:70
  650.3 14.4 fusion.89
  664.7 141.3 %all-gather.22.cloned.1.call-done = bf16[2048,6144]{1,0:T(8,128)(2,1)} async-done(((bf16[64,6144]{1,0:T(8,128)(2,1)}), bf16[2048,6144]{1,0:T(8,128)(2,1)}) %all-gather.22.cloned.1.call-update) | async-done | bytes 25165840 | tf_op jit(solution)/shard_map/all_gather | solution.py:72
  806.1 20.8 multiply_convert_fusion
  826.8 13.5 fusion.91
  840.3 15.1 multiply_reduce_fusion.5
  857.6 6.4 fusion.46
  875.7 10.9 slice.720
  886.6 6.6 slice.722
  921.3 6.8 slice.770
  954.2 5.7 pad.226
  966.8 13.2 rev.8
  982.6 5.8 pad.240
  992.0 21.0 rev.9
  1013.1 82.7 %while.26 = (s32[]{:T(128)}, f32[2,2560]{1,0:T(2,128)S(1)}, f32[2,2560]{1,0:T(2,128)S(1)}, f32[2,2560]{1,0:T(2,128)S(1)}, s32[]{:T(128)}) while((s32[]{:T(128)}, f32[2,2560]{1,0:T(2,128)S(1)}, f32[2,2560]{1,0:T(2,128)S(1)}, f32[2,2560]{1,0:T(2,128)S(1)}, s32[]{:T(128)}) %tuple.167), condition=%wide.region_8.9_spmd, body=%wide.region_7.8_spmd.sunk | while | flops 10242 | bytes 163941 | solution.py:191
  1095.8 9.5 convert_reduce_fusion
  1130.0 5.3 copy.81
  1135.4 5.5 multiply_reduce_fusion.4
  1146.4 7.8 scatter-add.19
  1158.1 7.7 scatter-add.20
  1171.2 8.7 bitcast_dynamic-update-slice_fusion.2
  1187.5 10.2 bitcast_dynamic-update-slice_fusion.1
  1197.7 8.6 convolution_dynamic-update-slice_fusion.2
  1206.3 21.2 convolution_dynamic-update-slice_fusion.1
  1227.4 21.1 convolution_dynamic-update-slice_fusion
  1248.6 21.4 bitcast_dynamic-update-slice_fusion
  1270.0 5.1 fusion.93
  1275.2 13.9 fusion.24
  1289.1 6.0 fusion.92
  1295.1 8.9 fusion.30
  1304.0 49.7 %all-reduce.67 = (f32[2560]{0:T(1024)S(1)}, f32[2560]{0:T(1024)S(1)}, f32[2048]{0:T(1024)S(1)}, f32[2048]{0:T(1024)S(1)}) all-reduce(f32[2560]{0:T(1024)S(1)} %copy-done.79, f32[2560]{0:T(1024)S(1)} %copy-done.80, f32[2048]{0:T(1024)S(1)} %get-tuple-element.127, ...), channel_id=6, replica_groups=mesh['seq'=16,'batch'=2] {'seq','batch'}, use_global_device_ids=true, to_apply=%region_21.22.clone | all-reduce | flops 9216 | bytes 73728
  1361.0 22.3 reduce-scatter.15.cloned.1.call-done
  1384.7 1686.4 %reduce-scatter.9.cloned.1.call-done = f32[64,26112]{1,0:T(8,128)} async-done(((f32[2048,26112]{1,0:T(8,128)}), f32[64,26112]{1,0:T(8,128)}) %reduce-scatter.9.cloned.1.call-update) | async-done | bytes 6684688 | tf_op jit(solution)/shard_map/reduce_scatter | solution.py:254
  3078.6 102.7 %reduce-scatter.11.cloned.1.call-done = f32[80,320]{1,0:T(8,128)} async-done(((f32[2560,320]{1,0:T(8,128)}), f32[80,320]{1,0:T(8,128)}) %reduce-scatter.11.cloned.1.call-update) | async-done | bytes 102416 | tf_op jit(solution)/shard_map/reduce_scatter | solution.py:243
  (614 shorter events, 396.7 us)
Async XLA Ops:
  7.2 49.2 %copy-start.100 = (bf16[2,80]{1,0:T(2,128)(2,1)S(1)}, bf16[2,80]{1,0:T(2,128)(2,1)}, u32[]{:S(2)}) copy-start(bf16[2,80]{1,0:T(2,128)(2,1)} %param.40) | copy-start | bytes 964
  7.2 115.4 %copy-start.99 = (bf16[4,80]{1,0:T(4,128)(2,1)S(1)}, bf16[4,80]{1,0:T(4,128)(2,1)}, u32[]{:S(2)}) copy-start(bf16[4,80]{1,0:T(4,128)(2,1)} %param.41) | copy-start | bytes 1924
  7.3 179.2 %copy-start.4 = (bf16[2,128,2048]{2,1,0:T(8,128)(2,1)S(1)}, bf16[2,128,2048]{2,1,0:T(8,128)(2,1)}, u32[]{:S(2)}) copy-start(bf16[2,128,2048]{2,1,0:T(8,128)(2,1)} %param.30) | copy-start | bytes 3145732
  7.3 180.9 %all-gather.10.cloned.1.call-start = ((), (), s32[]{:S(2)}) async-start(), calls=%async_computation.4 | async-start | bytes 10813440 | tf_op jit(solution)/shard_map/all_gather | solution.py:68
  8.0 199.6 %all-gather.12.cloned.1.call-start = ((), (), s32[]{:S(2)}) async-start(), calls=%async_computation.5 | async-start | bytes 2027520 | tf_op jit(solution)/shard_map/all_gather | solution.py:73
  8.7 483.9 %all-gather.14.cloned.1.call-start = ((), (), s32[]{:S(2)}) async-start(), calls=%async_computation.6 | async-start | bytes 10813440 | tf_op jit(solution)/shard_map/all_gather | solution.py:67
  9.5 495.1 %all-gather.16.cloned.1.call-start = ((), (), s32[]{:S(2)}) async-start(), calls=%async_computation.7 | async-start | bytes 10813440 | tf_op jit(solution)/shard_map/all_gather | solution.py:69
  10.1 501.2 %all-gather.20.cloned.1.call-start = ((), (), s32[]{:S(2)}) async-start(), calls=%async_computation.9 | async-start | bytes 25952256 | tf_op jit(solution)/shard_map/all_gather | solution.py:71
  10.6 639.6 %all-gather.18.cloned.1.call-start = ((), (), s32[]{:S(2)}) async-start(), calls=%async_computation.8 | async-start | bytes 25952256 | tf_op jit(solution)/shard_map/all_gather | solution.py:70
  11.2 794.8 %all-gather.22.cloned.1.call-start = ((), (), s32[]{:S(2)}) async-start(), calls=%async_computation.10 | async-start | bytes 25952256 | tf_op jit(solution)/shard_map/all_gather | solution.py:72
  12.0 1347.6 %reduce-scatter.13.cloned.1.call-start = ((), (), s32[]{:S(2)}) async-start(), calls=%async_computation.13 | async-start | bytes 1351680
  56.4 139.0 %copy-start.81 = (bf16[2560]{0:T(1024)(128)(2,1)}, bf16[2560]{0:T(1024)(128)(2,1)S(1)}, u32[]{:S(2)}) copy-start(bf16[2560]{0:T(1024)(128)(2,1)S(1)} %get-tuple-element.156) | copy-start | bytes 15364
  56.4 436.3 %copy-start.47 = (f32[2048]{0:T(1024)}, f32[2048]{0:T(1024)S(1)}, u32[]{:S(2)}) copy-start(f32[2048]{0:T(1024)S(1)} %convert_element_type.109) | copy-start | bytes 24580
  186.8 305.9 %copy-start.63 = (f32[2,128]{1,0:T(2,128)}, f32[2,128]{1,0:T(2,128)S(1)}, u32[]{:S(2)}) copy-start(f32[2,128]{1,0:T(2,128)S(1)} %fusion.70) | copy-start | bytes 3076
  186.9 46.1 %copy-start.96 = (pred[2,128]{1,0:T(4,128)(4,1)}, pred[2,128]{1,0:T(4,128)(4,1)S(1)}, u32[]{:S(2)}) copy-start(pred[2,128]{1,0:T(4,128)(4,1)S(1)} %get-tuple-element.257) | copy-start | bytes 772
  186.9 46.1 %copy-start.61 = (f32[2560]{0:T(1024)}, f32[2560]{0:T(1024)S(1)}, u32[]{:S(2)}) copy-start(f32[2560]{0:T(1024)S(1)} %broadcast_multiply_fusion) | copy-start | bytes 30724
  195.5 2.2 collective-permute-start.2
  196.8 36.2 %copy-start.49 = (f32[2560]{0:T(1024)}, f32[2560]{0:T(1024)S(1)}, u32[]{:S(2)}) copy-start(f32[2560]{0:T(1024)S(1)} %get-tuple-element.134) | copy-start | bytes 30724
  196.8 36.2 %copy-start.51 = (f32[2560]{0:T(1024)}, f32[2560]{0:T(1024)S(1)}, u32[]{:S(2)}) copy-start(f32[2560]{0:T(1024)S(1)} %get-tuple-element.135) | copy-start | bytes 30724
  384.6 2.9 collective-permute-start
  387.5 4.2 collective-permute-start
  391.7 5.7 collective-permute-start
  397.5 5.3 collective-permute-start
  402.8 5.1 collective-permute-start
  407.9 5.1 collective-permute-start
  413.0 5.1 collective-permute-start
  418.2 5.3 collective-permute-start
  423.5 5.5 collective-permute-start
  429.0 5.5 collective-permute-start
  434.6 5.5 collective-permute-start
  440.1 5.5 collective-permute-start
  445.6 5.6 collective-permute-start
  451.2 6.4 collective-permute-start
  457.6 6.2 collective-permute-start
  463.8 22.3 copy-start.44
  464.4 21.7 copy-start.32
  511.0 344.4 %copy-start.23 = (f32[256,2048]{1,0:T(8,128)}, f32[256,2048]{1,0:T(8,128)S(1)}, u32[]{:S(2)}) copy-start(f32[256,2048]{1,0:T(8,128)S(1)} %get-tuple-element.260) | copy-start | bytes 6291460
  511.3 139.0 %copy-start.14 = (bf16[256,2048]{1,0:T(8,128)(2,1)}, bf16[256,2048]{1,0:T(8,128)(2,1)S(1)}, u32[]{:S(2)}) copy-start(bf16[256,2048]{1,0:T(8,128)(2,1)S(1)} %multiply_convert_fusion.3) | copy-start | bytes 3145732
  992.0 103.7 %copy-start.7 = (f32[2,128,2560]{2,1,0:T(8,128)S(1)}, f32[2,128,2560]{2,1,0:T(8,128)}, u32[]{:S(2)}) copy-start(f32[2,128,2560]{2,1,0:T(8,128)} %copy.77) | copy-start | bytes 7864324
  992.0 103.7 %copy-start.50 = (f32[2560]{0:T(1024)S(1)}, f32[2560]{0:T(1024)}, u32[]{:S(2)}) copy-start(f32[2560]{0:T(1024)} %copy-done.49) | copy-start | bytes 30724
  992.0 103.7 %copy-start.52 = (f32[2560]{0:T(1024)S(1)}, f32[2560]{0:T(1024)}, u32[]{:S(2)}) copy-start(f32[2560]{0:T(1024)} %copy-done.51) | copy-start | bytes 30724
  992.0 103.7 %copy-start.62 = (f32[2560]{0:T(1024)S(1)}, f32[2560]{0:T(1024)}, u32[]{:S(2)}) copy-start(f32[2560]{0:T(1024)} %copy-done.61) | copy-start | bytes 30724
  992.0 103.7 %copy-start.65 = (f32[2,1,2560]{2,1,0:T(1,128)S(1)}, f32[2,1,2560]{2,1,0:T(1,128)}, u32[]{:S(2)}) copy-start(f32[2,1,2560]{2,1,0:T(1,128)} %broadcast_in_dim.116) | copy-start | bytes 61444
  992.0 103.7 %copy-start.97 = (pred[2,128]{1,0:T(4,128)(4,1)S(1)}, pred[2,128]{1,0:T(4,128)(4,1)}, u32[]{:S(2)}) copy-start(pred[2,128]{1,0:T(4,128)(4,1)} %copy-done.96) | copy-start | bytes 772
  1013.1 3.1 collective-permute-start.1
  1016.2 4.9 collective-permute-start.1
  1021.1 5.1 collective-permute-start.1
  1026.2 5.1 collective-permute-start.1
  1031.3 5.1 collective-permute-start.1
  1036.4 5.1 collective-permute-start.1
  1041.6 6.0 collective-permute-start.1
  1047.6 6.0 collective-permute-start.1
  1053.6 6.0 collective-permute-start.1
  1059.6 6.0 collective-permute-start.1
  1065.6 6.0 collective-permute-start.1
  1071.7 6.0 collective-permute-start.1
  1077.7 6.0 collective-permute-start.1
  1083.7 6.0 collective-permute-start.1
  1089.7 6.0 collective-permute-start.1
  1108.5 274.7 %reduce-scatter.15.cloned.1.call-start = ((), (), s32[]{:S(2)}) async-start(), calls=%async_computation.14 | async-start | bytes 1351680
  1169.9 14.8 collective-permute-start.3
  1184.7 1886.4 %reduce-scatter.9.cloned.1.call-start = ((), (), s32[]{:S(2)}) async-start(), calls=%async_computation.11 | async-start | bytes 220594176 | tf_op jit(solution)/shard_map/reduce_scatter | solution.py:254
  1270.0 1911.2 %reduce-scatter.11.cloned.1.call-start = ((), (), s32[]{:S(2)}) async-start(), calls=%async_computation.12 | async-start | bytes 4055040 | tf_op jit(solution)/shard_map/reduce_scatter | solution.py:243
  1295.1 60.9 %copy-start.84 = (f32[2,128]{1,0:T(2,128)S(1)}, f32[2,128]{1,0:T(2,128)}, u32[]{:S(2)}) copy-start(f32[2,128]{1,0:T(2,128)} %copy-done.83) | copy-start | bytes 3076
  (84 other events, 477.4 us)
Sparse Core Ops, SparseCore 0:
  11.0 89.9 all-gather.9
  103.9 54.7 all-gather.11
  161.7 85.9 all-gather.13
  250.5 85.3 all-gather.15
  338.6 155.8 all-gather.19
  497.3 152.9 all-gather.17
  653.2 152.8 all-gather.21
  1108.6 140.8 reduce-scatter.12
  1251.9 131.3 reduce-scatter.14
  1389.5 1681.5 reduce-scatter.8
  3078.0 103.2 reduce-scatter.10
where the time goes:
time: 3200 us; the launch traced here: 3190 us
  waiting for transfers between devices  2160 us (68%)
  local copies, waits for them, and re-layouts  357 us (11%)
  matrix products  241 us (8%)
  blocking collectives  222 us (7%)
  other arithmetic  105 us (3%)
  starting transfers between devices  88.9 us (3%)
    reduce_scatter x1, waiting for transfers between devices, shards(): lax.psum_scatter(jnp.concatenate([jnp.concatenate([outer_rows(normed, gra...  1690 us
    all_gather x1, waiting for transfers between devices, shards(): lax.all_gather(w_down, ('seq', 'batch'), axis=0, tiled=True)  141 us
    all_gather x1, waiting for transfers between devices, shards(): lax.all_gather(w_gate, ('seq', 'batch'), axis=0, tiled=True)  124 us
    reduce_scatter x1, waiting for transfers between devices, shards(): lax.psum_scatter(heads_term, ('seq', 'batch'), scatter_dimension=0, tiled...  103 us
    slice x49, local copies, waits for them, and re-layouts, shards(): lax.associative_scan(link, (following, grad_state), reverse=True, axis=1)  98.1 us
    unnamed x2, blocking collectives  92.8 us
    dot_general x6, matrix products, outer_rows(): lax.dot_general(left_side, right_side, rows_contract, preferred_element_t...  91.2 us
    ppermute x32, starting transfers between devices, from_behind(): lax.ppermute(value, axis, [(source, source + steps) for source in range(i...  88.4 us
  transfers between devices with their start and end apart: 43, of which 36 were waited for; matrix products, arithmetic and copies ran while one was open for 15% of the time, Pallas kernels for 0%

commit v1 on v0

v1 whole, which is shorter than its diff:
```python
import functools

import jax
import jax.numpy as jnp
from jax import lax
from jax.experimental import pallas as pl
from jax.experimental.pallas import tpu as pltpu
from jax.sharding import Mesh, PartitionSpec as P

HEADS = 16
WIDTH = 160
LANES = 128
EPS = 1e-6
F32 = jnp.float32
BF16 = jnp.bfloat16
PLANE = ("pair", "core", "batch")
ALL = ("line", "pair", "core", "batch")
VMEM_LIMIT = 60 * 1024 * 1024
MESH = pl.DeviceIdType.MESH
GELU_A = 0.7978845608028654
GELU_B = 0.044715

rows_contract = (((0,), (0,)), ((), ()))
last_contract = (((1,), (1,)), ((), ()))


def outer_rows(left_side, right_side):
    return lax.dot_general(left_side, right_side, rows_contract, preferred_element_type=F32)


def times_back(left_side, weight):
    return lax.dot_general(left_side, weight, last_contract, preferred_element_type=F32)


def times(left_side, weight):
    return jnp.dot(left_side, weight, preferred_element_type=F32)


def gelu_parts(v):
    t = jnp.tanh(GELU_A * (v + GELU_B * v * v * v))
    value = 0.5 * v * (1.0 + t)
    slope = 0.5 * (1.0 + t) + 0.5 * v * (1.0 - t * t) * (GELU_A * (1.0 + 3.0 * GELU_B * v * v))
    return value, slope


def one_less_exp(y):
    series = y * (1 + y / 2 * (1 + y / 3 * (1 + y / 4 * (1 + y / 5 * (1 + y / 6 * (1 + y / 7))))))
    return -jnp.where(y > -0.35, series, jnp.exp(y) - 1.0)


def vmem_call(kernel, outs, scratch=()):
    return pl.pallas_call(
        kernel,
        out_shape=tuple(jax.ShapeDtypeStruct(*o) for o in outs),
        scratch_shapes=list(scratch),
        compiler_params=pltpu.CompilerParams(vmem_limit_bytes=VMEM_LIMIT),
    )


def put(dst, rows, value):
    for c in range(dst.shape[0]):
        piece = value[:, c * LANES : (c + 1) * LANES]
        if piece.shape[1] < LANES:
            piece = jnp.concatenate(
                [piece, jnp.zeros((piece.shape[0], LANES - piece.shape[1]), piece.dtype)], axis=1
            )
        dst[c, rows, :] = piece


def take(src, rows, width):
    return jnp.concatenate([src[c, rows, :] for c in range(src.shape[0])], axis=1)[:, :width]


def split_lanes(value):
    return tuple(value[:, c * LANES : (c + 1) * LANES] for c in range(value.shape[1] // LANES))


def fill_inner(ext, inner, halo, groups, streams, span):
    ext[pl.ds(0, streams), 0:8, :] = halo[...].astype(F32)

    @pl.loop(0, groups)
    def _(g):
        rows = pl.ds(pl.multiple_of(g * span, span), span)
        ext[g, 8 : 8 + span, :] = inner[rows, :].astype(F32)

    @pl.loop(streams, groups)
    def _(g):
        ext[g, 0:8, :] = ext[g - streams, span : span + 8, :]


def gates_kernel(
    groups, streams, span, inner, halo, off, wbd, vec, conv, rate, keep, scale, decay, driven, ends, ext
):
    fill_inner(ext, inner, halo, groups, streams, span)
    width = inner.shape[1]
    tiles = decay.shape[0]
    soft = vec[7:8, :]

    @pl.loop(0, groups)
    def _(g):
        rows = pl.ds(pl.multiple_of(g * span, span), span)
        place = off[rows, :]
        out = jnp.broadcast_to(vec[4:5, :], (span, width)) + vec[0:1, :] * ext[g, 8 : 8 + span, :]
        for k in range(1, 4):
            out = out + jnp.where(place >= k, vec[k : k + 1, :] * ext[g, 8 - k : 8 - k + span, :], 0.0)
        conv[rows, :] = out
        pre = jnp.dot(out.astype(BF16), wbd[...], preferred_element_type=F32)
        rate_g = jax.nn.sigmoid(pre[:, :width] + vec[5:6, :])
        keep_g = jax.nn.sigmoid(pre[:, width:] + vec[6:7, :])
        rate[rows, :] = rate_g
        keep[rows, :] = keep_g
        log_decay = -8.0 * rate_g * soft
        scale_g = jnp.where(place == 0, 1.0, jnp.sqrt(one_less_exp(2.0 * log_decay)))
        scale[rows, :] = scale_g
        put(decay, rows, jnp.where(place == 0, 0.0, jnp.exp(log_decay)))
        put(driven, rows, out * keep_g * scale_g)

    def step(p, carry):
        at = pl.ds(p, groups, stride=span)
        done = []
        for c in range(tiles):
            d = decay[c, at, :]
            done.append((carry[c][0] * d, d * carry[c][1] + driven[c, at, :]))
        return tuple(done)

    one, zero = jnp.ones((groups, LANES), F32), jnp.zeros((groups, LANES), F32)
    done = lax.fori_loop(0, span, step, ((one, zero),) * tiles, unroll=4)
    for c in range(tiles):
        ends[0, :, c * LANES : (c + 1) * LANES] = done[c][0]
        ends[1, :, c * LANES : (c + 1) * LANES] = done[c][1]


def states_kernel(groups, span, decay, driven, enter, branch, states, mixed):
    width = branch.shape[1]

    def step(p, carry):
        at = pl.ds(p, groups, stride=span)
        done = []
        for c in range(len(carry)):
            s = decay[c, at, :] * carry[c] + driven[c, at, :]
            states[c, at, :] = s
            done.append(s)
        return tuple(done)

    lax.fori_loop(0, span, step, split_lanes(enter[...]), unroll=4)

    @pl.loop(0, groups)
    def _(g):
        rows = pl.ds(pl.multiple_of(g * span, span), span)
        mixed[rows, :] = (take(states, rows, width) * gelu_parts(branch[rows, :])[0]).astype(BF16)


def back_ends_kernel(groups, span, grad_mixed, branch, states, decay, grad_state, grad_branch, ends):
    width = branch.shape[1]
    tiles = decay.shape[0]

    @pl.loop(0, groups)
    def _(g):
        rows = pl.ds(pl.multiple_of(g * span, span), span)
        value, slope = gelu_parts(branch[rows, :])
        grad = grad_mixed[rows, :]
        put(grad_state, rows, grad * value)
        grad_branch[rows, :] = (grad * take(states, rows, width) * slope).astype(BF16)

    def step(i, carry):
        at = pl.ds(span - 1 - i, groups, stride=span)
        return tuple(decay[c, at, :] * (grad_state[c, at, :] + carry[c]) for c in range(tiles))

    zero = jnp.zeros((groups, LANES), F32)
    ends[...] = jnp.concatenate(lax.fori_loop(0, span, step, (zero,) * tiles, unroll=4), axis=1)


def back_kernel(
    groups, streams, span,
    grad_state, decay, rate, keep, scale, conv, states, enter, carry_in, inner, halo, off, offx, wbd, vec,
    grad_inner, tail, head, heads, sums,
    adj, ext, gext,
):
    width = inner.shape[1]

    def step(i, carry):
        at = pl.ds(span - 1 - i, groups, stride=span)
        done = []
        for c in range(len(carry)):
            a = grad_state[c, at, :] + carry[c]
            adj[c, at, :] = a
            done.append(decay[c, at, :] * a)
        return tuple(done)

    lax.fori_loop(0, span, step, split_lanes(carry_in[...]), unroll=4)
    fill_inner(ext, inner, halo, groups, streams, span)
    heads[...] = jnp.zeros(heads.shape, F32)
    sums[...] = jnp.zeros(sums.shape, F32)
    first_row = lax.broadcasted_iota(jnp.int32, (span, width), 0) == 0

    @pl.loop(0, groups)
    def _(g):
        rows = pl.ds(pl.multiple_of(g * span, span), span)
        place = off[rows, :]
        adj_g, rate_g, keep_g = take(adj, rows, width), rate[rows, :], keep[rows, :]
        scale_g, conv_g, decay_g = scale[rows, :], conv[rows, :], take(decay, rows, width)
        before = enter[pl.ds(g, 1), :][:, :width]
        prev = jnp.where(first_row, before, pltpu.roll(take(states, rows, width), 1, 0))
        grad_log = jnp.where(
            place > 0,
            adj_g * (decay_g * prev - conv_g * keep_g * (decay_g * decay_g) / scale_g),
            0.0,
        )
        rate_log = grad_log * rate_g
        grad_rate = (rate_log * (-8.0 * vec[7:8, :]) * (1.0 - rate_g)).astype(BF16)
        grad_keep = (adj_g * conv_g * scale_g * keep_g * (1.0 - keep_g)).astype(BF16)
        pre = jnp.concatenate([grad_rate, grad_keep], axis=1)
        grad_conv = adj_g * keep_g * scale_g + lax.dot_general(
            pre, wbd[...], last_contract, preferred_element_type=F32
        )
        heads[...] += lax.dot_general(
            conv_g.astype(BF16), pre, rows_contract, preferred_element_type=F32
        )
        gext[g, 8 : 8 + span, :] = grad_conv
        total = functools.partial(jnp.sum, axis=0, keepdims=True)
        sums[0:1, :] += total(grad_conv * ext[g, 8 : 8 + span, :])
        for k in range(1, 4):
            sums[k : k + 1, :] += total(
                jnp.where(place >= k, grad_conv * ext[g, 8 - k : 8 - k + span, :], 0.0)
            )
        sums[4:5, :] += total(grad_conv)
        sums[5:6, :] += total(grad_rate.astype(F32))
        sums[6:7, :] += total(grad_keep.astype(F32))
        sums[7:8, :] += total(rate_log) * (-8.0 * vec[8:9, :])

    for g in range(groups):
        gext[g, 0:8, :] = jnp.zeros((8, width), F32)
        if g + streams < groups:
            gext[g, 8 + span : 16 + span, :] = gext[g + streams, 8:16, :]
        else:
            gext[g, 8 + span : 16 + span, :] = jnp.zeros((8, width), F32)

    def spread(g, low, count):
        out = vec[0:1, :] * gext[g, low : low + count, :]
        for k in range(1, 4):
            lower = low + k
            out = out + jnp.where(
                offx[g, lower : lower + count, :] >= k,
                vec[k : k + 1, :] * gext[g, lower : lower + count, :],
                0.0,
            )
        return out

    @pl.loop(0, groups)
    def _(g):
        rows = pl.ds(pl.multiple_of(g * span, span), span)
        grad_inner[rows, :] = spread(g, 8, span).astype(BF16)

    for s in range(streams):
        head[s] = spread(s, 0, 8)
        tail[s] = spread(groups - streams + s, span, 8)


def norm_forward(values, gain):
    inverse = lax.rsqrt(jnp.mean(values * values, axis=-1, keepdims=True) + EPS)
    return (values * inverse * gain).astype(BF16)


def norm_back(values, gain, grad):
    inverse = lax.rsqrt(jnp.mean(values * values, axis=-1, keepdims=True) + EPS)
    z = values * inverse
    dz = grad * gain
    gain_grad = jnp.sum(grad * z, axis=0, keepdims=True)
    return inverse * (dz - z * jnp.mean(dz * z, axis=-1, keepdims=True)), gain_grad


def where_am_i():
    z, p, c, b = (lax.axis_index(name) for name in ALL)
    return (z, p, c, b), (z, p, 1 - c, b), (z, 1 - p, c, b), (z, p, c, 1 - b)


def number(place):
    return (place[1] * 2 + place[2]) * 2 + place[3]


def greet(partners):
    barrier = pltpu.get_barrier_semaphore()
    for partner in partners:
        pl.semaphore_signal(barrier, inc=1, device_id=partner, device_id_type=MESH)
    pl.semaphore_wait(barrier, len(partners))


def sender(send_sem, recv_sem):
    def send(k, src, dst, partner):
        copy = pltpu.make_async_remote_copy(
            src_ref=src,
            dst_ref=dst,
            send_sem=send_sem.at[k],
            recv_sem=recv_sem.at[k],
            device_id=partner,
            device_id_type=MESH,
        )
        copy.start()
        return copy

    return send


def block_rows(t, count, low=0, size=None):
    return pl.ds(pl.multiple_of(t * count + low, 16), count if size is None else size)


GATHER_SEMS = 9
REDUCE_SEMS = 10


def gather_start(own, out, send, base, local_sem, spot):
    me, sib, xn, yn = spot
    count = own.shape[0]
    here = out.at[block_rows(number(me), count), :]
    local = pltpu.make_async_copy(own, here, local_sem)
    local.start()
    x = send(base, own, here, xn)
    y = send(base + 1, own, here, yn)
    s = send(base + 2, own, here, sib)
    return local, x, y, s


def gather_finish(started, count, out, send, base, spot):
    me, sib, xn, yn = spot
    local, x, y, s = started
    half = count // 2
    tx, ty = number(xn), number(yn)
    td = number((me[0], 1 - me[1], me[2], 1 - me[3]))
    x.wait_recv()
    top = out.at[block_rows(tx, count, 0, half), :]
    xa = send(base + 3, top, top, yn)
    whole = out.at[block_rows(tx, count), :]
    xs = send(base + 4, whole, whole, sib)
    y.wait_recv()
    low = out.at[block_rows(ty, count, half, half), :]
    yb = send(base + 5, low, low, xn)
    whole = out.at[block_rows(ty, count), :]
    ys = send(base + 6, whole, whole, sib)
    xa.wait_recv()
    top = out.at[block_rows(td, count, 0, half), :]
    da = send(base + 7, top, top, sib)
    yb.wait_recv()
    low = out.at[block_rows(td, count, half, half), :]
    db = send(base + 8, low, low, sib)
    for copy in (s, xs, ys, da, db):
        copy.wait_recv()
    for copy in (x, y, s, xa, xs, yb, ys, da, db):
        copy.wait_send()
    local.wait()


def reduce_plane(pairs, acc, bufs, send, base, spot):
    sib_out, sib_in, s3, s2, s1, keep_a, keep_b, ua0, ua1, ub0, ub2, ta, tb, va, vb = bufs
    me, sib, xn, yn = spot
    count, cols = acc.shape
    half = count // 2
    tile = 512
    dn = (((1,), (1,)), ((), ()))

    def block(r, core, store):
        place = (me[0], me[1] if r < 2 else 1 - me[1], core, me[3] if r % 2 == 0 else 1 - me[3])
        rows = block_rows(number(place), count)

        @pl.loop(0, cols // tile)
        def _(j):
            at = pl.ds(pl.multiple_of(j * tile, tile), tile)
            total = None
            for a, b in pairs:
                part = lax.dot_general(a[rows, :], b[at, :], dn, preferred_element_type=F32)
                total = part if total is None else total + part
            store(at, total)

    def to_sibling(r):
        def store(at, total):
            sib_out[r, :, at] = total.astype(BF16)

        block(r, 1 - me[2], store)
        return send(base + r, sib_out.at[r], sib_in.at[r], sib)

    copies = {}
    for r in (3, 2, 1):
        copies[r] = to_sibling(r)

    copies[3].wait_recv()

    def store3(at, total):
        s3[:, at] = (total + sib_in[3, :, at].astype(F32)).astype(BF16)

    block(3, me[2], store3)
    a3 = send(base + 4, s3.at[pl.ds(0, half), :], ua1, xn)
    b3 = send(base + 5, s3.at[pl.ds(half, half), :], ub2, yn)
    copies[2].wait_recv()

    def store2(at, total):
        total = total + sib_in[2, :, at].astype(F32)
        s2[:, at] = total[:half].astype(BF16)
        keep_b[:, at] = total[half:]

    block(2, me[2], store2)
    a2 = send(base + 6, s2, ua0, xn)
    copies[1].wait_recv()

    def store1(at, total):
        total = total + sib_in[1, :, at].astype(F32)
        s1[:, at] = total[half:].astype(BF16)
        keep_a[:, at] = total[:half]

    block(1, me[2], store1)
    b1 = send(base + 7, s1, ub0, yn)
    copies[0] = to_sibling(0)
    a3.wait_recv()
    ta[...] = (keep_a[...] + ua1[...].astype(F32)).astype(BF16)
    a1 = send(base + 8, ta, va, yn)
    b3.wait_recv()
    tb[...] = (keep_b[...] + ub2[...].astype(F32)).astype(BF16)
    b2 = send(base + 9, tb, vb, xn)
    copies[0].wait_recv()

    def store0(at, total):
        acc[:, at] = total + sib_in[0, :, at].astype(F32)

    block(0, me[2], store0)
    for copy in (a2, b1, a1, b2):
        copy.wait_recv()
    return [copies[r] for r in range(4)] + [a3, b3, a2, b1, a1, b2]


def reduce_buffers(count, cols):
    half = pltpu.VMEM((count // 2, cols), BF16)
    half32 = pltpu.VMEM((count // 2, cols), F32)
    return [
        pltpu.VMEM((count, cols), F32),
        pltpu.VMEM((4, count, cols), BF16),
        pltpu.VMEM((4, count, cols), BF16),
        pltpu.VMEM((count, cols), BF16),
        half, half, half32, half32, half, half, half, half, half, half, half, half,
    ]


def for_total_rows(acc, bufs, body):
    half = acc.shape[0] // 2
    step = 16
    for first, second, start in ((bufs[7], bufs[13], 0), (bufs[9], bufs[14], half)):

        @pl.loop(0, half // step)
        def _(i):
            at = pl.ds(pl.multiple_of(i * step, step), step)
            rows = pl.ds(pl.multiple_of(start + i * step, step), step)
            body(rows, acc[rows, :] + first[at, :].astype(F32) + second[at, :].astype(F32))


def middle_kernel(mixed, weight, tokens, gain, middle, second, own, acc, *rest):
    bufs, (send_sem, recv_sem, local_sem) = rest[:15], rest[15:]
    spot = where_am_i()
    greet(spot[1:])
    send = sender(send_sem, recv_sem)
    open_copies = reduce_plane([(mixed, weight)], acc, bufs, send, 0, spot)

    def body(rows, total):
        value = tokens[rows, :].astype(F32) + total
        middle[rows, :] = value
        own[rows, :] = norm_forward(value, gain[...])

    for_total_rows(acc, bufs, body)
    started = gather_start(own, second, send, REDUCE_SEMS, local_sem, spot)
    gather_finish(started, own.shape[0], second, send, REDUCE_SEMS, spot)
    for copy in open_copies:
        copy.wait_send()


def grad_middle_kernel(
    ga, wa, gb, wb, middle, cot, gain, grad_middle, gain_grad, gathered, own, acc, *rest
):
    bufs, (send_sem, recv_sem, local_sem) = rest[:15], rest[15:]
    spot = where_am_i()
    greet(spot[1:])
    send = sender(send_sem, recv_sem)
    open_copies = reduce_plane([(ga, wa), (gb, wb)], acc, bufs, send, 0, spot)
    gain_grad[...] = jnp.zeros(gain_grad.shape, F32)

    def body(rows, total):
        back, term = norm_back(middle[rows, :], gain[...], total)
        value = cot[rows, :].astype(F32) + back
        grad_middle[rows, :] = value
        own[rows, :] = value.astype(BF16)
        gain_grad[0:1, :] += term

    for_total_rows(acc, bufs, body)
    started = gather_start(own, gathered, send, REDUCE_SEMS, local_sem, spot)
    gather_finish(started, own.shape[0], gathered, send, REDUCE_SEMS, spot)
    for copy in open_copies:
        copy.wait_send()


def input_grad_kernel(ga, wa, gb, wb, tokens, grad_middle, gain, input_grad, gain_grad, acc, *rest):
    bufs, (send_sem, recv_sem) = rest[:15], rest[15:]
    spot = where_am_i()
    greet(spot[1:])
    send = sender(send_sem, recv_sem)
    open_copies = reduce_plane([(ga, wa), (gb, wb)], acc, bufs, send, 0, spot)
    gain_grad[...] = jnp.zeros(gain_grad.shape, F32)

    def body(rows, total):
        back, term = norm_back(tokens[rows, :].astype(F32), gain[...], total)
        input_grad[rows, :] = grad_middle[rows, :] + back
        gain_grad[0:1, :] += term

    for_total_rows(acc, bufs, body)
    for copy in open_copies:
        copy.wait_send()


def plane_peers(me):
    peers = []
    for i in range(1, 8):
        peers.append(
            (
                me[0],
                1 - me[1] if i & 4 else me[1],
                1 - me[2] if i & 2 else me[2],
                1 - me[3] if i & 1 else me[3],
            )
        )
    return peers


def first_kernel(line, mix, out, gain, mix_in, out_in, gains, send_sem, recv_sem, local_sem):
    me = where_am_i()[0]
    t = number(me)
    peers = plane_peers(me)
    others = [(lax.rem(me[0] + k, line),) + me[1:] for k in range(1, line)]
    greet(peers + others)
    send = sender(send_sem, recv_sem)
    row = gains.at[me[0]]
    sent = [send(i, gain, row.at[t], peer) for i, peer in enumerate(peers)]
    locals_ = [
        pltpu.make_async_copy(mix.at[t], mix_in.at[t], local_sem.at[0]),
        pltpu.make_async_copy(out.at[t], out_in.at[t], local_sem.at[1]),
        pltpu.make_async_copy(gain, row.at[t], local_sem.at[2]),
    ]
    for copy in locals_:
        copy.start()
    swaps = []
    for i, peer in enumerate(peers):
        swaps.append(send(7 + i, mix.at[number(peer)], mix_in.at[t], peer))
    for i, peer in enumerate(peers):
        swaps.append(send(14 + i, out.at[number(peer)], out_in.at[t], peer))
    for copy in sent:
        copy.wait_recv()
    locals_[2].wait()
    far = [send(21 + i, row, row, other) for i, other in enumerate(others)]
    for copy in swaps + far:
        copy.wait_recv()
    for copy in sent + swaps + far:
        copy.wait_send()
    locals_[0].wait()
    locals_[1].wait()


def second_kernel(
    tokens, cot, gain, gate, up, down, normed, cot_all, gate_in, up_in, down_in, own, send_sem, recv_sem, local_sem
):
    spot = where_am_i()
    me = spot[0]
    t = number(me)
    peers = plane_peers(me)
    greet(peers)
    send = sender(send_sem, recv_sem)
    count, hid = own.shape[0], gate_in.shape[2]

    @pl.loop(0, count // 16)
    def _(i):
        rows = pl.ds(pl.multiple_of(i * 16, 16), 16)
        own[rows, :] = norm_forward(tokens[rows, :].astype(F32), gain[...])

    base = 21
    started = gather_start(own, normed, send, base, local_sem.at[0], spot)
    gather_finish(started, count, normed, send, base, spot)
    mine = pl.ds(pl.multiple_of(t * hid, LANES), hid)
    locals_ = []
    for k, (src, dst) in enumerate(((gate, gate_in), (up, up_in), (down, down_in))):
        locals_.append(pltpu.make_async_copy(src.at[:, mine], dst.at[t], local_sem.at[1 + k]))
        locals_[-1].start()
    swaps = []
    for k, (src, dst) in enumerate(((gate, gate_in), (up, up_in), (down, down_in))):
        for i, peer in enumerate(peers):
            cols = pl.ds(pl.multiple_of(number(peer) * hid, LANES), hid)
            swaps.append(send(7 * k + i, src.at[:, cols], dst.at[t], peer))
    base = 21 + GATHER_SEMS
    started = gather_start(cot, cot_all, send, base, local_sem.at[4], spot)
    gather_finish(started, count, cot_all, send, base, spot)
    for copy in swaps:
        copy.wait_recv()
    for copy in swaps:
        copy.wait_send()
    for copy in locals_:
        copy.wait()


def gain_kernel(line, parts, result, near, far, mid, send_sem, recv_sem, local_sem):
    me = where_am_i()[0]
    t = number(me)
    peers = plane_peers(me)
    others = [(lax.rem(me[0] + k, line),) + me[1:] for k in range(1, line)]
    greet(peers + others)
    send = sender(send_sem, recv_sem)
    local = pltpu.make_async_copy(parts.at[t], near.at[7], local_sem)
    local.start()
    sent = [send(i, parts.at[number(peer)], near.at[i], peer) for i, peer in enumerate(peers)]
    local.wait()
    for copy in sent:
        copy.wait_recv()
    total = near[7]
    for i in range(7):
        total = total + near[i]
    for z in range(line):
        mid[z] = jnp.broadcast_to(total[z : z + 1, :], mid.shape[1:])
    out = [
        send(7 + k, mid.at[other[0]], far.at[k], other) for k, other in enumerate(others)
    ]
    value = mid[me[0]]
    for copy in out:
        copy.wait_recv()
    for k in range(line - 1):
        value = value + far[k]
    result[...] = value
    for copy in sent + out:
        copy.wait_send()


ANY = pl.BlockSpec(memory_space=pl.ANY)
VMEM = pl.BlockSpec(memory_space=pltpu.VMEM)


def comm_call(kernel, cid, ins, outs, scratch, micros):
    return pl.pallas_call(
        kernel,
        in_specs=list(ins),
        out_shape=tuple(jax.ShapeDtypeStruct(shape, dtype) for shape, dtype, _ in outs),
        out_specs=tuple(spec for _, _, spec in outs),
        scratch_shapes=list(scratch),
        compiler_params=pltpu.CompilerParams(
            collective_id=cid, has_side_effects=True, vmem_limit_bytes=VMEM_LIMIT
        ),
        cost_estimate=pl.CostEstimate(flops=int(micros * 1e9), bytes_accessed=1 << 20, transcendentals=0),
    )


def sems(count):
    return [pltpu.SemaphoreType.DMA((count,)), pltpu.SemaphoreType.DMA((count,))]


def shift_line(value, steps):
    count = lax.axis_size("line")
    low, high = max(0, -steps), min(count, count - steps)
    return lax.ppermute(value, "line", [(i, i + steps) for i in range(low, high)])


def chain(ends, steps):
    count = lax.axis_size("line")
    got = [shift_line(ends, steps * hop) for hop in range(1, count)]
    arriving = jnp.zeros_like(ends[1])
    for part in reversed(got):
        arriving = part[1] + part[0] * arriving
    return arriving


def swap_axis(value, axis):
    return lax.ppermute(value, axis, [(0, 1), (1, 0)])


def halves(value, axis):
    mine = lax.axis_index(axis)
    return (
        lax.dynamic_index_in_dim(value, mine, 0, keepdims=False),
        lax.dynamic_index_in_dim(value, 1 - mine, 0, keepdims=False),
    )


def plane_reduce(value):
    rows = value.shape[0] // 8
    value = value.reshape(2, 2, 2, rows, -1).transpose(1, 0, 2, 3, 4)
    for axis in ("core", "pair", "batch"):
        mine, yours = halves(value, axis)
        value = mine.astype(F32) + swap_axis(yours.astype(BF16), axis).astype(F32)
    return value


def line_gather(value):
    return lax.all_gather(value, "line", axis=0, tiled=True)


def line_reduce(value):
    return lax.psum_scatter(value.astype(BF16), "line", scatter_dimension=0, tiled=True)


def plane_swap(value):
    return lax.all_to_all(value, PLANE, split_axis=0, concat_axis=0, tiled=False)


def shards(
    tokens, cotangent, doc_lengths, w_branch, w_input, w_output, w_gate, w_up, w_down,
    gate_weight, gate_bias, conv_weight, conv_bias, lru_param, mixer_gain, mlp_gain,
):
    streams_own, span, d_model = tokens.shape
    line, batches = lax.axis_size("line"), lax.axis_size("batch")
    places = lax.axis_size("pair") * lax.axis_size("core")
    plane = places * batches
    streams = streams_own * batches
    groups = places * streams
    own = streams_own * span
    own_rows = w_branch.shape[0]
    rw, ff = w_branch.shape[1], w_gate.shape[1]
    width, hid = rw // plane, ff // plane
    my_line = lax.axis_index("line")

    def by_target(weight):
        return weight.reshape(own_rows, plane, width).transpose(1, 0, 2)

    gain_tile = jnp.concatenate([mixer_gain, mlp_gain]).astype(F32)
    gain_tile = jnp.pad(gain_tile, (0, LANES - gain_tile.shape[0]))
    gain_tile = jnp.broadcast_to(gain_tile[None], (8, LANES))
    mix_swapped, out_swapped, gains = comm_call(
        functools.partial(first_kernel, line),
        1,
        [ANY] * 3,
        [
            ((plane, own_rows, 2 * width), BF16, ANY),
            ((plane, own_rows, width), BF16, ANY),
            ((line, plane, 8, LANES), F32, ANY),
        ],
        sems(20 + line) + [pltpu.SemaphoreType.DMA((3,))],
        15,
    )(jnp.concatenate([by_target(w_branch), by_target(w_input)], axis=2), by_target(w_output), gain_tile)
    gains = gains[:, :, 0]
    mixer_scale = gains[:, :, :own_rows].reshape(1, d_model)
    mlp_scale = gains[:, :, own_rows : 2 * own_rows].reshape(1, d_model)
    mixer_in = line_gather(mix_swapped.reshape(plane * own_rows, 2 * width))
    output_w = line_gather(out_swapped.reshape(plane * own_rows, width))
    x = tokens.reshape(own, d_model)
    cot = cotangent.reshape(own, d_model)
    tall = ((plane * own, d_model), BF16, ANY)
    normed, cot_all, gate_s, up_s, down_s = comm_call(
        second_kernel,
        2,
        [VMEM, ANY, VMEM, ANY, ANY, ANY],
        [tall, tall] + [((plane, own_rows, hid), BF16, ANY)] * 3,
        [pltpu.VMEM((own, d_model), BF16)]
        + sems(21 + 2 * GATHER_SEMS)
        + [pltpu.SemaphoreType.DMA((5,))],
        80,
    )(x, cot, mixer_scale, w_gate, w_up, w_down)
    gate_w, up_w, down_w = (
        line_gather(w.reshape(plane * own_rows, hid)) for w in (gate_s, up_s, down_s)
    )
    branch_w, input_w = mixer_in[:, :width], mixer_in[:, width:]

    chunk = gate_bias.shape[1]
    minor = jnp.concatenate(
        [conv_weight, conv_bias[None], gate_bias, lru_param[None]], axis=0
    )
    extra = -(-8 * chunk // (2 * WIDTH))
    spare = extra * 2 * WIDTH - 8 * chunk
    minor = jnp.pad(minor.reshape(8 * chunk), (0, spare)).reshape(extra, 2 * WIDTH)
    packed = jnp.concatenate([gate_weight, minor], axis=0)
    devices = line * plane
    arrived = []
    for k in range(line):
        perm = []
        for z in range(line):
            for t in range(plane):
                perm.append((t * line + (z + k) % line, z * plane + t))
        arrived.append(lax.ppermute(packed, ALL, perm))
    arrived = jnp.roll(jnp.stack(arrived), my_line, axis=0)
    heads_w = arrived[:, :chunk].reshape(width, 2 * WIDTH)
    minor = arrived[:, chunk:].reshape(line, -1)[:, : 8 * chunk].reshape(line, 8, chunk)
    minor = minor.transpose(1, 0, 2).reshape(8, width).astype(F32)
    taps, shift, bias, lru = minor[0:4], minor[4:5], minor[5:7], minor[7:8]
    vec = jnp.concatenate(
        [taps, shift, bias, jax.nn.softplus(lru), jax.nn.sigmoid(lru), jnp.zeros((7, width), F32)], axis=0
    )
    local_heads = width // WIDTH
    wbd = jnp.zeros((width, 2 * width), BF16)
    for h in range(local_heads):
        low = h * WIDTH
        block = heads_w[low : low + WIDTH]
        wbd = wbd.at[low : low + WIDTH, low : low + WIDTH].set(block[:, :WIDTH])
        wbd = wbd.at[low : low + WIDTH, width + low : width + low + WIDTH].set(block[:, WIDTH:])

    their = swap_axis(doc_lengths, "batch")
    first = lax.axis_index("batch") == 0
    both = jnp.concatenate([jnp.where(first, doc_lengths, their), jnp.where(first, their, doc_lengths)], axis=0)
    starts = jnp.cumsum(both, axis=1, dtype=jnp.int32) - both
    spots = (
        (my_line * places + jnp.arange(places, dtype=jnp.int32))[:, None] * span
        + jnp.arange(-8, span + 8, dtype=jnp.int32)[None]
    )
    reached = spots[:, None, :, None] >= starts[None, :, None, :]
    begins = jnp.max(jnp.where(reached, starts[None, :, None, :], 0), axis=3)
    offx = (spots[:, None, :] - begins).reshape(groups, span + 16, 1)
    off = offx[:, 8 : 8 + span].reshape(groups * span, 1)

    count = normed.shape[0]
    inner = times(normed, input_w).astype(BF16)
    branch = times(normed, branch_w)
    inner_tail = inner.reshape(groups, span, width)[groups - streams :, span - 8 :]
    halo = shift_line(inner_tail, 1)
    full = ((count, width), F32)
    tiles = -(-width // LANES)
    wide = tiles * LANES
    tiled = ((tiles, count, LANES), F32)
    conv, rate, keep, scale, decay, driven, ends = vmem_call(
        functools.partial(gates_kernel, groups, streams, span),
        [full] * 4 + [tiled] * 2 + [((2, groups, wide), F32)],
        [pltpu.VMEM((groups, span + 8, width), F32)],
    )(inner, halo, off, wbd, vec)
    by_place = ends.reshape(2, places, streams, wide)
    product, total = by_place[0, 0], by_place[1, 0]
    for q in range(1, places):
        product, total = product * by_place[0, q], by_place[1, q] + by_place[0, q] * total
    arriving = chain(jnp.stack([product, total]), 1)
    enter = []
    for q in range(places):
        enter.append(arriving)
        arriving = by_place[1, q] + by_place[0, q] * arriving
    enter = jnp.concatenate(enter, axis=0)
    states, mixed = vmem_call(
        functools.partial(states_kernel, groups, span), [tiled, ((count, width), BF16)]
    )(decay, driven, enter, branch)
    own32 = ((own, d_model), F32, VMEM)
    middle, second = comm_call(
        middle_kernel,
        3,
        [VMEM] * 4,
        [own32, tall],
        [pltpu.VMEM((own, d_model), BF16)]
        + reduce_buffers(own, d_model)
        + sems(REDUCE_SEMS + GATHER_SEMS)
        + [pltpu.SemaphoreType.DMA],
        80,
    )(mixed, output_w, x, mlp_scale)

    gate_pre = times(second, gate_w)
    up_pre = times(second, up_w)
    grad_hidden = times(cot_all, down_w)
    gate_value, gate_slope = gelu_parts(gate_pre)
    hidden = (gate_value * up_pre).astype(BF16)
    grad_gate = (grad_hidden * up_pre * gate_slope).astype(BF16)
    grad_up = (grad_hidden * gate_value).astype(BF16)
    gain_rows = ((8, d_model), F32, VMEM)
    grad_middle, mlp_gain_term, grad_att = comm_call(
        grad_middle_kernel,
        4,
        [VMEM] * 7,
        [own32, gain_rows, tall],
        [pltpu.VMEM((own, d_model), BF16)]
        + reduce_buffers(own, d_model)
        + sems(REDUCE_SEMS + GATHER_SEMS)
        + [pltpu.SemaphoreType.DMA],
        90,
    )(grad_gate, gate_w, grad_up, up_w, middle, cot, mlp_scale)
    block_output = (middle + plane_reduce(times_back(hidden, down_w))).astype(BF16)
    block_output = block_output.reshape(streams_own, span, d_model)

    def finish(total_rows):
        got = plane_swap(total_rows.reshape(plane, own_rows, -1))
        return got.transpose(1, 0, 2).reshape(own_rows, -1).astype(F32)

    w_gate_grad = finish(line_reduce(outer_rows(second, grad_gate)))
    w_up_grad = finish(line_reduce(outer_rows(second, grad_up)))
    w_down_grad = finish(line_reduce(outer_rows(cot_all, hidden)))

    grad_mixed = times(grad_att, output_w)
    w_output_grad = finish(line_reduce(outer_rows(grad_att, mixed)))
    grad_state, grad_branch, back_ends = vmem_call(
        functools.partial(back_ends_kernel, groups, span),
        [tiled, ((count, width), BF16), ((groups, wide), F32)],
    )(grad_mixed, branch, states, decay)
    back_place = back_ends.reshape(places, streams, wide)
    total = back_place[places - 1]
    for q in range(places - 2, -1, -1):
        total = back_place[q] + by_place[0, q] * total
    arriving = chain(jnp.stack([product, total]), -1)
    carry_in = [None] * places
    for q in range(places - 1, -1, -1):
        carry_in[q] = arriving
        arriving = back_place[q] + by_place[0, q] * arriving
    carry_in = jnp.concatenate(carry_in, axis=0)
    grad_inner, tail, head, heads_full, sums = vmem_call(
        functools.partial(back_kernel, groups, streams, span),
        [
            ((count, width), BF16),
            ((streams, 8, width), F32),
            ((streams, 8, width), F32),
            ((width, 2 * width), F32),
            ((8, width), F32),
        ],
        [
            pltpu.VMEM((tiles, count, LANES), F32),
            pltpu.VMEM((groups, span + 8, width), F32),
            pltpu.VMEM((groups, span + 16, width), F32),
        ],
    )(grad_state, decay, rate, keep, scale, conv, states, enter, carry_in, inner, halo, off, offx, wbd, vec)
    returned = shift_line(head.astype(BF16), -1).astype(F32)
    fixed = (tail + returned).astype(BF16)
    grad_inner = (
        grad_inner.reshape(groups, span, width)
        .at[groups - streams :, span - 8 :]
        .set(fixed)
        .reshape(count, width)
    )
    input_grad, mixer_gain_term = comm_call(
        input_grad_kernel,
        5,
        [VMEM] * 7,
        [own32, gain_rows],
        reduce_buffers(own, d_model) + sems(REDUCE_SEMS),
        50,
    )(grad_branch, branch_w, grad_inner, input_w, x, grad_middle, mixer_scale)
    input_grad = input_grad.reshape(streams_own, span, d_model)
    w_branch_grad = finish(line_reduce(outer_rows(normed, grad_branch)))
    w_input_grad = finish(line_reduce(outer_rows(normed, grad_inner)))

    heads_grad = jnp.concatenate(
        [
            jnp.concatenate(
                [
                    heads_full[h * WIDTH : (h + 1) * WIDTH, h * WIDTH : (h + 1) * WIDTH],
                    heads_full[h * WIDTH : (h + 1) * WIDTH, width + h * WIDTH : width + (h + 1) * WIDTH],
                ],
                axis=1,
            )
            for h in range(local_heads)
        ],
        axis=0,
    )
    out_pack = jnp.concatenate(
        [
            heads_grad.reshape(line, chunk, 2 * WIDTH),
            jnp.pad(
                sums.reshape(8, line, chunk).transpose(1, 0, 2).reshape(line, 8 * chunk), ((0, 0), (0, spare))
            ).reshape(line, extra, 2 * WIDTH),
        ],
        axis=1,
    )
    rolled = jnp.roll(out_pack, -my_line, axis=0)
    summed = None
    for k in range(line):
        perm = []
        for z in range(line):
            for t in range(plane):
                perm.append((z * plane + t, t * line + (z + k) % line))
        got = lax.ppermute(rolled[k], ALL, perm)
        summed = got if summed is None else summed + got
    gate_weight_grad = summed[:chunk]
    minor_grad = summed[chunk:].reshape(-1)[: 8 * chunk].reshape(8, chunk)
    gain_terms = jnp.stack([mixer_gain_term[0], mlp_gain_term[0]], axis=0).reshape(2, line, plane, own_rows)
    gain_terms = gain_terms.transpose(2, 1, 0, 3).reshape(plane, line, 2 * own_rows)
    deep = -(-line // 8) * 8
    gain_terms = jnp.pad(gain_terms, ((0, 0), (0, deep - line), (0, LANES - 2 * own_rows)))
    gain_grads = comm_call(
        functools.partial(gain_kernel, line),
        6,
        [VMEM],
        [((8, LANES), F32, VMEM)],
        [
            pltpu.VMEM((8, deep, LANES), F32),
            pltpu.VMEM((line - 1, 8, LANES), F32),
            pltpu.VMEM((line, 8, LANES), F32),
        ]
        + sems(7 + line - 1)
        + [pltpu.SemaphoreType.DMA],
        10,
    )(gain_terms)[0][0]
    return (
        block_output,
        input_grad,
        w_branch_grad,
        w_input_grad,
        w_output_grad,
        w_gate_grad,
        w_up_grad,
        w_down_grad,
        gate_weight_grad,
        minor_grad[5:7],
        minor_grad[0:4],
        minor_grad[4],
        minor_grad[7],
        gain_grads[:own_rows],
        gain_grads[own_rows : 2 * own_rows],
    )


def solution(mesh):
    seq, batch = mesh.shape["seq"], mesh.shape["batch"]
    grid = Mesh(mesh.devices.reshape(seq // 4, 2, 2, batch), ALL)
    split = P(ALL, None)
    lanes = P(None, ALL)
    act = P("batch", ("line", "pair", "core"), None)
    flat = P(ALL)
    return jax.shard_map(
        shards,
        mesh=grid,
        in_specs=(act, act, P("batch", None)) + (split,) * 7 + (lanes, lanes) + (flat,) * 4,
        out_specs=(act, act) + (split,) * 7 + (lanes, lanes) + (flat,) * 4,
        check_vma=False,
    )
```

time: 3200 us -> 889 us (0.28)
  waiting for transfers between devices: 2160 us -> 50.5 us
  Pallas kernels: 0 us -> 506 us
  local copies, waits for them, and re-layouts: 357 us -> 69 us
  blocking collectives: 222 us -> 0 us
  matrix products: 241 us -> 140 us
  other arithmetic: 105 us -> 22.4 us
    reduce_scatter x2 -> x6, waiting for transfers between devices: 1790 us -> 0.02 us  [line_reduce(): lax.psum_scatter(value.astype(BF16), 'line', scatter_dimension=0, tiled=T...]
    pallas_call x0 -> x10, Pallas kernels: none -> 506 us  [the longest x1 112 us: shards(): comm_call(second_kernel, 2, [VMEM, ANY, VMEM, ANY, ANY, ANY], [tall, tall...]
    all_gather x7 -> x5, waiting for transfers between devices: 265 us -> 0.05 us  [line_gather(): return lax.all_gather(value, 'line', axis=0, tiled=True)]
    slice x102 -> x21, local copies, waits for them, and re-layouts: 171 us -> 9.52 us  [the longest x1 2.47 us: shards(): branch_w, input_w = (mixer_in[:, :width], mixer_in[:, width:])]
    all_gather x2 -> x0, blocking collectives: 130 us -> none  [the longest x1 66.1 us: shards(): lax.all_gather(gate_bias, ('seq', 'batch'), axis=1, tiled=True)]
    unnamed x2 -> x0, blocking collectives: 92.8 us -> none
    ppermute x32 -> x20, waiting for transfers between devices: 75.9 us -> 10.3 us  [the longest x8 10.3 us: shift_line(): lax.ppermute(value, 'line', [(i, i + steps) for i in range(low, high)])]
    pad x48 -> x1, local copies, waits for them, and re-layouts: 62.7 us -> 0.62 us  [shards(): jnp.pad(gain_terms, ((0, 0), (0, deep - line), (0, LANES - 2 * own_rows)))]
  transfers between devices with their start and end apart: 43 -> 37, of which waited for: 36 -> 8; matrix products, arithmetic and copies ran while one was open for 15% -> 19% of each run, Pallas kernels for 0% -> 44%
where the time goes in v1:
time: 889 us; the launch traced here: 878 us
  Pallas kernels  506 us (57%)
  matrix products  140 us (16%)
  starting transfers between devices  75.2 us (8%)
  local copies, waits for them, and re-layouts  69 us (8%)
  waiting for transfers between devices  50.5 us (6%)
  other arithmetic  22.4 us (3%)
  between operations  15.1 us (2%)
    pallas_call x1, Pallas kernels, shards(): comm_call(second_kernel, 2, [VMEM, ANY, VMEM, ANY, ANY, ANY], [tall, tall...  112 us
    pallas_call x1, Pallas kernels, shards(): comm_call(grad_middle_kernel, 4, [VMEM] * 7, [own32, gain_rows, tall], [p...  97.6 us
    pallas_call x1, Pallas kernels, shards(): comm_call(middle_kernel, 3, [VMEM] * 4, [own32, tall], [pltpu.VMEM((own,...  89.6 us
    dot_general x6, matrix products, times(): return jnp.dot(left_side, weight, preferred_element_type=F32)  77.7 us
    dot_general x6, matrix products, outer_rows(): lax.dot_general(left_side, right_side, rows_contract, preferred_element_t...  54.7 us
    pallas_call x1, Pallas kernels, shards(): comm_call(input_grad_kernel, 5, [VMEM] * 7, [own32, gain_rows], reduce_bu...  53.6 us
    pallas_call x1, Pallas kernels, shards(): comm_call(functools.partial(gain_kernel, line), 6, [VMEM], [((8, LANES),...  52 us
    all_to_all x6, waiting for transfers between devices, plane_swap(): lax.all_to_all(value, PLANE, split_axis=0, concat_axis=0, tiled=False)  38.8 us
  transfers between devices with their start and end apart: 37, of which 8 were waited for; matrix products, arithmetic and copies ran while one was open for 19% of the time, Pallas kernels for 44%

profile of v1, /device:TPU:0, one launch (start us, length us, event | category | flops | bytes accessed | tf_op | source)
XLA Modules:
  0.0 878.0 jit_solution(3280436363476392664)
XLA Ops:
  13.8 19.4 %shard_map.271 = (bf16[8,64,640]{2,1,0:T(8,128)(2,1)}, bf16[8,64,320]{2,1,0:T(8,128)(2,1)}, f32[4,8,8,128]{3,2,1,0:T(8,128)}) custom-call(bf16[8,64,640]{2,1,0:T(8,128)(2,1)} %pad_maximum_fusion.mix, bf16[8,64,320]{2,1,0:T(8,128)(2,1)} %bitcast.213, f32[8,128]{1,0:T(8,128)} %broadcast_in_dim.14.gain), custom_call_target="tpu_custom_call" | custom-call | flops 15000000512 | bytes 1048576 | tf_op jit(solution)/shard_map/pallas_call | solution.py:724
  35.7 111.8 %shard_map.272 = (bf16[2048,2048]{1,0:T(8,128)(2,1)}, bf16[2048,2048]{1,0:T(8,128)(2,1)}, bf16[8,64,768]{2,1,0:T(8,128)(2,1)}, bf16[8,64,768]{2,1,0:T(8,128)(2,1)}, bf16[8,64,768]{2,1,0:T(8,128)(2,1)}) custom-call(bf16[256,2048]{1,0:T(8,128)(2,1)} %bitcast.227, bf16[256,2048]{1,0:T(8,128)(2,1)} %bitcast.225, f32[1,2048]{1,0:T(1,128)} %reshape.576.gain, ...), custom_call_target="tpu_custom_call" | custom-call | flops 80000000000 | bytes 1048576 | tf_op jit(solution)/shard_map/pallas_call | solution.py:744
  149.0 7.7 collective-permute-start.3
  158.2 1.9 collective-permute-start.5
  160.2 1.5 collective-permute-start.1
  166.4 2.2 fusion.16
  168.6 8.6 convolution_convert_fusion.3.inner
  177.2 4.5 collective-permute-start
  182.5 3.4 scatter.19
  185.8 1.9 scatter.20
  187.8 1.6 scatter.21.wbd
  190.8 22.5 %shard_map.273 = (f32[2048,320]{1,0:T(8,128)}, f32[2048,320]{1,0:T(8,128)}, f32[2048,320]{1,0:T(8,128)}, f32[2048,320]{1,0:T(8,128)}, f32[3,2048,128]{2,1,0:T(8,...) custom-call(bf16[2048,320]{1,0:T(8,128)(2,1)} %copy-done.4, bf16[4,8,320]{2,1,0:T(8,128)(2,1)} %copy-done.13, ...), custom_call_target="tpu_custom_call" | custom-call | tf_op jit(solution)/shard_map/pallas_call | solution.py:813
  214.7 3.2 collective-permute-start.6
  217.9 1.7 collective-permute-start.7
  219.6 1.5 collective-permute-start.8
  221.2 10.5 %fusion.44.branch = f32[2048,320]{1,0:T(8,128)} fusion(bf16[2048,2048]{1,0:T(8,128)(2,1)} %get-tuple-element.108, bf16[2048,640]{1,0:T(8,128)(2,1)} %all-gather.6.cloned.1.call-done), kind=kOutput, calls=%fused_computation.135 | convolution fusion | flops 2684354560 | bytes 12582912 | tf_op jit(solution)/shard_map/dot_general | solution.py:36
  232.4 13.3 %shard_map.274 = (f32[3,2048,128]{2,1,0:T(8,128)}, bf16[2048,320]{1,0:T(8,128)(2,1)}) custom-call(f32[3,2048,128]{2,1,0:T(8,128)} %get-tuple-element.110.decay, f32[3,2048,128]{2,1,0:T(8,128)} %get-tuple-element.111.driven, f32[16,384]{1,0:T(8,128)} %pad_maximum_fusion.1.enter, f32[2048,320]{1,0:T(8,128)} %fusion.44.branch), custom_call_target="tpu_custom_call" | custom-call | tf_op jit(solution)/shard_map/pallas_call | solution.py:828
  245.7 89.6 %shard_map.275 = (f32[256,2048]{1,0:T(8,128)}, bf16[2048,2048]{1,0:T(8,128)(2,1)}) custom-call(bf16[2048,320]{1,0:T(8,128)(2,1)} %get-tuple-element.113.mixed, bf16[2048,320]{1,0:T(8,128)(2,1)} %all-gather.8.cloned.1.call-done.weight, bf16[256,2048]{1,0:T(8,128)(2,1)} %bitcast.228, f32[1,2048]{1,0:T(1,128)} %reshape.585.gain), custom_call_target="tpu_custom_call" | custom-call | flops 80000000000 | bytes 1048576 | tf_op jit(solution)/shard_map/pallas_call | solution.py:832
  335.3 11.7 %fusion.59 = f32[2048,768]{1,0:T(8,128)} fusion(bf16[2048,2048]{1,0:T(8,128)(2,1)} %get-tuple-element.116, bf16[2048,768]{1,0:T(8,128)(2,1)} %all-gather.12.cloned.1.call-done.wb), kind=kOutput, calls=%fused_computation.144 | convolution fusion | flops 6442450944 | bytes 17825792 | tf_op jit(solution)/shard_map/dot_general | solution.py:36
  347.0 11.6 %fusion.58 = f32[2048,768]{1,0:T(8,128)} fusion(bf16[2048,2048]{1,0:T(8,128)(2,1)} %get-tuple-element.116, bf16[2048,768]{1,0:T(8,128)(2,1)} %all-gather.10.cloned.1.call-done.wa), kind=kOutput, calls=%fused_computation.143 | convolution fusion | flops 6442450944 | bytes 17825792 | tf_op jit(solution)/shard_map/dot_general | solution.py:36
  358.6 26.8 %multiply_convert_fusion = (bf16[2048,768]{1,0:T(8,128)(2,1)}, bf16[2048,768]{1,0:T(8,128)(2,1)}, bf16[2048,768]{1,0:T(8,128)(2,1)}) fusion(f32[2048,768]{1,0:T(8,128)} %fusion.58, f32[2048,768]{1,0:T(8,128)} %fusion.59, bf16[2048,2048]{1,0:T(8,128)(2,1)} %get-tuple-element.120, bf16[2048,768]{1,0:T(8,128)(2,1)} %all-gather.14.cloned.1.call-done), kind=kOutput, calls=%fused_computation.12 | convolution fusion | flops 6481772544 | bytes 33554432 | tf_op jit(solution)/shard_map/dot_general | solution.py:36
  385.4 97.6 %shard_map.276 = (f32[256,2048]{1,0:T(8,128)}, f32[8,2048]{1,0:T(8,128)}, bf16[2048,2048]{1,0:T(8,128)(2,1)}) custom-call(bf16[2048,768]{1,0:T(8,128)(2,1)} %get-tuple-element.148.ga, bf16[2048,768]{1,0:T(8,128)(2,1)} %all-gather.10.cloned.1.call-done.wa, bf16[2048,768]{1,0:T(8,128)(2,1)} %get-tuple-element.147.gb, ...), custom_call_target="tpu_custom_call" | custom-call | flops 89999998976 | bytes 1048576 | tf_op jit(solution)/shard_map/pallas_call | solution.py:852
  483.1 7.5 convolution_convert_fusion.4
  490.7 8.6 fusion.61.grad_mixed
  499.2 16.2 %shard_map.277 = (f32[3,2048,128]{2,1,0:T(8,128)}, bf16[2048,320]{1,0:T(8,128)(2,1)}, f32[16,384]{1,0:T(8,128)}) custom-call(f32[2048,320]{1,0:T(8,128)} %fusion.61.grad_mixed, f32[2048,320]{1,0:T(8,128)} %fusion.44.branch, f32[3,2048,128]{2,1,0:T(8,128)} %get-tuple-element.122.states, f32[3,2048,128]{2,1,0:T(8,128)} %get-tuple-element.110.decay), custom_call_target="tpu_custom_call" | custom-call | tf_op jit(solution)/shard_map/pallas_call | solution.py:876
  515.5 7.9 convolution_convert_fusion.6
  529.2 2.9 collective-permute-done.13
  532.0 2.9 collective-permute-done.14
  535.6 30.1 %shard_map.278 = (bf16[2048,320]{1,0:T(8,128)(2,1)}, f32[4,8,320]{2,1,0:T(8,128)}, f32[4,8,320]{2,1,0:T(8,128)}, f32[320,640]{1,0:T(8,128)}, f32[8,320]{1,0:T(8,128)}) custom-call(f32[3,2048,128]{2,1,0:T(8,128)} %get-tuple-element.124.grad_state, f32[3,2048,128]{2,1,0:T(8,128)} %get-tuple-element.110.decay, f32[2048,320]{1,0:T(8,128)} %get-tuple-element.125.rate, ...), custom_call_target="tpu_custom_call" | custom-call | tf_op jit(solution)/shard_map/pallas_call | solution.py:890
  567.8 4.4 collective-permute-done.15
  573.6 7.9 convolution_convert_fusion.5
  581.7 10.4 %convolution_convert_fusion.2 = bf16[2048,768]{1,0:T(8,128)(2,1)} fusion(bf16[2048,2048]{1,0:T(8,128)(2,1)} %get-tuple-element.116, bf16[2048,768]{1,0:T(8,128)(2,1)S(1)} %copy-done.33), kind=kOutput, calls=%fused_computation.20 | convolution fusion | flops 6444023808 | bytes 14680064 | tf_op jit(solution)/shard_map/dot_general | solution.py:28
  592.2 1.8 copy-done.32
  594.0 10.5 %convolution_convert_fusion.1 = bf16[2048,768]{1,0:T(8,128)(2,1)} fusion(bf16[2048,2048]{1,0:T(8,128)(2,1)} %get-tuple-element.116, bf16[2048,768]{1,0:T(8,128)(2,1)S(1)} %copy-done.32), kind=kOutput, calls=%fused_computation.19 | convolution fusion | flops 6444023808 | bytes 14680064 | tf_op jit(solution)/shard_map/dot_general | solution.py:28
  606.2 2.5 fusion.53
  610.2 7.2 fusion.60
  617.4 5.8 copy-done.3
  623.2 2.6 fusion.8
  625.8 10.5 %convolution_convert_fusion = bf16[2048,768]{1,0:T(8,128)(2,1)} fusion(bf16[2048,2048]{1,0:T(8,128)(2,1)} %get-tuple-element.120, bf16[2048,768]{1,0:T(8,128)(2,1)S(1)} %copy-done.31), kind=kOutput, calls=%fused_computation.18 | convolution fusion | flops 6444023808 | bytes 14680064 | tf_op jit(solution)/shard_map/dot_general | solution.py:28
  638.9 6.3 collective-permute-start.17
  645.5 4.4 collective-permute-start.19
  649.9 53.6 %shard_map.279 = (f32[256,2048]{1,0:T(8,128)}, f32[8,2048]{1,0:T(8,128)}) custom-call(bf16[2048,320]{1,0:T(8,128)(2,1)} %get-tuple-element.123.ga, bf16[2048,320]{1,0:T(8,128)(2,1)} %get-tuple-element.151.wa, bf16[2048,320]{1,0:T(8,128)(2,1)} %bitcast.224, bf16[2048,320]{1,0:T(8,128)(2,1)} %get-tuple-element.150.wb, bf16[256,2048]{1,0:T(8,128)(2,1)} %bitcast.229, ...), custom_call_target="tpu_custom_call" | custom-call | flops 49999998976 | bytes 1048576 | tf_op jit(solution)/shard_map/pallas_call | solution.py:913
  705.3 1.9 copy.105
  707.2 11.5 %all-to-all-start.2 = ((bf16[8,64,320]{2,1,0:T(8,128)(2,1)}), bf16[8,64,320]{2,1,0:T(8,128)(2,1)S(1)}, u32[]{:S(2)}, u32[]{:S(2)}) async-start(bf16[8,64,320]{2,1,0:T(8,128)(2,1)} %bitcast.51), calls=%async_computation.5 | async-start | bytes 786432 | tf_op jit(solution)/shard_map/all_to_all | solution.py:699
  718.7 1.9 copy.101
  720.6 6.0 bitcast_add_fusion
  726.6 3.3 copy-done
  729.9 1.6 fusion.9
  731.6 2.0 collective-permute-start.10
  733.6 3.5 all-to-all-start
  737.0 52.0 %shard_map.280 = f32[8,128]{1,0:T(8,128)} custom-call(f32[8,8,128]{2,1,0:T(8,128)} %pad.27.parts), custom_call_target="tpu_custom_call" | custom-call | flops 10000000000 | bytes 1048576 | tf_op jit(solution)/shard_map/pallas_call | solution.py:962
  790.4 1.9 copy.103
  792.3 3.5 all-to-all-start.1
  797.8 5.3 all-to-all-done.1
  803.1 3.5 all-to-all-start.3
  810.3 8.0 all-to-all-done.3
  818.3 3.5 all-to-all-start.4
  821.9 3.4 bitcast_add_fusion.1
  825.3 2.0 copy-done.1
  828.5 1.9 collective-permute-start.11
  830.4 3.2 all-to-all-done.4
  833.6 3.5 all-to-all-start.5
  841.5 22.3 %all-to-all-done.5 = bf16[8,64,768]{2,1,0:T(8,128)(2,1)S(1)} async-done(((bf16[8,64,768]{2,1,0:T(8,128)(2,1)}), bf16[8,64,768]{2,1,0:T(8,128)(2,1)S(1)}, u32[]{:S(2)}, u32[]{:S(2)}) %all-to-all-start.5) | async-done | bytes 786464 | tf_op jit(solution)/shard_map/all_to_all | solution.py:699
  866.6 3.3 fusion.11
  (232 shorter events, 55.1 us)
Async XLA Ops:
  7.2 5.9 copy-start.28
  7.2 5.9 copy-start.27
  7.2 161.4 %all-gather.6.cloned.1.call-start = ((), (), s32[]{:S(2)}) async-start(), calls=%async_computation.12 | async-start | bytes 3276800 | tf_op jit(solution)/shard_map/all_gather | solution.py:691
  33.2 212.5 %all-gather.8.cloned.1.call-start = ((), (), s32[]{:S(2)}) async-start(), calls=%async_computation.13 | async-start | bytes 1966080 | tf_op jit(solution)/shard_map/all_gather | solution.py:691
  33.9 301.4 %all-gather.12.cloned.1.call-start = ((), (), s32[]{:S(2)}) async-start(), calls=%async_computation.15 | async-start | bytes 3932160 | tf_op jit(solution)/shard_map/all_gather | solution.py:691
  35.6 112.5 %copy-start.19 = (bf16[4,80]{1,0:T(4,128)(2,1)S(1)}, bf16[4,80]{1,0:T(4,128)(2,1)}, u32[]{:S(2)}) copy-start(bf16[4,80]{1,0:T(4,128)(2,1)} %param.37) | copy-start | bytes 1924
  35.6 112.5 %copy-start.21 = (bf16[80]{0:T(256)(128)(2,1)S(1)}, bf16[80]{0:T(256)(128)(2,1)}, u32[]{:S(2)}) copy-start(bf16[80]{0:T(256)(128)(2,1)} %param.39) | copy-start | bytes 484
  35.6 112.5 %copy-start.22 = (bf16[2,80]{1,0:T(2,128)(2,1)S(1)}, bf16[2,80]{1,0:T(2,128)(2,1)}, u32[]{:S(2)}) copy-start(bf16[2,80]{1,0:T(2,128)(2,1)} %param.36) | copy-start | bytes 964
  35.6 112.5 %copy-start.23 = (bf16[80]{0:T(256)(128)(2,1)S(1)}, bf16[80]{0:T(256)(128)(2,1)}, u32[]{:S(2)}) copy-start(bf16[80]{0:T(256)(128)(2,1)} %param.38) | copy-start | bytes 484
  35.7 112.7 %copy-start.15 = (bf16[80,320]{1,0:T(8,128)(2,1)S(1)}, bf16[80,320]{1,0:T(8,128)(2,1)}, u32[]{:S(2)}) copy-start(bf16[80,320]{1,0:T(8,128)(2,1)} %param.35) | copy-start | bytes 153604
  35.7 124.5 %copy-start.20 = (s32[2,4]{1,0:T(2,128)S(1)}, s32[2,4]{1,0:T(2,128)}, u32[]{:S(2)}) copy-start(s32[2,4]{1,0:T(2,128)} %param.28) | copy-start | bytes 100
  35.7 126.7 %copy-start.29 = (s32[2]{0:T(128)S(1)}, s32[2]{0:T(128)}, u32[]{:S(2)}) copy-start(s32[2]{0:T(128)} %constant.222.clone.1) | copy-start | bytes 28
  147.5 199.5 %all-gather.10.cloned.1.call-start = ((), (), s32[]{:S(2)}) async-start(), calls=%async_computation.14 | async-start | bytes 3932160 | tf_op jit(solution)/shard_map/all_gather | solution.py:691
  148.1 210.5 %all-gather.14.cloned.1.call-start = ((), (), s32[]{:S(2)}) async-start(), calls=%async_computation.16 | async-start | bytes 3932160 | tf_op jit(solution)/shard_map/all_gather | solution.py:691
  148.3 17.4 %collective-permute-start.2 = (bf16[82,320]{1,0:T(8,128)(2,1)S(1)}, bf16[82,320]{1,0:T(8,128)(2,1)S(1)}, u32[]{:S(2)}, u32[]{:S(2)}) collective-permute-start(bf16[82,320]{1,0:T(8,128)(2,1)S(1)} %constant_dynamic-update-slice_fusion), channel_id=1, source_target_pairs={{0,0},{4,1},{8,2},{12,3},{16,4},{20,5},{24,6},{28,7},{1,8},{5,9},{... | collective-permute-start | bytes 157448 | tf_op jit(solution)/shard_map/ppermute | solution.py:774
  149.0 16.7 %collective-permute-start.3 = (bf16[82,320]{1,0:T(8,128)(2,1)S(1)}, bf16[82,320]{1,0:T(8,128)(2,1)S(1)}, u32[]{:S(2)}, u32[]{:S(2)}) collective-permute-start(bf16[82,320]{1,0:T(8,128)(2,1)S(1)} %constant_dynamic-update-slice_fusion), channel_id=1, source_target_pairs={{1,0},{5,1},{9,2},{13,3},{17,4},{21,5},{25,6},{29,7},{2,8},{6,9},{... | collective-permute-start | bytes 157448 | tf_op jit(solution)/shard_map/ppermute | solution.py:774
  156.7 9.0 %collective-permute-start.4 = (bf16[82,320]{1,0:T(8,128)(2,1)S(1)}, bf16[82,320]{1,0:T(8,128)(2,1)S(1)}, u32[]{:S(2)}, u32[]{:S(2)}) collective-permute-start(bf16[82,320]{1,0:T(8,128)(2,1)S(1)} %constant_dynamic-update-slice_fusion), channel_id=1, source_target_pairs={{2,0},{6,1},{10,2},{14,3},{18,4},{22,5},{26,6},{30,7},{3,8},{7,9},... | collective-permute-start | bytes 157448 | tf_op jit(solution)/shard_map/ppermute | solution.py:774
  158.2 7.5 collective-permute-start.5
  160.2 3.7 collective-permute-start.1
  161.7 543.5 %reduce-scatter.11.cloned.1.call-start = ((), (), s32[]{:S(2)}) async-start(), calls=%async_computation.19 | async-start | bytes 1638400 | tf_op jit(solution)/shard_map/reduce_scatter | solution.py:695
  177.2 12.3 %copy-start.4 = (bf16[2048,320]{1,0:T(8,128)(2,1)}, bf16[2048,320]{1,0:T(8,128)(2,1)S(1)}, u32[]{:S(2)}) copy-start(bf16[2048,320]{1,0:T(8,128)(2,1)S(1)} %convolution_convert_fusion.3.inner) | copy-start | bytes 3932164
  177.2 12.2 %collective-permute-start = (bf16[4,8,320]{2,1,0:T(8,128)(2,1)S(1)}, bf16[4,8,320]{2,1,0:T(8,128)(2,1)S(1)}, u32[]{:S(2)}, u32[]{:S(2)}) collective-permute-start(bf16[4,8,320]{2,1,0:T(8,128)(2,1)S(1)} %slice.414), channel_id=1, source_target_pairs={{0,8},{8,16},{16,24},{1,9},{9,17},{17,25},{2,10},{10,18},{18,26},{... | collective-permute-start | bytes 61448 | tf_op jit(solution)/shard_map/ppermute | solution.py:657
  214.1 17.6 %copy-start.8 = (f32[2,4,4,384]{3,2,1,0:T(4,128)}, f32[2,4,4,384]{3,2,1,0:T(4,128)S(1)}, u32[]{:S(2)}) copy-start(f32[2,4,4,384]{3,2,1,0:T(4,128)S(1)} %reshape.583) | copy-start | bytes 147460
  214.7 17.0 %collective-permute-start.6 = (f32[2,4,384]{2,1,0:T(4,128)S(1)}, f32[2,4,384]{2,1,0:T(4,128)S(1)}, u32[]{:S(2)}, u32[]{:S(2)}) collective-permute-start(f32[2,4,384]{2,1,0:T(4,128)S(1)} %pad_maximum_fusion.5), channel_id=1, source_target_pairs={{0,8},{8,16},{16,24},{1,9},{9,17},{17,25},{2,10},{10,18},{18,26},{... | collective-permute-start | bytes 36872 | tf_op jit(solution)/shard_map/ppermute | solution.py:657
  217.9 13.8 %collective-permute-start.7 = (f32[2,4,384]{2,1,0:T(4,128)S(1)}, f32[2,4,384]{2,1,0:T(4,128)S(1)}, u32[]{:S(2)}, u32[]{:S(2)}) collective-permute-start(f32[2,4,384]{2,1,0:T(4,128)S(1)} %pad_maximum_fusion.5), channel_id=1, source_target_pairs={{0,16},{8,24},{1,17},{9,25},{2,18},{10,26},{3,19},{11,27},{4,20},{... | collective-permute-start | bytes 36872 | tf_op jit(solution)/shard_map/ppermute | solution.py:657
  219.6 12.1 %collective-permute-start.8 = (f32[2,4,384]{2,1,0:T(4,128)S(1)}, f32[2,4,384]{2,1,0:T(4,128)S(1)}, u32[]{:S(2)}, u32[]{:S(2)}) collective-permute-start(f32[2,4,384]{2,1,0:T(4,128)S(1)} %pad_maximum_fusion.5), channel_id=1, source_target_pairs={{0,24},{1,25},{2,26},{3,27},{4,28},{5,29},{6,30},{7,31}} | collective-permute-start | bytes 36872 | tf_op jit(solution)/shard_map/ppermute | solution.py:657
  385.4 97.6 %copy-start.26 = (bf16[2048,320]{1,0:T(8,128)(2,1)S(1)}, bf16[2048,320]{1,0:T(8,128)(2,1)}, u32[]{:S(2)}) copy-start(bf16[2048,320]{1,0:T(8,128)(2,1)} %get-tuple-element.113.mixed) | copy-start | bytes 3932164
  483.0 7.6 copy-start.25
  490.6 228.1 %reduce-scatter.7.cloned.1.call-start = ((), (), s32[]{:S(2)}) async-start(), calls=%async_computation.17 | async-start | bytes 1638400 | tf_op jit(solution)/shard_map/reduce_scatter | solution.py:695
  515.4 8.0 copy-start.9
  515.4 8.0 copy-start.14
  515.4 8.0 copy-start.17
  515.4 12.2 %copy-start.12 = (s32[16,144,1]{1,0,2:T(8,128)S(1)}, s32[16,144,1]{1,0,2:T(8,128)}, u32[]{:S(2)}) copy-start(s32[16,144,1]{1,0,2:T(8,128)} %copy-done.11) | copy-start | bytes 27652
  523.4 267.0 %reduce-scatter.9.cloned.1.call-start = ((), (), s32[]{:S(2)}) async-start(), calls=%async_computation.18 | async-start | bytes 1638400 | tf_op jit(solution)/shard_map/reduce_scatter | solution.py:695
  523.5 5.7 collective-permute-start.12
  524.8 7.2 collective-permute-start.13
  526.1 8.8 %collective-permute-start.14 = (f32[2,4,384]{2,1,0:T(4,128)S(1)}, f32[2,4,384]{2,1,0:T(4,128)S(1)}, u32[]{:S(2)}, u32[]{:S(2)}) collective-permute-start(f32[2,4,384]{2,1,0:T(4,128)S(1)} %pad_maximum_fusion.4), channel_id=1, source_target_pairs={{24,0},{25,1},{26,2},{27,3},{28,4},{29,5},{30,6},{31,7}} | collective-permute-start | bytes 36872 | tf_op jit(solution)/shard_map/ppermute | solution.py:657
  566.5 5.7 collective-permute-start.15
  573.6 8.0 copy-start.33
  581.6 221.5 %reduce-scatter.13.cloned.1.call-start = ((), (), s32[]{:S(2)}) async-start(), calls=%async_computation.20 | async-start | bytes 3932160 | tf_op jit(solution)/shard_map/reduce_scatter | solution.py:695
  592.1 1.9 copy-start.32
  592.1 218.2 %reduce-scatter.15.cloned.1.call-start = ((), (), s32[]{:S(2)}) async-start(), calls=%async_computation.21 | async-start | bytes 3932160 | tf_op jit(solution)/shard_map/reduce_scatter | solution.py:695
  604.5 225.9 %reduce-scatter.17.cloned.1.call-start = ((), (), s32[]{:S(2)}) async-start(), calls=%async_computation.22 | async-start | bytes 3932160 | tf_op jit(solution)/shard_map/reduce_scatter | solution.py:695
  606.2 3.9 copy-start.24
  606.2 4.0 copy-start.30
  617.4 5.8 copy-start.3
  623.2 2.6 copy-start.31
  625.8 94.8 %collective-permute-start.9 = (bf16[2,2,256,2048]{3,2,1,0:T(8,128)(2,1)}, bf16[2,2,256,2048]{3,2,1,0:T(8,128)(2,1)}, u32[]{:S(2)}, u32[]{:S(2)}) collective-permute-start(bf16[2,2,256,2048]{3,2,1,0:T(8,128)(2,1)} %fusion.8), channel_id=1, source_target_pairs={{0,2},{2,0},{1,3},{3,1},{4,6},{6,4},{5,7},{7,5},{8,10},{10,8},{9,1... | collective-permute-start | bytes 12582920 | tf_op jit(solution)/shard_map/ppermute | solution.py:670
  638.2 157.5 %collective-permute-start.16 = (f32[82,320]{1,0:T(8,128)S(1)}, f32[82,320]{1,0:T(8,128)S(1)}, u32[]{:S(2)}, u32[]{:S(2)}) collective-permute-start(f32[82,320]{1,0:T(8,128)S(1)} %get-tuple-element.158), channel_id=1, source_target_pairs={{0,0},{1,4},{2,8},{3,12},{4,16},{5,20},{6,24},{7,28},{8,1},{9,5},{... | collective-permute-start | bytes 314888 | tf_op jit(solution)/shard_map/ppermute | solution.py:954
  638.9 156.9 %collective-permute-start.17 = (f32[82,320]{1,0:T(8,128)S(1)}, f32[82,320]{1,0:T(8,128)S(1)}, u32[]{:S(2)}, u32[]{:S(2)}) collective-permute-start(f32[82,320]{1,0:T(8,128)S(1)} %get-tuple-element.156), channel_id=1, source_target_pairs={{0,1},{1,5},{2,9},{3,13},{4,17},{5,21},{6,25},{7,29},{8,2},{9,6},{... | collective-permute-start | bytes 314888 | tf_op jit(solution)/shard_map/ppermute | solution.py:954
  645.2 150.6 %collective-permute-start.18 = (f32[82,320]{1,0:T(8,128)S(1)}, f32[82,320]{1,0:T(8,128)S(1)}, u32[]{:S(2)}, u32[]{:S(2)}) collective-permute-start(f32[82,320]{1,0:T(8,128)S(1)} %get-tuple-element.157), channel_id=1, source_target_pairs={{0,2},{1,6},{2,10},{3,14},{4,18},{5,22},{6,26},{7,30},{8,3},{9,7},... | collective-permute-start | bytes 314888 | tf_op jit(solution)/shard_map/ppermute | solution.py:954
  645.5 150.3 %collective-permute-start.19 = (f32[82,320]{1,0:T(8,128)S(1)}, f32[82,320]{1,0:T(8,128)S(1)}, u32[]{:S(2)}, u32[]{:S(2)}) collective-permute-start(f32[82,320]{1,0:T(8,128)S(1)} %get-tuple-element.159), channel_id=1, source_target_pairs={{0,3},{1,7},{2,11},{3,15},{4,19},{5,23},{6,27},{7,31},{8,0},{9,4},... | collective-permute-start | bytes 314888 | tf_op jit(solution)/shard_map/ppermute | solution.py:954
  707.2 26.4 %all-to-all-start.2 = ((bf16[8,64,320]{2,1,0:T(8,128)(2,1)}), bf16[8,64,320]{2,1,0:T(8,128)(2,1)S(1)}, u32[]{:S(2)}, u32[]{:S(2)}) async-start(bf16[8,64,320]{2,1,0:T(8,128)(2,1)} %bitcast.51), calls=%async_computation.5 | async-start | bytes 786432 | tf_op jit(solution)/shard_map/all_to_all | solution.py:699
  726.6 3.3 copy-start
  731.6 90.3 %collective-permute-start.10 = (bf16[2,256,2048]{2,1,0:T(8,128)(2,1)}, bf16[2,256,2048]{2,1,0:T(8,128)(2,1)}, u32[]{:S(2)}, u32[]{:S(2)}) collective-permute-start(bf16[2,256,2048]{2,1,0:T(8,128)(2,1)} %fusion.9), channel_id=1, source_target_pairs={{0,4},{4,0},{1,5},{5,1},{2,6},{6,2},{3,7},{7,3},{8,12},{12,8},{9,1... | collective-permute-start | bytes 6291464 | tf_op jit(solution)/shard_map/ppermute | solution.py:670
  733.6 58.7 %all-to-all-start = ((bf16[8,64,320]{2,1,0:T(8,128)(2,1)}), bf16[8,64,320]{2,1,0:T(8,128)(2,1)S(1)}, u32[]{:S(2)}, u32[]{:S(2)}) async-start(bf16[8,64,320]{2,1,0:T(8,128)(2,1)} %bitcast.47), calls=%async_computation.1 | async-start | bytes 786432 | tf_op jit(solution)/shard_map/all_to_all | solution.py:699
  792.3 10.8 %all-to-all-start.1 = ((bf16[8,64,320]{2,1,0:T(8,128)(2,1)}), bf16[8,64,320]{2,1,0:T(8,128)(2,1)S(1)}, u32[]{:S(2)}, u32[]{:S(2)}) async-start(bf16[8,64,320]{2,1,0:T(8,128)(2,1)} %bitcast.49), calls=%async_computation.3 | async-start | bytes 786432 | tf_op jit(solution)/shard_map/all_to_all | solution.py:699
  803.1 15.2 %all-to-all-start.3 = ((bf16[8,64,768]{2,1,0:T(8,128)(2,1)}), bf16[8,64,768]{2,1,0:T(8,128)(2,1)S(1)}, u32[]{:S(2)}, u32[]{:S(2)}) async-start(bf16[8,64,768]{2,1,0:T(8,128)(2,1)} %bitcast.203), calls=%async_computation.7 | async-start | bytes 1572864 | tf_op jit(solution)/shard_map/all_to_all | solution.py:699
  818.3 15.2 %all-to-all-start.4 = ((bf16[8,64,768]{2,1,0:T(8,128)(2,1)}), bf16[8,64,768]{2,1,0:T(8,128)(2,1)S(1)}, u32[]{:S(2)}, u32[]{:S(2)}) async-start(bf16[8,64,768]{2,1,0:T(8,128)(2,1)} %bitcast.202), calls=%async_computation.9 | async-start | bytes 1572864 | tf_op jit(solution)/shard_map/all_to_all | solution.py:699
  825.3 2.0 copy-start.1
  828.5 36.8 %collective-permute-start.11 = (bf16[256,2048]{1,0:T(8,128)(2,1)}, bf16[256,2048]{1,0:T(8,128)(2,1)}, u32[]{:S(2)}, u32[]{:S(2)}) collective-permute-start(bf16[256,2048]{1,0:T(8,128)(2,1)} %fusion.12), channel_id=1, source_target_pairs={{0,1},{1,0},{2,3},{3,2},{4,5},{5,4},{6,7},{7,6},{8,9},{9,8},{10,11... | collective-permute-start | bytes 3145736 | tf_op jit(solution)/shard_map/ppermute | solution.py:670
  833.6 30.3 %all-to-all-start.5 = ((bf16[8,64,768]{2,1,0:T(8,128)(2,1)}), bf16[8,64,768]{2,1,0:T(8,128)(2,1)S(1)}, u32[]{:S(2)}, u32[]{:S(2)}) async-start(bf16[8,64,768]{2,1,0:T(8,128)(2,1)} %bitcast.207), calls=%async_computation.11 | async-start | bytes 1572864 | tf_op jit(solution)/shard_map/all_to_all | solution.py:699
  863.9 2.8 copy-start.2
  865.3 4.7 copy-start.7
  (7 other events, 7.6 us)
Sparse Core Ops, SparseCore 0:
  33.3 54.1 all-gather.5
  89.0 35.7 all-gather.7
  147.7 66.1 all-gather.11
  215.3 62.5 all-gather.9
  279.3 62.1 all-gather.13
  490.7 28.7 reduce-scatter.10
  523.5 29.2 reduce-scatter.6
  581.7 28.6 reduce-scatter.8
  612.7 74.3 reduce-scatter.12
  689.3 66.6 reduce-scatter.14
  758.3 60.5 reduce-scatter.16

commit v2 on v0

v2 whole, which is shorter than its diff:
```python
import functools

import jax
import jax.numpy as jnp
from jax import lax
from jax.experimental import pallas as pl
from jax.experimental.pallas import tpu as pltpu
from jax.sharding import Mesh, PartitionSpec as P

HEADS = 16
WIDTH = 160
LANES = 128
EPS = 1e-6
F32 = jnp.float32
BF16 = jnp.bfloat16
PLANE = ("pair", "core", "batch")
ALL = ("line", "pair", "core", "batch")
VMEM_LIMIT = 60 * 1024 * 1024
MESH = pl.DeviceIdType.MESH
GELU_A = 0.7978845608028654
GELU_B = 0.044715
FF_FIRST = (0, 512, 768)
FF_SECOND = (512, 256, 768)

rows_contract = (((0,), (0,)), ((), ()))
last_contract = (((1,), (1,)), ((), ()))


def outer_rows(left_side, right_side):
    return lax.dot_general(left_side, right_side, rows_contract, preferred_element_type=F32)


def times_back(left_side, weight):
    return lax.dot_general(left_side, weight, last_contract, preferred_element_type=F32)


def times(left_side, weight):
    return jnp.dot(left_side, weight, preferred_element_type=F32)


def gelu_parts(v):
    t = jnp.tanh(GELU_A * (v + GELU_B * v * v * v))
    value = 0.5 * v * (1.0 + t)
    slope = 0.5 * (1.0 + t) + 0.5 * v * (1.0 - t * t) * (GELU_A * (1.0 + 3.0 * GELU_B * v * v))
    return value, slope


def one_less_exp(y):
    series = y * (1 + y / 2 * (1 + y / 3 * (1 + y / 4 * (1 + y / 5 * (1 + y / 6 * (1 + y / 7))))))
    return -jnp.where(y > -0.35, series, jnp.exp(y) - 1.0)


def put(dst, rows, value):
    for c in range(dst.shape[0]):
        piece = value[:, c * LANES : (c + 1) * LANES]
        if piece.shape[1] < LANES:
            piece = jnp.concatenate(
                [piece, jnp.zeros((piece.shape[0], LANES - piece.shape[1]), piece.dtype)], axis=1
            )
        dst[c, rows, :] = piece


def take(src, rows, width):
    return jnp.concatenate([src[c, rows, :] for c in range(src.shape[0])], axis=1)[:, :width]


def split_lanes(value):
    return tuple(value[:, c * LANES : (c + 1) * LANES] for c in range(value.shape[1] // LANES))


def norm_forward(values, gain):
    inverse = lax.rsqrt(jnp.mean(values * values, axis=-1, keepdims=True) + EPS)
    return (values * inverse * gain).astype(BF16)


def norm_back(values, gain, grad):
    inverse = lax.rsqrt(jnp.mean(values * values, axis=-1, keepdims=True) + EPS)
    z = values * inverse
    dz = grad * gain
    gain_grad = jnp.sum(grad * z, axis=0, keepdims=True)
    return inverse * (dz - z * jnp.mean(dz * z, axis=-1, keepdims=True)), gain_grad


def where_am_i():
    z, p, c, b = (lax.axis_index(name) for name in ALL)
    return (z, p, c, b), (z, p, 1 - c, b), (z, 1 - p, c, b), (z, p, c, 1 - b)


def number(place):
    return (place[1] * 2 + place[2]) * 2 + place[3]


def holder(z, t):
    return (z, t // 4, lax.rem(t // 2, 2), lax.rem(t, 2))


def greet(partners):
    barrier = pltpu.get_barrier_semaphore()
    for partner in partners:
        pl.semaphore_signal(barrier, inc=1, device_id=partner, device_id_type=MESH)
    pl.semaphore_wait(barrier, len(partners))


def sender(send_sem, recv_sem):
    def send(k, src, dst, partner):
        copy = pltpu.make_async_remote_copy(
            src_ref=src,
            dst_ref=dst,
            send_sem=send_sem.at[k],
            recv_sem=recv_sem.at[k],
            device_id=partner,
            device_id_type=MESH,
        )
        copy.start()
        return copy

    return send


def block_rows(t, count, low=0, size=None):
    return pl.ds(pl.multiple_of(t * count + low, 16), count if size is None else size)


GATHER_SEMS = 9
REDUCE_SEMS = 10


def gather_start(own, out, send, base, local_sem, spot):
    me, sib, xn, yn = spot
    count = own.shape[0]
    here = out.at[block_rows(number(me), count), :]
    local = pltpu.make_async_copy(own, here, local_sem)
    local.start()
    x = send(base, own, here, xn)
    y = send(base + 1, own, here, yn)
    s = send(base + 2, own, here, sib)
    return local, x, y, s


def gather_pass(started, count, out, send, base, spot):
    me, sib, xn, yn = spot
    local, x, y, s = started
    half = count // 2
    x.wait_recv()
    top = out.at[block_rows(number(xn), count, 0, half), :]
    xa = send(base + 3, top, top, yn)
    whole = out.at[block_rows(number(xn), count), :]
    xs = send(base + 4, whole, whole, sib)
    y.wait_recv()
    low = out.at[block_rows(number(yn), count, half, half), :]
    yb = send(base + 5, low, low, xn)
    whole = out.at[block_rows(number(yn), count), :]
    ys = send(base + 6, whole, whole, sib)
    return started + (xa, xs, yb, ys)


def gather_end(started, count, out, send, base, spot):
    me, sib, xn, yn = spot
    local, x, y, s, xa, xs, yb, ys = started
    half = count // 2
    td = number((me[0], 1 - me[1], me[2], 1 - me[3]))
    xa.wait_recv()
    top = out.at[block_rows(td, count, 0, half), :]
    da = send(base + 7, top, top, sib)
    yb.wait_recv()
    low = out.at[block_rows(td, count, half, half), :]
    db = send(base + 8, low, low, sib)
    for copy in (s, xs, ys, da, db):
        copy.wait_recv()
    for copy in (x, y, s, xa, xs, yb, ys, da, db):
        copy.wait_send()
    local.wait()


def gather_finish(started, count, out, send, base, spot):
    passed = gather_pass(started, count, out, send, base, spot)
    gather_end(passed, count, out, send, base, spot)


def reduce_plane(pairs, acc, bufs, send, base, spot):
    sib_out, sib_in, s3, s2, s1, keep_a, keep_b, ua0, ua1, ub0, ub2, ta, tb, va, vb = bufs
    me, sib, xn, yn = spot
    count, cols = acc.shape
    half = count // 2
    tile = 512
    dn = (((1,), (1,)), ((), ()))

    def block(r, core, store):
        place = (me[0], me[1] if r < 2 else 1 - me[1], core, me[3] if r % 2 == 0 else 1 - me[3])
        rows = block_rows(number(place), count)

        @pl.loop(0, cols // tile)
        def _(j):
            at = pl.ds(pl.multiple_of(j * tile, tile), tile)
            total = None
            for a, b in pairs:
                part = lax.dot_general(a[rows, :], b[at, :], dn, preferred_element_type=F32)
                total = part if total is None else total + part
            store(at, total)

    def to_sibling(r):
        def store(at, total):
            sib_out[r % 2, :, at] = total.astype(BF16)

        if r < 2:
            copies[r + 2].wait_send()
        block(r, 1 - me[2], store)
        return send(base + r, sib_out.at[r % 2], sib_in.at[r], sib)

    copies = {}
    for r in (3, 2, 1):
        copies[r] = to_sibling(r)

    copies[3].wait_recv()

    def store3(at, total):
        s3[:, at] = (total + sib_in[3, :, at].astype(F32)).astype(BF16)

    block(3, me[2], store3)
    a3 = send(base + 4, s3.at[pl.ds(0, half), :], ua1, xn)
    b3 = send(base + 5, s3.at[pl.ds(half, half), :], ub2, yn)
    copies[2].wait_recv()

    def store2(at, total):
        total = total + sib_in[2, :, at].astype(F32)
        s2[:, at] = total[:half].astype(BF16)
        keep_b[:, at] = total[half:]

    block(2, me[2], store2)
    a2 = send(base + 6, s2, ua0, xn)
    copies[1].wait_recv()

    def store1(at, total):
        total = total + sib_in[1, :, at].astype(F32)
        s1[:, at] = total[half:].astype(BF16)
        keep_a[:, at] = total[:half]

    block(1, me[2], store1)
    b1 = send(base + 7, s1, ub0, yn)
    copies[0] = to_sibling(0)
    yield None
    a3.wait_recv()
    ta[...] = (keep_a[...] + ua1[...].astype(F32)).astype(BF16)
    a1 = send(base + 8, ta, va, yn)
    b3.wait_recv()
    tb[...] = (keep_b[...] + ub2[...].astype(F32)).astype(BF16)
    b2 = send(base + 9, tb, vb, xn)
    copies[0].wait_recv()

    def store0(at, total):
        acc[:, at] = total + sib_in[0, :, at].astype(F32)

    block(0, me[2], store0)
    yield None
    for copy in (a2, b1, a1, b2):
        copy.wait_recv()
    yield [copies[r] for r in range(2)] + [a3, b3, a2, b1, a1, b2]


def reduce_buffers(count, cols):
    half = pltpu.VMEM((count // 2, cols), BF16)
    half32 = pltpu.VMEM((count // 2, cols), F32)
    return [
        pltpu.VMEM((count, cols), F32),
        pltpu.VMEM((2, count, cols), BF16),
        pltpu.VMEM((4, count, cols), BF16),
        pltpu.VMEM((count, cols), BF16),
        half, half, half32, half32, half, half, half, half, half, half, half, half,
    ]


def for_total_rows(acc, bufs, body):
    half = acc.shape[0] // 2
    step = 16
    for first, second, start in ((bufs[7], bufs[13], 0), (bufs[9], bufs[14], half)):

        @pl.loop(0, half // step)
        def _(i):
            at = pl.ds(pl.multiple_of(i * step, step), step)
            rows = pl.ds(pl.multiple_of(start + i * step, step), step)
            body(rows, acc[rows, :] + first[at, :].astype(F32) + second[at, :].astype(F32))


def load_columns(pairs, load_sem):
    loads = []
    for k, (src, low, dst) in enumerate(pairs):
        loads.append(pltpu.make_async_copy(src.at[:, pl.ds(low, dst.shape[1])], dst, load_sem.at[k]))
        loads[-1].start()
    return loads


def middle_kernel(mixed, weight, tokens, gain, middle, second, own, acc, *rest):
    bufs, (send_sem, recv_sem, local_sem) = rest[:15], rest[15:]
    spot = where_am_i()
    greet(spot[1:])
    send = sender(send_sem, recv_sem)
    *_, open_copies = reduce_plane([(mixed, weight)], acc, bufs, send, 0, spot)

    def body(rows, total):
        value = tokens[rows, :].astype(F32) + total
        middle[rows, :] = value
        own[rows, :] = norm_forward(value, gain[...])

    for_total_rows(acc, bufs, body)
    started = gather_start(own, second, send, REDUCE_SEMS, local_sem, spot)
    gather_finish(started, own.shape[0], second, send, REDUCE_SEMS, spot)
    for copy in open_copies:
        copy.wait_send()


def grad_middle_kernel(
    g1, w1, g2, w2, middle, cot, gain, hidden, second, cot_all,
    grad_middle, gain_grad, gathered, outer, own, acc, *rest
):
    bufs, rest = rest[:15], rest[15:]
    send_sem, recv_sem, local_sem, v1, v2, load_sem, left, strip, left_sem, strip_sem = rest
    fill_tile = left.shape[3]
    fill_count = second.shape[1] // fill_tile

    def left_copies(i):
        cols, slot = pl.ds(pl.multiple_of(i * fill_tile, fill_tile), fill_tile), lax.rem(i, 2)
        return [
            pltpu.make_async_copy(src.at[:, cols], left.at[slot, k], left_sem.at[slot, k])
            for k, src in enumerate((second, cot_all))
        ]

    def strip_copy(i):
        slot = lax.rem(i, 2)
        return pltpu.make_async_copy(strip.at[slot], outer.at[block_rows(i, fill_tile), :], strip_sem.at[slot])

    for copy in left_copies(0):
        copy.start()
    loads = load_columns(((w1, 0, v1), (w2, 0, v2)), load_sem)
    spot = where_am_i()
    greet(spot[1:])
    send = sender(send_sem, recv_sem)
    pairs = [(g1, v1), (g2, v2)]
    for copy in loads:
        copy.wait()
    *_, open_copies = reduce_plane(pairs, acc, bufs, send, 0, spot)
    gain_grad[...] = jnp.zeros(gain_grad.shape, F32)

    def body(rows, total):
        back, term = norm_back(middle[rows, :], gain[...], total)
        value = cot[rows, :].astype(F32) + back
        grad_middle[rows, :] = value
        own[rows, :] = value.astype(BF16)
        gain_grad[0:1, :] += term

    for_total_rows(acc, bufs, body)
    started = gather_start(own, gathered, send, REDUCE_SEMS, local_sem, spot)
    size = g2.shape[1]

    @pl.loop(0, fill_count)
    def _(i):
        @pl.when(i + 1 < fill_count)
        def _():
            for copy in left_copies(i + 1):
                copy.start()

        for copy in left_copies(i):
            copy.wait()
        slot = lax.rem(i, 2)

        @pl.when(i >= 2)
        def _():
            strip_copy(i - 2).wait()

        for k, (right, low) in enumerate(((g2, 0), (hidden, size))):
            part = lax.dot_general(left[slot, k], right[...], rows_contract, preferred_element_type=F32)
            strip[slot, :, low : low + right.shape[1]] = part.astype(BF16)
        strip_copy(i).start()

    gather_finish(started, own.shape[0], gathered, send, REDUCE_SEMS, spot)
    strip_copy(fill_count - 2).wait()
    strip_copy(fill_count - 1).wait()
    for copy in open_copies:
        copy.wait_send()


def plane_peers(me):
    peers = []
    for i in range(1, 8):
        peers.append(
            (
                me[0],
                1 - me[1] if i & 4 else me[1],
                1 - me[2] if i & 2 else me[2],
                1 - me[3] if i & 1 else me[3],
            )
        )
    return peers


def first_kernel(line, mix, gain, packed, mix_in, gains, arrived, send_sem, recv_sem, local_sem):
    me = where_am_i()[0]
    t = number(me)
    plane = mix.shape[0]
    peers = plane_peers(me)
    others = [(lax.rem(me[0] + k, line),) + me[1:] for k in range(1, line)]
    index = me[0] * plane + t
    slice_of, chunk_of = index // line, lax.rem(index, line)
    to_self = slice_of == t

    barrier = pltpu.get_barrier_semaphore()
    for partner in peers + others:
        pl.semaphore_signal(barrier, inc=1, device_id=partner, device_id_type=MESH)
    for j in range(line):
        source = t * line + j

        @pl.when(source != index)
        def _():
            partner = holder(source // plane, lax.rem(source, plane))
            pl.semaphore_signal(barrier, inc=1, device_id=partner, device_id_type=MESH)

    pl.semaphore_wait(barrier, len(peers) + 2 * len(others) + jnp.where(to_self, 0, 1))

    send = sender(send_sem, recv_sem)
    row = gains.at[me[0]]
    sent = [send(i, gain, row.at[t], peer) for i, peer in enumerate(peers)]
    locals_ = [
        pltpu.make_async_copy(mix.at[t], mix_in.at[t], local_sem.at[0]),
        pltpu.make_async_copy(gain, row.at[t], local_sem.at[1]),
    ]
    for copy in locals_:
        copy.start()
    swaps = []
    for i, peer in enumerate(peers):
        swaps.append(send(7 + i, mix.at[number(peer)], mix_in.at[t], peer))
    far_base, pack_base = 14, 13 + line

    def pack_copy(k):
        return pltpu.make_async_remote_copy(
            src_ref=packed,
            dst_ref=arrived.at[chunk_of],
            send_sem=send_sem.at[pack_base + k],
            recv_sem=recv_sem.at[pack_base + chunk_of],
            device_id=holder(lax.rem(me[0] + k, line), slice_of),
            device_id_type=MESH,
        )

    for k in range(1, line):
        pack_copy(k).start()
    own_pack = pltpu.make_async_copy(packed, arrived.at[chunk_of], local_sem.at[2])

    @pl.when(to_self)
    def _():
        own_pack.start()

    @pl.when(jnp.logical_not(to_self))
    def _():
        pack_copy(0).start()

    for copy in sent:
        copy.wait_recv()
    locals_[1].wait()
    far = [send(far_base + i, row, row, other) for i, other in enumerate(others)]
    for copy in swaps + far:
        copy.wait_recv()
    for j in range(line):

        @pl.when(t * line + j != index)
        def _():
            pltpu.make_async_remote_copy(
                src_ref=packed,
                dst_ref=arrived.at[j],
                send_sem=send_sem.at[pack_base + j],
                recv_sem=recv_sem.at[pack_base + j],
                device_id=others[0],
                device_id_type=MESH,
            ).wait_recv()

    @pl.when(to_self)
    def _():
        own_pack.wait()

    @pl.when(jnp.logical_not(to_self))
    def _():
        pack_copy(0).wait_send()

    for k in range(1, line):
        pack_copy(k).wait_send()
    for copy in sent + swaps + far:
        copy.wait_send()
    locals_[0].wait()


def swap_start(sources, target, part, send, base, local_sem, me, peers):
    low, size, hid = part
    t = number(me)

    def cols(place):
        return pl.ds(pl.multiple_of(number(place) * hid + low, LANES), size)

    locals_, swaps = [], []
    for k, src in enumerate(sources):
        dst = target.at[t, :, pl.ds(k * size, size)]
        locals_.append(pltpu.make_async_copy(src.at[:, cols(me)], dst, local_sem.at[k]))
        locals_[-1].start()
        for i, peer in enumerate(peers):
            swaps.append(send(base + 7 * k + i, src.at[:, cols(peer)], dst, peer))
    return locals_, swaps


def swap_end(started):
    locals_, swaps = started
    for copy in swaps:
        copy.wait_recv()
    for copy in swaps:
        copy.wait_send()
    for copy in locals_:
        copy.wait()


def second_kernel(tokens, gain, gate, up, down, normed, ff_in, own, send_sem, recv_sem, local_sem):
    spot = where_am_i()
    me = spot[0]
    peers = plane_peers(me)
    greet(peers)
    send = sender(send_sem, recv_sem)
    count = own.shape[0]

    @pl.loop(0, count // 16)
    def _(i):
        rows = pl.ds(pl.multiple_of(i * 16, 16), 16)
        own[rows, :] = norm_forward(tokens[rows, :].astype(F32), gain[...])

    started = gather_start(own, normed, send, 21, local_sem.at[3], spot)
    passed = gather_pass(started, count, normed, send, 21, spot)
    swaps = swap_start((gate, up, down), ff_in, FF_FIRST, send, 0, local_sem, me, peers)
    gather_end(passed, count, normed, send, 21, spot)
    swap_end(swaps)


def last_kernel(
    line, own_rows,
    grads, mixer_w, tokens, grad_middle, gain, mlp_term, pack,
    input_grad, pack_sum, gain_sum,
    *rest,
):
    first, rest = rest[:16], rest[16:]
    held, mixer_term, pack_in, gain_out, near, mid, far, send_sem, recv_sem, load_sem = rest
    spot = where_am_i()
    me = spot[0]
    t = number(me)
    plane = 8
    loads = load_columns(((mixer_w, 0, held),), load_sem)
    peers = plane_peers(me)
    others = [(lax.rem(me[0] + k, line),) + me[1:] for k in range(1, line)]
    index = me[0] * plane + t
    slice_of, to_self = index // line, index // line == t
    barrier = pltpu.get_barrier_semaphore()
    for partner in peers + others:
        pl.semaphore_signal(barrier, inc=1, device_id=partner, device_id_type=MESH)
    for k in range(line):

        def signal(k=k):
            partner = holder(lax.rem(me[0] + k, line), slice_of)
            pl.semaphore_signal(barrier, inc=1, device_id=partner, device_id_type=MESH)

        signal() if k else pl.when(jnp.logical_not(to_self))(signal)
    pl.semaphore_wait(barrier, len(peers) + 2 * len(others) + jnp.where(to_self, 0, 1))

    send = sender(send_sem, recv_sem)
    pack_base = REDUCE_SEMS

    def pack_copy(j, slot):
        target = t * line + j
        return pltpu.make_async_remote_copy(
            src_ref=pack.at[j],
            dst_ref=pack_in.at[slot],
            send_sem=send_sem.at[pack_base + j],
            recv_sem=recv_sem.at[pack_base + slot],
            device_id=holder(target // plane, lax.rem(target, plane)),
            device_id_type=MESH,
        )

    for j in range(line):
        own_pack = pltpu.make_async_copy(pack.at[j], pack_in.at[me[0]], load_sem.at[1])
        pl.when(t * line + j != index)(pack_copy(j, me[0]).start)
        pl.when(t * line + j == index)(own_pack.start)
    loads[0].wait()
    *_, open_a = reduce_plane([(grads, held)], first[0], first[1:], send, 0, spot)
    mixer_term[...] = jnp.zeros(mixer_term.shape, F32)

    def body(rows, total):
        back, term = norm_back(tokens[rows, :].astype(F32), gain[...], total)
        input_grad[rows, :] = grad_middle[rows, :] + back
        mixer_term[0:1, :] += term

    for_total_rows(first[0], first[1:], body)
    per = plane * own_rows
    for z in range(line):
        for q in range(per // LANES):
            cols = slice(z * per + q * LANES, z * per + (q + 1) * LANES)
            gain_out[q, 2 * z : 2 * z + 1, :] = mixer_term[0:1, cols]
            gain_out[q, 2 * z + 1 : 2 * z + 2, :] = mlp_term[0:1, cols]
    gain_base = pack_base + line

    def tile_of(place):
        return number(place) * own_rows // LANES

    sent = [send(gain_base + i, gain_out.at[tile_of(peer)], near.at[i], peer) for i, peer in enumerate(peers)]
    for copy in sent:
        copy.wait_recv()
    total = gain_out[tile_of(me)]
    for i in range(7):
        total = total + near[i]
    for z in range(line):
        mid[z] = jnp.concatenate([total[2 * z : 2 * z + 2], jnp.zeros((6, LANES), F32)], axis=0)
    out = [send(gain_base + 7 + k, mid.at[other[0]], far.at[k], other) for k, other in enumerate(others)]
    for z in range(line):
        source_is_me = jnp.logical_and(to_self, me[0] == z)
        pl.when(jnp.logical_not(source_is_me))(pack_copy(z, z).wait_recv)
        own_pack = pltpu.make_async_copy(pack.at[z], pack_in.at[z], load_sem.at[1])
        pl.when(source_is_me)(own_pack.wait)
    total = pack_in[0]
    for z in range(1, line):
        total = total + pack_in[z]
    pack_sum[...] = total
    value = mid[me[0]]
    for copy in out:
        copy.wait_recv()
    for k in range(line - 1):
        value = value + far[k]
    gain_sum[...] = value
    for copy in open_a + sent + out:
        copy.wait_send()
    for j in range(line):
        pl.when(t * line + j != index)(pack_copy(j, me[0]).wait_send)


def chain_exchange(msg, arrived, send, base, me, line, direction):
    sent = []
    for k in range(1, line):
        to = (lax.rem(me[0] + direction * k + line, line),) + me[1:]
        sent.append(send(base + k - 1, msg, arrived.at[k - 1], to))
    return sent


def chain_value(arrived, me, line, direction, streams):
    value = jnp.zeros((streams, arrived.shape[2]), F32)
    for k in range(line - 1, 0, -1):
        there = me[0] >= k if direction > 0 else me[0] + k < line
        part = arrived[k - 1]
        value = jnp.where(there, part[8 : 8 + streams] + part[:streams] * value, value)
    return value


def mixer_forward_kernel(
    line, groups, streams, span,
    normed, mix_w, off, wbd, vec, cot, gate, up, down,
    branch, inner, conv, rate, keep, scale, decay, states, mixed, enter, ends, halo, cot_all, ff_in,
    driven, ext, tail_out, tail_in, chain_out, chain_in, send_sem, recv_sem, local_sem,
):
    spot = where_am_i()
    me = spot[0]
    peers = plane_peers(me)
    others = [(lax.rem(me[0] + k, line),) + me[1:] for k in range(1, line)]
    greet(peers + others)
    send = sender(send_sem, recv_sem)
    gather_base, halo_base = 21, 21 + GATHER_SEMS
    count = cot.shape[0]
    started = gather_start(cot, cot_all, send, gather_base, local_sem.at[3], spot)
    swaps = swap_start((gate, up, down), ff_in, FF_SECOND, send, 0, local_sem, me, peers)

    width = inner.shape[1]
    tiles = decay.shape[0]
    soft = vec[7:8, :]
    place_rows = streams * span

    def project(q):
        rows = block_rows(q, place_rows)
        both = jnp.dot(normed[rows, :], mix_w[:, : 2 * width], preferred_element_type=F32)
        branch[rows, :] = both[:, :width]
        part = both[:, width:].astype(BF16)
        inner[rows, :] = part
        for j in range(streams):
            ext[q * streams + j, 8 : 8 + span, :] = part[j * span : (j + 1) * span].astype(F32)

    last = groups // streams - 1
    project(last)
    pad = jnp.zeros((8, tail_out.shape[1] - width), F32)
    for j in range(streams):
        rows = ext[last * streams + j, span : span + 8, :]
        tail_out[8 * j : 8 * j + 8, :] = jnp.concatenate([rows, pad], axis=1)
    following = (lax.rem(me[0] + 1, line),) + me[1:]
    halo_copy = send(halo_base, tail_out, tail_in, following)
    for q in range(last):
        project(q)
    halo_copy.wait_recv()
    halo[...] = jnp.where(me[0] > 0, tail_in[...], 0.0)
    for j in range(streams):
        ext[j, 0:8, :] = halo[8 * j : 8 * j + 8, :width]
    for g in range(streams, groups):
        ext[g, 0:8, :] = ext[g - streams, span : span + 8, :]

    @pl.loop(0, groups)
    def _(g):
        rows = block_rows(g, span)
        place = off[rows, :]
        out = jnp.broadcast_to(vec[4:5, :], (span, width)) + vec[0:1, :] * ext[g, 8 : 8 + span, :]
        for k in range(1, 4):
            out = out + jnp.where(place >= k, vec[k : k + 1, :] * ext[g, 8 - k : 8 - k + span, :], 0.0)
        conv[rows, :] = out
        pre = jnp.dot(out.astype(BF16), wbd[...], preferred_element_type=F32)
        rate_g = jax.nn.sigmoid(pre[:, :width] + vec[5:6, :])
        keep_g = jax.nn.sigmoid(pre[:, width:] + vec[6:7, :])
        rate[rows, :] = rate_g
        keep[rows, :] = keep_g
        log_decay = -8.0 * rate_g * soft
        scale_g = jnp.where(place == 0, 1.0, jnp.sqrt(one_less_exp(2.0 * log_decay)))
        scale[rows, :] = scale_g
        put(decay, rows, jnp.where(place == 0, 0.0, jnp.exp(log_decay)))
        put(driven, rows, out * keep_g * scale_g)

    passed = gather_pass(started, count, cot_all, send, gather_base, spot)

    def step(p, carry):
        at = pl.ds(p, groups, stride=span)
        done = []
        for c in range(tiles):
            d = decay[c, at, :]
            done.append((carry[c][0] * d, d * carry[c][1] + driven[c, at, :]))
        return tuple(done)

    one, zero = jnp.ones((groups, LANES), F32), jnp.zeros((groups, LANES), F32)
    done = lax.fori_loop(0, span, step, ((one, zero),) * tiles, unroll=4)
    products = jnp.concatenate([part[0] for part in done], axis=1)
    totals = jnp.concatenate([part[1] for part in done], axis=1)
    ends[...] = products
    product, total = products[:streams], totals[:streams]
    for q in range(1, groups // streams):
        at = slice(q * streams, (q + 1) * streams)
        product, total = product * products[at], totals[at] + products[at] * total
    chain_out[0:streams, :] = product
    chain_out[8 : 8 + streams, :] = total
    chains = chain_exchange(chain_out, chain_in, send, halo_base + 1, me, line, 1)
    for copy in chains:
        copy.wait_recv()
    arriving = chain_value(chain_in, me, line, 1, streams)
    for q in range(groups // streams):
        at = slice(q * streams, (q + 1) * streams)
        enter[at, :] = arriving
        arriving = totals[at] + products[at] * arriving

    def walk(p, carry):
        at = pl.ds(p, groups, stride=span)
        done = []
        for c in range(tiles):
            s = decay[c, at, :] * carry[c] + driven[c, at, :]
            states[c, at, :] = s
            done.append(s)
        return tuple(done)

    lax.fori_loop(0, span, walk, split_lanes(enter[...]), unroll=4)

    @pl.loop(0, groups)
    def _(g):
        rows = block_rows(g, span)
        mixed[rows, :] = (take(states, rows, width) * gelu_parts(branch[rows, :])[0]).astype(BF16)

    gather_end(passed, count, cot_all, send, gather_base, spot)
    swap_end(swaps)
    for copy in [halo_copy] + chains:
        copy.wait_send()


def mixer_back_kernel(
    line, groups, streams, span,
    grad_att, out_w, branch, states, decay, rate, keep, scale, conv, enter, products, inner, halo, off, offx, wbd, vec,
    hidden_a, part_a, hidden_b, part_b, middle,
    grads, heads, sums, block_output,
    fetch, adj, ext, gext, head_out, head_in, chain_out, chain_in, kept, held_a, held_b, *rest,
):
    (acc, *bufs), (send_sem, recv_sem, local_sem, load_sem, kept_sem) = rest[:16], rest[16:]
    spot = where_am_i()
    me = spot[0]
    size_a, size_b = held_a.shape[1], held_b.shape[1]
    loads = load_columns(((part_a, 2 * size_a, held_a), (part_b, 2 * size_b, held_b)), load_sem)

    def kept_copies(g):
        rows, slot = block_rows(g, span), lax.rem(g, 2)
        return [
            pltpu.make_async_copy(src.at[rows, :], kept.at[slot, k], kept_sem.at[slot, k])
            for k, src in enumerate((rate, keep, scale, conv))
        ]

    for copy in kept_copies(0):
        copy.start()
    others = [(lax.rem(me[0] + k, line),) + me[1:] for k in range(1, line)]
    greet(list(spot[1:]) + others)
    send = sender(send_sem, recv_sem)
    for copy in loads:
        copy.wait()
    mlp = reduce_plane([(hidden_a, held_a), (hidden_b, held_b)], acc, bufs, send, line, spot)
    next(mlp)
    width = inner.shape[1]
    tiles = decay.shape[0]
    place_rows = streams * span
    places = groups // streams
    some = fetch.shape[1]
    pieces = groups * span // some

    def load(q):
        copy = pltpu.make_async_copy(grad_att.at[block_rows(q, some), :], fetch.at[q % 2], local_sem.at[q % 2])
        copy.start()
        return copy

    copies = [load(0)]
    for q in range(pieces):
        if q + 1 < pieces:
            copies.append(load(q + 1))
        copies[q].wait()
        put(adj, block_rows(q, some), jnp.dot(fetch[q % 2], out_w[...], preferred_element_type=F32))

    @pl.loop(0, groups)
    def _(g):
        rows = block_rows(g, span)
        value, slope = gelu_parts(branch[rows, :])
        grad = take(adj, rows, width)
        grads[rows, :width] = (grad * take(states, rows, width) * slope).astype(BF16)
        put(adj, rows, grad * value)

    next(mlp)

    def step(i, carry):
        at = pl.ds(span - 1 - i, groups, stride=span)
        return tuple(decay[c, at, :] * (adj[c, at, :] + carry[c]) for c in range(tiles))

    zero = jnp.zeros((groups, LANES), F32)
    totals = jnp.concatenate(lax.fori_loop(0, span, step, (zero,) * tiles, unroll=4), axis=1)
    prods = products[...]
    at = slice((places - 1) * streams, places * streams)
    product, total = prods[at], totals[at]
    for q in range(places - 2, -1, -1):
        at = slice(q * streams, (q + 1) * streams)
        product, total = product * prods[at], totals[at] + prods[at] * total
    chain_out[0:streams, :] = product
    chain_out[8 : 8 + streams, :] = total
    chains = chain_exchange(chain_out, chain_in, send, 1, me, line, -1)
    for j in range(streams):
        ext[j, 0:8, :] = halo[8 * j : 8 * j + 8, :width]

    @pl.loop(0, groups)
    def _(g):
        ext[g, 8 : 8 + span, :] = inner[block_rows(g, span), :].astype(F32)

    for g in range(streams, groups):
        ext[g, 0:8, :] = ext[g - streams, span : span + 8, :]
    heads[...] = jnp.zeros(heads.shape, F32)
    sums[...] = jnp.zeros(sums.shape, F32)
    for copy in chains:
        copy.wait_recv()
    arriving = chain_value(chain_in, me, line, -1, streams)
    carry_in = [None] * places
    for q in range(places - 1, -1, -1):
        at = slice(q * streams, (q + 1) * streams)
        carry_in[q] = arriving
        arriving = totals[at] + prods[at] * arriving

    def walk(i, carry):
        at = pl.ds(span - 1 - i, groups, stride=span)
        done = []
        for c in range(tiles):
            a = adj[c, at, :] + carry[c]
            adj[c, at, :] = a
            done.append(decay[c, at, :] * a)
        return tuple(done)

    lax.fori_loop(0, span, walk, split_lanes(jnp.concatenate(carry_in, axis=0)), unroll=4)
    first_row = lax.broadcasted_iota(jnp.int32, (span, width), 0) == 0

    @pl.loop(0, groups)
    def _(g):
        rows = block_rows(g, span)
        place = off[rows, :]

        @pl.when(g + 1 < groups)
        def _():
            for copy in kept_copies(g + 1):
                copy.start()

        for copy in kept_copies(g):
            copy.wait()
        slot = lax.rem(g, 2)
        adj_g, rate_g, keep_g = take(adj, rows, width), kept[slot, 0], kept[slot, 1]
        scale_g, conv_g, decay_g = kept[slot, 2], kept[slot, 3], take(decay, rows, width)
        before = enter[pl.ds(g, 1), :][:, :width]
        prev = jnp.where(first_row, before, pltpu.roll(take(states, rows, width), 1, 0))
        grad_log = jnp.where(
            place > 0,
            adj_g * (decay_g * prev - conv_g * keep_g * (decay_g * decay_g) / scale_g),
            0.0,
        )
        rate_log = grad_log * rate_g
        grad_rate = (rate_log * (-8.0 * vec[7:8, :]) * (1.0 - rate_g)).astype(BF16)
        grad_keep = (adj_g * conv_g * scale_g * keep_g * (1.0 - keep_g)).astype(BF16)
        pre = jnp.concatenate([grad_rate, grad_keep], axis=1)
        grad_conv = adj_g * keep_g * scale_g + lax.dot_general(
            pre, wbd[...], last_contract, preferred_element_type=F32
        )
        heads[...] += lax.dot_general(
            conv_g.astype(BF16), pre, rows_contract, preferred_element_type=F32
        )
        gext[g, 8 : 8 + span, :] = grad_conv
        total = functools.partial(jnp.sum, axis=0, keepdims=True)
        sums[0:1, :] += total(grad_conv * ext[g, 8 : 8 + span, :])
        for k in range(1, 4):
            sums[k : k + 1, :] += total(
                jnp.where(place >= k, grad_conv * ext[g, 8 - k : 8 - k + span, :], 0.0)
            )
        sums[4:5, :] += total(grad_conv)
        sums[5:6, :] += total(grad_rate.astype(F32))
        sums[6:7, :] += total(grad_keep.astype(F32))
        sums[7:8, :] += total(rate_log) * (-8.0 * vec[8:9, :])

    for g in range(groups):
        gext[g, 0:8, :] = jnp.zeros((8, width), F32)
        if g + streams < groups:
            gext[g, 8 + span : 16 + span, :] = gext[g + streams, 8:16, :]
        else:
            gext[g, 8 + span : 16 + span, :] = jnp.zeros((8, width), F32)

    def spread(g, low, count):
        out = vec[0:1, :] * gext[g, low : low + count, :]
        for k in range(1, 4):
            lower = low + k
            out = out + jnp.where(
                offx[g, lower : lower + count, :] >= k,
                vec[k : k + 1, :] * gext[g, lower : lower + count, :],
                0.0,
            )
        return out

    pad = jnp.zeros((8, head_out.shape[1] - width), F32)
    for j in range(streams):
        head_out[8 * j : 8 * j + 8, :] = jnp.concatenate([spread(j, 0, 8), pad], axis=1)
    previous = (lax.rem(me[0] + line - 1, line),) + me[1:]
    head_copy = send(0, head_out, head_in, previous)
    open_mlp = next(mlp)

    def body(rows, total):
        block_output[rows, :] = (middle[rows, :] + total).astype(BF16)

    for_total_rows(acc, bufs, body)

    @pl.loop(0, groups)
    def _(g):
        grads[block_rows(g, span), width:] = spread(g, 8, span).astype(BF16)

    head_copy.wait_recv()
    for j in range(streams):
        g = groups - streams + j
        more = jnp.where(me[0] + 1 < line, head_in[8 * j : 8 * j + 8, :width], 0.0)
        ending = spread(g, span - 8, 16) + jnp.concatenate([jnp.zeros((8, width), F32), more], axis=0)
        grads[g * span + span - 16 : (g + 1) * span, width:] = ending.astype(BF16)
    for copy in [head_copy] + chains + open_mlp:
        copy.wait_send()


def ff_kernel(second, cot, gate_w, up_w, down_w, grads, hidden):
    size = hidden.shape[1]
    gate_pre = jnp.dot(second[...], gate_w[...], preferred_element_type=F32)
    up_pre = jnp.dot(second[...], up_w[...], preferred_element_type=F32)
    grad_hidden = jnp.dot(cot[...], down_w[...], preferred_element_type=F32)
    value, slope = gelu_parts(gate_pre)
    hidden[...] = (value * up_pre).astype(BF16)
    grads[:, :size] = (grad_hidden * up_pre * slope).astype(BF16)
    grads[:, size:] = (grad_hidden * value).astype(BF16)


def ff_call(second, cot, weights):
    count, d_model = second.shape
    size = weights.shape[1] // 3
    tile = 256
    tokens = pl.BlockSpec((tile, d_model), lambda i: (i, 0))

    def weight(k):
        return pl.BlockSpec((d_model, size), lambda i: (0, k), pipeline_mode=pl.Buffered(1))

    return pl.pallas_call(
        ff_kernel,
        grid=(count // tile,),
        in_specs=[tokens, tokens, weight(0), weight(1), weight(2)],
        out_specs=(
            pl.BlockSpec((tile, 2 * size), lambda i: (i, 0)),
            pl.BlockSpec((tile, size), lambda i: (i, 0)),
        ),
        out_shape=(
            jax.ShapeDtypeStruct((count, 2 * size), BF16),
            jax.ShapeDtypeStruct((count, size), BF16),
        ),
        compiler_params=pltpu.CompilerParams(vmem_limit_bytes=VMEM_LIMIT),
        cost_estimate=pl.CostEstimate(
            flops=6 * count * d_model * size, bytes_accessed=4 * count * d_model, transcendentals=0
        ),
    )(second, cot, weights, weights, weights)


def outer_kernel(*refs):
    out, pairs = refs[-1], refs[:-1]
    low = 0
    for a, b in zip(pairs[::2], pairs[1::2]):
        size = b.shape[1]
        part = lax.dot_general(a[...], b[...], rows_contract, preferred_element_type=F32)
        out[:, low : low + size] = part.astype(BF16)
        low += size


def outer_call(*pairs):
    count, d_model = pairs[0].shape
    tile = 256
    sizes = [b.shape[1] for b in pairs[1::2]]
    specs = []
    for size in sizes:
        specs.append(pl.BlockSpec((count, tile), lambda i: (0, i)))
        specs.append(pl.BlockSpec((count, size), lambda i: (0, 0), pipeline_mode=pl.Buffered(1)))
    return pl.pallas_call(
        outer_kernel,
        grid=(d_model // tile,),
        in_specs=specs,
        out_specs=pl.BlockSpec((tile, sum(sizes)), lambda i: (i, 0)),
        out_shape=jax.ShapeDtypeStruct((d_model, sum(sizes)), BF16),
        compiler_params=pltpu.CompilerParams(vmem_limit_bytes=VMEM_LIMIT),
        cost_estimate=pl.CostEstimate(
            flops=2 * count * d_model * sum(sizes),
            bytes_accessed=2 * count * (d_model * len(sizes) + sum(sizes)),
            transcendentals=0,
        ),
    )(*pairs)


ANY = pl.BlockSpec(memory_space=pl.ANY)
VMEM = pl.BlockSpec(memory_space=pltpu.VMEM)


def comm_call(kernel, cid, ins, outs, scratch, micros):
    return pl.pallas_call(
        kernel,
        in_specs=list(ins),
        out_shape=tuple(jax.ShapeDtypeStruct(shape, dtype) for shape, dtype, _ in outs),
        out_specs=tuple(spec for _, _, spec in outs),
        scratch_shapes=list(scratch),
        compiler_params=pltpu.CompilerParams(
            collective_id=cid, has_side_effects=True, vmem_limit_bytes=VMEM_LIMIT
        ),
        cost_estimate=pl.CostEstimate(flops=int(micros * 1e9), bytes_accessed=1 << 20, transcendentals=0),
    )


def sems(count):
    return [pltpu.SemaphoreType.DMA((count,)), pltpu.SemaphoreType.DMA((count,))]


def swap_axis(value, axis):
    return lax.ppermute(value, axis, [(0, 1), (1, 0)])


def line_gather(value):
    return lax.all_gather(value, "line", axis=0, tiled=True)


def line_reduce(value):
    return lax.psum_scatter(value.astype(BF16), "line", scatter_dimension=0, tiled=True)


def plane_swap(value):
    return lax.all_to_all(value, PLANE, split_axis=0, concat_axis=0, tiled=False)


def shards(
    tokens, cotangent, doc_lengths, w_branch, w_input, w_output, w_gate, w_up, w_down,
    gate_weight, gate_bias, conv_weight, conv_bias, lru_param, mixer_gain, mlp_gain,
):
    streams_own, span, d_model = tokens.shape
    line, batches = lax.axis_size("line"), lax.axis_size("batch")
    places = lax.axis_size("pair") * lax.axis_size("core")
    plane = places * batches
    streams = streams_own * batches
    groups = places * streams
    own = streams_own * span
    own_rows = w_branch.shape[0]
    rw, ff = w_branch.shape[1], w_gate.shape[1]
    width, hid = rw // plane, ff // plane
    my_line = lax.axis_index("line")

    def by_target(weight):
        return weight.reshape(own_rows, plane, width).transpose(1, 0, 2)

    gain_tile = jnp.concatenate([mixer_gain, mlp_gain]).astype(F32)
    gain_tile = jnp.pad(gain_tile, (0, LANES - gain_tile.shape[0]))
    gain_tile = jnp.broadcast_to(gain_tile[None], (8, LANES))
    chunk = gate_bias.shape[1]
    minor = jnp.concatenate([conv_weight, conv_bias[None], gate_bias, lru_param[None]], axis=0)
    extra = -(-8 * chunk // (2 * WIDTH))
    spare = extra * 2 * WIDTH - 8 * chunk
    minor = jnp.pad(minor.reshape(8 * chunk), (0, spare)).reshape(extra, 2 * WIDTH)
    pack_rows = -(-(chunk + extra) // 16) * 16
    packed = jnp.concatenate(
        [gate_weight, minor, jnp.zeros((pack_rows - chunk - extra, 2 * WIDTH), BF16)], axis=0
    )
    mix_swapped, gains, arrived = comm_call(
        functools.partial(first_kernel, line),
        1,
        [ANY] * 3,
        [
            ((plane, own_rows, 3 * width), BF16, ANY),
            ((line, plane, 8, LANES), F32, ANY),
            ((line, pack_rows, 2 * WIDTH), BF16, ANY),
        ],
        sems(13 + 2 * line) + [pltpu.SemaphoreType.DMA((3,))],
        15,
    )(
        jnp.concatenate([by_target(w) for w in (w_branch, w_input, w_output)], axis=2),
        gain_tile,
        packed,
    )
    gains = gains[:, :, 0]
    mixer_scale = gains[:, :, :own_rows].reshape(1, d_model)
    mlp_scale = gains[:, :, own_rows : 2 * own_rows].reshape(1, d_model)
    mixer_w = line_gather(mix_swapped.reshape(plane * own_rows, 3 * width))
    output_w = mixer_w[:, 2 * width :]
    x = tokens.reshape(own, d_model)
    cot = cotangent.reshape(own, d_model)
    tall = ((plane * own, d_model), BF16, ANY)

    def swapped(part):
        return [((plane, own_rows, 3 * part[1]), BF16, ANY)]

    normed, first_part = comm_call(
        second_kernel,
        2,
        [VMEM, VMEM, ANY, ANY, ANY],
        [tall] + swapped(FF_FIRST),
        [pltpu.VMEM((own, d_model), BF16)] + sems(21 + GATHER_SEMS) + [pltpu.SemaphoreType.DMA((4,))],
        60,
    )(x, mixer_scale, w_gate, w_up, w_down)

    heads_w = arrived[:, :chunk].reshape(width, 2 * WIDTH)
    minor = arrived[:, chunk : chunk + extra].reshape(line, -1)[:, : 8 * chunk].reshape(line, 8, chunk)
    minor = minor.transpose(1, 0, 2).reshape(8, width).astype(F32)
    taps, shift, bias, lru = minor[0:4], minor[4:5], minor[5:7], minor[7:8]
    vec = jnp.concatenate(
        [taps, shift, bias, jax.nn.softplus(lru), jax.nn.sigmoid(lru), jnp.zeros((7, width), F32)], axis=0
    )
    local_heads = width // WIDTH
    head_row = jnp.arange(width, dtype=jnp.int32)[:, None] // WIDTH
    wbd = jnp.concatenate(
        [
            jnp.where(head_row == h, heads_w[:, low : low + WIDTH], jnp.zeros((), BF16))
            for low in (0, WIDTH)
            for h in range(local_heads)
        ],
        axis=1,
    )

    their = swap_axis(doc_lengths, "batch")
    first = lax.axis_index("batch") == 0
    both = jnp.concatenate([jnp.where(first, doc_lengths, their), jnp.where(first, their, doc_lengths)], axis=0)
    starts = jnp.cumsum(both, axis=1, dtype=jnp.int32) - both
    spots = (
        (my_line * places + jnp.arange(places, dtype=jnp.int32))[:, None] * span
        + jnp.arange(-8, span + 8, dtype=jnp.int32)[None]
    )
    reached = spots[:, None, :, None] >= starts[None, :, None, :]
    begins = jnp.max(jnp.where(reached, starts[None, :, None, :], 0), axis=3)
    offx = (spots[:, None, :] - begins).reshape(groups, span + 16, 1)
    off = offx[:, 8 : 8 + span].reshape(groups * span, 1)

    count = plane * own
    tiles = -(-width // LANES)
    wide = tiles * LANES
    full = ((count, width), F32, VMEM)
    short = ((count, width), BF16, VMEM)
    tiled = ((tiles, count, LANES), F32, VMEM)
    edge = ((8 * streams, wide), F32)
    (
        branch, inner, conv, rate, keep, scale, decay, states, mixed, enter, ends, halo, cot_all, second_part
    ) = comm_call(
        functools.partial(mixer_forward_kernel, line, groups, streams, span),
        3,
        [VMEM] * 5 + [ANY] * 4,
        [full, short, full, full, full, full, tiled, tiled, short]
        + [((groups, wide), F32, VMEM)] * 2
        + [edge + (VMEM,), tall]
        + swapped(FF_SECOND),
        [
            pltpu.VMEM((tiles, count, LANES), F32),
            pltpu.VMEM((groups, span + 8, width), F32),
            pltpu.VMEM(*edge),
            pltpu.VMEM(*edge),
            pltpu.VMEM((16, wide), F32),
            pltpu.VMEM((line - 1, 16, wide), F32),
        ]
        + sems(21 + GATHER_SEMS + line)
        + [pltpu.SemaphoreType.DMA((4,))],
        50,
    )(normed, mixer_w, off, wbd, vec, cot, w_gate, w_up, w_down)

    parts = [line_gather(w.reshape(plane * own_rows, w.shape[2])) for w in (first_part, second_part)]
    own32 = ((own, d_model), F32, VMEM)
    middle, second = comm_call(
        middle_kernel,
        4,
        [VMEM] * 4,
        [own32, tall],
        [pltpu.VMEM((own, d_model), BF16)]
        + reduce_buffers(own, d_model)
        + sems(REDUCE_SEMS + GATHER_SEMS)
        + [pltpu.SemaphoreType.DMA],
        80,
    )(mixed, output_w, x, mlp_scale)

    grads_a, hidden_a = ff_call(second, cot_all, parts[0])
    sums_a = outer_call(second, grads_a, cot_all, hidden_a)
    second, sums_a = lax.optimization_barrier((second, sums_a))
    grads_b, hidden_b = ff_call(second, cot_all, parts[1])
    gain_rows = ((8, d_model), F32, VMEM)
    grad_middle, mlp_gain_term, grad_att, sums_b = comm_call(
        grad_middle_kernel,
        5,
        [VMEM, ANY, VMEM, ANY] + [VMEM] * 4 + [ANY] * 2,
        [own32, gain_rows, tall, ((d_model, 3 * FF_SECOND[1]), BF16, ANY)],
        [pltpu.VMEM((own, d_model), BF16)]
        + reduce_buffers(own, d_model)
        + sems(REDUCE_SEMS + GATHER_SEMS)
        + [
            pltpu.SemaphoreType.DMA,
            pltpu.VMEM((d_model, 2 * FF_FIRST[1]), BF16),
            pltpu.VMEM((d_model, 2 * FF_SECOND[1]), BF16),
            pltpu.SemaphoreType.DMA((2,)),
            pltpu.VMEM((2, 2, count, 256), BF16),
            pltpu.VMEM((2, 256, 3 * FF_SECOND[1]), BF16),
            pltpu.SemaphoreType.DMA((2, 2)),
            pltpu.SemaphoreType.DMA((2,)),
        ],
        90,
    )(grads_a, parts[0], grads_b, parts[1], middle, cot, mlp_scale, hidden_b, second, cot_all)
    ff_sums = [line_reduce(sums_a), line_reduce(sums_b)]
    def finish(total_rows, count_of):
        got = plane_swap(total_rows.reshape(plane, own_rows, -1)).reshape(plane, own_rows, count_of, -1)
        return [got[:, :, k] for k in range(count_of)]

    def widen(pieces):
        return jnp.concatenate(pieces, axis=2).transpose(1, 0, 2).reshape(own_rows, -1).astype(F32)

    grad_att, ff_sums[0] = lax.optimization_barrier((grad_att, ff_sums[0]))
    grads_mix, heads_full, sums, block_output = comm_call(
        functools.partial(mixer_back_kernel, line, groups, streams, span),
        6,
        [ANY] + [VMEM] * 4 + [ANY] * 4 + [VMEM] * 9 + [ANY, VMEM, ANY, VMEM],
        [
            ((count, 2 * width), BF16, VMEM),
            ((width, 2 * width), F32, VMEM),
            ((8, width), F32, VMEM),
            ((own, d_model), BF16, VMEM),
        ],
        [
            pltpu.VMEM((2, 256, d_model), BF16),
            pltpu.VMEM((tiles, count, LANES), F32),
            pltpu.VMEM((groups, span + 8, width), F32),
            pltpu.VMEM((groups, span + 16, width), F32),
            pltpu.VMEM(*edge),
            pltpu.VMEM(*edge),
            pltpu.VMEM((16, wide), F32),
            pltpu.VMEM((line - 1, 16, wide), F32),
            pltpu.VMEM((2, 4, span, width), F32),
            pltpu.VMEM((d_model, FF_FIRST[1]), BF16),
            pltpu.VMEM((d_model, FF_SECOND[1]), BF16),
        ]
        + reduce_buffers(own, d_model)
        + sems(line + REDUCE_SEMS)
        + [pltpu.SemaphoreType.DMA((2,))] * 2
        + [pltpu.SemaphoreType.DMA((2, 4))],
        70,
    )(
        grad_att, output_w, branch, states, decay, rate, keep, scale, conv, enter, ends, inner, halo, off, offx,
        wbd, vec, hidden_a, parts[0], hidden_b, parts[1], middle,
    )
    (w_output_grad,) = (widen([p]) for p in finish(line_reduce(outer_call(grad_att, mixed)), 1))
    grads_mix, ff_sums[1] = lax.optimization_barrier((grads_mix, ff_sums[1]))
    sums_mix = outer_call(normed, grads_mix)
    grads_mix, sums_mix = lax.optimization_barrier((grads_mix, sums_mix))
    halves_a, halves_b = (finish(total, 3) for total in ff_sums)
    w_gate_grad, w_up_grad, w_down_grad = (widen([p, q]) for p, q in zip(halves_a, halves_b))

    w_branch_grad, w_input_grad = (widen([p]) for p in finish(line_reduce(sums_mix), 2))

    heads_grad = jnp.concatenate(
        [
            jnp.concatenate(
                [
                    heads_full[h * WIDTH : (h + 1) * WIDTH, h * WIDTH : (h + 1) * WIDTH],
                    heads_full[h * WIDTH : (h + 1) * WIDTH, width + h * WIDTH : width + (h + 1) * WIDTH],
                ],
                axis=1,
            )
            for h in range(local_heads)
        ],
        axis=0,
    )
    pack_rows = -(-(chunk + extra) // 8) * 8
    minor_pack = sums.reshape(8, line, chunk).transpose(1, 0, 2).reshape(line, 8 * chunk)
    minor_pack = jnp.pad(minor_pack, ((0, 0), (0, spare))).reshape(line, extra, 2 * WIDTH)
    out_pack = jnp.concatenate([heads_grad.reshape(line, chunk, 2 * WIDTH), minor_pack], axis=1)
    out_pack = jnp.pad(out_pack, ((0, 0), (0, pack_rows - chunk - extra), (0, 0)))
    pack32 = (pack_rows, 2 * WIDTH)
    gain_tiles = plane * own_rows // LANES
    deep = -(-2 * line // 8) * 8
    input_grad, summed, gain_sum = comm_call(
        functools.partial(last_kernel, line, own_rows),
        7,
        [VMEM, ANY] + [VMEM] * 5,
        [own32, (pack32, F32, VMEM), ((8, LANES), F32, VMEM)],
        reduce_buffers(own, d_model)
        + [
            pltpu.VMEM((d_model, 2 * width), BF16),
            pltpu.VMEM((8, d_model), F32),
            pltpu.VMEM((line,) + pack32, F32),
            pltpu.VMEM((gain_tiles, deep, LANES), F32),
            pltpu.VMEM((7, deep, LANES), F32),
            pltpu.VMEM((line, 8, LANES), F32),
            pltpu.VMEM((line - 1, 8, LANES), F32),
        ]
        + sems(REDUCE_SEMS + line + 7 + line - 1)
        + [pltpu.SemaphoreType.DMA((2,))],
        60,
    )(
        grads_mix, mixer_w, x, grad_middle, mixer_scale, mlp_gain_term, out_pack,
    )
    input_grad = input_grad.reshape(streams_own, span, d_model)
    block_output = block_output.reshape(streams_own, span, d_model)
    gate_weight_grad = summed[:chunk]
    minor_grad = summed[chunk : chunk + extra].reshape(-1)[: 8 * chunk].reshape(8, chunk)
    low = lax.rem((lax.axis_index("pair") * 2 + lax.axis_index("core")) * 2 + lax.axis_index("batch"), LANES // own_rows)
    gain_grads = lax.dynamic_slice(gain_sum, (0, low * own_rows), (2, own_rows))
    return (
        block_output,
        input_grad,
        w_branch_grad,
        w_input_grad,
        w_output_grad,
        w_gate_grad,
        w_up_grad,
        w_down_grad,
        gate_weight_grad,
        minor_grad[5:7],
        minor_grad[0:4],
        minor_grad[4],
        minor_grad[7],
        gain_grads[0],
        gain_grads[1],
    )


def solution(mesh):
    seq, batch = mesh.shape["seq"], mesh.shape["batch"]
    grid = Mesh(mesh.devices.reshape(seq // 4, 2, 2, batch), ALL)
    split = P(ALL, None)
    lanes = P(None, ALL)
    act = P("batch", ("line", "pair", "core"), None)
    flat = P(ALL)
    return jax.shard_map(
        shards,
        mesh=grid,
        in_specs=(act, act, P("batch", None)) + (split,) * 7 + (lanes, lanes) + (flat,) * 4,
        out_specs=(act, act) + (split,) * 7 + (lanes, lanes) + (flat,) * 4,
        check_vma=False,
    )
```

time: 3200 us -> 692 us (0.22)
  waiting for transfers between devices: 2160 us -> 18.3 us
  Pallas kernels: 0 us -> 577 us
  local copies, waits for them, and re-layouts: 357 us -> 45.8 us
  matrix products: 241 us -> 0 us
  blocking collectives: 222 us -> 0 us
  other arithmetic: 105 us -> 8.66 us
  starting transfers between devices: 88.9 us -> 16.2 us
    reduce_scatter x2 -> x4, waiting for transfers between devices: 1790 us -> 0.04 us  [line_reduce(): lax.psum_scatter(value.astype(BF16), 'line', scatter_dimension=0, tiled=T...]
    pallas_call x0 -> x12, Pallas kernels: none -> 577 us  [the longest x1 98.9 us: shards(): comm_call(grad_middle_kernel, 5, [VMEM, ANY, VMEM, ANY] + [VMEM] * 4 + [A...]
    all_gather x7 -> x3, waiting for transfers between devices: 265 us -> 11.7 us  [line_gather(): return lax.all_gather(value, 'line', axis=0, tiled=True)]
    dot_general x21 -> x0, matrix products: 241 us -> none  [the longest x6 91.2 us: outer_rows(): lax.dot_general(left_side, right_side, rows_contract, preferred_element_t...]
    slice x102 -> x18, local copies, waits for them, and re-layouts: 171 us -> 14.1 us  [the longest x3 5.74 us: finish(): return [got[:, :, k] for k in range(count_of)]]
    all_gather x2 -> x0, blocking collectives: 130 us -> none  [the longest x1 66.1 us: shards(): lax.all_gather(gate_bias, ('seq', 'batch'), axis=1, tiled=True)]
    unnamed x2 -> x0, blocking collectives: 92.8 us -> none
    ppermute x32 -> x1, starting transfers between devices: 88.4 us -> 0.71 us  [swap_axis(): return lax.ppermute(value, axis, [(0, 1), (1, 0)])]
  transfers between devices with their start and end apart: 43 -> 12, of which waited for: 36 -> 3; matrix products, arithmetic and copies ran while one was open for 15% -> 6% of each run, Pallas kernels for 0% -> 81%
where the time goes in v2:
time: 692 us; the launch traced here: 681 us
  Pallas kernels  577 us (83%)
  local copies, waits for them, and re-layouts  45.8 us (7%)
  waiting for transfers between devices  18.3 us (3%)
  starting transfers between devices  16.2 us (2%)
  between operations  15.1 us (2%)
  other arithmetic  8.66 us (1%)
    pallas_call x1, Pallas kernels, shards(): comm_call(grad_middle_kernel, 5, [VMEM, ANY, VMEM, ANY] + [VMEM] * 4 + [A...  98.9 us
    pallas_call x1, Pallas kernels, shards(): comm_call(functools.partial(last_kernel, line, own_rows), 7, [VMEM, ANY]...  88.8 us
    pallas_call x1, Pallas kernels, shards(): comm_call(middle_kernel, 4, [VMEM] * 4, [own32, tall], [pltpu.VMEM((own,...  88.1 us
    pallas_call x1, Pallas kernels, shards(): comm_call(functools.partial(mixer_back_kernel, line, groups, streams, spa...  78.4 us
    pallas_call x1, Pallas kernels, shards(): comm_call(functools.partial(mixer_forward_kernel, line, groups, streams,...  64.5 us
    pallas_call x1, Pallas kernels, shards(): comm_call(second_kernel, 2, [VMEM, VMEM, ANY, ANY, ANY], [tall] + swapped...  60.5 us
    pallas_call x3, Pallas kernels, outer_call(): pl.pallas_call(outer_kernel, grid=(d_model // tile,), in_specs=specs, out...  41.9 us
    pallas_call x2, Pallas kernels, ff_call(): pl.pallas_call(ff_kernel, grid=(count // tile,), in_specs=[tokens, tokens...  33.5 us
  transfers between devices with their start and end apart: 12, of which 3 were waited for; matrix products, arithmetic and copies ran while one was open for 6% of the time, Pallas kernels for 81%

profile of v2, /device:TPU:0, one launch (start us, length us, event | category | flops | bytes accessed | tf_op | source)
XLA Modules:
  0.0 681.2 jit_solution(9112339533229287854)
XLA Ops:
  7.3 0.8 pad_maximum_fusion.2
  8.1 1.3 reshape.283
  9.5 1.3 reshape.284
  11.4 0.7 maximum_maximum_fusion.1.packed
  12.1 1.3 pad_maximum_fusion.mix
  13.4 0.6 broadcast_in_dim.65.gain
  14.0 22.6 %shard_map.271 = (bf16[8,64,960]{2,1,0:T(8,128)(2,1)}, f32[4,8,8,128]{3,2,1,0:T(8,128)}, bf16[4,96,320]{2,1,0:T(8,128)(2,1)}) custom-call(bf16[8,64,960]{2,1,0:T(8,128)(2,1)} %pad_maximum_fusion.mix, f32[8,128]{1,0:T(8,128)} %broadcast_in_dim.65.gain, bf16[96,320]{1,0:T(8,128)(2,1)} %maximum_maximum_fusion.1.packed), custom_call_target="tpu_custom_call" | custom-call | flops 15000000512 | bytes 1048576 | tf_op jit(solution)/shard_map/pallas_call | solution.py:1103
  36.7 0.9 slice.108
  37.7 0.7 reshape.287.gain
  38.3 60.5 %shard_map.272 = (bf16[2048,2048]{1,0:T(8,128)(2,1)}, bf16[8,64,1536]{2,1,0:T(8,128)(2,1)}) custom-call(bf16[256,2048]{1,0:T(8,128)(2,1)} %bitcast.113, f32[1,2048]{1,0:T(1,128)} %reshape.287.gain, bf16[64,6144]{1,0:T(8,128)(2,1)} %gate.3, bf16[64,6144]{1,0:T(8,128)(2,1)} %up.3, bf16[64,6144]{1,0:T(8,128)(2,1)} %down.3), custom_call_target="tpu_custom_call" | custom-call | flops 60000002048 | bytes 1048576 | tf_op jit(solution)/shard_map/pallas_call | solution.py:1131
  98.9 0.7 collective-permute-start
  100.0 0.7 reshape.292.gain
  100.9 1.0 pad_maximum_fusion.1.wbd
  102.1 0.7 maximum_maximum_fusion.2.vec
  103.2 1.4 copy.92.off
  104.6 11.7 %all-gather.4.cloned.1.call-done.mix_w.mixer_w = bf16[2048,960]{1,0:T(8,128)(2,1)} async-done(((bf16[512,960]{1,0:T(8,128)(2,1)}), bf16[2048,960]{1,0:T(8,128)(2,1)}) %all-gather.4.cloned.1.call-update) | async-done | bytes 3932176 | tf_op jit(solution)/shard_map/all_gather | solution.py:1061
  116.2 64.5 %shard_map.273 = (f32[2048,320]{1,0:T(8,128)}, bf16[2048,320]{1,0:T(8,128)(2,1)}, f32[2048,320]{1,0:T(8,128)}, f32[2048,320]{1,0:T(8,128)}, f32[2048,320]{1,0:T(...) custom-call(bf16[2048,2048]{1,0:T(8,128)(2,1)} %get-tuple-element.60, ...), custom_call_target="tpu_custom_call" | custom-call | flops 49999998976 | bytes 1048576 | tf_op jit(solution)/shard_map/pallas_call | solution.py:1180
  181.1 2.7 slice.148.weight.out_w
  183.8 88.1 %shard_map.274 = (f32[256,2048]{1,0:T(8,128)}, bf16[2048,2048]{1,0:T(8,128)(2,1)}) custom-call(bf16[2048,320]{1,0:T(8,128)(2,1)} %get-tuple-element.63.mixed.refs_1_, bf16[2048,320]{1,0:T(8,128)(2,1)} %slice.148.weight.out_w, bf16[256,2048]{1,0:T(8,128)(2,1)} %bitcast.114, f32[1,2048]{1,0:T(1,128)} %reshape.292.gain), custom_call_target="tpu_custom_call" | custom-call | flops 80000000000 | bytes 1048576 | tf_op jit(solution)/shard_map/pallas_call | solution.py:1203
  271.9 19.3 %shard_map.275 = (bf16[2048,1024]{1,0:T(8,128)(2,1)}, bf16[2048,512]{1,0:T(8,128)(2,1)}) custom-call(bf16[2048,2048]{1,0:T(8,128)(2,1)} %get-tuple-element.69.second.refs_0_, bf16[2048,2048]{1,0:T(8,128)(2,1)} %get-tuple-element.65.cot.refs_2_.cot_all, bf16[2048,1536]{1,0:T(8,128)(2,1)} %all-gather.6.cloned.1.call-done.gate_w.up_w.down_w.w1.part_a, ...), custom_call_target="tpu_custom_call" | custom-call | flops 12884901888 | bytes 16777216 | tf_op jit(solution)/shard_map/pallas_call | solution.py:982
  291.2 19.2 %shard_map.276 = bf16[2048,1536]{1,0:T(8,128)(2,1)} custom-call(bf16[2048,2048]{1,0:T(8,128)(2,1)} %get-tuple-element.69.second.refs_0_, bf16[2048,1024]{1,0:T(8,128)(2,1)} %get-tuple-element.67.refs_1_.g1, bf16[2048,2048]{1,0:T(8,128)(2,1)} %get-tuple-element.65.cot.refs_2_.cot_all, bf16[2048,512]{1,0:T(8,128)(2,1)} %get-tuple-element.68.refs_3_.hidden_a), custom_call_target="tpu_custom_call" | custom-call | flops 12884901888 | bytes 23068672 | tf_op jit(solution)/shard_map/pallas_call | solution.py:1019
  310.5 14.2 %shard_map.277 = (bf16[2048,512]{1,0:T(8,128)(2,1)}, bf16[2048,256]{1,0:T(8,128)(2,1)}) custom-call(bf16[2048,2048]{1,0:T(8,128)(2,1)} %get-tuple-element.69.second.refs_0_, bf16[2048,2048]{1,0:T(8,128)(2,1)} %get-tuple-element.65.cot.refs_2_.cot_all, bf16[2048,768]{1,0:T(8,128)(2,1)} %all-gather.8.cloned.1.call-done.gate_w.up_w.down_w.w2.part_b, ...), custom_call_target="tpu_custom_call" | custom-call | flops 6442450944 | bytes 16777216 | tf_op jit(solution)/shard_map/pallas_call | solution.py:982
  324.7 98.9 %shard_map.278 = (f32[256,2048]{1,0:T(8,128)}, f32[8,2048]{1,0:T(8,128)}, bf16[2048,2048]{1,0:T(8,128)(2,1)}, bf16[2048,768]{1,0:T(8,128)(2,1)}) custom-call(bf16[2048,1024]{1,0:T(8,128)(2,1)} %get-tuple-element.67.refs_1_.g1, bf16[2048,1536]{1,0:T(8,128)(2,1)} %all-gather.6.cloned.1.call-done.gate_w.up_w.down_w.w1.part_a, ...), custom_call_target="tpu_custom_call" | custom-call | flops 89999998976 | bytes 1048576 | tf_op jit(solution)/shard_map/pallas_call | solution.py:1220
  424.3 1.5 copy.94.offx
  425.8 10.5 %shard_map.282 = bf16[2048,320]{1,0:T(8,128)(2,1)} custom-call(bf16[2048,2048]{1,0:T(8,128)(2,1)} %get-tuple-element.76.grad_att.refs_0_, bf16[2048,320]{1,0:T(8,128)(2,1)} %get-tuple-element.63.mixed.refs_1_), custom_call_target="tpu_custom_call" | custom-call | flops 2684354560 | bytes 9699328 | tf_op jit(solution)/shard_map/pallas_call | solution.py:1019
  436.3 78.4 %shard_map.279 = (bf16[2048,640]{1,0:T(8,128)(2,1)}, f32[320,640]{1,0:T(8,128)}, f32[8,320]{1,0:T(8,128)}, bf16[256,2048]{1,0:T(8,128)(2,1)}) custom-call(bf16[2048,2048]{1,0:T(8,128)(2,1)} %get-tuple-element.76.grad_att.refs_0_, bf16[2048,320]{1,0:T(8,128)(2,1)} %slice.148.weight.out_w, f32[2048,320]{1,0:T(8,128)} %get-tuple-element.77.branch, ...), custom_call_target="tpu_custom_call" | custom-call | flops 70000001024 | bytes 1048576 | tf_op jit(solution)/shard_map/pallas_call | solution.py:1249
  514.7 3.6 all-to-all-start.3
  518.4 12.2 %shard_map.280 = bf16[2048,640]{1,0:T(8,128)(2,1)} custom-call(bf16[2048,2048]{1,0:T(8,128)(2,1)} %get-tuple-element.60.normed.refs_0_, bf16[2048,640]{1,0:T(8,128)(2,1)} %get-tuple-element.92.refs_1_.grads), custom_call_target="tpu_custom_call" | custom-call | flops 5368709120 | bytes 11010048 | tf_op jit(solution)/shard_map/pallas_call | solution.py:1019
  530.8 0.9 copy-done.5
  532.1 0.8 select_maximum_fusion.pack
  532.9 4.3 all-to-all-start.2
  537.2 88.8 %shard_map.281 = (f32[256,2048]{1,0:T(8,128)}, f32[88,320]{1,0:T(8,128)}, f32[8,128]{1,0:T(8,128)}) custom-call(bf16[2048,640]{1,0:T(8,128)(2,1)} %get-tuple-element.92.refs_1_.grads, bf16[2048,960]{1,0:T(8,128)(2,1)} %all-gather.4.cloned.1.call-done.mix_w.mixer_w, bf16[256,2048]{1,0:T(8,128)(2,1)} %bitcast.115, f32[256,2048]{1,0:T(8,128)} %get-tuple-element.93.grad_middle, ...), custom_call_target="tpu_custom_call" | custom-call | flops 60000002048 | bytes 1048576 | tf_op jit(solution)/shard_map/pallas_call | solution.py:1311
  626.0 0.7 slice.134
  626.7 1.6 slice.133
  628.3 0.7 slice_reduce_fusion
  629.0 0.7 slice.137
  629.7 0.6 slice.135
  630.3 0.7 constant_dynamic-slice_fusion
  631.1 0.5 slice_bitcast_fusion
  631.6 0.5 slice_bitcast_fusion.2
  632.5 1.6 fusion.5
  634.0 0.7 copy.136
  634.8 0.7 copy.137
  635.5 0.7 copy.135
  636.3 4.6 reshape.304
  640.9 3.5 all-to-all-start.1
  644.4 3.1 fusion.4
  647.4 0.9 copy.133
  648.4 3.4 all-to-all-done.1
  651.8 3.5 all-to-all-start
  655.3 1.2 convert_bitcast_fusion.2
  656.8 1.3 copy.111
  658.2 1.3 copy.112
  659.7 1.3 copy.113
  661.0 0.5 copy.98
  661.5 1.0 reshape.309
  662.5 3.0 all-to-all-done
  665.5 0.6 reshape.301
  666.2 1.1 fusion.7
  667.3 0.5 convert_bitcast_fusion.3
  667.8 1.0 reshape.308
  669.3 1.0 reshape.307
  670.3 2.3 copy.142
  672.6 1.3 copy.143
  (97 shorter events, 5.2 us)
Async XLA Ops:
  7.2 3.6 copy-start.6
  7.2 3.9 copy-start.13
  7.2 3.9 copy-start.14
  7.2 109.0 %all-gather.4.cloned.1.call-start = ((), (), s32[]{:S(2)}) async-start(), calls=%async_computation.8 | async-start | bytes 5242880 | tf_op jit(solution)/shard_map/all_gather | solution.py:1061
  8.1 3.3 copy-start.10
  36.6 235.3 %all-gather.6.cloned.1.call-start = ((), (), s32[]{:S(2)}) async-start(), calls=%async_computation.9 | async-start | bytes 7864320 | tf_op jit(solution)/shard_map/all_gather | solution.py:1061
  38.3 60.6 %copy-start.12 = (s32[2,4]{1,0:T(2,128)S(1)}, s32[2,4]{1,0:T(2,128)}, u32[]{:S(2)}) copy-start(s32[2,4]{1,0:T(2,128)} %param.18) | copy-start | bytes 100
  38.3 61.3 %copy-start.7 = (bf16[4,96,320]{2,1,0:T(8,128)(2,1)S(1)}, bf16[4,96,320]{2,1,0:T(8,128)(2,1)}, u32[]{:S(2)}) copy-start(bf16[4,96,320]{2,1,0:T(8,128)(2,1)} %get-tuple-element.62) | copy-start | bytes 737284
  98.9 211.6 %all-gather.8.cloned.1.call-start = ((), (), s32[]{:S(2)}) async-start(), calls=%async_computation.10 | async-start | bytes 3932160 | tf_op jit(solution)/shard_map/all_gather | solution.py:1061
  98.9 3.8 collective-permute-start
  103.1 77.7 %copy-start.8 = (s32[16,144,1]{1,0,2:T(8,128)}, s32[16,144,1]{1,0,2:T(8,128)S(1)}, u32[]{:S(2)}) copy-start(s32[16,144,1]{1,0,2:T(8,128)S(1)} %sub.40) | copy-start | bytes 27652
  180.8 245.0 %reduce-scatter.5.cloned.1.call-start = ((), (), s32[]{:S(2)}) async-start(), calls=%async_computation.11 | async-start | bytes 7864320 | tf_op jit(solution)/shard_map/reduce_scatter | solution.py:1065
  310.4 204.3 %reduce-scatter.7.cloned.1.call-start = ((), (), s32[]{:S(2)}) async-start(), calls=%async_computation.12 | async-start | bytes 3932160 | tf_op jit(solution)/shard_map/reduce_scatter | solution.py:1065
  423.6 0.7 copy-start.9
  423.6 217.3 %reduce-scatter.11.cloned.1.call-start = ((), (), s32[]{:S(2)}) async-start(), calls=%async_computation.14 | async-start | bytes 1966080 | tf_op jit(solution)/shard_map/reduce_scatter | solution.py:1065
  514.7 18.2 %all-to-all-start.3 = ((bf16[8,64,768]{2,1,0:T(8,128)(2,1)}), bf16[8,64,768]{2,1,0:T(8,128)(2,1)S(1)}, u32[]{:S(2)}, u32[]{:S(2)}) async-start(bf16[8,64,768]{2,1,0:T(8,128)(2,1)} %bitcast.100), calls=%async_computation.7 | async-start | bytes 1572864 | tf_op jit(solution)/shard_map/all_to_all | solution.py:1069
  518.3 12.3 %copy-start.11 = (f32[8,320]{1,0:T(8,128)S(1)}, f32[8,320]{1,0:T(8,128)}, u32[]{:S(2)}) copy-start(f32[8,320]{1,0:T(8,128)} %get-tuple-element.96) | copy-start | bytes 30724
  518.3 133.5 %reduce-scatter.9.cloned.1.call-start = ((), (), s32[]{:S(2)}) async-start(), calls=%async_computation.13 | async-start | bytes 3276800 | tf_op jit(solution)/shard_map/reduce_scatter | solution.py:1065
  530.6 1.1 copy-start.5
  532.9 103.4 %all-to-all-start.2 = ((bf16[8,64,1536]{2,1,0:T(8,128)(2,1)}), bf16[8,64,1536]{2,1,0:T(8,128)(2,1)}, u32[]{:S(2)}, u32[]{:S(2)}) async-start(bf16[8,64,1536]{2,1,0:T(8,128)(2,1)} %bitcast.25), calls=%async_computation.6 | async-start | bytes 3145728 | tf_op jit(solution)/shard_map/all_to_all | solution.py:1069
  640.9 10.9 %all-to-all-start.1 = ((bf16[8,64,320]{2,1,0:T(8,128)(2,1)}), bf16[8,64,320]{2,1,0:T(8,128)(2,1)S(1)}, u32[]{:S(2)}, u32[]{:S(2)}) async-start(bf16[8,64,320]{2,1,0:T(8,128)(2,1)} %bitcast.103), calls=%async_computation.5 | async-start | bytes 786432 | tf_op jit(solution)/shard_map/all_to_all | solution.py:1069
  647.4 7.9 %copy-start.4 = (bf16[8,64,1,256]{3,1,0,2:T(8,128)(2,1)S(1)}, bf16[8,64,1,256]{3,1,0,2:T(8,128)(2,1)}, u32[]{:S(2)}) copy-start(bf16[8,64,1,256]{3,1,0,2:T(8,128)(2,1)} %copy.135) | copy-start | bytes 786436
  648.4 8.2 %copy-start = (bf16[8,64,1,512]{3,2,1,0:T(2,128)(2,1)S(1)}, bf16[8,64,1,512]{3,2,1,0:T(2,128)(2,1)}, u32[]{:S(2)}) copy-start(bf16[8,64,1,512]{3,2,1,0:T(2,128)(2,1)} %get-tuple-element.103) | copy-start | bytes 1572868
  651.8 13.8 %all-to-all-start = ((bf16[8,64,640]{2,1,0:T(8,128)(2,1)}), bf16[8,64,640]{2,1,0:T(8,128)(2,1)S(1)}, u32[]{:S(2)}, u32[]{:S(2)}) async-start(bf16[8,64,640]{2,1,0:T(8,128)(2,1)} %bitcast.102), calls=%async_computation.3 | async-start | bytes 1310720 | tf_op jit(solution)/shard_map/all_to_all | solution.py:1069
  656.7 1.4 copy-start.3
  658.2 1.3 copy-start.2
  669.3 3.4 copy-start.1
Sparse Core Ops, SparseCore 0:
  36.7 79.4 all-gather.3
  117.8 115.9 all-gather.5
  235.4 61.8 all-gather.7
  310.5 109.9 reduce-scatter.4
  423.8 61.2 reduce-scatter.6
  487.8 36.3 reduce-scatter.10
  530.9 72.7 reduce-scatter.8

commit v3 on v2

--- a/solution.py
+++ b/solution.py
@@ -123,48 +123,50 @@
 
 GATHER_SEMS = 9
 REDUCE_SEMS = 10
-
-
-def gather_start(own, out, send, base, local_sem, spot):
+PARTS = 2
+
+
+def gather_start(own, out, send, base, local_sem, spot, whole=None, low=0):
     me, sib, xn, yn = spot
     count = own.shape[0]
-    here = out.at[block_rows(number(me), count), :]
+    whole = whole or count
+    here = out.at[block_rows(number(me), whole, low, count), :]
     local = pltpu.make_async_copy(own, here, local_sem)
     local.start()
     x = send(base, own, here, xn)
     y = send(base + 1, own, here, yn)
     s = send(base + 2, own, here, sib)
-    return local, x, y, s
-
-
-def gather_pass(started, count, out, send, base, spot):
+    return (whole, low, count, out, base), (local, x, y, s)
+
+
+def gather_pass(started, send, spot):
     me, sib, xn, yn = spot
-    local, x, y, s = started
+    (whole, low, count, out, base), (local, x, y, s) = started
     half = count // 2
     x.wait_recv()
-    top = out.at[block_rows(number(xn), count, 0, half), :]
+    top = out.at[block_rows(number(xn), whole, low, half), :]
     xa = send(base + 3, top, top, yn)
-    whole = out.at[block_rows(number(xn), count), :]
-    xs = send(base + 4, whole, whole, sib)
+    block = out.at[block_rows(number(xn), whole, low, count), :]
+    xs = send(base + 4, block, block, sib)
     y.wait_recv()
-    low = out.at[block_rows(number(yn), count, half, half), :]
-    yb = send(base + 5, low, low, xn)
-    whole = out.at[block_rows(number(yn), count), :]
-    ys = send(base + 6, whole, whole, sib)
-    return started + (xa, xs, yb, ys)
-
-
-def gather_end(started, count, out, send, base, spot):
+    under = out.at[block_rows(number(yn), whole, low + half, half), :]
+    yb = send(base + 5, under, under, xn)
+    block = out.at[block_rows(number(yn), whole, low, count), :]
+    ys = send(base + 6, block, block, sib)
+    return started[0], (local, x, y, s, xa, xs, yb, ys)
+
+
+def gather_end(started, send, spot):
     me, sib, xn, yn = spot
-    local, x, y, s, xa, xs, yb, ys = started
+    (whole, low, count, out, base), (local, x, y, s, xa, xs, yb, ys) = started
     half = count // 2
     td = number((me[0], 1 - me[1], me[2], 1 - me[3]))
     xa.wait_recv()
-    top = out.at[block_rows(td, count, 0, half), :]
+    top = out.at[block_rows(td, whole, low, half), :]
     da = send(base + 7, top, top, sib)
     yb.wait_recv()
-    low = out.at[block_rows(td, count, half, half), :]
-    db = send(base + 8, low, low, sib)
+    under = out.at[block_rows(td, whole, low + half, half), :]
+    db = send(base + 8, under, under, sib)
     for copy in (s, xs, ys, da, db):
         copy.wait_recv()
     for copy in (x, y, s, xa, xs, yb, ys, da, db):
@@ -172,12 +174,7 @@
     local.wait()
 
 
-def gather_finish(started, count, out, send, base, spot):
-    passed = gather_pass(started, count, out, send, base, spot)
-    gather_end(passed, count, out, send, base, spot)
-
-
-def reduce_plane(pairs, acc, bufs, send, base, spot):
+def reduce_plane(pairs, acc, bufs, send, base, spot, whole=None, low=0):
     sib_out, sib_in, s3, s2, s1, keep_a, keep_b, ua0, ua1, ub0, ub2, ta, tb, va, vb = bufs
     me, sib, xn, yn = spot
     count, cols = acc.shape
@@ -187,7 +184,7 @@
 
     def block(r, core, store):
         place = (me[0], me[1] if r < 2 else 1 - me[1], core, me[3] if r % 2 == 0 else 1 - me[3])
-        rows = block_rows(number(place), count)
+        rows = block_rows(number(place), whole or count, low, count)
 
         @pl.loop(0, cols // tile)
         def _(j):
@@ -210,7 +207,7 @@
     copies = {}
     for r in (3, 2, 1):
         copies[r] = to_sibling(r)
-
+        yield None
     copies[3].wait_recv()
 
     def store3(at, total):
@@ -219,6 +216,7 @@
     block(3, me[2], store3)
     a3 = send(base + 4, s3.at[pl.ds(0, half), :], ua1, xn)
     b3 = send(base + 5, s3.at[pl.ds(half, half), :], ub2, yn)
+    yield None
     copies[2].wait_recv()
 
     def store2(at, total):
@@ -228,6 +226,7 @@
 
     block(2, me[2], store2)
     a2 = send(base + 6, s2, ua0, xn)
+    yield None
     copies[1].wait_recv()
 
     def store1(at, total):
@@ -237,6 +236,7 @@
 
     block(1, me[2], store1)
     b1 = send(base + 7, s1, ub0, yn)
+    yield None
     copies[0] = to_sibling(0)
     yield None
     a3.wait_recv()
@@ -269,7 +269,7 @@
     ]
 
 
-def for_total_rows(acc, bufs, body):
+def for_total_rows(acc, bufs, body, low=0):
     half = acc.shape[0] // 2
     step = 16
     for first, second, start in ((bufs[7], bufs[13], 0), (bufs[9], bufs[14], half)):
@@ -278,7 +278,35 @@
         def _(i):
             at = pl.ds(pl.multiple_of(i * step, step), step)
             rows = pl.ds(pl.multiple_of(start + i * step, step), step)
-            body(rows, acc[rows, :] + first[at, :].astype(F32) + second[at, :].astype(F32))
+            places = pl.ds(pl.multiple_of(low + start + i * step, step), step)
+            body(places, acc[rows, :] + first[at, :].astype(F32) + second[at, :].astype(F32))
+
+
+def plane_sum(pairs, sets, send, spot, body, own=None, out=None, local_sem=None, slow=False):
+    parts = len(sets) // 16
+    sets = [sets[16 * i : 16 * i + 16] for i in range(parts)]
+    count = sets[0][0].shape[0]
+    whole = parts * count
+    runs = [
+        reduce_plane(pairs, held[0], held[1:], send, i * REDUCE_SEMS, spot, whole, i * count)
+        for i, held in enumerate(sets)
+    ]
+    if slow:
+        order = [0] * 7 + [1] * 3 + [0] + [1] * 2 + [0] + [1] * 4
+    else:
+        order = [0] * 7 + [1] * 7 + [0, 1, 0, 1]
+    opened, started = [], []
+    for i in order:
+        got = next(runs[i])
+        if got is None:
+            continue
+        opened += got
+        for_total_rows(sets[i][0], sets[i][1:], body, i * count)
+        if own is not None:
+            part = own.at[pl.ds(i * count, count), :]
+            base = parts * REDUCE_SEMS + i * GATHER_SEMS
+            started.append(gather_start(part, out, send, base, local_sem.at[i], spot, whole, i * count))
+    return opened, started
 
 
 def load_columns(pairs, load_sem):
@@ -289,30 +317,109 @@
     return loads
 
 
-def middle_kernel(mixed, weight, tokens, gain, middle, second, own, acc, *rest):
-    bufs, (send_sem, recv_sem, local_sem) = rest[:15], rest[15:]
+def stream(arrays, slots, sem, count):
+    def copies(i, out=False):
+        rows, slot = block_rows(i, count), lax.rem(i, 2)
+        made = []
+        for k, (array, held) in enumerate(zip(arrays, slots)):
+            part = array.at[rows, :] if len(array.shape) == 2 else array.at[:, rows, :]
+            src, dst = (held.at[slot], part) if out else (part, held.at[slot])
+            made.append(pltpu.make_async_copy(src, dst, sem.at[slot, k]))
+        return made
+
+    return copies
+
+
+def middle_kernel(
+    mixed, weight, tokens, gain, off, vec, enter, slope, conv, rate, keep, scale, decay, states,
+    middle, second, state_slope, rate_factor, log_factor, keep_factor, conv_factor, own, *rest
+):
+    sets, rest = rest[: 16 * PARTS], rest[16 * PARTS :]
+    send_sem, recv_sem, local_sem, flat_in, tile_in, flat_out, in_sem, out_sem = rest
     spot = where_am_i()
+    span, width = flat_in.shape[2], conv.shape[1]
+    groups = conv.shape[0] // span
+    fetch = stream(
+        (slope, conv, rate, keep, scale, decay, states),
+        [flat_in.at[k] for k in range(5)] + [tile_in.at[k] for k in range(2)],
+        in_sem,
+        span,
+    )
+    write = stream(
+        (state_slope, rate_factor, log_factor, keep_factor, conv_factor),
+        [flat_out.at[k] for k in range(5)],
+        out_sem,
+        span,
+    )
+    for copy in fetch(0):
+        copy.start()
     greet(spot[1:])
     send = sender(send_sem, recv_sem)
-    *_, open_copies = reduce_plane([(mixed, weight)], acc, bufs, send, 0, spot)
 
     def body(rows, total):
         value = tokens[rows, :].astype(F32) + total
         middle[rows, :] = value
         own[rows, :] = norm_forward(value, gain[...])
 
-    for_total_rows(acc, bufs, body)
-    started = gather_start(own, second, send, REDUCE_SEMS, local_sem, spot)
-    gather_finish(started, own.shape[0], second, send, REDUCE_SEMS, spot)
-    for copy in open_copies:
+    opened, started = plane_sum([(mixed, weight)], sets, send, spot, body, own, second, local_sem)
+    first_row = lax.broadcasted_iota(jnp.int32, (span, width), 0) == 0
+
+    def fill(g):
+        @pl.when(g + 1 < groups)
+        def _():
+            for copy in fetch(g + 1):
+                copy.start()
+
+        for copy in fetch(g):
+            copy.wait()
+
+        @pl.when(g >= 2)
+        def _():
+            for copy in write(g - 2, out=True):
+                copy.wait()
+
+        slot = lax.rem(g, 2)
+        slope_g, conv_g, rate_g, keep_g, scale_g = (flat_in[k, slot] for k in range(5))
+        decay_g, states_g = (
+            jnp.concatenate([tile_in[k, slot, c] for c in range(tile_in.shape[2])], axis=1)[:, :width]
+            for k in range(2)
+        )
+        place = off[block_rows(g, span), :]
+        before = enter[pl.ds(g, 1), :][:, :width]
+        prev = jnp.where(first_row, before, pltpu.roll(states_g, 1, 0))
+        kept = keep_g * scale_g
+        factor = jnp.where(
+            place > 0, decay_g * prev - conv_g * keep_g * (decay_g * decay_g) / scale_g, 0.0
+        )
+        by_rate = factor * rate_g
+        flat_out[0, slot] = states_g * slope_g
+        flat_out[1, slot] = by_rate * (-8.0 * vec[7:8, :]) * (1.0 - rate_g)
+        flat_out[2, slot] = by_rate
+        flat_out[3, slot] = conv_g * kept * (1.0 - keep_g)
+        flat_out[4, slot] = kept
+        for copy in write(g, out=True):
+            copy.start()
+
+    passed = []
+    cuts = (0, groups // 3, 2 * groups // 3, groups)
+    for i in range(3):
+        pl.loop(cuts[i], cuts[i + 1])(fill)
+        if i < 2:
+            passed.append(gather_pass(started[i], send, spot))
+    for one in passed:
+        gather_end(one, send, spot)
+    for g in (groups - 2, groups - 1):
+        for copy in write(g, out=True):
+            copy.wait()
+    for copy in opened:
         copy.wait_send()
 
 
 def grad_middle_kernel(
     g1, w1, g2, w2, middle, cot, gain, hidden, second, cot_all,
-    grad_middle, gain_grad, gathered, outer, own, acc, *rest
+    grad_middle, gain_grad, gathered, outer, own, *rest
 ):
-    bufs, rest = rest[:15], rest[15:]
+    sets, rest = rest[: 16 * PARTS], rest[16 * PARTS :]
     send_sem, recv_sem, local_sem, v1, v2, load_sem, left, strip, left_sem, strip_sem = rest
     fill_tile = left.shape[3]
     fill_count = second.shape[1] // fill_tile
@@ -337,7 +444,6 @@
     pairs = [(g1, v1), (g2, v2)]
     for copy in loads:
         copy.wait()
-    *_, open_copies = reduce_plane(pairs, acc, bufs, send, 0, spot)
     gain_grad[...] = jnp.zeros(gain_grad.shape, F32)
 
     def body(rows, total):
@@ -347,12 +453,10 @@
         own[rows, :] = value.astype(BF16)
         gain_grad[0:1, :] += term
 
-    for_total_rows(acc, bufs, body)
-    started = gather_start(own, gathered, send, REDUCE_SEMS, local_sem, spot)
+    opened, started = plane_sum(pairs, sets, send, spot, body, own, gathered, local_sem, slow=True)
     size = g2.shape[1]
 
-    @pl.loop(0, fill_count)
-    def _(i):
+    def fill(i):
         @pl.when(i + 1 < fill_count)
         def _():
             for copy in left_copies(i + 1):
@@ -371,10 +475,38 @@
             strip[slot, :, low : low + right.shape[1]] = part.astype(BF16)
         strip_copy(i).start()
 
-    gather_finish(started, own.shape[0], gathered, send, REDUCE_SEMS, spot)
+    passed = [gather_pass(started[0], send, spot)]
+    pl.loop(0, fill_count // 2)(fill)
+    passed.append(gather_pass(started[1], send, spot))
+    pl.loop(fill_count // 2, fill_count)(fill)
+    for one in passed:
+        gather_end(one, send, spot)
     strip_copy(fill_count - 2).wait()
     strip_copy(fill_count - 1).wait()
-    for copy in open_copies:
+    for copy in opened:
+        copy.wait_send()
+
+
+def tail_kernel(line, summed_mix, summed_out, mid, swapped_mix, swapped_out, gain_sum, far, send_sem, recv_sem, local_sem):
+    me = where_am_i()[0]
+    peers = plane_peers(me)
+    others = [(lax.rem(me[0] + k, line),) + me[1:] for k in range(1, line)]
+    greet(peers + others)
+    send = sender(send_sem, recv_sem)
+    swaps = [
+        swap_back_start(src, dst, send, 7 * k, local_sem.at[k], me, peers)
+        for k, (src, dst) in enumerate(((summed_mix, swapped_mix), (summed_out, swapped_out)))
+    ]
+    out = [send(14 + k, mid.at[other[0]], far.at[k], other) for k, other in enumerate(others)]
+    value = mid[me[0]]
+    for copy in out:
+        copy.wait_recv()
+    for k in range(line - 1):
+        value = value + far[k]
+    gain_sum[...] = value
+    for swap in swaps:
+        swap_end(swap)
+    for copy in out:
         copy.wait_send()
 
 
@@ -502,6 +634,13 @@
     return locals_, swaps
 
 
+def swap_back_start(src, dst, send, base, local_sem, me, peers):
+    t = number(me)
+    local = pltpu.make_async_copy(src.at[t], dst.at[t], local_sem)
+    local.start()
+    return [local], [send(base + i, src.at[number(peer)], dst.at[t], peer) for i, peer in enumerate(peers)]
+
+
 def swap_end(started):
     locals_, swaps = started
     for copy in swaps:
@@ -526,20 +665,20 @@
         own[rows, :] = norm_forward(tokens[rows, :].astype(F32), gain[...])
 
     started = gather_start(own, normed, send, 21, local_sem.at[3], spot)
-    passed = gather_pass(started, count, normed, send, 21, spot)
+    passed = gather_pass(started, send, spot)
     swaps = swap_start((gate, up, down), ff_in, FF_FIRST, send, 0, local_sem, me, peers)
-    gather_end(passed, count, normed, send, 21, spot)
+    gather_end(passed, send, spot)
     swap_end(swaps)
 
 
 def last_kernel(
     line, own_rows,
-    grads, mixer_w, tokens, grad_middle, gain, mlp_term, pack,
-    input_grad, pack_sum, gain_sum,
+    grads, mixer_w, tokens, grad_middle, gain, mlp_term, pack, summed,
+    input_grad, pack_sum, mid, swapped,
     *rest,
 ):
-    first, rest = rest[:16], rest[16:]
-    held, mixer_term, pack_in, gain_out, near, mid, far, send_sem, recv_sem, load_sem = rest
+    sets, rest = rest[: 16 * PARTS], rest[16 * PARTS :]
+    held, mixer_term, pack_in, gain_out, near, send_sem, recv_sem, load_sem = rest
     spot = where_am_i()
     me = spot[0]
     t = number(me)
@@ -562,7 +701,7 @@
     pl.semaphore_wait(barrier, len(peers) + 2 * len(others) + jnp.where(to_self, 0, 1))
 
     send = sender(send_sem, recv_sem)
-    pack_base = REDUCE_SEMS
+    pack_base = PARTS * REDUCE_SEMS
 
     def pack_copy(j, slot):
         target = t * line + j
@@ -580,7 +719,8 @@
         pl.when(t * line + j != index)(pack_copy(j, me[0]).start)
         pl.when(t * line + j == index)(own_pack.start)
     loads[0].wait()
-    *_, open_a = reduce_plane([(grads, held)], first[0], first[1:], send, 0, spot)
+    gain_base = pack_base + line
+    swap = swap_back_start(summed, swapped, send, gain_base + 7, load_sem.at[2], me, peers)
     mixer_term[...] = jnp.zeros(mixer_term.shape, F32)
 
     def body(rows, total):
@@ -588,14 +728,13 @@
         input_grad[rows, :] = grad_middle[rows, :] + back
         mixer_term[0:1, :] += term
 
-    for_total_rows(first[0], first[1:], body)
+    opened, _ = plane_sum([(grads, held)], sets, send, spot, body)
     per = plane * own_rows
     for z in range(line):
         for q in range(per // LANES):
             cols = slice(z * per + q * LANES, z * per + (q + 1) * LANES)
             gain_out[q, 2 * z : 2 * z + 1, :] = mixer_term[0:1, cols]
             gain_out[q, 2 * z + 1 : 2 * z + 2, :] = mlp_term[0:1, cols]
-    gain_base = pack_base + line
 
     def tile_of(place):
         return number(place) * own_rows // LANES
@@ -608,24 +747,18 @@
         total = total + near[i]
     for z in range(line):
         mid[z] = jnp.concatenate([total[2 * z : 2 * z + 2], jnp.zeros((6, LANES), F32)], axis=0)
-    out = [send(gain_base + 7 + k, mid.at[other[0]], far.at[k], other) for k, other in enumerate(others)]
     for z in range(line):
         source_is_me = jnp.logical_and(to_self, me[0] == z)
         pl.when(jnp.logical_not(source_is_me))(pack_copy(z, z).wait_recv)
         own_pack = pltpu.make_async_copy(pack.at[z], pack_in.at[z], load_sem.at[1])
         pl.when(source_is_me)(own_pack.wait)
-    total = pack_in[0]
+    total = pack_in[0].astype(F32)
     for z in range(1, line):
-        total = total + pack_in[z]
+        total = total + pack_in[z].astype(F32)
     pack_sum[...] = total
-    value = mid[me[0]]
-    for copy in out:
-        copy.wait_recv()
-    for k in range(line - 1):
-        value = value + far[k]
-    gain_sum[...] = value
-    for copy in open_a + sent + out:
+    for copy in opened + sent:
         copy.wait_send()
+    swap_end(swap)
     for j in range(line):
         pl.when(t * line + j != index)(pack_copy(j, me[0]).wait_send)
 
@@ -650,8 +783,9 @@
 def mixer_forward_kernel(
     line, groups, streams, span,
     normed, mix_w, off, wbd, vec, cot, gate, up, down,
-    branch, inner, conv, rate, keep, scale, decay, states, mixed, enter, ends, halo, cot_all, ff_in,
-    driven, ext, tail_out, tail_in, chain_out, chain_in, send_sem, recv_sem, local_sem,
+    value_out, slope_out, inner, head_rows, conv_out, rate_out, keep_out, scale_out, decay_out, states_out, mixed, enter, ends, halo,
+    cot_all, ff_in,
+    branch, slope, conv, rate, keep, scale, decay, states, save_sem, driven, ext, tail_out, tail_in, chain_out, chain_in, send_sem, recv_sem, local_sem,
 ):
     spot = where_am_i()
     me = spot[0]
@@ -659,8 +793,14 @@
     others = [(lax.rem(me[0] + k, line),) + me[1:] for k in range(1, line)]
     greet(peers + others)
     send = sender(send_sem, recv_sem)
+    saves = []
+
+    def save(*pairs):
+        for src, dst in pairs:
+            saves.append(pltpu.make_async_copy(src, dst, save_sem.at[len(saves)]))
+            saves[-1].start()
+
     gather_base, halo_base = 21, 21 + GATHER_SEMS
-    count = cot.shape[0]
     started = gather_start(cot, cot_all, send, gather_base, local_sem.at[3], spot)
     swaps = swap_start((gate, up, down), ff_in, FF_SECOND, send, 0, local_sem, me, peers)
 
@@ -703,7 +843,9 @@
         for k in range(1, 4):
             out = out + jnp.where(place >= k, vec[k : k + 1, :] * ext[g, 8 - k : 8 - k + span, :], 0.0)
         conv[rows, :] = out
-        pre = jnp.dot(out.astype(BF16), wbd[...], preferred_element_type=F32)
+        rounded = out.astype(BF16)
+        head_rows[rows, :] = rounded
+        pre = jnp.dot(rounded, wbd[...], preferred_element_type=F32)
         rate_g = jax.nn.sigmoid(pre[:, :width] + vec[5:6, :])
         keep_g = jax.nn.sigmoid(pre[:, width:] + vec[6:7, :])
         rate[rows, :] = rate_g
@@ -714,7 +856,8 @@
         put(decay, rows, jnp.where(place == 0, 0.0, jnp.exp(log_decay)))
         put(driven, rows, out * keep_g * scale_g)
 
-    passed = gather_pass(started, count, cot_all, send, gather_base, spot)
+    save((conv, conv_out), (rate, rate_out), (keep, keep_out), (scale, scale_out), (decay, decay_out))
+    passed = gather_pass(started, send, spot)
 
     def step(p, carry):
         at = pl.ds(p, groups, stride=span)
@@ -736,6 +879,15 @@
     chain_out[0:streams, :] = product
     chain_out[8 : 8 + streams, :] = total
     chains = chain_exchange(chain_out, chain_in, send, halo_base + 1, me, line, 1)
+
+    @pl.loop(0, groups)
+    def _(g):
+        rows = block_rows(g, span)
+        value_g, slope_g = gelu_parts(branch[rows, :])
+        branch[rows, :] = value_g
+        slope[rows, :] = slope_g
+
+    save((branch, value_out), (slope, slope_out))
     for copy in chains:
         copy.wait_recv()
     arriving = chain_value(chain_in, me, line, 1, streams)
@@ -754,75 +906,64 @@
         return tuple(done)
 
     lax.fori_loop(0, span, walk, split_lanes(enter[...]), unroll=4)
+    save((states, states_out))
 
     @pl.loop(0, groups)
     def _(g):
         rows = block_rows(g, span)
-        mixed[rows, :] = (take(states, rows, width) * gelu_parts(branch[rows, :])[0]).astype(BF16)
-
-    gather_end(passed, count, cot_all, send, gather_base, spot)
+        mixed[rows, :] = (take(states, rows, width) * branch[rows, :]).astype(BF16)
+
+    gather_end(passed, send, spot)
     swap_end(swaps)
     for copy in [halo_copy] + chains:
         copy.wait_send()
+    for copy in saves:
+        copy.wait()
 
 
 def mixer_back_kernel(
     line, groups, streams, span,
-    grad_att, out_w, branch, states, decay, rate, keep, scale, conv, enter, products, inner, halo, off, offx, wbd, vec,
-    hidden_a, part_a, hidden_b, part_b, middle,
-    grads, heads, sums, block_output,
-    fetch, adj, ext, gext, head_out, head_in, chain_out, chain_in, kept, held_a, held_b, *rest,
+    grad_att, out_w, value, state_slope, rate_factor, log_factor, keep_factor, conv_factor,
+    decay, products, inner, head_rows, halo, off, offx, wbd, vec, hidden_a, part_a, hidden_b, part_b, middle, summed,
+    grads, heads, sums, block_output, swapped,
+    fetch, adj, ext, gext, head_out, head_in, chain_out, chain_in, gelu_held, held, held_a, held_b, *rest,
 ):
-    (acc, *bufs), (send_sem, recv_sem, local_sem, load_sem, kept_sem) = rest[:16], rest[16:]
+    (acc, *bufs), (send_sem, recv_sem, local_sem, load_sem, gelu_sem, held_sem) = rest[:16], rest[16:]
     spot = where_am_i()
     me = spot[0]
     size_a, size_b = held_a.shape[1], held_b.shape[1]
-    loads = load_columns(((part_a, 2 * size_a, held_a), (part_b, 2 * size_b, held_b)), load_sem)
-
-    def kept_copies(g):
-        rows, slot = block_rows(g, span), lax.rem(g, 2)
-        return [
-            pltpu.make_async_copy(src.at[rows, :], kept.at[slot, k], kept_sem.at[slot, k])
-            for k, src in enumerate((rate, keep, scale, conv))
-        ]
-
-    for copy in kept_copies(0):
-        copy.start()
-    others = [(lax.rem(me[0] + k, line),) + me[1:] for k in range(1, line)]
-    greet(list(spot[1:]) + others)
-    send = sender(send_sem, recv_sem)
-    for copy in loads:
-        copy.wait()
-    mlp = reduce_plane([(hidden_a, held_a), (hidden_b, held_b)], acc, bufs, send, line, spot)
-    next(mlp)
     width = inner.shape[1]
     tiles = decay.shape[0]
-    place_rows = streams * span
     places = groups // streams
     some = fetch.shape[1]
     pieces = groups * span // some
 
     def load(q):
-        copy = pltpu.make_async_copy(grad_att.at[block_rows(q, some), :], fetch.at[q % 2], local_sem.at[q % 2])
+        return pltpu.make_async_copy(grad_att.at[block_rows(q, some), :], fetch.at[q % 2], local_sem.at[q % 2])
+
+    gelus = stream((value, state_slope), [gelu_held.at[k] for k in range(2)], gelu_sem, some)
+    factors = stream(
+        (rate_factor, log_factor, keep_factor, conv_factor), [held.at[k] for k in range(4)], held_sem, some
+    )
+    for copy in [load(0)] + gelus(0) + factors(0):
         copy.start()
-        return copy
-
-    copies = [load(0)]
+    loads = load_columns(((part_a, 2 * size_a, held_a), (part_b, 2 * size_b, held_b)), load_sem)
+    others = [(lax.rem(me[0] + k, line),) + me[1:] for k in range(1, line)]
+    peers = plane_peers(me)
+    greet(peers + others)
+    send = sender(send_sem, recv_sem)
+    swap = swap_back_start(summed, swapped, send, line + REDUCE_SEMS, local_sem.at[2], me, peers)
+
     for q in range(pieces):
         if q + 1 < pieces:
-            copies.append(load(q + 1))
-        copies[q].wait()
-        put(adj, block_rows(q, some), jnp.dot(fetch[q % 2], out_w[...], preferred_element_type=F32))
-
-    @pl.loop(0, groups)
-    def _(g):
-        rows = block_rows(g, span)
-        value, slope = gelu_parts(branch[rows, :])
-        grad = take(adj, rows, width)
-        grads[rows, :width] = (grad * take(states, rows, width) * slope).astype(BF16)
-        put(adj, rows, grad * value)
-
-    next(mlp)
+            for copy in [load(q + 1)] + gelus(q + 1):
+                copy.start()
+        for copy in [load(q)] + gelus(q):
+            copy.wait()
+        rows = block_rows(q, some)
+        grad = jnp.dot(fetch[q % 2], out_w[...], preferred_element_type=F32)
+        put(adj, rows, grad * gelu_held[0, q % 2])
+        grads[rows, :width] = (grad * gelu_held[1, q % 2]).astype(BF16)
 
     def step(i, carry):
         at = pl.ds(span - 1 - i, groups, stride=span)
@@ -839,6 +980,11 @@
     chain_out[0:streams, :] = product
     chain_out[8 : 8 + streams, :] = total
     chains = chain_exchange(chain_out, chain_in, send, 1, me, line, -1)
+    for copy in loads:
+        copy.wait()
+    mlp = reduce_plane([(hidden_a, held_a), (hidden_b, held_b)], acc, bufs, send, line, spot)
+    for _ in range(7):
+        next(mlp)
     for j in range(streams):
         ext[j, 0:8, :] = halo[8 * j : 8 * j + 8, :width]
 
@@ -869,51 +1015,45 @@
         return tuple(done)
 
     lax.fori_loop(0, span, walk, split_lanes(jnp.concatenate(carry_in, axis=0)), unroll=4)
-    first_row = lax.broadcasted_iota(jnp.int32, (span, width), 0) == 0
-
-    @pl.loop(0, groups)
-    def _(g):
-        rows = block_rows(g, span)
-        place = off[rows, :]
-
-        @pl.when(g + 1 < groups)
+    each = some // span
+
+    def gradients(q):
+        @pl.when(q + 1 < pieces)
         def _():
-            for copy in kept_copies(g + 1):
+            for copy in factors(q + 1):
                 copy.start()
 
-        for copy in kept_copies(g):
+        for copy in factors(q):
             copy.wait()
-        slot = lax.rem(g, 2)
-        adj_g, rate_g, keep_g = take(adj, rows, width), kept[slot, 0], kept[slot, 1]
-        scale_g, conv_g, decay_g = kept[slot, 2], kept[slot, 3], take(decay, rows, width)
-        before = enter[pl.ds(g, 1), :][:, :width]
-        prev = jnp.where(first_row, before, pltpu.roll(take(states, rows, width), 1, 0))
-        grad_log = jnp.where(
-            place > 0,
-            adj_g * (decay_g * prev - conv_g * keep_g * (decay_g * decay_g) / scale_g),
-            0.0,
-        )
-        rate_log = grad_log * rate_g
-        grad_rate = (rate_log * (-8.0 * vec[7:8, :]) * (1.0 - rate_g)).astype(BF16)
-        grad_keep = (adj_g * conv_g * scale_g * keep_g * (1.0 - keep_g)).astype(BF16)
+        slot = lax.rem(q, 2)
+        rows = block_rows(q, some)
+        adj_q = take(adj, rows, width)
+        grad_rate = (adj_q * held[0, slot]).astype(BF16)
+        grad_keep = (adj_q * held[2, slot]).astype(BF16)
         pre = jnp.concatenate([grad_rate, grad_keep], axis=1)
-        grad_conv = adj_g * keep_g * scale_g + lax.dot_general(
+        grad_conv = adj_q * held[3, slot] + lax.dot_general(
             pre, wbd[...], last_contract, preferred_element_type=F32
         )
-        heads[...] += lax.dot_general(
-            conv_g.astype(BF16), pre, rows_contract, preferred_element_type=F32
-        )
-        gext[g, 8 : 8 + span, :] = grad_conv
+        heads[...] += lax.dot_general(head_rows[rows, :], pre, rows_contract, preferred_element_type=F32)
         total = functools.partial(jnp.sum, axis=0, keepdims=True)
-        sums[0:1, :] += total(grad_conv * ext[g, 8 : 8 + span, :])
-        for k in range(1, 4):
-            sums[k : k + 1, :] += total(
-                jnp.where(place >= k, grad_conv * ext[g, 8 - k : 8 - k + span, :], 0.0)
-            )
         sums[4:5, :] += total(grad_conv)
         sums[5:6, :] += total(grad_rate.astype(F32))
         sums[6:7, :] += total(grad_keep.astype(F32))
-        sums[7:8, :] += total(rate_log) * (-8.0 * vec[8:9, :])
+        sums[7:8, :] += total(adj_q * held[1, slot]) * (-8.0 * vec[8:9, :])
+        for j in range(each):
+            g = q * each + j
+            part = grad_conv[j * span : (j + 1) * span]
+            place = off[block_rows(g, span), :]
+            gext[g, 8 : 8 + span, :] = part
+            sums[0:1, :] += total(part * ext[g, 8 : 8 + span, :])
+            for k in range(1, 4):
+                sums[k : k + 1, :] += total(
+                    jnp.where(place >= k, part * ext[g, 8 - k : 8 - k + span, :], 0.0)
+                )
+
+    pl.loop(0, pieces // 2)(gradients)
+    next(mlp)
+    pl.loop(pieces // 2, pieces)(gradients)
 
     for g in range(groups):
         gext[g, 0:8, :] = jnp.zeros((8, width), F32)
@@ -938,17 +1078,17 @@
         head_out[8 * j : 8 * j + 8, :] = jnp.concatenate([spread(j, 0, 8), pad], axis=1)
     previous = (lax.rem(me[0] + line - 1, line),) + me[1:]
     head_copy = send(0, head_out, head_in, previous)
-    open_mlp = next(mlp)
-
-    def body(rows, total):
-        block_output[rows, :] = (middle[rows, :] + total).astype(BF16)
-
-    for_total_rows(acc, bufs, body)
 
     @pl.loop(0, groups)
     def _(g):
         grads[block_rows(g, span), width:] = spread(g, 8, span).astype(BF16)
 
+    open_mlp = next(mlp)
+
+    def body(rows, total):
+        block_output[rows, :] = (middle[rows, :] + total).astype(BF16)
+
+    for_total_rows(acc, bufs, body)
     head_copy.wait_recv()
     for j in range(streams):
         g = groups - streams + j
@@ -957,6 +1097,7 @@
         grads[g * span + span - 16 : (g + 1) * span, width:] = ending.astype(BF16)
     for copy in [head_copy] + chains + open_mlp:
         copy.wait_send()
+    swap_end(swap)
 
 
 def ff_kernel(second, cot, gate_w, up_w, down_w, grads, hidden):
@@ -1063,10 +1204,6 @@
 
 def line_reduce(value):
     return lax.psum_scatter(value.astype(BF16), "line", scatter_dimension=0, tiled=True)
-
-
-def plane_swap(value):
-    return lax.all_to_all(value, PLANE, split_axis=0, concat_axis=0, tiled=False)
 
 
 def shards(
@@ -1171,21 +1308,25 @@
     count = plane * own
     tiles = -(-width // LANES)
     wide = tiles * LANES
-    full = ((count, width), F32, VMEM)
+    full = ((count, width), F32, ANY)
     short = ((count, width), BF16, VMEM)
-    tiled = ((tiles, count, LANES), F32, VMEM)
+    tiled = ((tiles, count, LANES), F32, ANY)
     edge = ((8 * streams, wide), F32)
     (
-        branch, inner, conv, rate, keep, scale, decay, states, mixed, enter, ends, halo, cot_all, second_part
+        value, slope, inner, head_rows, conv, rate, keep, scale, decay, states, mixed, enter, ends, halo, cot_all,
+        second_part,
     ) = comm_call(
         functools.partial(mixer_forward_kernel, line, groups, streams, span),
         3,
         [VMEM] * 5 + [ANY] * 4,
-        [full, short, full, full, full, full, tiled, tiled, short]
+        [full, full, short, short, full, full, full, full, tiled, tiled, short]
         + [((groups, wide), F32, VMEM)] * 2
         + [edge + (VMEM,), tall]
         + swapped(FF_SECOND),
-        [
+        [pltpu.VMEM((count, width), F32)] * 6
+        + [pltpu.VMEM((tiles, count, LANES), F32)] * 2
+        + [
+            pltpu.SemaphoreType.DMA((8,)),
             pltpu.VMEM((tiles, count, LANES), F32),
             pltpu.VMEM((groups, span + 8, width), F32),
             pltpu.VMEM(*edge),
@@ -1200,17 +1341,24 @@
 
     parts = [line_gather(w.reshape(plane * own_rows, w.shape[2])) for w in (first_part, second_part)]
     own32 = ((own, d_model), F32, VMEM)
-    middle, second = comm_call(
+    middle, second, *factors = comm_call(
         middle_kernel,
         4,
-        [VMEM] * 4,
-        [own32, tall],
+        [VMEM] * 7 + [ANY] * 7,
+        [own32, tall] + [full] * 5,
         [pltpu.VMEM((own, d_model), BF16)]
-        + reduce_buffers(own, d_model)
-        + sems(REDUCE_SEMS + GATHER_SEMS)
-        + [pltpu.SemaphoreType.DMA],
+        + reduce_buffers(own // PARTS, d_model) * PARTS
+        + sems((REDUCE_SEMS + GATHER_SEMS) * PARTS)
+        + [
+            pltpu.SemaphoreType.DMA((PARTS,)),
+            pltpu.VMEM((5, 2, span, width), F32),
+            pltpu.VMEM((2, 2, tiles, span, LANES), F32),
+            pltpu.VMEM((5, 2, span, width), F32),
+            pltpu.SemaphoreType.DMA((2, 7)),
+            pltpu.SemaphoreType.DMA((2, 5)),
+        ],
         80,
-    )(mixed, output_w, x, mlp_scale)
+    )(mixed, output_w, x, mlp_scale, off, vec, enter, slope, conv, rate, keep, scale, decay, states)
 
     grads_a, hidden_a = ff_call(second, cot_all, parts[0])
     sums_a = outer_call(second, grads_a, cot_all, hidden_a)
@@ -1223,10 +1371,10 @@
         [VMEM, ANY, VMEM, ANY] + [VMEM] * 4 + [ANY] * 2,
         [own32, gain_rows, tall, ((d_model, 3 * FF_SECOND[1]), BF16, ANY)],
         [pltpu.VMEM((own, d_model), BF16)]
-        + reduce_buffers(own, d_model)
-        + sems(REDUCE_SEMS + GATHER_SEMS)
+        + reduce_buffers(own // PARTS, d_model) * PARTS
+        + sems((REDUCE_SEMS + GATHER_SEMS) * PARTS)
         + [
-            pltpu.SemaphoreType.DMA,
+            pltpu.SemaphoreType.DMA((PARTS,)),
             pltpu.VMEM((d_model, 2 * FF_FIRST[1]), BF16),
             pltpu.VMEM((d_model, 2 * FF_SECOND[1]), BF16),
             pltpu.SemaphoreType.DMA((2,)),
@@ -1238,23 +1386,24 @@
         90,
     )(grads_a, parts[0], grads_b, parts[1], middle, cot, mlp_scale, hidden_b, second, cot_all)
     ff_sums = [line_reduce(sums_a), line_reduce(sums_b)]
-    def finish(total_rows, count_of):
-        got = plane_swap(total_rows.reshape(plane, own_rows, -1)).reshape(plane, own_rows, count_of, -1)
-        return [got[:, :, k] for k in range(count_of)]
+    def by_owner(total_rows):
+        return total_rows.reshape(plane, own_rows, -1)
 
     def widen(pieces):
         return jnp.concatenate(pieces, axis=2).transpose(1, 0, 2).reshape(own_rows, -1).astype(F32)
 
-    grad_att, ff_sums[0] = lax.optimization_barrier((grad_att, ff_sums[0]))
-    grads_mix, heads_full, sums, block_output = comm_call(
+    sums_out = outer_call(grad_att, mixed)
+    grad_att, sums_out = lax.optimization_barrier((grad_att, sums_out))
+    grads_mix, heads_full, sums, block_output, swapped_a = comm_call(
         functools.partial(mixer_back_kernel, line, groups, streams, span),
         6,
-        [ANY] + [VMEM] * 4 + [ANY] * 4 + [VMEM] * 9 + [ANY, VMEM, ANY, VMEM],
+        [ANY, VMEM] + [ANY] * 6 + [VMEM] * 9 + [VMEM, ANY, VMEM, ANY, VMEM, ANY],
         [
             ((count, 2 * width), BF16, VMEM),
             ((width, 2 * width), F32, VMEM),
             ((8, width), F32, VMEM),
             ((own, d_model), BF16, VMEM),
+            ((plane, own_rows, 3 * FF_FIRST[1]), BF16, ANY),
         ],
         [
             pltpu.VMEM((2, 256, d_model), BF16),
@@ -1265,27 +1414,23 @@
             pltpu.VMEM(*edge),
             pltpu.VMEM((16, wide), F32),
             pltpu.VMEM((line - 1, 16, wide), F32),
-            pltpu.VMEM((2, 4, span, width), F32),
+            pltpu.VMEM((2, 2, 256, width), F32),
+            pltpu.VMEM((4, 2, 256, width), F32),
             pltpu.VMEM((d_model, FF_FIRST[1]), BF16),
             pltpu.VMEM((d_model, FF_SECOND[1]), BF16),
         ]
         + reduce_buffers(own, d_model)
-        + sems(line + REDUCE_SEMS)
-        + [pltpu.SemaphoreType.DMA((2,))] * 2
-        + [pltpu.SemaphoreType.DMA((2, 4))],
+        + sems(line + REDUCE_SEMS + 7)
+        + [pltpu.SemaphoreType.DMA((3,)), pltpu.SemaphoreType.DMA((2,))]
+        + [pltpu.SemaphoreType.DMA((2, 2)), pltpu.SemaphoreType.DMA((2, 4))],
         70,
     )(
-        grad_att, output_w, branch, states, decay, rate, keep, scale, conv, enter, ends, inner, halo, off, offx,
-        wbd, vec, hidden_a, parts[0], hidden_b, parts[1], middle,
+        grad_att, output_w, value, *factors, decay, ends, inner, head_rows, halo, off, offx, wbd, vec,
+        hidden_a, parts[0], hidden_b, parts[1], middle, by_owner(ff_sums[0]),
     )
-    (w_output_grad,) = (widen([p]) for p in finish(line_reduce(outer_call(grad_att, mixed)), 1))
     grads_mix, ff_sums[1] = lax.optimization_barrier((grads_mix, ff_sums[1]))
     sums_mix = outer_call(normed, grads_mix)
     grads_mix, sums_mix = lax.optimization_barrier((grads_mix, sums_mix))
-    halves_a, halves_b = (finish(total, 3) for total in ff_sums)
-    w_gate_grad, w_up_grad, w_down_grad = (widen([p, q]) for p, q in zip(halves_a, halves_b))
-
-    w_branch_grad, w_input_grad = (widen([p]) for p in finish(line_reduce(sums_mix), 2))
 
     heads_grad = jnp.concatenate(
         [
@@ -1300,35 +1445,57 @@
         ],
         axis=0,
     )
-    pack_rows = -(-(chunk + extra) // 8) * 8
+    pack_rows = -(-(chunk + extra) // 16) * 16
     minor_pack = sums.reshape(8, line, chunk).transpose(1, 0, 2).reshape(line, 8 * chunk)
     minor_pack = jnp.pad(minor_pack, ((0, 0), (0, spare))).reshape(line, extra, 2 * WIDTH)
     out_pack = jnp.concatenate([heads_grad.reshape(line, chunk, 2 * WIDTH), minor_pack], axis=1)
-    out_pack = jnp.pad(out_pack, ((0, 0), (0, pack_rows - chunk - extra), (0, 0)))
+    out_pack = jnp.pad(out_pack, ((0, 0), (0, pack_rows - chunk - extra), (0, 0))).astype(BF16)
     pack32 = (pack_rows, 2 * WIDTH)
     gain_tiles = plane * own_rows // LANES
     deep = -(-2 * line // 8) * 8
-    input_grad, summed, gain_sum = comm_call(
+    input_grad, summed, gain_mid, swapped_b = comm_call(
         functools.partial(last_kernel, line, own_rows),
         7,
-        [VMEM, ANY] + [VMEM] * 5,
-        [own32, (pack32, F32, VMEM), ((8, LANES), F32, VMEM)],
-        reduce_buffers(own, d_model)
+        [VMEM, ANY] + [VMEM] * 5 + [ANY],
+        [
+            own32,
+            (pack32, F32, VMEM),
+            ((line, 8, LANES), F32, VMEM),
+            ((plane, own_rows, 3 * FF_SECOND[1]), BF16, ANY),
+        ],
+        reduce_buffers(own // PARTS, d_model) * PARTS
         + [
             pltpu.VMEM((d_model, 2 * width), BF16),
             pltpu.VMEM((8, d_model), F32),
-            pltpu.VMEM((line,) + pack32, F32),
+            pltpu.VMEM((line,) + pack32, BF16),
             pltpu.VMEM((gain_tiles, deep, LANES), F32),
             pltpu.VMEM((7, deep, LANES), F32),
-            pltpu.VMEM((line, 8, LANES), F32),
-            pltpu.VMEM((line - 1, 8, LANES), F32),
         ]
-        + sems(REDUCE_SEMS + line + 7 + line - 1)
-        + [pltpu.SemaphoreType.DMA((2,))],
+        + sems(PARTS * REDUCE_SEMS + line + 14)
+        + [pltpu.SemaphoreType.DMA((3,))],
         60,
     )(
-        grads_mix, mixer_w, x, grad_middle, mixer_scale, mlp_gain_term, out_pack,
+        grads_mix, mixer_w, x, grad_middle, mixer_scale, mlp_gain_term, out_pack, by_owner(ff_sums[1]),
     )
+    swapped_mix, swapped_out, gain_sum = comm_call(
+        functools.partial(tail_kernel, line),
+        8,
+        [ANY, ANY, VMEM],
+        [
+            ((plane, own_rows, 2 * width), BF16, ANY),
+            ((plane, own_rows, width), BF16, ANY),
+            ((8, LANES), F32, VMEM),
+        ],
+        [pltpu.VMEM((line - 1, 8, LANES), F32)] + sems(14 + line - 1) + [pltpu.SemaphoreType.DMA((2,))],
+        10,
+    )(by_owner(line_reduce(sums_mix)), by_owner(line_reduce(sums_out)), gain_mid)
+    third = FF_FIRST[1], FF_SECOND[1]
+    w_gate_grad, w_up_grad, w_down_grad = (
+        widen([swapped_a[:, :, k * third[0] : (k + 1) * third[0]], swapped_b[:, :, k * third[1] : (k + 1) * third[1]]])
+        for k in range(3)
+    )
+    w_branch_grad, w_input_grad = widen([swapped_mix[:, :, :width]]), widen([swapped_mix[:, :, width:]])
+    w_output_grad = widen([swapped_out])
     input_grad = input_grad.reshape(streams_own, span, d_model)
     block_output = block_output.reshape(streams_own, span, d_model)
     gate_weight_grad = summed[:chunk]

time: 692 us -> 635 us (0.918)
  Pallas kernels: 577 us -> 556 us
  starting transfers between devices: 16.2 us -> 1.79 us
  local copies, waits for them, and re-layouts: 45.8 us -> 32.3 us
    pallas_call x1, Pallas kernels: 88.8 us -> 68.7 us  [shards(): comm_call(functools.partial(last_kernel, line, own_rows), 7, [VMEM, ANY]...]
    all_to_all x4 -> x0, starting transfers between devices: 14.9 us -> none  [plane_swap(): lax.all_to_all(value, PLANE, split_axis=0, concat_axis=0, tiled=False)]
    pallas_call x1 -> x2, Pallas kernels: 88.1 us -> 98.7 us  [the longest x1 82.1 us: shards(): comm_call(middle_kernel, 4, [VMEM] * 7 + [ANY] * 7, [own32, tall] + [full...]
    pallas_call x1, Pallas kernels: 78.4 us -> 70.2 us  [shards(): comm_call(functools.partial(mixer_back_kernel, line, groups, streams, spa...]
  transfers between devices with their start and end apart: 12 -> 8, of which waited for: 3 -> 1; matrix products, arithmetic and copies ran while one was open for 6% -> 4% of each run, Pallas kernels for 81% -> 83%
where the time goes in v3:
time: 635 us; the launch traced here: 624 us
  Pallas kernels  556 us (88%)
  local copies, waits for them, and re-layouts  32.3 us (5%)
  between operations  14.8 us (2%)
  waiting for transfers between devices  11.9 us (2%)
  other arithmetic  7.9 us (1%)
    pallas_call x1, Pallas kernels, shards(): comm_call(grad_middle_kernel, 5, [VMEM, ANY, VMEM, ANY] + [VMEM] * 4 + [A...  99.8 us
    pallas_call x1, Pallas kernels, shards(): comm_call(middle_kernel, 4, [VMEM] * 7 + [ANY] * 7, [own32, tall] + [full...  82.1 us
    pallas_call x1, Pallas kernels, shards(): comm_call(functools.partial(mixer_back_kernel, line, groups, streams, spa...  70.2 us
    pallas_call x1, Pallas kernels, shards(): comm_call(functools.partial(last_kernel, line, own_rows), 7, [VMEM, ANY]...  68.7 us
    pallas_call x1, Pallas kernels, shards(): comm_call(second_kernel, 2, [VMEM, VMEM, ANY, ANY, ANY], [tall] + swapped...  60.5 us
    pallas_call x1, Pallas kernels, shards(): comm_call(functools.partial(mixer_forward_kernel, line, groups, streams,...  59.4 us
    pallas_call x3, Pallas kernels, outer_call(): pl.pallas_call(outer_kernel, grid=(d_model // tile,), in_specs=specs, out...  42 us
    pallas_call x2, Pallas kernels, ff_call(): pl.pallas_call(ff_kernel, grid=(count // tile,), in_specs=[tokens, tokens...  33.7 us
  transfers between devices with their start and end apart: 8, of which 1 were waited for; matrix products, arithmetic and copies ran while one was open for 4% of the time, Pallas kernels for 83%

profile of v3, /device:TPU:0, one launch (start us, length us, event | category | flops | bytes accessed | tf_op | source)
XLA Modules:
  0.0 624.2 jit_solution(2794745137112733863)
XLA Ops:
  7.3 0.8 pad_maximum_fusion.2
  8.1 1.3 reshape.273
  9.5 1.3 reshape.274
  10.8 0.3 reshape.275
  11.4 0.7 maximum_maximum_fusion.1.packed
  12.1 1.3 pad_maximum_fusion.mix
  13.4 0.6 broadcast_in_dim.65.gain
  14.0 22.6 %shard_map.271 = (bf16[8,64,960]{2,1,0:T(8,128)(2,1)}, f32[4,8,8,128]{3,2,1,0:T(8,128)}, bf16[4,96,320]{2,1,0:T(8,128)(2,1)}) custom-call(bf16[8,64,960]{2,1,0:T(8,128)(2,1)} %pad_maximum_fusion.mix, f32[8,128]{1,0:T(8,128)} %broadcast_in_dim.65.gain, bf16[96,320]{1,0:T(8,128)(2,1)} %maximum_maximum_fusion.1.packed), custom_call_target="tpu_custom_call" | custom-call | flops 15000000512 | bytes 1048576 | tf_op jit(solution)/shard_map/pallas_call | solution.py:1240
  36.7 0.9 slice.112
  37.7 0.7 reshape.277.gain
  38.3 60.5 %shard_map.272 = (bf16[2048,2048]{1,0:T(8,128)(2,1)}, bf16[8,64,1536]{2,1,0:T(8,128)(2,1)}) custom-call(bf16[256,2048]{1,0:T(8,128)(2,1)} %bitcast.77, f32[1,2048]{1,0:T(1,128)} %reshape.277.gain, bf16[64,6144]{1,0:T(8,128)(2,1)} %gate.3, bf16[64,6144]{1,0:T(8,128)(2,1)} %up.3, bf16[64,6144]{1,0:T(8,128)(2,1)} %down.3), custom_call_target="tpu_custom_call" | custom-call | flops 60000002048 | bytes 1048576 | tf_op jit(solution)/shard_map/pallas_call | solution.py:1268
  98.9 0.7 collective-permute-start
  100.0 0.7 reshape.282.gain
  100.7 0.2 broadcast_select_fusion.3
  100.9 1.0 pad_maximum_fusion.1.wbd
  102.1 0.7 maximum_maximum_fusion.2.vec
  102.8 0.2 reduce_window_sum.11
  103.0 0.1 select_reduce_fusion
  103.2 1.4 copy.55.off
  104.6 11.7 %all-gather.4.cloned.1.call-done.mix_w.mixer_w = bf16[2048,960]{1,0:T(8,128)(2,1)} async-done(((bf16[512,960]{1,0:T(8,128)(2,1)}), bf16[2048,960]{1,0:T(8,128)(2,1)}) %all-gather.4.cloned.1.call-update) | async-done | bytes 3932176 | tf_op jit(solution)/shard_map/all_gather | solution.py:1202
  116.2 59.4 %shard_map.273 = (f32[2048,320]{1,0:T(8,128)}, f32[2048,320]{1,0:T(8,128)}, bf16[2048,320]{1,0:T(8,128)(2,1)}, bf16[2048,320]{1,0:T(8,128)(2,1)}, f32[2048,320]{...) custom-call(bf16[2048,2048]{1,0:T(8,128)(2,1)} %get-tuple-element.72, ...), custom_call_target="tpu_custom_call" | custom-call | flops 49999998976 | bytes 1048576 | tf_op jit(solution)/shard_map/pallas_call | solution.py:1318
  175.7 0.3 reduce-scatter.5.cloned.1.call-start
  175.9 2.7 slice.152.weight.out_w
  178.6 82.1 %shard_map.274 = (f32[256,2048]{1,0:T(8,128)}, bf16[2048,2048]{1,0:T(8,128)(2,1)}, f32[2048,320]{1,0:T(8,128)}, f32[2048,320]{1,0:T(8,128)}, f32[2048,320]{1,0:T...) custom-call(bf16[2048,320]{1,0:T(8,128)(2,1)} %get-tuple-element.75.mixed.refs_1_, ...), custom_call_target="tpu_custom_call" | custom-call | flops 80000000000 | bytes 1048576 | tf_op jit(solution)/shard_map/pallas_call | solution.py:1344
  260.7 19.3 %shard_map.275 = (bf16[2048,1024]{1,0:T(8,128)(2,1)}, bf16[2048,512]{1,0:T(8,128)(2,1)}) custom-call(bf16[2048,2048]{1,0:T(8,128)(2,1)} %get-tuple-element.89.second.refs_0_, bf16[2048,2048]{1,0:T(8,128)(2,1)} %get-tuple-element.85.cot.refs_2_.cot_all, bf16[2048,1536]{1,0:T(8,128)(2,1)} %all-gather.6.cloned.1.call-done.gate_w.up_w.down_w.w1.part_a, ...), custom_call_target="tpu_custom_call" | custom-call | flops 12884901888 | bytes 16777216 | tf_op jit(solution)/shard_map/pallas_call | solution.py:1123
  280.0 19.2 %shard_map.276 = bf16[2048,1536]{1,0:T(8,128)(2,1)} custom-call(bf16[2048,2048]{1,0:T(8,128)(2,1)} %get-tuple-element.89.second.refs_0_, bf16[2048,1024]{1,0:T(8,128)(2,1)} %get-tuple-element.87.refs_1_.g1, bf16[2048,2048]{1,0:T(8,128)(2,1)} %get-tuple-element.85.cot.refs_2_.cot_all, bf16[2048,512]{1,0:T(8,128)(2,1)} %get-tuple-element.88.refs_3_.hidden_a), custom_call_target="tpu_custom_call" | custom-call | flops 12884901888 | bytes 23068672 | tf_op jit(solution)/shard_map/pallas_call | solution.py:1160
  299.2 0.4 reduce-scatter.7.cloned.1.call-start
  299.7 14.5 %shard_map.277 = (bf16[2048,512]{1,0:T(8,128)(2,1)}, bf16[2048,256]{1,0:T(8,128)(2,1)}) custom-call(bf16[2048,2048]{1,0:T(8,128)(2,1)} %get-tuple-element.89.second.refs_0_, bf16[2048,2048]{1,0:T(8,128)(2,1)} %get-tuple-element.85.cot.refs_2_.cot_all, bf16[2048,768]{1,0:T(8,128)(2,1)} %all-gather.8.cloned.1.call-done.gate_w.up_w.down_w.w2.part_b, ...), custom_call_target="tpu_custom_call" | custom-call | flops 6442450944 | bytes 16777216 | tf_op jit(solution)/shard_map/pallas_call | solution.py:1123
  314.2 99.8 %shard_map.278 = (f32[256,2048]{1,0:T(8,128)}, f32[8,2048]{1,0:T(8,128)}, bf16[2048,2048]{1,0:T(8,128)(2,1)}, bf16[2048,768]{1,0:T(8,128)(2,1)}) custom-call(bf16[2048,1024]{1,0:T(8,128)(2,1)} %get-tuple-element.87.refs_1_.g1, bf16[2048,1536]{1,0:T(8,128)(2,1)} %all-gather.6.cloned.1.call-done.gate_w.up_w.down_w.w1.part_a, ...), custom_call_target="tpu_custom_call" | custom-call | flops 89999998976 | bytes 1048576 | tf_op jit(solution)/shard_map/pallas_call | solution.py:1368
  414.1 0.6 copy-done.8
  414.7 1.5 copy.58.offx
  416.2 10.5 %shard_map.279 = bf16[2048,320]{1,0:T(8,128)(2,1)} custom-call(bf16[2048,2048]{1,0:T(8,128)(2,1)} %get-tuple-element.95.refs_0_.grad_att, bf16[2048,320]{1,0:T(8,128)(2,1)} %get-tuple-element.75.mixed.refs_1_), custom_call_target="tpu_custom_call" | custom-call | flops 2684354560 | bytes 9699328 | tf_op jit(solution)/shard_map/pallas_call | solution.py:1160
  426.7 0.2 reduce-scatter.9.cloned.1.call-start
  426.9 70.2 %shard_map.280 = (bf16[2048,640]{1,0:T(8,128)(2,1)}, f32[320,640]{1,0:T(8,128)}, f32[8,320]{1,0:T(8,128)}, bf16[256,2048]{1,0:T(8,128)(2,1)}, bf16[8,64,1536]{2,1,0:T(8,128)(2,1)}) custom-call(bf16[2048,2048]{1,0:T(8,128)(2,1)} %get-tuple-element.95.refs_0_.grad_att, bf16[2048,320]{1,0:T(8,128)(2,1)} %slice.152.weight.out_w, ...), custom_call_target="tpu_custom_call" | custom-call | flops 70000001024 | bytes 1048576 | tf_op jit(solution)/shard_map/pallas_call | solution.py:1397
  497.2 12.3 %shard_map.281 = bf16[2048,640]{1,0:T(8,128)(2,1)} custom-call(bf16[2048,2048]{1,0:T(8,128)(2,1)} %get-tuple-element.72.normed.refs_0_, bf16[2048,640]{1,0:T(8,128)(2,1)} %get-tuple-element.111.refs_1_.grads), custom_call_target="tpu_custom_call" | custom-call | flops 5368709120 | bytes 11010048 | tf_op jit(solution)/shard_map/pallas_call | solution.py:1160
  509.7 0.1 fusion.9
  510.0 0.8 fusion.2.pack
  510.8 68.7 %shard_map.282 = (f32[256,2048]{1,0:T(8,128)}, f32[96,320]{1,0:T(8,128)}, f32[4,8,128]{2,1,0:T(8,128)}, bf16[8,64,768]{2,1,0:T(8,128)(2,1)}) custom-call(bf16[2048,640]{1,0:T(8,128)(2,1)} %get-tuple-element.111.refs_1_.grads, bf16[2048,960]{1,0:T(8,128)(2,1)} %all-gather.4.cloned.1.call-done.mix_w.mixer_w, bf16[256,2048]{1,0:T(8,128)(2,1)} %bitcast.79, ...), custom_call_target="tpu_custom_call" | custom-call | flops 60000002048 | bytes 1048576 | tf_op jit(solution)/shard_map/pallas_call | solution.py:1456
  579.5 0.8 slice.138
  580.3 1.6 slice.137
  581.9 0.7 slice_reduce_fusion
  582.6 0.7 slice.141
  583.3 0.6 slice.139
  583.9 1.2 fusion.8
  585.1 0.1 fusion.7
  585.2 0.1 convert_bitcast_fusion
  585.4 1.3 copy.68
  586.8 1.3 copy.67
  588.2 1.3 copy.66
  589.5 0.5 slice_bitcast_fusion.2
  590.0 16.6 %shard_map.283 = (bf16[8,64,640]{2,1,0:T(8,128)(2,1)}, bf16[8,64,320]{2,1,0:T(8,128)(2,1)}, f32[8,128]{1,0:T(8,128)}) custom-call(bf16[8,64,640]{2,1,0:T(8,128)(2,1)} %bitcast.81, bf16[8,64,320]{2,1,0:T(8,128)(2,1)} %bitcast.82, f32[4,8,128]{2,1,0:T(8,128)} %get-tuple-element.120.mid), custom_call_target="tpu_custom_call" | custom-call | flops 10000000000 | bytes 1048576 | tf_op jit(solution)/shard_map/pallas_call | solution.py:1480
  606.7 0.8 constant_dynamic-slice_fusion
  607.5 0.5 slice_bitcast_fusion
  608.0 1.1 convert_bitcast_fusion.3
  609.1 0.5 copy.62
  609.6 1.0 reshape.296
  610.6 0.2 convert_bitcast_fusion.4
  610.8 0.5 copy.61
  611.3 1.0 reshape.295
  612.4 0.5 copy.60
  612.8 1.0 reshape.294
  613.9 1.0 copy.79
  614.8 1.0 copy-done
  615.8 1.3 copy.80
  (81 shorter events, 2.2 us)
Async XLA Ops:
  7.2 3.6 copy-start.5
  7.2 3.9 copy-start.12
  7.2 3.9 copy-start.13
  7.2 109.0 %all-gather.4.cloned.1.call-start = ((), (), s32[]{:S(2)}) async-start(), calls=%async_computation.4 | async-start | bytes 5242880 | tf_op jit(solution)/shard_map/all_gather | solution.py:1202
  8.1 3.3 copy-start.9
  36.6 224.1 %all-gather.6.cloned.1.call-start = ((), (), s32[]{:S(2)}) async-start(), calls=%async_computation.5 | async-start | bytes 7864320 | tf_op jit(solution)/shard_map/all_gather | solution.py:1202
  38.3 60.6 %copy-start.11 = (s32[2,4]{1,0:T(2,128)S(1)}, s32[2,4]{1,0:T(2,128)}, u32[]{:S(2)}) copy-start(s32[2,4]{1,0:T(2,128)} %param.18) | copy-start | bytes 100
  38.3 61.3 %copy-start.6 = (bf16[4,96,320]{2,1,0:T(8,128)(2,1)S(1)}, bf16[4,96,320]{2,1,0:T(8,128)(2,1)}, u32[]{:S(2)}) copy-start(bf16[4,96,320]{2,1,0:T(8,128)(2,1)} %get-tuple-element.74) | copy-start | bytes 737284
  98.9 200.8 %all-gather.8.cloned.1.call-start = ((), (), s32[]{:S(2)}) async-start(), calls=%async_computation.6 | async-start | bytes 3932160 | tf_op jit(solution)/shard_map/all_gather | solution.py:1202
  98.9 3.8 collective-permute-start
  103.1 72.5 %copy-start.7 = (s32[16,144,1]{1,0,2:T(8,128)}, s32[16,144,1]{1,0,2:T(8,128)S(1)}, u32[]{:S(2)}) copy-start(s32[16,144,1]{1,0,2:T(8,128)S(1)} %sub.40) | copy-start | bytes 27652
  175.7 251.3 %reduce-scatter.5.cloned.1.call-start = ((), (), s32[]{:S(2)}) async-start(), calls=%async_computation.7 | async-start | bytes 7864320 | tf_op jit(solution)/shard_map/reduce_scatter | solution.py:1206
  299.2 197.9 %reduce-scatter.7.cloned.1.call-start = ((), (), s32[]{:S(2)}) async-start(), calls=%async_computation.8 | async-start | bytes 3932160 | tf_op jit(solution)/shard_map/reduce_scatter | solution.py:1206
  414.0 0.7 copy-start.8
  414.0 176.0 %reduce-scatter.11.cloned.1.call-start = ((), (), s32[]{:S(2)}) async-start(), calls=%async_computation.10 | async-start | bytes 1966080 | tf_op jit(solution)/shard_map/reduce_scatter | solution.py:1206
  426.7 163.3 %reduce-scatter.9.cloned.1.call-start = ((), (), s32[]{:S(2)}) async-start(), calls=%async_computation.9 | async-start | bytes 3276800 | tf_op jit(solution)/shard_map/reduce_scatter | solution.py:1206
  497.2 12.3 %copy-start.10 = (f32[8,320]{1,0:T(8,128)S(1)}, f32[8,320]{1,0:T(8,128)}, u32[]{:S(2)}) copy-start(f32[8,320]{1,0:T(8,128)} %get-tuple-element.115) | copy-start | bytes 30724
  497.2 12.5 %copy-start.4 = (f32[320,640]{1,0:T(8,128)S(1)}, f32[320,640]{1,0:T(8,128)}, u32[]{:S(2)}) copy-start(f32[320,640]{1,0:T(8,128)} %get-tuple-element.114) | copy-start | bytes 2457604
  579.5 5.6 copy-start.1
  608.0 2.6 copy-start.3
  611.3 2.5 copy-start.2
  613.9 2.0 copy-start
Sparse Core Ops, SparseCore 0:
  36.7 79.4 all-gather.3
  117.8 115.9 all-gather.5
  235.4 61.8 all-gather.7
  299.5 109.8 reduce-scatter.4
  414.1 60.9 reduce-scatter.6
  477.3 35.3 reduce-scatter.10
  514.9 55.5 reduce-scatter.8

commit v4 on v3

--- a/solution.py
+++ b/solution.py
@@ -124,6 +124,8 @@
 GATHER_SEMS = 9
 REDUCE_SEMS = 10
 PARTS = 2
+SUM_SEMS = 4 + 6 * PARTS
+SUM_BUFS = 2 + 14 * PARTS
 
 
 def gather_start(own, out, send, base, local_sem, spot, whole=None, low=0):
@@ -269,10 +271,10 @@
     ]
 
 
-def for_total_rows(acc, bufs, body, low=0):
+def for_total_rows(acc, firsts, seconds, body, low=0):
     half = acc.shape[0] // 2
     step = 16
-    for first, second, start in ((bufs[7], bufs[13], 0), (bufs[9], bufs[14], half)):
+    for (first, second), start in ((firsts, 0), (seconds, half)):
 
         @pl.loop(0, half // step)
         def _(i):
@@ -282,31 +284,106 @@
             body(places, acc[rows, :] + first[at, :].astype(F32) + second[at, :].astype(F32))
 
 
-def plane_sum(pairs, sets, send, spot, body, own=None, out=None, local_sem=None, slow=False):
-    parts = len(sets) // 16
-    sets = [sets[16 * i : 16 * i + 16] for i in range(parts)]
-    count = sets[0][0].shape[0]
-    whole = parts * count
-    runs = [
-        reduce_plane(pairs, held[0], held[1:], send, i * REDUCE_SEMS, spot, whole, i * count)
-        for i, held in enumerate(sets)
-    ]
-    if slow:
-        order = [0] * 7 + [1] * 3 + [0] + [1] * 2 + [0] + [1] * 4
-    else:
-        order = [0] * 7 + [1] * 7 + [0, 1, 0, 1]
-    opened, started = [], []
-    for i in order:
-        got = next(runs[i])
-        if got is None:
-            continue
-        opened += got
-        for_total_rows(sets[i][0], sets[i][1:], body, i * count)
+def plane_sum(pairs, bufs, send, spot, body, own=None, out=None, local_sem=None):
+    sib_out, sib_in = bufs[:2]
+    sets = [bufs[2 + 14 * i : 16 + 14 * i] for i in range(PARTS)]
+    me, sib, xn, yn = spot
+    count, cols = sib_in.shape[1:]
+    part = count // PARTS
+    half = part // 2
+    tile = 512
+
+    def block(r, core, store):
+        place = (me[0], me[1] if r < 2 else 1 - me[1], core, me[3] if r % 2 == 0 else 1 - me[3])
+        rows = block_rows(number(place), count)
+
+        @pl.loop(0, cols // tile)
+        def _(j):
+            at = pl.ds(pl.multiple_of(j * tile, tile), tile)
+            total = None
+            for a, b in pairs:
+                product = lax.dot_general(a[rows, :], b[at, :], last_contract, preferred_element_type=F32)
+                total = product if total is None else total + product
+            store(at, total)
+
+    siblings, sent = {}, [[] for _ in sets]
+
+    def to_sibling(r):
+        def store(at, total):
+            sib_out[r % 2, :, at] = total.astype(BF16)
+
+        if r < 2:
+            siblings[r + 2].wait_send()
+        block(r, 1 - me[2], store)
+        siblings[r] = send(r, sib_out.at[r % 2], sib_in.at[r], sib)
+
+    def own_block(r, store):
+        def both(at, total):
+            total = total + sib_in[r, :, at].astype(F32)
+            for i, held in enumerate(sets):
+                store(held, at, total[i * part : (i + 1) * part])
+
+        siblings[r].wait_recv()
+        block(r, me[2], both)
+
+    def store3(held, at, total):
+        held[1][:, at] = total.astype(BF16)
+
+    def store2(held, at, total):
+        held[2][:, at] = total[:half].astype(BF16)
+        held[5][:, at] = total[half:]
+
+    def store1(held, at, total):
+        held[3][:, at] = total[half:].astype(BF16)
+        held[4][:, at] = total[:half]
+
+    def store0(held, at, total):
+        held[0][:, at] = total
+
+    def base(i):
+        return 4 + 6 * i
+
+    to_sibling(3)
+    to_sibling(2)
+    own_block(3, store3)
+    for i, held in enumerate(sets):
+        sent[i].append(send(base(i), held[1].at[pl.ds(0, half), :], held[7], xn))
+        sent[i].append(send(base(i) + 1, held[1].at[pl.ds(half, half), :], held[9], yn))
+    to_sibling(1)
+    own_block(2, store2)
+    for i, held in enumerate(sets):
+        sent[i].append(send(base(i) + 2, held[2], held[6], xn))
+    own_block(1, store1)
+    for i, held in enumerate(sets):
+        sent[i].append(send(base(i) + 3, held[3], held[8], yn))
+    to_sibling(0)
+    own_block(0, store0)
+    for i, held in enumerate(sets):
+        sent[i][0].wait_recv()
+        held[10][...] = (held[4][...] + held[7][...].astype(F32)).astype(BF16)
+        sent[i].append(send(base(i) + 4, held[10], held[12], yn))
+        sent[i][1].wait_recv()
+        held[11][...] = (held[5][...] + held[9][...].astype(F32)).astype(BF16)
+        sent[i].append(send(base(i) + 5, held[11], held[13], xn))
+    opened, started = [siblings[0], siblings[1]], []
+    for i, held in enumerate(sets):
+        for copy in sent[i][2:]:
+            copy.wait_recv()
+        opened += sent[i]
+        for_total_rows(held[0], (held[6], held[12]), (held[8], held[13]), body, i * part)
         if own is not None:
-            part = own.at[pl.ds(i * count, count), :]
-            base = parts * REDUCE_SEMS + i * GATHER_SEMS
-            started.append(gather_start(part, out, send, base, local_sem.at[i], spot, whole, i * count))
+            rows = own.at[pl.ds(i * part, part), :]
+            gather_base = SUM_SEMS + i * GATHER_SEMS
+            started.append(gather_start(rows, out, send, gather_base, local_sem.at[i], spot, count, i * part))
     return opened, started
+
+
+def sum_buffers(count, cols):
+    part = count // PARTS
+    half = pltpu.VMEM((part // 2, cols), BF16)
+    half32 = pltpu.VMEM((part // 2, cols), F32)
+    one = [pltpu.VMEM((part, cols), F32), pltpu.VMEM((part, cols), BF16), half, half, half32, half32] + [half] * 8
+    return [pltpu.VMEM((2, count, cols), BF16), pltpu.VMEM((4, count, cols), BF16)] + one * PARTS
 
 
 def load_columns(pairs, load_sem):
@@ -334,7 +411,7 @@
     mixed, weight, tokens, gain, off, vec, enter, slope, conv, rate, keep, scale, decay, states,
     middle, second, state_slope, rate_factor, log_factor, keep_factor, conv_factor, own, *rest
 ):
-    sets, rest = rest[: 16 * PARTS], rest[16 * PARTS :]
+    bufs, rest = rest[:SUM_BUFS], rest[SUM_BUFS:]
     send_sem, recv_sem, local_sem, flat_in, tile_in, flat_out, in_sem, out_sem = rest
     spot = where_am_i()
     span, width = flat_in.shape[2], conv.shape[1]
@@ -361,7 +438,7 @@
         middle[rows, :] = value
         own[rows, :] = norm_forward(value, gain[...])
 
-    opened, started = plane_sum([(mixed, weight)], sets, send, spot, body, own, second, local_sem)
+    opened, started = plane_sum([(mixed, weight)], bufs, send, spot, body, own, second, local_sem)
     first_row = lax.broadcasted_iota(jnp.int32, (span, width), 0) == 0
 
     def fill(g):
@@ -419,7 +496,7 @@
     g1, w1, g2, w2, middle, cot, gain, hidden, second, cot_all,
     grad_middle, gain_grad, gathered, outer, own, *rest
 ):
-    sets, rest = rest[: 16 * PARTS], rest[16 * PARTS :]
+    bufs, rest = rest[:SUM_BUFS], rest[SUM_BUFS:]
     send_sem, recv_sem, local_sem, v1, v2, load_sem, left, strip, left_sem, strip_sem = rest
     fill_tile = left.shape[3]
     fill_count = second.shape[1] // fill_tile
@@ -453,7 +530,7 @@
         own[rows, :] = value.astype(BF16)
         gain_grad[0:1, :] += term
 
-    opened, started = plane_sum(pairs, sets, send, spot, body, own, gathered, local_sem, slow=True)
+    opened, started = plane_sum(pairs, bufs, send, spot, body, own, gathered, local_sem)
     size = g2.shape[1]
 
     def fill(i):
@@ -487,27 +564,92 @@
         copy.wait_send()
 
 
-def tail_kernel(line, summed_mix, summed_out, mid, swapped_mix, swapped_out, gain_sum, far, send_sem, recv_sem, local_sem):
+def signal_pack(me, line, sources):
+    t = number(me)
+    plane = 8
+    index = me[0] * plane + t
+    slice_of = index // line
+    to_self = slice_of == t
+    barrier = pltpu.get_barrier_semaphore()
+    for k in range(line):
+        if sources:
+            partner = holder((t * line + k) // plane, lax.rem(t * line + k, plane))
+            other = t * line + k != index
+        else:
+            partner = holder(lax.rem(me[0] + k, line), slice_of)
+            other = jnp.logical_not(to_self) if k == 0 else None
+
+        def signal(partner=partner):
+            pl.semaphore_signal(barrier, inc=1, device_id=partner, device_id_type=MESH)
+
+        signal() if other is None else pl.when(other)(signal)
+    return line - 1 + jnp.where(to_self, 0, 1)
+
+
+def greet_also(partners, more):
+    barrier = pltpu.get_barrier_semaphore()
+    for partner in partners:
+        pl.semaphore_signal(barrier, inc=1, device_id=partner, device_id_type=MESH)
+    pl.semaphore_wait(barrier, len(partners) + more)
+
+
+def tail_kernel(
+    line, summed, mid, pack, branch_grad, input_grad, gain_sum, pack_sum,
+    land, far, pack_in, send_sem, recv_sem, local_sem
+):
     me = where_am_i()[0]
+    t = number(me)
+    plane = 8
+    index = me[0] * plane + t
+    to_self = index // line == t
     peers = plane_peers(me)
     others = [(lax.rem(me[0] + k, line),) + me[1:] for k in range(1, line)]
-    greet(peers + others)
+    greet_also(peers + others, signal_pack(me, line, sources=False))
     send = sender(send_sem, recv_sem)
-    swaps = [
-        swap_back_start(src, dst, send, 7 * k, local_sem.at[k], me, peers)
-        for k, (src, dst) in enumerate(((summed_mix, swapped_mix), (summed_out, swapped_out)))
-    ]
-    out = [send(14 + k, mid.at[other[0]], far.at[k], other) for k, other in enumerate(others)]
+    swap = swap_back_start(summed, land, send, 0, local_sem.at[0], me, peers)
+    out = [send(7 + k, mid.at[other[0]], far.at[k], other) for k, other in enumerate(others)]
+    pack_base = 6 + line
+
+    def pack_copy(j, slot):
+        target = t * line + j
+        return pltpu.make_async_remote_copy(
+            src_ref=pack.at[j],
+            dst_ref=pack_in.at[slot],
+            send_sem=send_sem.at[pack_base + j],
+            recv_sem=recv_sem.at[pack_base + slot],
+            device_id=holder(target // plane, lax.rem(target, plane)),
+            device_id_type=MESH,
+        )
+
+    for j in range(line):
+        own_pack = pltpu.make_async_copy(pack.at[j], pack_in.at[me[0]], local_sem.at[1])
+        pl.when(t * line + j != index)(pack_copy(j, me[0]).start)
+        pl.when(t * line + j == index)(own_pack.start)
+    width = land.shape[2] // 2
+    swap_end(swap)
+    for dst, low in ((branch_grad, 0), (input_grad, width)):
+        for i in range(0, plane, 2):
+            both = [land[i + j, :, low : low + width].astype(F32) for j in range(2)]
+            dst[:, i * width : (i + 2) * width] = jnp.concatenate(both, axis=1)
     value = mid[me[0]]
     for copy in out:
         copy.wait_recv()
     for k in range(line - 1):
         value = value + far[k]
     gain_sum[...] = value
-    for swap in swaps:
-        swap_end(swap)
+    for z in range(line):
+        source_is_me = jnp.logical_and(to_self, me[0] == z)
+        pl.when(jnp.logical_not(source_is_me))(pack_copy(z, z).wait_recv)
+        own_pack = pltpu.make_async_copy(pack.at[z], pack_in.at[z], local_sem.at[1])
+        pl.when(source_is_me)(own_pack.wait)
+    total = pack_in[0].astype(F32)
+    for z in range(1, line):
+        total = total + pack_in[z].astype(F32)
+    pack_sum[...] = total
     for copy in out:
         copy.wait_send()
+    for j in range(line):
+        pl.when(t * line + j != index)(pack_copy(j, me[0]).wait_send)
 
 
 def plane_peers(me):
@@ -524,42 +666,29 @@
     return peers
 
 
-def first_kernel(line, mix, gain, packed, mix_in, gains, arrived, send_sem, recv_sem, local_sem):
+def first_kernel(
+    line, branch, inner, out, gain, packed, mix_in, gains, arrived, mix, send_sem, recv_sem, local_sem
+):
     me = where_am_i()[0]
     t = number(me)
-    plane = mix.shape[0]
     peers = plane_peers(me)
     others = [(lax.rem(me[0] + k, line),) + me[1:] for k in range(1, line)]
+    plane = mix.shape[0]
+    width = branch.shape[1] // plane
+    for i in range(plane):
+        cols = slice(i * width, (i + 1) * width)
+        mix[i] = jnp.concatenate([branch[:, cols], inner[:, cols], out[:, cols]], axis=1)
     index = me[0] * plane + t
     slice_of, chunk_of = index // line, lax.rem(index, line)
     to_self = slice_of == t
-
-    barrier = pltpu.get_barrier_semaphore()
-    for partner in peers + others:
-        pl.semaphore_signal(barrier, inc=1, device_id=partner, device_id_type=MESH)
-    for j in range(line):
-        source = t * line + j
-
-        @pl.when(source != index)
-        def _():
-            partner = holder(source // plane, lax.rem(source, plane))
-            pl.semaphore_signal(barrier, inc=1, device_id=partner, device_id_type=MESH)
-
-    pl.semaphore_wait(barrier, len(peers) + 2 * len(others) + jnp.where(to_self, 0, 1))
-
+    greet_also(peers + others, signal_pack(me, line, sources=True))
     send = sender(send_sem, recv_sem)
     row = gains.at[me[0]]
     sent = [send(i, gain, row.at[t], peer) for i, peer in enumerate(peers)]
-    locals_ = [
-        pltpu.make_async_copy(mix.at[t], mix_in.at[t], local_sem.at[0]),
-        pltpu.make_async_copy(gain, row.at[t], local_sem.at[1]),
-    ]
-    for copy in locals_:
-        copy.start()
-    swaps = []
-    for i, peer in enumerate(peers):
-        swaps.append(send(7 + i, mix.at[number(peer)], mix_in.at[t], peer))
-    far_base, pack_base = 14, 13 + line
+    own_gain = pltpu.make_async_copy(gain, row.at[t], local_sem.at[0])
+    own_gain.start()
+    swap = swap_back_start(mix, mix_in, send, 7, local_sem.at[1], me, peers)
+    pack_base = 13 + line
 
     def pack_copy(k):
         return pltpu.make_async_remote_copy(
@@ -574,47 +703,34 @@
     for k in range(1, line):
         pack_copy(k).start()
     own_pack = pltpu.make_async_copy(packed, arrived.at[chunk_of], local_sem.at[2])
-
-    @pl.when(to_self)
-    def _():
-        own_pack.start()
-
-    @pl.when(jnp.logical_not(to_self))
-    def _():
-        pack_copy(0).start()
-
+    pl.when(to_self)(own_pack.start)
+    pl.when(jnp.logical_not(to_self))(pack_copy(0).start)
     for copy in sent:
         copy.wait_recv()
-    locals_[1].wait()
-    far = [send(far_base + i, row, row, other) for i, other in enumerate(others)]
-    for copy in swaps + far:
+    own_gain.wait()
+    far = [send(14 + i, row, row, other) for i, other in enumerate(others)]
+    for copy in far:
         copy.wait_recv()
+    swap_end(swap)
+    for copy in sent + far:
+        copy.wait_send()
     for j in range(line):
 
-        @pl.when(t * line + j != index)
-        def _():
+        def arrival(j=j):
             pltpu.make_async_remote_copy(
                 src_ref=packed,
                 dst_ref=arrived.at[j],
                 send_sem=send_sem.at[pack_base + j],
                 recv_sem=recv_sem.at[pack_base + j],
-                device_id=others[0],
+                device_id=peers[0],
                 device_id_type=MESH,
             ).wait_recv()
 
-    @pl.when(to_self)
-    def _():
-        own_pack.wait()
-
-    @pl.when(jnp.logical_not(to_self))
-    def _():
-        pack_copy(0).wait_send()
-
+        pl.when(t * line + j != index)(arrival)
+    pl.when(to_self)(own_pack.wait)
+    pl.when(jnp.logical_not(to_self))(pack_copy(0).wait_send)
     for k in range(1, line):
         pack_copy(k).wait_send()
-    for copy in sent + swaps + far:
-        copy.wait_send()
-    locals_[0].wait()
 
 
 def swap_start(sources, target, part, send, base, local_sem, me, peers):
@@ -651,12 +767,12 @@
         copy.wait()
 
 
-def second_kernel(tokens, gain, gate, up, down, normed, ff_in, own, send_sem, recv_sem, local_sem):
+def second_kernel(
+    tokens, gain, gate, up, down, normed, ff_in, own, send_sem, recv_sem, local_sem
+):
     spot = where_am_i()
     me = spot[0]
     peers = plane_peers(me)
-    greet(peers)
-    send = sender(send_sem, recv_sem)
     count = own.shape[0]
 
     @pl.loop(0, count // 16)
@@ -664,6 +780,8 @@
         rows = pl.ds(pl.multiple_of(i * 16, 16), 16)
         own[rows, :] = norm_forward(tokens[rows, :].astype(F32), gain[...])
 
+    greet(peers)
+    send = sender(send_sem, recv_sem)
     started = gather_start(own, normed, send, 21, local_sem.at[3], spot)
     passed = gather_pass(started, send, spot)
     swaps = swap_start((gate, up, down), ff_in, FF_FIRST, send, 0, local_sem, me, peers)
@@ -673,54 +791,23 @@
 
 def last_kernel(
     line, own_rows,
-    grads, mixer_w, tokens, grad_middle, gain, mlp_term, pack, summed,
-    input_grad, pack_sum, mid, swapped,
+    grads, mixer_w, tokens, grad_middle, gain, mlp_term, summed,
+    input_grad, mid, swapped,
     *rest,
 ):
-    sets, rest = rest[: 16 * PARTS], rest[16 * PARTS :]
-    held, mixer_term, pack_in, gain_out, near, send_sem, recv_sem, load_sem = rest
+    bufs, rest = rest[:SUM_BUFS], rest[SUM_BUFS:]
+    held, mixer_term, gain_out, near, send_sem, recv_sem, load_sem = rest
     spot = where_am_i()
     me = spot[0]
     t = number(me)
     plane = 8
     loads = load_columns(((mixer_w, 0, held),), load_sem)
     peers = plane_peers(me)
-    others = [(lax.rem(me[0] + k, line),) + me[1:] for k in range(1, line)]
-    index = me[0] * plane + t
-    slice_of, to_self = index // line, index // line == t
-    barrier = pltpu.get_barrier_semaphore()
-    for partner in peers + others:
-        pl.semaphore_signal(barrier, inc=1, device_id=partner, device_id_type=MESH)
-    for k in range(line):
-
-        def signal(k=k):
-            partner = holder(lax.rem(me[0] + k, line), slice_of)
-            pl.semaphore_signal(barrier, inc=1, device_id=partner, device_id_type=MESH)
-
-        signal() if k else pl.when(jnp.logical_not(to_self))(signal)
-    pl.semaphore_wait(barrier, len(peers) + 2 * len(others) + jnp.where(to_self, 0, 1))
-
+    greet(peers)
     send = sender(send_sem, recv_sem)
-    pack_base = PARTS * REDUCE_SEMS
-
-    def pack_copy(j, slot):
-        target = t * line + j
-        return pltpu.make_async_remote_copy(
-            src_ref=pack.at[j],
-            dst_ref=pack_in.at[slot],
-            send_sem=send_sem.at[pack_base + j],
-            recv_sem=recv_sem.at[pack_base + slot],
-            device_id=holder(target // plane, lax.rem(target, plane)),
-            device_id_type=MESH,
-        )
-
-    for j in range(line):
-        own_pack = pltpu.make_async_copy(pack.at[j], pack_in.at[me[0]], load_sem.at[1])
-        pl.when(t * line + j != index)(pack_copy(j, me[0]).start)
-        pl.when(t * line + j == index)(own_pack.start)
+    gain_base = SUM_SEMS
+    swap = swap_back_start(summed, swapped, send, gain_base + 7, load_sem.at[1], me, peers)
     loads[0].wait()
-    gain_base = pack_base + line
-    swap = swap_back_start(summed, swapped, send, gain_base + 7, load_sem.at[2], me, peers)
     mixer_term[...] = jnp.zeros(mixer_term.shape, F32)
 
     def body(rows, total):
@@ -728,7 +815,7 @@
         input_grad[rows, :] = grad_middle[rows, :] + back
         mixer_term[0:1, :] += term
 
-    opened, _ = plane_sum([(grads, held)], sets, send, spot, body)
+    opened, _ = plane_sum([(grads, held)], bufs, send, spot, body)
     per = plane * own_rows
     for z in range(line):
         for q in range(per // LANES):
@@ -747,20 +834,9 @@
         total = total + near[i]
     for z in range(line):
         mid[z] = jnp.concatenate([total[2 * z : 2 * z + 2], jnp.zeros((6, LANES), F32)], axis=0)
-    for z in range(line):
-        source_is_me = jnp.logical_and(to_self, me[0] == z)
-        pl.when(jnp.logical_not(source_is_me))(pack_copy(z, z).wait_recv)
-        own_pack = pltpu.make_async_copy(pack.at[z], pack_in.at[z], load_sem.at[1])
-        pl.when(source_is_me)(own_pack.wait)
-    total = pack_in[0].astype(F32)
-    for z in range(1, line):
-        total = total + pack_in[z].astype(F32)
-    pack_sum[...] = total
     for copy in opened + sent:
         copy.wait_send()
     swap_end(swap)
-    for j in range(line):
-        pl.when(t * line + j != index)(pack_copy(j, me[0]).wait_send)
 
 
 def chain_exchange(msg, arrived, send, base, me, line, direction):
@@ -1088,7 +1164,7 @@
     def body(rows, total):
         block_output[rows, :] = (middle[rows, :] + total).astype(BF16)
 
-    for_total_rows(acc, bufs, body)
+    for_total_rows(acc, (bufs[7], bufs[13]), (bufs[9], bufs[14]), body)
     head_copy.wait_recv()
     for j in range(streams):
         g = groups - streams + j
@@ -1140,20 +1216,27 @@
 
 
 def outer_kernel(*refs):
-    out, pairs = refs[-1], refs[:-1]
+    out, refs = refs[-1], refs[:-1]
     low = 0
-    for a, b in zip(pairs[::2], pairs[1::2]):
+    if len(refs) % 2:
+        low = refs[0].shape[1]
+        out[:, :low] = refs[0][...]
+        refs = refs[1:]
+    for a, b in zip(refs[::2], refs[1::2]):
         size = b.shape[1]
         part = lax.dot_general(a[...], b[...], rows_contract, preferred_element_type=F32)
         out[:, low : low + size] = part.astype(BF16)
         low += size
 
 
-def outer_call(*pairs):
+def outer_call(*pairs, first=None):
     count, d_model = pairs[0].shape
     tile = 256
     sizes = [b.shape[1] for b in pairs[1::2]]
-    specs = []
+    specs, low = [], 0
+    if first is not None:
+        low = first.shape[1]
+        specs.append(pl.BlockSpec((tile, low), lambda i: (i, 0)))
     for size in sizes:
         specs.append(pl.BlockSpec((count, tile), lambda i: (0, i)))
         specs.append(pl.BlockSpec((count, size), lambda i: (0, 0), pipeline_mode=pl.Buffered(1)))
@@ -1161,15 +1244,15 @@
         outer_kernel,
         grid=(d_model // tile,),
         in_specs=specs,
-        out_specs=pl.BlockSpec((tile, sum(sizes)), lambda i: (i, 0)),
-        out_shape=jax.ShapeDtypeStruct((d_model, sum(sizes)), BF16),
+        out_specs=pl.BlockSpec((tile, low + sum(sizes)), lambda i: (i, 0)),
+        out_shape=jax.ShapeDtypeStruct((d_model, low + sum(sizes)), BF16),
         compiler_params=pltpu.CompilerParams(vmem_limit_bytes=VMEM_LIMIT),
         cost_estimate=pl.CostEstimate(
             flops=2 * count * d_model * sum(sizes),
             bytes_accessed=2 * count * (d_model * len(sizes) + sum(sizes)),
             transcendentals=0,
         ),
-    )(*pairs)
+    )(*(() if first is None else (first,)), *pairs)
 
 
 ANY = pl.BlockSpec(memory_space=pl.ANY)
@@ -1222,9 +1305,6 @@
     width, hid = rw // plane, ff // plane
     my_line = lax.axis_index("line")
 
-    def by_target(weight):
-        return weight.reshape(own_rows, plane, width).transpose(1, 0, 2)
-
     gain_tile = jnp.concatenate([mixer_gain, mlp_gain]).astype(F32)
     gain_tile = jnp.pad(gain_tile, (0, LANES - gain_tile.shape[0]))
     gain_tile = jnp.broadcast_to(gain_tile[None], (8, LANES))
@@ -1240,19 +1320,15 @@
     mix_swapped, gains, arrived = comm_call(
         functools.partial(first_kernel, line),
         1,
-        [ANY] * 3,
+        [VMEM] * 3 + [ANY] * 2,
         [
             ((plane, own_rows, 3 * width), BF16, ANY),
             ((line, plane, 8, LANES), F32, ANY),
             ((line, pack_rows, 2 * WIDTH), BF16, ANY),
         ],
-        sems(13 + 2 * line) + [pltpu.SemaphoreType.DMA((3,))],
+        [pltpu.VMEM((plane, own_rows, 3 * width), BF16)] + sems(13 + 2 * line) + [pltpu.SemaphoreType.DMA((3,))],
         15,
-    )(
-        jnp.concatenate([by_target(w) for w in (w_branch, w_input, w_output)], axis=2),
-        gain_tile,
-        packed,
-    )
+    )(w_branch, w_input, w_output, gain_tile, packed)
     gains = gains[:, :, 0]
     mixer_scale = gains[:, :, :own_rows].reshape(1, d_model)
     mlp_scale = gains[:, :, own_rows : 2 * own_rows].reshape(1, d_model)
@@ -1347,8 +1423,8 @@
         [VMEM] * 7 + [ANY] * 7,
         [own32, tall] + [full] * 5,
         [pltpu.VMEM((own, d_model), BF16)]
-        + reduce_buffers(own // PARTS, d_model) * PARTS
-        + sems((REDUCE_SEMS + GATHER_SEMS) * PARTS)
+        + sum_buffers(own, d_model)
+        + sems(SUM_SEMS + GATHER_SEMS * PARTS)
         + [
             pltpu.SemaphoreType.DMA((PARTS,)),
             pltpu.VMEM((5, 2, span, width), F32),
@@ -1371,8 +1447,8 @@
         [VMEM, ANY, VMEM, ANY] + [VMEM] * 4 + [ANY] * 2,
         [own32, gain_rows, tall, ((d_model, 3 * FF_SECOND[1]), BF16, ANY)],
         [pltpu.VMEM((own, d_model), BF16)]
-        + reduce_buffers(own // PARTS, d_model) * PARTS
-        + sems((REDUCE_SEMS + GATHER_SEMS) * PARTS)
+        + sum_buffers(own, d_model)
+        + sems(SUM_SEMS + GATHER_SEMS * PARTS)
         + [
             pltpu.SemaphoreType.DMA((PARTS,)),
             pltpu.VMEM((d_model, 2 * FF_FIRST[1]), BF16),
@@ -1385,15 +1461,16 @@
         ],
         90,
     )(grads_a, parts[0], grads_b, parts[1], middle, cot, mlp_scale, hidden_b, second, cot_all)
-    ff_sums = [line_reduce(sums_a), line_reduce(sums_b)]
+    ff_sums = [line_reduce(sums_a)]
     def by_owner(total_rows):
         return total_rows.reshape(plane, own_rows, -1)
 
     def widen(pieces):
         return jnp.concatenate(pieces, axis=2).transpose(1, 0, 2).reshape(own_rows, -1).astype(F32)
 
-    sums_out = outer_call(grad_att, mixed)
+    sums_out = outer_call(grad_att, mixed, first=sums_b)
     grad_att, sums_out = lax.optimization_barrier((grad_att, sums_out))
+    ff_sums.append(line_reduce(sums_out))
     grads_mix, heads_full, sums, block_output, swapped_a = comm_call(
         functools.partial(mixer_back_kernel, line, groups, streams, span),
         6,
@@ -1428,7 +1505,6 @@
         grad_att, output_w, value, *factors, decay, ends, inner, head_rows, halo, off, offx, wbd, vec,
         hidden_a, parts[0], hidden_b, parts[1], middle, by_owner(ff_sums[0]),
     )
-    grads_mix, ff_sums[1] = lax.optimization_barrier((grads_mix, ff_sums[1]))
     sums_mix = outer_call(normed, grads_mix)
     grads_mix, sums_mix = lax.optimization_barrier((grads_mix, sums_mix))
 
@@ -1445,61 +1521,56 @@
         ],
         axis=0,
     )
-    pack_rows = -(-(chunk + extra) // 16) * 16
-    minor_pack = sums.reshape(8, line, chunk).transpose(1, 0, 2).reshape(line, 8 * chunk)
-    minor_pack = jnp.pad(minor_pack, ((0, 0), (0, spare))).reshape(line, extra, 2 * WIDTH)
-    out_pack = jnp.concatenate([heads_grad.reshape(line, chunk, 2 * WIDTH), minor_pack], axis=1)
-    out_pack = jnp.pad(out_pack, ((0, 0), (0, pack_rows - chunk - extra), (0, 0))).astype(BF16)
+    pack_rows = -(-(chunk + 8) // 16) * 16
+    minor_pack = sums.reshape(8, line, chunk).transpose(1, 0, 2)
+    minor_pack = jnp.pad(minor_pack, ((0, 0), (0, pack_rows - chunk - 8), (0, 2 * WIDTH - chunk)))
+    out_pack = jnp.concatenate([heads_grad.reshape(line, chunk, 2 * WIDTH), minor_pack], axis=1).astype(BF16)
     pack32 = (pack_rows, 2 * WIDTH)
     gain_tiles = plane * own_rows // LANES
     deep = -(-2 * line // 8) * 8
-    input_grad, summed, gain_mid, swapped_b = comm_call(
+    mids = ((line, 8, LANES), F32, VMEM)
+    input_grad, gain_mid, swapped_b = comm_call(
         functools.partial(last_kernel, line, own_rows),
         7,
-        [VMEM, ANY] + [VMEM] * 5 + [ANY],
-        [
-            own32,
-            (pack32, F32, VMEM),
-            ((line, 8, LANES), F32, VMEM),
-            ((plane, own_rows, 3 * FF_SECOND[1]), BF16, ANY),
-        ],
-        reduce_buffers(own // PARTS, d_model) * PARTS
+        [VMEM, ANY] + [VMEM] * 4 + [ANY],
+        [own32, mids, ((plane, own_rows, 3 * FF_SECOND[1] + width), BF16, ANY)],
+        sum_buffers(own, d_model)
         + [
             pltpu.VMEM((d_model, 2 * width), BF16),
             pltpu.VMEM((8, d_model), F32),
-            pltpu.VMEM((line,) + pack32, BF16),
             pltpu.VMEM((gain_tiles, deep, LANES), F32),
             pltpu.VMEM((7, deep, LANES), F32),
         ]
-        + sems(PARTS * REDUCE_SEMS + line + 14)
-        + [pltpu.SemaphoreType.DMA((3,))],
+        + sems(SUM_SEMS + 14)
+        + [pltpu.SemaphoreType.DMA((2,))],
         60,
     )(
-        grads_mix, mixer_w, x, grad_middle, mixer_scale, mlp_gain_term, out_pack, by_owner(ff_sums[1]),
+        grads_mix, mixer_w, x, grad_middle, mixer_scale, mlp_gain_term, by_owner(ff_sums[1]),
     )
-    swapped_mix, swapped_out, gain_sum = comm_call(
+    w_branch_grad, w_input_grad, gain_sum, summed = comm_call(
         functools.partial(tail_kernel, line),
         8,
-        [ANY, ANY, VMEM],
+        [ANY, VMEM, VMEM],
+        [((own_rows, rw), F32, VMEM)] * 2 + [((8, LANES), F32, VMEM), (pack32, F32, VMEM)],
         [
-            ((plane, own_rows, 2 * width), BF16, ANY),
-            ((plane, own_rows, width), BF16, ANY),
-            ((8, LANES), F32, VMEM),
-        ],
-        [pltpu.VMEM((line - 1, 8, LANES), F32)] + sems(14 + line - 1) + [pltpu.SemaphoreType.DMA((2,))],
-        10,
-    )(by_owner(line_reduce(sums_mix)), by_owner(line_reduce(sums_out)), gain_mid)
+            pltpu.VMEM((plane, own_rows, 2 * width), BF16),
+            pltpu.VMEM((line - 1, 8, LANES), F32),
+            pltpu.VMEM((line,) + pack32, BF16),
+        ]
+        + sems(6 + 2 * line)
+        + [pltpu.SemaphoreType.DMA((2,))],
+        15,
+    )(by_owner(line_reduce(sums_mix)), gain_mid, out_pack)
+    w_output_grad = widen([swapped_b[:, :, 3 * FF_SECOND[1] :]])
     third = FF_FIRST[1], FF_SECOND[1]
     w_gate_grad, w_up_grad, w_down_grad = (
         widen([swapped_a[:, :, k * third[0] : (k + 1) * third[0]], swapped_b[:, :, k * third[1] : (k + 1) * third[1]]])
         for k in range(3)
     )
-    w_branch_grad, w_input_grad = widen([swapped_mix[:, :, :width]]), widen([swapped_mix[:, :, width:]])
-    w_output_grad = widen([swapped_out])
     input_grad = input_grad.reshape(streams_own, span, d_model)
     block_output = block_output.reshape(streams_own, span, d_model)
     gate_weight_grad = summed[:chunk]
-    minor_grad = summed[chunk : chunk + extra].reshape(-1)[: 8 * chunk].reshape(8, chunk)
+    minor_grad = summed[chunk : chunk + 8, :chunk]
     low = lax.rem((lax.axis_index("pair") * 2 + lax.axis_index("core")) * 2 + lax.axis_index("batch"), LANES // own_rows)
     gain_grads = lax.dynamic_slice(gain_sum, (0, low * own_rows), (2, own_rows))
     return (

time: 635 us -> 623 us (0.981)
  the two profiles are of different devices: /device:TPU:0 before, /device:TPU:3 now
where the time goes in v4:
time: 623 us; the launch traced here: 614 us
  Pallas kernels  548 us (88%)
  local copies, waits for them, and re-layouts  27.4 us (4%)
  between operations  14.7 us (2%)
  waiting for transfers between devices  13.2 us (2%)
  other arithmetic  7.77 us (1%)
    pallas_call x1, Pallas kernels, shards(): comm_call(grad_middle_kernel, 5, [VMEM, ANY, VMEM, ANY] + [VMEM] * 4 + [A...  87.9 us
    pallas_call x1, Pallas kernels, shards(): comm_call(middle_kernel, 4, [VMEM] * 7 + [ANY] * 7, [own32, tall] + [full...  82.5 us
    pallas_call x1, Pallas kernels, shards(): comm_call(functools.partial(mixer_back_kernel, line, groups, streams, spa...  70.7 us
    pallas_call x1, Pallas kernels, shards(): comm_call(second_kernel, 2, [VMEM, VMEM, ANY, ANY, ANY], [tall] + swapped...  60.5 us
    pallas_call x1, Pallas kernels, shards(): comm_call(functools.partial(last_kernel, line, own_rows), 7, [VMEM, ANY]...  60.4 us
    pallas_call x1, Pallas kernels, shards(): comm_call(functools.partial(mixer_forward_kernel, line, groups, streams,...  59.9 us
    pallas_call x3, Pallas kernels, outer_call(): pl.pallas_call(outer_kernel, grid=(d_model // tile,), in_specs=specs, out...  43.1 us
    pallas_call x2, Pallas kernels, ff_call(): pl.pallas_call(ff_kernel, grid=(count // tile,), in_specs=[tokens, tokens...  33.5 us
  transfers between devices with their start and end apart: 7, of which 2 were waited for; matrix products, arithmetic and copies ran while one was open for 3% of the time, Pallas kernels for 81%

profile of v4, /device:TPU:3, one launch (start us, length us, event | category | flops | bytes accessed | tf_op | source)
XLA Modules:
  0.0 613.5 jit_solution(4802433068948038809)
XLA Ops:
  7.2 0.7 pad_maximum_fusion.1
  8.0 0.1 reshape.248
  8.1 0.7 maximum_convert_fusion
  8.9 1.5 maximum_maximum_fusion.1.packed
  10.4 0.6 broadcast_in_dim.65.gain
  11.0 23.0 %shard_map.271 = (bf16[8,64,960]{2,1,0:T(8,128)(2,1)}, f32[4,8,8,128]{3,2,1,0:T(8,128)}, bf16[4,96,320]{2,1,0:T(8,128)(2,1)}) custom-call(bf16[64,2560]{1,0:T(8,128)(2,1)} %branch.1, bf16[64,2560]{1,0:T(8,128)(2,1)} %inner.1, bf16[64,2560]{1,0:T(8,128)(2,1)} %out.1, f32[8,128]{1,0:T(8,128)} %broadcast_in_dim.65.gain, ...), custom_call_target="tpu_custom_call" | custom-call | flops 15000000512 | bytes 1048576 | tf_op jit(solution)/shard_map/pallas_call | solution.py:1320
  34.1 0.9 slice.107
  35.1 0.7 reshape.249.gain
  35.8 60.5 %shard_map.272 = (bf16[2048,2048]{1,0:T(8,128)(2,1)}, bf16[8,64,1536]{2,1,0:T(8,128)(2,1)}) custom-call(bf16[256,2048]{1,0:T(8,128)(2,1)} %bitcast.65, f32[1,2048]{1,0:T(1,128)} %reshape.249.gain, bf16[64,6144]{1,0:T(8,128)(2,1)} %gate.3, bf16[64,6144]{1,0:T(8,128)(2,1)} %up.3, bf16[64,6144]{1,0:T(8,128)(2,1)} %down.3), custom_call_target="tpu_custom_call" | custom-call | flops 60000002048 | bytes 1048576 | tf_op jit(solution)/shard_map/pallas_call | solution.py:1344
  96.5 1.1 collective-permute-start
  97.6 0.1 reshape.268
  97.7 0.1 slice.115
  97.8 0.1 slice.117
  97.9 0.7 reshape.254.gain
  98.6 0.2 broadcast_select_fusion.3
  98.8 1.0 pad_maximum_fusion.wbd
  100.0 0.7 maximum_maximum_fusion.2.vec
  100.7 0.2 reduce_window_sum.11
  100.9 0.1 select_reduce_fusion
  101.1 1.4 copy.46.off
  102.5 10.8 %all-gather.4.cloned.1.call-done.mix_w.mixer_w = bf16[2048,960]{1,0:T(8,128)(2,1)} async-done(((bf16[512,960]{1,0:T(8,128)(2,1)}), bf16[2048,960]{1,0:T(8,128)(2,1)}) %all-gather.4.cloned.1.call-update) | async-done | bytes 3932176 | tf_op jit(solution)/shard_map/all_gather | solution.py:1285
  113.3 59.9 %shard_map.273 = (f32[2048,320]{1,0:T(8,128)}, f32[2048,320]{1,0:T(8,128)}, bf16[2048,320]{1,0:T(8,128)(2,1)}, bf16[2048,320]{1,0:T(8,128)(2,1)}, f32[2048,320]{...) custom-call(bf16[2048,2048]{1,0:T(8,128)(2,1)} %get-tuple-element.70, ...), custom_call_target="tpu_custom_call" | custom-call | flops 49999998976 | bytes 1048576 | tf_op jit(solution)/shard_map/pallas_call | solution.py:1394
  173.2 0.6 reduce-scatter.4.cloned.1.call-start
  173.8 2.7 slice.144.weight.out_w
  176.5 82.5 %shard_map.274 = (f32[256,2048]{1,0:T(8,128)}, bf16[2048,2048]{1,0:T(8,128)(2,1)}, f32[2048,320]{1,0:T(8,128)}, f32[2048,320]{1,0:T(8,128)}, f32[2048,320]{1,0:T...) custom-call(bf16[2048,320]{1,0:T(8,128)(2,1)} %get-tuple-element.73.mixed.refs_2_, ...), custom_call_target="tpu_custom_call" | custom-call | flops 80000000000 | bytes 1048576 | tf_op jit(solution)/shard_map/pallas_call | solution.py:1420
  259.1 19.3 %shard_map.275 = (bf16[2048,1024]{1,0:T(8,128)(2,1)}, bf16[2048,512]{1,0:T(8,128)(2,1)}) custom-call(bf16[2048,2048]{1,0:T(8,128)(2,1)} %get-tuple-element.87.second.refs_0_, bf16[2048,2048]{1,0:T(8,128)(2,1)} %get-tuple-element.83.cot.refs_2_.cot_all, bf16[2048,1536]{1,0:T(8,128)(2,1)} %all-gather.6.cloned.1.call-done.gate_w.up_w.down_w.w1.part_a, ...), custom_call_target="tpu_custom_call" | custom-call | flops 12884901888 | bytes 16777216 | tf_op jit(solution)/shard_map/pallas_call | solution.py:1199
  278.4 19.2 %shard_map.276 = bf16[2048,1536]{1,0:T(8,128)(2,1)} custom-call(bf16[2048,2048]{1,0:T(8,128)(2,1)} %get-tuple-element.87.second.refs_0_, bf16[2048,1024]{1,0:T(8,128)(2,1)} %get-tuple-element.85.refs_1_.g1, bf16[2048,2048]{1,0:T(8,128)(2,1)} %get-tuple-element.83.cot.refs_2_.cot_all, bf16[2048,512]{1,0:T(8,128)(2,1)} %get-tuple-element.86.refs_3_.hidden_a), custom_call_target="tpu_custom_call" | custom-call | flops 12884901888 | bytes 23068672 | tf_op jit(solution)/shard_map/pallas_call | solution.py:1243
  297.5 0.2 reduce-scatter.6.cloned.1.call-start
  297.8 14.2 %shard_map.277 = (bf16[2048,512]{1,0:T(8,128)(2,1)}, bf16[2048,256]{1,0:T(8,128)(2,1)}) custom-call(bf16[2048,2048]{1,0:T(8,128)(2,1)} %get-tuple-element.87.second.refs_0_, bf16[2048,2048]{1,0:T(8,128)(2,1)} %get-tuple-element.83.cot.refs_2_.cot_all, bf16[2048,768]{1,0:T(8,128)(2,1)} %all-gather.8.cloned.1.call-done.gate_w.up_w.down_w.w2.part_b, ...), custom_call_target="tpu_custom_call" | custom-call | flops 6442450944 | bytes 16777216 | tf_op jit(solution)/shard_map/pallas_call | solution.py:1199
  312.0 87.9 %shard_map.278 = (f32[256,2048]{1,0:T(8,128)}, f32[8,2048]{1,0:T(8,128)}, bf16[2048,2048]{1,0:T(8,128)(2,1)}, bf16[2048,768]{1,0:T(8,128)(2,1)}) custom-call(bf16[2048,1024]{1,0:T(8,128)(2,1)} %get-tuple-element.85.refs_1_.g1, bf16[2048,1536]{1,0:T(8,128)(2,1)} %all-gather.6.cloned.1.call-done.gate_w.up_w.down_w.w1.part_a, ...), custom_call_target="tpu_custom_call" | custom-call | flops 89999998976 | bytes 1048576 | tf_op jit(solution)/shard_map/pallas_call | solution.py:1444
  400.0 11.7 %shard_map.279 = bf16[2048,1088]{1,0:T(8,128)(2,1)} custom-call(bf16[2048,768]{1,0:T(8,128)(2,1)} %get-tuple-element.93.refs_0_, bf16[2048,2048]{1,0:T(8,128)(2,1)} %get-tuple-element.94.refs_1_.grad_att, bf16[2048,320]{1,0:T(8,128)(2,1)} %get-tuple-element.73.mixed.refs_2_), custom_call_target="tpu_custom_call" | custom-call | flops 2684354560 | bytes 9699328 | tf_op jit(solution)/shard_map/pallas_call | solution.py:1243
  411.7 0.3 reduce-scatter.8.cloned.1.call-start
  412.0 0.4 copy-done.8
  412.4 1.5 copy.49.offx
  413.9 70.7 %shard_map.280 = (bf16[2048,640]{1,0:T(8,128)(2,1)}, f32[320,640]{1,0:T(8,128)}, f32[8,320]{1,0:T(8,128)}, bf16[256,2048]{1,0:T(8,128)(2,1)}, bf16[8,64,1536]{2,1,0:T(8,128)(2,1)}) custom-call(bf16[2048,2048]{1,0:T(8,128)(2,1)} %get-tuple-element.94.refs_1_.grad_att, bf16[2048,320]{1,0:T(8,128)(2,1)} %slice.144.weight.out_w, ...), custom_call_target="tpu_custom_call" | custom-call | flops 70000001024 | bytes 1048576 | tf_op jit(solution)/shard_map/pallas_call | solution.py:1474
  484.5 12.2 %shard_map.281 = bf16[2048,640]{1,0:T(8,128)(2,1)} custom-call(bf16[2048,2048]{1,0:T(8,128)(2,1)} %get-tuple-element.70.normed.refs_0_, bf16[2048,640]{1,0:T(8,128)(2,1)} %get-tuple-element.108.refs_1_.grads), custom_call_target="tpu_custom_call" | custom-call | flops 5368709120 | bytes 11010048 | tf_op jit(solution)/shard_map/pallas_call | solution.py:1243
  496.8 2.3 reduce-scatter.6.cloned.1.call-done
  499.1 60.4 %shard_map.282 = (f32[256,2048]{1,0:T(8,128)}, f32[4,8,128]{2,1,0:T(8,128)}, bf16[8,64,1088]{2,1,0:T(8,128)(2,1)}) custom-call(bf16[2048,640]{1,0:T(8,128)(2,1)} %get-tuple-element.108.refs_1_.grads, bf16[2048,960]{1,0:T(8,128)(2,1)} %all-gather.4.cloned.1.call-done.mix_w.mixer_w, bf16[256,2048]{1,0:T(8,128)(2,1)} %bitcast.67, ...), custom_call_target="tpu_custom_call" | custom-call | flops 60000002048 | bytes 1048576 | tf_op jit(solution)/shard_map/pallas_call | solution.py:1532
  559.7 1.1 convert_bitcast_fusion.3
  560.7 0.5 copy.51
  561.2 1.0 reshape.264
  562.2 1.2 fusion.7
  563.4 0.1 fusion.6
  563.6 0.1 convert_bitcast_fusion
  563.7 1.3 copy.57
  565.0 0.1 convert_bitcast_fusion.1
  565.1 1.3 copy.56
  566.4 0.1 convert_bitcast_fusion.2
  566.6 1.3 copy.55
  567.9 0.1 fusion.8
  568.0 0.1 maximum_maximum_fusion
  568.1 0.7 fusion.1.pack
  568.9 26.6 %shard_map.283 = (f32[64,2560]{1,0:T(8,128)}, f32[64,2560]{1,0:T(8,128)}, f32[8,128]{1,0:T(8,128)}, f32[96,320]{1,0:T(8,128)}) custom-call(bf16[8,64,640]{2,1,0:T(8,128)(2,1)} %bitcast.68, f32[4,8,128]{2,1,0:T(8,128)} %get-tuple-element.114.mid, bf16[4,96,320]{2,1,0:T(8,128)(2,1)} %fusion.1.pack), custom_call_target="tpu_custom_call" | custom-call | flops 15000000512 | bytes 1048576 | tf_op jit(solution)/shard_map/pallas_call | solution.py:1550
  595.5 1.4 slice.132
  596.9 1.3 slice_bitcast_fusion.2
  598.2 1.3 slice.133
  599.4 1.6 slice.131
  601.0 0.8 constant_dynamic-slice_fusion
  601.7 0.5 slice_bitcast_fusion
  602.2 1.0 copy.66
  603.2 1.3 copy.67
  604.5 0.2 copy-done.5
  604.8 0.8 copy.68
  605.6 0.8 copy.69
  (59 shorter events, 1.0 us)
Async XLA Ops:
  7.2 106.1 %all-gather.4.cloned.1.call-start = ((), (), s32[]{:S(2)}) async-start(), calls=%async_computation.3 | async-start | bytes 5242880 | tf_op jit(solution)/shard_map/all_gather | solution.py:1285
  34.1 225.0 %all-gather.6.cloned.1.call-start = ((), (), s32[]{:S(2)}) async-start(), calls=%async_computation.4 | async-start | bytes 7864320 | tf_op jit(solution)/shard_map/all_gather | solution.py:1285
  35.8 60.6 %copy-start.10 = (s32[2,4]{1,0:T(2,128)S(1)}, s32[2,4]{1,0:T(2,128)}, u32[]{:S(2)}) copy-start(s32[2,4]{1,0:T(2,128)} %param.18) | copy-start | bytes 100
  35.8 61.7 %copy-start.6 = (bf16[4,96,320]{2,1,0:T(8,128)(2,1)S(1)}, bf16[4,96,320]{2,1,0:T(8,128)(2,1)}, u32[]{:S(2)}) copy-start(bf16[4,96,320]{2,1,0:T(8,128)(2,1)} %get-tuple-element.72) | copy-start | bytes 737284
  96.4 201.4 %all-gather.8.cloned.1.call-start = ((), (), s32[]{:S(2)}) async-start(), calls=%async_computation.5 | async-start | bytes 3932160 | tf_op jit(solution)/shard_map/all_gather | solution.py:1285
  96.5 4.2 collective-permute-start
  101.0 72.2 %copy-start.7 = (s32[16,144,1]{1,0,2:T(8,128)}, s32[16,144,1]{1,0,2:T(8,128)S(1)}, u32[]{:S(2)}) copy-start(s32[16,144,1]{1,0,2:T(8,128)S(1)} %sub.40) | copy-start | bytes 27652
  173.2 240.6 %reduce-scatter.4.cloned.1.call-start = ((), (), s32[]{:S(2)}) async-start(), calls=%async_computation.6 | async-start | bytes 7864320 | tf_op jit(solution)/shard_map/reduce_scatter | solution.py:1289
  297.5 201.6 %reduce-scatter.6.cloned.1.call-start = ((), (), s32[]{:S(2)}) async-start(), calls=%async_computation.7 | async-start | bytes 5898240 | tf_op jit(solution)/shard_map/reduce_scatter | solution.py:1289
  411.7 0.7 copy-start.8
  411.7 157.2 %reduce-scatter.8.cloned.1.call-start = ((), (), s32[]{:S(2)}) async-start(), calls=%async_computation.8 | async-start | bytes 3276800 | tf_op jit(solution)/shard_map/reduce_scatter | solution.py:1289
  499.1 60.4 %copy-start.9 = (f32[8,320]{1,0:T(8,128)S(1)}, f32[8,320]{1,0:T(8,128)}, u32[]{:S(2)}) copy-start(f32[8,320]{1,0:T(8,128)} %get-tuple-element.116) | copy-start | bytes 30724
  499.1 60.5 %copy-start.3 = (f32[320,640]{1,0:T(8,128)S(1)}, f32[320,640]{1,0:T(8,128)}, u32[]{:S(2)}) copy-start(f32[320,640]{1,0:T(8,128)} %get-tuple-element.115) | copy-start | bytes 2457604
  560.7 2.7 copy-start.1
  568.9 33.4 %copy-start.2 = (bf16[256,2048]{1,0:T(8,128)(2,1)S(1)}, bf16[256,2048]{1,0:T(8,128)(2,1)}, u32[]{:S(2)}) copy-start(bf16[256,2048]{1,0:T(8,128)(2,1)} %get-tuple-element.106) | copy-start | bytes 3145732
  595.5 7.7 %copy-start = (f32[256,2048]{1,0:T(8,128)S(1)}, f32[256,2048]{1,0:T(8,128)}, u32[]{:S(2)}) copy-start(f32[256,2048]{1,0:T(8,128)} %get-tuple-element.112) | copy-start | bytes 6291460
  603.2 1.5 copy-start.5
  603.2 2.4 copy-start.4
Sparse Core Ops, SparseCore 0:
  34.2 78.9 all-gather.3
  114.8 116.0 all-gather.5
  232.5 61.6 all-gather.7
  297.7 109.4 reduce-scatter.3
  411.8 87.2 reduce-scatter.5
  501.3 52.3 reduce-scatter.7

commit v5 on v4

--- a/solution.py
+++ b/solution.py
@@ -284,7 +284,7 @@
             body(places, acc[rows, :] + first[at, :].astype(F32) + second[at, :].astype(F32))
 
 
-def plane_sum(pairs, bufs, send, spot, body, own=None, out=None, local_sem=None):
+def plane_sum(pairs, bufs, send, spot, body, own=None, out=None, local_sem=None, after_sends=None):
     sib_out, sib_in = bufs[:2]
     sets = [bufs[2 + 14 * i : 16 + 14 * i] for i in range(PARTS)]
     me, sib, xn, yn = spot
@@ -365,6 +365,8 @@
         sent[i][1].wait_recv()
         held[11][...] = (held[5][...] + held[9][...].astype(F32)).astype(BF16)
         sent[i].append(send(base(i) + 5, held[11], held[13], xn))
+    if after_sends is not None:
+        after_sends()
     opened, started = [siblings[0], siblings[1]], []
     for i, held in enumerate(sets):
         for copy in sent[i][2:]:
@@ -493,11 +495,13 @@
 
 
 def grad_middle_kernel(
-    g1, w1, g2, w2, middle, cot, gain, hidden, second, cot_all,
+    g1_in, w1, g2_in, w2, middle_in, cot_in, gain, hidden_in, second, cot_all,
     grad_middle, gain_grad, gathered, outer, own, *rest
 ):
     bufs, rest = rest[:SUM_BUFS], rest[SUM_BUFS:]
-    send_sem, recv_sem, local_sem, v1, v2, load_sem, left, strip, left_sem, strip_sem = rest
+    send_sem, recv_sem, local_sem, v1, v2, load_sem, left, strip, left_sem, strip_sem = rest[:10]
+    g1, g2, middle, cot, hidden, stage_sem = rest[10:]
+    early = stage(((g1_in, g1), (g2_in, g2)), stage_sem)
     fill_tile = left.shape[3]
     fill_count = second.shape[1] // fill_tile
 
@@ -512,14 +516,15 @@
         slot = lax.rem(i, 2)
         return pltpu.make_async_copy(strip.at[slot], outer.at[block_rows(i, fill_tile), :], strip_sem.at[slot])
 
+    loads = load_columns(((w1, 0, v1), (w2, 0, v2)), load_sem)
+    late = stage(((middle_in, middle), (cot_in, cot), (hidden_in, hidden)), stage_sem.at[pl.ds(2, 3)])
     for copy in left_copies(0):
         copy.start()
-    loads = load_columns(((w1, 0, v1), (w2, 0, v2)), load_sem)
     spot = where_am_i()
     greet(spot[1:])
     send = sender(send_sem, recv_sem)
     pairs = [(g1, v1), (g2, v2)]
-    for copy in loads:
+    for copy in early + loads:
         copy.wait()
     gain_grad[...] = jnp.zeros(gain_grad.shape, F32)
 
@@ -530,7 +535,12 @@
         own[rows, :] = value.astype(BF16)
         gain_grad[0:1, :] += term
 
-    opened, started = plane_sum(pairs, bufs, send, spot, body, own, gathered, local_sem)
+
+    def arrived():
+        for copy in late:
+            copy.wait()
+
+    opened, started = plane_sum(pairs, bufs, send, spot, body, own, gathered, local_sem, after_sends=arrived)
     size = g2.shape[1]
 
     def fill(i):
@@ -586,47 +596,52 @@
     return line - 1 + jnp.where(to_self, 0, 1)
 
 
-def greet_also(partners, more):
+def greet_also(partners, more, meanwhile):
     barrier = pltpu.get_barrier_semaphore()
     for partner in partners:
         pl.semaphore_signal(barrier, inc=1, device_id=partner, device_id_type=MESH)
+    meanwhile()
     pl.semaphore_wait(barrier, len(partners) + more)
 
 
+def stage(pairs, sem):
+    loads = []
+    for k, (src, dst) in enumerate(pairs):
+        loads.append(pltpu.make_async_copy(src, dst, sem.at[k]))
+        loads[-1].start()
+    return loads
+
+
 def tail_kernel(
-    line, summed, mid, pack, branch_grad, input_grad, gain_sum, pack_sum,
-    land, far, pack_in, send_sem, recv_sem, local_sem
+    line, summed, terms, branch_grad, input_grad, gain_sum, land, near, mid, far, send_sem, recv_sem, local_sem
 ):
     me = where_am_i()[0]
     t = number(me)
-    plane = 8
-    index = me[0] * plane + t
-    to_self = index // line == t
+    plane, own_rows = land.shape[:2]
     peers = plane_peers(me)
     others = [(lax.rem(me[0] + k, line),) + me[1:] for k in range(1, line)]
-    greet_also(peers + others, signal_pack(me, line, sources=False))
+    greet(peers + others)
     send = sender(send_sem, recv_sem)
-    swap = swap_back_start(summed, land, send, 0, local_sem.at[0], me, peers)
-    out = [send(7 + k, mid.at[other[0]], far.at[k], other) for k, other in enumerate(others)]
-    pack_base = 6 + line
-
-    def pack_copy(j, slot):
-        target = t * line + j
-        return pltpu.make_async_remote_copy(
-            src_ref=pack.at[j],
-            dst_ref=pack_in.at[slot],
-            send_sem=send_sem.at[pack_base + j],
-            recv_sem=recv_sem.at[pack_base + slot],
-            device_id=holder(target // plane, lax.rem(target, plane)),
-            device_id_type=MESH,
-        )
-
-    for j in range(line):
-        own_pack = pltpu.make_async_copy(pack.at[j], pack_in.at[me[0]], local_sem.at[1])
-        pl.when(t * line + j != index)(pack_copy(j, me[0]).start)
-        pl.when(t * line + j == index)(own_pack.start)
+
+    def rows_of(place):
+        return summed.at[block_rows(number(place), own_rows), :]
+
+    def tile_of(place):
+        return number(place) * own_rows // LANES
+
+    gains = [send(7 + i, terms.at[tile_of(peer)], near.at[i], peer) for i, peer in enumerate(peers)]
+    local = pltpu.make_async_copy(rows_of(me), land.at[t], local_sem)
+    local.start()
+    swaps = [send(i, rows_of(peer), land.at[t], peer) for i, peer in enumerate(peers)]
+    total = terms[tile_of(me)]
+    for i, copy in enumerate(gains):
+        copy.wait_recv()
+        total = total + near[i]
+    for z in range(line):
+        mid[z] = jnp.concatenate([total[2 * z : 2 * z + 2], jnp.zeros((6, LANES), F32)], axis=0)
+    out = [send(14 + k, mid.at[other[0]], far.at[k], other) for k, other in enumerate(others)]
+    swap_end(([local], swaps))
     width = land.shape[2] // 2
-    swap_end(swap)
     for dst, low in ((branch_grad, 0), (input_grad, width)):
         for i in range(0, plane, 2):
             both = [land[i + j, :, low : low + width].astype(F32) for j in range(2)]
@@ -637,19 +652,8 @@
     for k in range(line - 1):
         value = value + far[k]
     gain_sum[...] = value
-    for z in range(line):
-        source_is_me = jnp.logical_and(to_self, me[0] == z)
-        pl.when(jnp.logical_not(source_is_me))(pack_copy(z, z).wait_recv)
-        own_pack = pltpu.make_async_copy(pack.at[z], pack_in.at[z], local_sem.at[1])
-        pl.when(source_is_me)(own_pack.wait)
-    total = pack_in[0].astype(F32)
-    for z in range(1, line):
-        total = total + pack_in[z].astype(F32)
-    pack_sum[...] = total
-    for copy in out:
+    for copy in gains + out:
         copy.wait_send()
-    for j in range(line):
-        pl.when(t * line + j != index)(pack_copy(j, me[0]).wait_send)
 
 
 def plane_peers(me):
@@ -675,13 +679,16 @@
     others = [(lax.rem(me[0] + k, line),) + me[1:] for k in range(1, line)]
     plane = mix.shape[0]
     width = branch.shape[1] // plane
-    for i in range(plane):
-        cols = slice(i * width, (i + 1) * width)
-        mix[i] = jnp.concatenate([branch[:, cols], inner[:, cols], out[:, cols]], axis=1)
+
+    def arrange():
+        for i in range(plane):
+            cols = slice(i * width, (i + 1) * width)
+            mix[i] = jnp.concatenate([branch[:, cols], inner[:, cols], out[:, cols]], axis=1)
+
     index = me[0] * plane + t
     slice_of, chunk_of = index // line, lax.rem(index, line)
     to_self = slice_of == t
-    greet_also(peers + others, signal_pack(me, line, sources=True))
+    greet_also(peers + others, signal_pack(me, line, sources=True), arrange)
     send = sender(send_sem, recv_sem)
     row = gains.at[me[0]]
     sent = [send(i, gain, row.at[t], peer) for i, peer in enumerate(peers)]
@@ -757,6 +764,17 @@
     return [local], [send(base + i, src.at[number(peer)], dst.at[t], peer) for i, peer in enumerate(peers)]
 
 
+def swap_rows_start(src, dst, low, rows, send, base, local_sem, me, peers):
+    t = number(me)
+    part = pl.ds(low, rows)
+    local = pltpu.make_async_copy(src.at[t, part, :], dst.at[t, part, :], local_sem)
+    local.start()
+    sent = [
+        send(base + i, src.at[number(peer), part, :], dst.at[t, part, :], peer) for i, peer in enumerate(peers)
+    ]
+    return [local], sent
+
+
 def swap_end(started):
     locals_, swaps = started
     for copy in swaps:
@@ -791,23 +809,26 @@
 
 def last_kernel(
     line, own_rows,
-    grads, mixer_w, tokens, grad_middle, gain, mlp_term, summed,
-    input_grad, mid, swapped,
+    grads_in, mixer_w, tokens_in, grad_middle_in, gain, mlp_term, summed,
+    input_grad, gain_out, swapped, output_grad,
     *rest,
 ):
     bufs, rest = rest[:SUM_BUFS], rest[SUM_BUFS:]
-    held, mixer_term, gain_out, near, send_sem, recv_sem, load_sem = rest
+    held, mixer_term, land, send_sem, recv_sem, load_sem, grads, tokens, grad_middle, stage_sem = rest
+    early = stage(((grads_in, grads),), stage_sem)
     spot = where_am_i()
     me = spot[0]
     t = number(me)
     plane = 8
     loads = load_columns(((mixer_w, 0, held),), load_sem)
+    late = stage(((tokens_in, tokens), (grad_middle_in, grad_middle)), stage_sem.at[pl.ds(1, 2)])
     peers = plane_peers(me)
     greet(peers)
     send = sender(send_sem, recv_sem)
-    gain_base = SUM_SEMS
-    swap = swap_back_start(summed, swapped, send, gain_base + 7, load_sem.at[1], me, peers)
+    cut = own_rows * 3 // 4 // 16 * 16 or own_rows
+    swaps = [swap_rows_start(summed, land, 0, cut, send, SUM_SEMS, load_sem.at[1], me, peers)]
     loads[0].wait()
+    early[0].wait()
     mixer_term[...] = jnp.zeros(mixer_term.shape, F32)
 
     def body(rows, total):
@@ -815,28 +836,29 @@
         input_grad[rows, :] = grad_middle[rows, :] + back
         mixer_term[0:1, :] += term
 
-    opened, _ = plane_sum([(grads, held)], bufs, send, spot, body)
+    def swap_now():
+        for copy in late:
+            copy.wait()
+        if cut < own_rows:
+            rest = own_rows - cut
+            swaps.append(swap_rows_start(summed, land, cut, rest, send, SUM_SEMS + 7, load_sem.at[2], me, peers))
+
+    opened, _ = plane_sum([(grads, held)], bufs, send, spot, body, after_sends=swap_now)
     per = plane * own_rows
     for z in range(line):
         for q in range(per // LANES):
             cols = slice(z * per + q * LANES, z * per + (q + 1) * LANES)
             gain_out[q, 2 * z : 2 * z + 1, :] = mixer_term[0:1, cols]
             gain_out[q, 2 * z + 1 : 2 * z + 2, :] = mlp_term[0:1, cols]
-
-    def tile_of(place):
-        return number(place) * own_rows // LANES
-
-    sent = [send(gain_base + i, gain_out.at[tile_of(peer)], near.at[i], peer) for i, peer in enumerate(peers)]
-    for copy in sent:
-        copy.wait_recv()
-    total = gain_out[tile_of(me)]
-    for i in range(7):
-        total = total + near[i]
-    for z in range(line):
-        mid[z] = jnp.concatenate([total[2 * z : 2 * z + 2], jnp.zeros((6, LANES), F32)], axis=0)
-    for copy in opened + sent:
+    for copy in opened:
         copy.wait_send()
-    swap_end(swap)
+    for swap in swaps:
+        swap_end(swap)
+    size, width = swapped.shape[2], grads.shape[1] // 2
+    swapped[...] = land[:, :, :size]
+    for i in range(0, plane, 2):
+        both = [land[i + j, :, size:].astype(F32) for j in range(2)]
+        output_grad[:, i * width : (i + 2) * width] = jnp.concatenate(both, axis=1)
 
 
 def chain_exchange(msg, arrived, send, base, me, line, direction):
@@ -858,13 +880,21 @@
 
 def mixer_forward_kernel(
     line, groups, streams, span,
-    normed, mix_w, off, wbd, vec, cot, gate, up, down,
+    normed_in, mix_w_in, off, wbd, vec, cot, gate, up, down,
     value_out, slope_out, inner, head_rows, conv_out, rate_out, keep_out, scale_out, decay_out, states_out, mixed, enter, ends, halo,
-    cot_all, ff_in,
-    branch, slope, conv, rate, keep, scale, decay, states, save_sem, driven, ext, tail_out, tail_in, chain_out, chain_in, send_sem, recv_sem, local_sem,
+    cot_all, ff_in, out_w,
+    normed, mix_w, stage_sem, branch, slope, conv, rate, keep, scale, decay, states, save_sem, driven, ext, tail_out, tail_in, chain_out, chain_in, send_sem, recv_sem, local_sem,
 ):
     spot = where_am_i()
     me = spot[0]
+    place_rows = streams * span
+    last = groups // streams - 1
+    order = [last] + list(range(last))
+    loads = stage(
+        [(mix_w_in, mix_w)]
+        + [(normed_in.at[pl.ds(q * place_rows, place_rows), :], normed.at[pl.ds(q * place_rows, place_rows), :]) for q in order],
+        stage_sem,
+    )
     peers = plane_peers(me)
     others = [(lax.rem(me[0] + k, line),) + me[1:] for k in range(1, line)]
     greet(peers + others)
@@ -883,9 +913,10 @@
     width = inner.shape[1]
     tiles = decay.shape[0]
     soft = vec[7:8, :]
-    place_rows = streams * span
+    loads[0].wait()
 
     def project(q):
+        loads[1 + order.index(q)].wait()
         rows = block_rows(q, place_rows)
         both = jnp.dot(normed[rows, :], mix_w[:, : 2 * width], preferred_element_type=F32)
         branch[rows, :] = both[:, :width]
@@ -894,7 +925,6 @@
         for j in range(streams):
             ext[q * streams + j, 8 : 8 + span, :] = part[j * span : (j + 1) * span].astype(F32)
 
-    last = groups // streams - 1
     project(last)
     pad = jnp.zeros((8, tail_out.shape[1] - width), F32)
     for j in range(streams):
@@ -983,6 +1013,7 @@
 
     lax.fori_loop(0, span, walk, split_lanes(enter[...]), unroll=4)
     save((states, states_out))
+    out_w[...] = mix_w[:, 2 * width :]
 
     @pl.loop(0, groups)
     def _(g):
@@ -1000,11 +1031,14 @@
 def mixer_back_kernel(
     line, groups, streams, span,
     grad_att, out_w, value, state_slope, rate_factor, log_factor, keep_factor, conv_factor,
-    decay, products, inner, head_rows, halo, off, offx, wbd, vec, hidden_a, part_a, hidden_b, part_b, middle, summed,
-    grads, heads, sums, block_output, swapped,
-    fetch, adj, ext, gext, head_out, head_in, chain_out, chain_in, gelu_held, held, held_a, held_b, *rest,
+    decay_in, products, inner_in, head_rows_in, halo, off_in, offx_in, wbd, vec, hidden_a_in, part_a, hidden_b_in, part_b,
+    middle_in, summed,
+    grads, block_output, swapped, mix_sums,
+    heads, sums, pack, fetch, adj, ext, gext, head_out, head_in, chain_out, chain_in, gelu_held, held, held_a, held_b, *rest,
 ):
-    (acc, *bufs), (send_sem, recv_sem, local_sem, load_sem, gelu_sem, held_sem) = rest[:16], rest[16:]
+    (acc, *bufs), rest = rest[:16], rest[16:]
+    send_sem, recv_sem, local_sem, load_sem, gelu_sem, held_sem, pack_sem = rest[:7]
+    decay, hidden_a, hidden_b, inner, head_rows, off, offx, middle, stage_sem = rest[7:]
     spot = where_am_i()
     me = spot[0]
     size_a, size_b = held_a.shape[1], held_b.shape[1]
@@ -1023,7 +1057,14 @@
     )
     for copy in [load(0)] + gelus(0) + factors(0):
         copy.start()
-    loads = load_columns(((part_a, 2 * size_a, held_a), (part_b, 2 * size_b, held_b)), load_sem)
+    loads = stage(
+        (
+            (decay_in, decay), (hidden_a_in, hidden_a), (hidden_b_in, hidden_b), (inner_in, inner),
+            (head_rows_in, head_rows), (off_in, off), (offx_in, offx), (middle_in, middle),
+        ),
+        stage_sem,
+    )
+    loads += load_columns(((part_a, 2 * size_a, held_a), (part_b, 2 * size_b, held_b)), load_sem)
     others = [(lax.rem(me[0] + k, line),) + me[1:] for k in range(1, line)]
     peers = plane_peers(me)
     greet(peers + others)
@@ -1040,6 +1081,8 @@
         grad = jnp.dot(fetch[q % 2], out_w[...], preferred_element_type=F32)
         put(adj, rows, grad * gelu_held[0, q % 2])
         grads[rows, :width] = (grad * gelu_held[1, q % 2]).astype(BF16)
+
+    loads[0].wait()
 
     def step(i, carry):
         at = pl.ds(span - 1 - i, groups, stride=span)
@@ -1056,7 +1099,7 @@
     chain_out[0:streams, :] = product
     chain_out[8 : 8 + streams, :] = total
     chains = chain_exchange(chain_out, chain_in, send, 1, me, line, -1)
-    for copy in loads:
+    for copy in loads[1:]:
         copy.wait()
     mlp = reduce_plane([(hidden_a, held_a), (hidden_b, held_b)], acc, bufs, send, line, spot)
     for _ in range(7):
@@ -1130,6 +1173,37 @@
     pl.loop(0, pieces // 2)(gradients)
     next(mlp)
     pl.loop(pieces // 2, pieces)(gradients)
+    chunk = width // line
+    pack_rows = pack.shape[1]
+    for j in range(line):
+        low = j * chunk // WIDTH * WIDTH
+        rows = slice(j * chunk, (j + 1) * chunk)
+        block = [heads[rows, low : low + WIDTH], heads[rows, width + low : width + low + WIDTH]]
+        wide = jnp.concatenate([part[: chunk // 2] for part in block] + [part[chunk // 2 :] for part in block], axis=1)
+        minor = jnp.concatenate([sums[:, rows], jnp.zeros((8, 2 * width - chunk), F32)], axis=1)
+        spare = jnp.zeros((pack_rows - chunk // 2 - 8, 2 * width), F32)
+        pack[j] = jnp.concatenate([wide, minor] + ([spare] if spare.shape[0] else []), axis=0).astype(BF16)
+    t = number(me)
+    pack_base = line + REDUCE_SEMS + 7
+    tail_rows = pl.ds(mix_sums.shape[1] - pack_rows, pack_rows)
+
+    def pack_copy(j, slot):
+        return pltpu.make_async_remote_copy(
+            src_ref=pack.at[j],
+            dst_ref=mix_sums.at[slot, tail_rows, :],
+            send_sem=send_sem.at[pack_base + j],
+            recv_sem=recv_sem.at[pack_base + slot],
+            device_id=holder(me[0], lax.rem(t * line + j, 8)),
+            device_id_type=MESH,
+        )
+
+    def own_pack(j, slot):
+        return pltpu.make_async_copy(pack.at[j], mix_sums.at[slot, tail_rows, :], pack_sem.at[slot])
+
+    for j in range(line):
+        goes_to, slot = lax.rem(t * line + j, 8), (t * line + j) // 8
+        pl.when(goes_to != t)(pack_copy(j, slot).start)
+        pl.when(goes_to == t)(own_pack(j, slot).start)
 
     for g in range(groups):
         gext[g, 0:8, :] = jnp.zeros((8, width), F32)
@@ -1173,6 +1247,12 @@
         grads[g * span + span - 16 : (g + 1) * span, width:] = ending.astype(BF16)
     for copy in [head_copy] + chains + open_mlp:
         copy.wait_send()
+    for slot in range(line):
+        comes_from = (slot * 8 + t) // line
+        pl.when(comes_from != t)(pack_copy(0, slot).wait_recv)
+        pl.when(comes_from == t)(own_pack(0, slot).wait)
+    for j in range(line):
+        pl.when(lax.rem(t * line + j, 8) != t)(pack_copy(j, 0).wait_send)
     swap_end(swap)
 
 
@@ -1253,6 +1333,33 @@
             transcendentals=0,
         ),
     )(*(() if first is None else (first,)), *pairs)
+
+
+def outer_into_kernel(filled, a, b, out):
+    out[0] = lax.dot_general(a[...], b[...], rows_contract, preferred_element_type=F32).astype(BF16)
+
+
+def outer_into(filled, a, b):
+    count, d_model = a.shape
+    parts, size = filled.shape[0], b.shape[1]
+    tile = min(256, d_model // parts)
+    per = d_model // parts // tile
+    return pl.pallas_call(
+        outer_into_kernel,
+        grid=(d_model // tile,),
+        in_specs=[
+            pl.BlockSpec(memory_space=pl.ANY),
+            pl.BlockSpec((count, tile), lambda i: (0, i)),
+            pl.BlockSpec((count, size), lambda i: (0, 0), pipeline_mode=pl.Buffered(1)),
+        ],
+        out_specs=pl.BlockSpec((1, tile, size), lambda i: (i // per, i % per, 0)),
+        out_shape=jax.ShapeDtypeStruct(filled.shape, BF16),
+        input_output_aliases={0: 0},
+        compiler_params=pltpu.CompilerParams(vmem_limit_bytes=VMEM_LIMIT),
+        cost_estimate=pl.CostEstimate(
+            flops=2 * count * d_model * size, bytes_accessed=2 * count * (d_model + size), transcendentals=0
+        ),
+    )(filled, a, b)
 
 
 ANY = pl.BlockSpec(memory_space=pl.ANY)
@@ -1333,7 +1440,6 @@
     mixer_scale = gains[:, :, :own_rows].reshape(1, d_model)
     mlp_scale = gains[:, :, own_rows : 2 * own_rows].reshape(1, d_model)
     mixer_w = line_gather(mix_swapped.reshape(plane * own_rows, 3 * width))
-    output_w = mixer_w[:, 2 * width :]
     x = tokens.reshape(own, d_model)
     cot = cotangent.reshape(own, d_model)
     tall = ((plane * own, d_model), BF16, ANY)
@@ -1390,16 +1496,22 @@
     edge = ((8 * streams, wide), F32)
     (
         value, slope, inner, head_rows, conv, rate, keep, scale, decay, states, mixed, enter, ends, halo, cot_all,
-        second_part,
+        second_part, output_w,
     ) = comm_call(
         functools.partial(mixer_forward_kernel, line, groups, streams, span),
         3,
-        [VMEM] * 5 + [ANY] * 4,
+        [ANY] * 2 + [VMEM] * 3 + [ANY] * 4,
         [full, full, short, short, full, full, full, full, tiled, tiled, short]
         + [((groups, wide), F32, VMEM)] * 2
         + [edge + (VMEM,), tall]
-        + swapped(FF_SECOND),
-        [pltpu.VMEM((count, width), F32)] * 6
+        + swapped(FF_SECOND)
+        + [((d_model, width), BF16, VMEM)],
+        [
+            pltpu.VMEM((count, d_model), BF16),
+            pltpu.VMEM((d_model, 3 * width), BF16),
+            pltpu.SemaphoreType.DMA((1 + places,)),
+        ]
+        + [pltpu.VMEM((count, width), F32)] * 6
         + [pltpu.VMEM((tiles, count, LANES), F32)] * 2
         + [
             pltpu.SemaphoreType.DMA((8,)),
@@ -1444,7 +1556,7 @@
     grad_middle, mlp_gain_term, grad_att, sums_b = comm_call(
         grad_middle_kernel,
         5,
-        [VMEM, ANY, VMEM, ANY] + [VMEM] * 4 + [ANY] * 2,
+        [ANY] * 6 + [VMEM] + [ANY] * 3,
         [own32, gain_rows, tall, ((d_model, 3 * FF_SECOND[1]), BF16, ANY)],
         [pltpu.VMEM((own, d_model), BF16)]
         + sum_buffers(own, d_model)
@@ -1458,6 +1570,12 @@
             pltpu.VMEM((2, 256, 3 * FF_SECOND[1]), BF16),
             pltpu.SemaphoreType.DMA((2, 2)),
             pltpu.SemaphoreType.DMA((2,)),
+            pltpu.VMEM((count, 2 * FF_FIRST[1]), BF16),
+            pltpu.VMEM((count, 2 * FF_SECOND[1]), BF16),
+            pltpu.VMEM((own, d_model), F32),
+            pltpu.VMEM((own, d_model), BF16),
+            pltpu.VMEM((count, FF_SECOND[1]), BF16),
+            pltpu.SemaphoreType.DMA((5,)),
         ],
         90,
     )(grads_a, parts[0], grads_b, parts[1], middle, cot, mlp_scale, hidden_b, second, cot_all)
@@ -1471,18 +1589,21 @@
     sums_out = outer_call(grad_att, mixed, first=sums_b)
     grad_att, sums_out = lax.optimization_barrier((grad_att, sums_out))
     ff_sums.append(line_reduce(sums_out))
-    grads_mix, heads_full, sums, block_output, swapped_a = comm_call(
+    pack_rows = -(-(chunk // 2 + 8) // 16) * 16
+    grads_mix, block_output, swapped_a, mix_sums = comm_call(
         functools.partial(mixer_back_kernel, line, groups, streams, span),
         6,
-        [ANY, VMEM] + [ANY] * 6 + [VMEM] * 9 + [VMEM, ANY, VMEM, ANY, VMEM, ANY],
+        [ANY, VMEM] + [ANY] * 7 + [VMEM] + [ANY] * 2 + [VMEM] + [ANY] * 2 + [VMEM] * 2 + [ANY] * 6,
         [
             ((count, 2 * width), BF16, VMEM),
-            ((width, 2 * width), F32, VMEM),
-            ((8, width), F32, VMEM),
             ((own, d_model), BF16, VMEM),
             ((plane, own_rows, 3 * FF_FIRST[1]), BF16, ANY),
+            ((line, d_model // line + pack_rows, 2 * width), BF16, ANY),
         ],
         [
+            pltpu.VMEM((width, 2 * width), F32),
+            pltpu.VMEM((8, width), F32),
+            pltpu.VMEM((line, pack_rows, 2 * width), BF16),
             pltpu.VMEM((2, 256, d_model), BF16),
             pltpu.VMEM((tiles, count, LANES), F32),
             pltpu.VMEM((groups, span + 8, width), F32),
@@ -1497,71 +1618,75 @@
             pltpu.VMEM((d_model, FF_SECOND[1]), BF16),
         ]
         + reduce_buffers(own, d_model)
-        + sems(line + REDUCE_SEMS + 7)
+        + sems(line + REDUCE_SEMS + 7 + line)
         + [pltpu.SemaphoreType.DMA((3,)), pltpu.SemaphoreType.DMA((2,))]
-        + [pltpu.SemaphoreType.DMA((2, 2)), pltpu.SemaphoreType.DMA((2, 4))],
+        + [pltpu.SemaphoreType.DMA((2, 2)), pltpu.SemaphoreType.DMA((2, 4)), pltpu.SemaphoreType.DMA((line,))]
+        + [
+            pltpu.VMEM((tiles, count, LANES), F32),
+            pltpu.VMEM((count, FF_FIRST[1]), BF16),
+            pltpu.VMEM((count, FF_SECOND[1]), BF16),
+            pltpu.VMEM((count, width), BF16),
+            pltpu.VMEM((count, width), BF16),
+            pltpu.VMEM(off.shape, jnp.int32),
+            pltpu.VMEM(offx.shape, jnp.int32),
+            pltpu.VMEM((own, d_model), F32),
+            pltpu.SemaphoreType.DMA((8,)),
+        ],
         70,
     )(
         grad_att, output_w, value, *factors, decay, ends, inner, head_rows, halo, off, offx, wbd, vec,
         hidden_a, parts[0], hidden_b, parts[1], middle, by_owner(ff_sums[0]),
     )
-    sums_mix = outer_call(normed, grads_mix)
+    sums_mix = outer_into(mix_sums, normed, grads_mix)
     grads_mix, sums_mix = lax.optimization_barrier((grads_mix, sums_mix))
 
-    heads_grad = jnp.concatenate(
-        [
-            jnp.concatenate(
-                [
-                    heads_full[h * WIDTH : (h + 1) * WIDTH, h * WIDTH : (h + 1) * WIDTH],
-                    heads_full[h * WIDTH : (h + 1) * WIDTH, width + h * WIDTH : width + (h + 1) * WIDTH],
-                ],
-                axis=1,
-            )
-            for h in range(local_heads)
-        ],
-        axis=0,
-    )
-    pack_rows = -(-(chunk + 8) // 16) * 16
-    minor_pack = sums.reshape(8, line, chunk).transpose(1, 0, 2)
-    minor_pack = jnp.pad(minor_pack, ((0, 0), (0, pack_rows - chunk - 8), (0, 2 * WIDTH - chunk)))
-    out_pack = jnp.concatenate([heads_grad.reshape(line, chunk, 2 * WIDTH), minor_pack], axis=1).astype(BF16)
-    pack32 = (pack_rows, 2 * WIDTH)
     gain_tiles = plane * own_rows // LANES
     deep = -(-2 * line // 8) * 8
-    mids = ((line, 8, LANES), F32, VMEM)
-    input_grad, gain_mid, swapped_b = comm_call(
+    input_grad, gain_terms, swapped_b, w_output_grad = comm_call(
         functools.partial(last_kernel, line, own_rows),
         7,
-        [VMEM, ANY] + [VMEM] * 4 + [ANY],
-        [own32, mids, ((plane, own_rows, 3 * FF_SECOND[1] + width), BF16, ANY)],
+        [ANY] * 4 + [VMEM] * 2 + [ANY],
+        [
+            own32,
+            ((gain_tiles, deep, LANES), F32, VMEM),
+            ((plane, own_rows, 3 * FF_SECOND[1]), BF16, VMEM),
+            ((own_rows, rw), F32, VMEM),
+        ],
         sum_buffers(own, d_model)
         + [
             pltpu.VMEM((d_model, 2 * width), BF16),
             pltpu.VMEM((8, d_model), F32),
-            pltpu.VMEM((gain_tiles, deep, LANES), F32),
-            pltpu.VMEM((7, deep, LANES), F32),
+            pltpu.VMEM((plane, own_rows, 3 * FF_SECOND[1] + width), BF16),
         ]
         + sems(SUM_SEMS + 14)
-        + [pltpu.SemaphoreType.DMA((2,))],
+        + [
+            pltpu.SemaphoreType.DMA((3,)),
+            pltpu.VMEM((count, 2 * width), BF16),
+            pltpu.VMEM((own, d_model), BF16),
+            pltpu.VMEM((own, d_model), F32),
+            pltpu.SemaphoreType.DMA((3,)),
+        ],
         60,
     )(
         grads_mix, mixer_w, x, grad_middle, mixer_scale, mlp_gain_term, by_owner(ff_sums[1]),
     )
-    w_branch_grad, w_input_grad, gain_sum, summed = comm_call(
+    mix_summed = line_reduce(sums_mix.reshape(-1, 2 * width))
+    w_branch_grad, w_input_grad, gain_sum = comm_call(
         functools.partial(tail_kernel, line),
         8,
-        [ANY, VMEM, VMEM],
-        [((own_rows, rw), F32, VMEM)] * 2 + [((8, LANES), F32, VMEM), (pack32, F32, VMEM)],
+        [ANY, VMEM],
+        [((own_rows, rw), F32, VMEM)] * 2 + [((8, LANES), F32, VMEM)],
         [
             pltpu.VMEM((plane, own_rows, 2 * width), BF16),
+            pltpu.VMEM((7, deep, LANES), F32),
+            pltpu.VMEM((line, 8, LANES), F32),
             pltpu.VMEM((line - 1, 8, LANES), F32),
-            pltpu.VMEM((line,) + pack32, BF16),
         ]
-        + sems(6 + 2 * line)
-        + [pltpu.SemaphoreType.DMA((2,))],
+        + sems(13 + line)
+        + [pltpu.SemaphoreType.DMA],
         15,
-    )(by_owner(line_reduce(sums_mix)), gain_mid, out_pack)
-    w_output_grad = widen([swapped_b[:, :, 3 * FF_SECOND[1] :]])
+    )(mix_summed, gain_terms)
+    small = mix_summed[plane * own_rows :].astype(F32)
     third = FF_FIRST[1], FF_SECOND[1]
     w_gate_grad, w_up_grad, w_down_grad = (
         widen([swapped_a[:, :, k * third[0] : (k + 1) * third[0]], swapped_b[:, :, k * third[1] : (k + 1) * third[1]]])
@@ -1569,8 +1694,8 @@
     )
     input_grad = input_grad.reshape(streams_own, span, d_model)
     block_output = block_output.reshape(streams_own, span, d_model)
-    gate_weight_grad = summed[:chunk]
-    minor_grad = summed[chunk : chunk + 8, :chunk]
+    gate_weight_grad = jnp.concatenate([small[: chunk // 2, :width], small[: chunk // 2, width:]], axis=0)
+    minor_grad = small[chunk // 2 : chunk // 2 + 8, :chunk]
     low = lax.rem((lax.axis_index("pair") * 2 + lax.axis_index("core")) * 2 + lax.axis_index("batch"), LANES // own_rows)
     gain_grads = lax.dynamic_slice(gain_sum, (0, low * own_rows), (2, own_rows))
     return (

time: 623 us -> 600 us (0.963)
  the two profiles are of different devices: /device:TPU:3 before, /device:TPU:0 now
where the time goes in v5:
time: 600 us; the launch traced here: 590 us
  Pallas kernels  527 us (88%)
  local copies, waits for them, and re-layouts  20.7 us (3%)
  waiting for transfers between devices  18.3 us (3%)
  between operations  14.6 us (2%)
  other arithmetic  7.3 us (1%)
    pallas_call x1, Pallas kernels, shards(): comm_call(grad_middle_kernel, 5, [ANY] * 6 + [VMEM] + [ANY] * 3, [own32,...  88.1 us
    pallas_call x1, Pallas kernels, shards(): comm_call(middle_kernel, 4, [VMEM] * 7 + [ANY] * 7, [own32, tall] + [full...  82.6 us
    pallas_call x1, Pallas kernels, shards(): comm_call(functools.partial(mixer_back_kernel, line, groups, streams, spa...  71.8 us
    pallas_call x1, Pallas kernels, shards(): comm_call(second_kernel, 2, [VMEM, VMEM, ANY, ANY, ANY], [tall] + swapped...  60.5 us
    pallas_call x1, Pallas kernels, shards(): comm_call(functools.partial(last_kernel, line, own_rows), 7, [ANY] * 4 +...  54.6 us
    pallas_call x1, Pallas kernels, shards(): comm_call(functools.partial(mixer_forward_kernel, line, groups, streams,...  53.9 us
    pallas_call x2, Pallas kernels, ff_call(): pl.pallas_call(ff_kernel, grid=(count // tile,), in_specs=[tokens, tokens...  33.5 us
    pallas_call x2, Pallas kernels, outer_call(): pl.pallas_call(outer_kernel, grid=(d_model // tile,), in_specs=specs, out...  31 us
  transfers between devices with their start and end apart: 7, of which 3 were waited for; matrix products, arithmetic and copies ran while one was open for 2% of the time, Pallas kernels for 83%

profile of v5, /device:TPU:0, one launch (start us, length us, event | category | flops | bytes accessed | tf_op | source)
XLA Modules:
  0.0 589.8 jit_solution(6650859518396303730)
XLA Ops:
  7.2 0.7 pad_maximum_fusion.2
  8.0 0.1 reshape.237
  8.1 0.7 maximum_convert_fusion
  8.8 0.1 pad.20.clone
  8.9 1.5 maximum_maximum_fusion.packed
  10.4 0.6 broadcast_in_dim.65.gain
  11.0 23.7 %shard_map.271 = (bf16[8,64,960]{2,1,0:T(8,128)(2,1)}, f32[4,8,8,128]{3,2,1,0:T(8,128)}, bf16[4,96,320]{2,1,0:T(8,128)(2,1)}) custom-call(bf16[64,2560]{1,0:T(8,128)(2,1)} %branch.1, bf16[64,2560]{1,0:T(8,128)(2,1)} %inner.1, bf16[64,2560]{1,0:T(8,128)(2,1)} %out.1, f32[8,128]{1,0:T(8,128)} %broadcast_in_dim.65.gain, bf16[96,320]{1,0:T(8,128)(2,1)} %maximum_maximum_fusion.packed), custom_call_target="tpu_custom_call" | custom-call | flops 15000000512 | bytes 1048576 | tf_op jit(solution)/shard_map/pallas_call | solution.py:1427
  34.8 0.9 slice.91
  35.8 0.7 reshape.238.gain
  36.5 60.5 %shard_map.272 = (bf16[2048,2048]{1,0:T(8,128)(2,1)}, bf16[8,64,1536]{2,1,0:T(8,128)(2,1)}) custom-call(bf16[256,2048]{1,0:T(8,128)(2,1)} %bitcast.58, f32[1,2048]{1,0:T(1,128)} %reshape.238.gain, bf16[64,6144]{1,0:T(8,128)(2,1)} %gate.3, bf16[64,6144]{1,0:T(8,128)(2,1)} %up.3, bf16[64,6144]{1,0:T(8,128)(2,1)} %down.3), custom_call_target="tpu_custom_call" | custom-call | flops 60000002048 | bytes 1048576 | tf_op jit(solution)/shard_map/pallas_call | solution.py:1450
  97.1 0.7 collective-permute-start
  97.9 0.1 reshape.254
  98.0 0.1 slice.99
  98.1 0.1 slice.101
  98.1 0.7 reshape.243.gain
  98.8 0.1 pad.11.clone
  98.9 0.2 broadcast_select_fusion.3
  99.1 1.0 pad_maximum_fusion.wbd
  100.3 0.7 maximum_maximum_fusion.1.vec
  101.0 0.2 reduce_window_sum.11
  101.1 0.1 select_reduce_fusion
  101.4 1.4 copy.45.off.off_in
  102.8 11.7 %all-gather.4.cloned.1.call-done.mix_w_in.mixer_w = bf16[2048,960]{1,0:T(8,128)(2,1)} async-done(((bf16[512,960]{1,0:T(8,128)(2,1)}), bf16[2048,960]{1,0:T(8,128)(2,1)}) %all-gather.4.cloned.1.call-update) | async-done | bytes 3932176 | tf_op jit(solution)/shard_map/all_gather | solution.py:1392
  114.4 53.9 %shard_map.273 = (f32[2048,320]{1,0:T(8,128)}, f32[2048,320]{1,0:T(8,128)}, bf16[2048,320]{1,0:T(8,128)(2,1)}, bf16[2048,320]{1,0:T(8,128)(2,1)}, f32[2048,320]{...) custom-call(bf16[2048,2048]{1,0:T(8,128)(2,1)} %get-tuple-element.70, ...), custom_call_target="tpu_custom_call" | custom-call | flops 49999998976 | bytes 1048576 | tf_op jit(solution)/shard_map/pallas_call | solution.py:1500
  168.4 0.6 reduce-scatter.4.cloned.1.call-start
  169.0 82.6 %shard_map.274 = (f32[256,2048]{1,0:T(8,128)}, bf16[2048,2048]{1,0:T(8,128)(2,1)}, f32[2048,320]{1,0:T(8,128)}, f32[2048,320]{1,0:T(8,128)}, f32[2048,320]{1,0:T...) custom-call(bf16[2048,320]{1,0:T(8,128)(2,1)} %get-tuple-element.73.mixed.refs_2_, ...), custom_call_target="tpu_custom_call" | custom-call | flops 80000000000 | bytes 1048576 | tf_op jit(solution)/shard_map/pallas_call | solution.py:1532
  251.6 19.3 %shard_map.275 = (bf16[2048,1024]{1,0:T(8,128)(2,1)}, bf16[2048,512]{1,0:T(8,128)(2,1)}) custom-call(bf16[2048,2048]{1,0:T(8,128)(2,1)} %get-tuple-element.88.second.refs_0_, bf16[2048,2048]{1,0:T(8,128)(2,1)} %get-tuple-element.84.cot.refs_2_.cot_all, bf16[2048,1536]{1,0:T(8,128)(2,1)} %all-gather.6.cloned.1.call-done.gate_w.up_w.down_w.w1.part_a, ...), custom_call_target="tpu_custom_call" | custom-call | flops 12884901888 | bytes 16777216 | tf_op jit(solution)/shard_map/pallas_call | solution.py:1279
  270.8 19.2 %shard_map.276 = bf16[2048,1536]{1,0:T(8,128)(2,1)} custom-call(bf16[2048,2048]{1,0:T(8,128)(2,1)} %get-tuple-element.88.second.refs_0_, bf16[2048,1024]{1,0:T(8,128)(2,1)} %get-tuple-element.86.refs_1_.g1_in, bf16[2048,2048]{1,0:T(8,128)(2,1)} %get-tuple-element.84.cot.refs_2_.cot_all, bf16[2048,512]{1,0:T(8,128)(2,1)} %get-tuple-element.87.refs_3_.hidden_a_in), custom_call_target="tpu_custom_call" | custom-call | flops 12884901888 | bytes 23068672 | tf_op jit(solution)/shard_map/pallas_call | solution.py:1323
  290.1 0.2 reduce-scatter.6.cloned.1.call-start
  290.3 4.9 all-gather.8.cloned.1.call-done.gate_w.up_w.down_w.w2.part_b
  295.2 14.3 %shard_map.277 = (bf16[2048,512]{1,0:T(8,128)(2,1)}, bf16[2048,256]{1,0:T(8,128)(2,1)}) custom-call(bf16[2048,2048]{1,0:T(8,128)(2,1)} %get-tuple-element.88.second.refs_0_, bf16[2048,2048]{1,0:T(8,128)(2,1)} %get-tuple-element.84.cot.refs_2_.cot_all, bf16[2048,768]{1,0:T(8,128)(2,1)} %all-gather.8.cloned.1.call-done.gate_w.up_w.down_w.w2.part_b, ...), custom_call_target="tpu_custom_call" | custom-call | flops 6442450944 | bytes 16777216 | tf_op jit(solution)/shard_map/pallas_call | solution.py:1279
  309.5 88.1 %shard_map.278 = (f32[256,2048]{1,0:T(8,128)}, f32[8,2048]{1,0:T(8,128)}, bf16[2048,2048]{1,0:T(8,128)(2,1)}, bf16[2048,768]{1,0:T(8,128)(2,1)}) custom-call(bf16[2048,1024]{1,0:T(8,128)(2,1)} %get-tuple-element.86.refs_1_.g1_in, bf16[2048,1536]{1,0:T(8,128)(2,1)} %all-gather.6.cloned.1.call-done.gate_w.up_w.down_w.w1.part_a, ...), custom_call_target="tpu_custom_call" | custom-call | flops 89999998976 | bytes 1048576 | tf_op jit(solution)/shard_map/pallas_call | solution.py:1556
  397.5 11.8 %shard_map.279 = bf16[2048,1088]{1,0:T(8,128)(2,1)} custom-call(bf16[2048,768]{1,0:T(8,128)(2,1)} %get-tuple-element.94.refs_0_, bf16[2048,2048]{1,0:T(8,128)(2,1)} %get-tuple-element.95.refs_1_.grad_att, bf16[2048,320]{1,0:T(8,128)(2,1)} %get-tuple-element.73.mixed.refs_2_), custom_call_target="tpu_custom_call" | custom-call | flops 2684354560 | bytes 9699328 | tf_op jit(solution)/shard_map/pallas_call | solution.py:1323
  409.4 0.3 reduce-scatter.8.cloned.1.call-start
  409.7 0.4 copy-done.8
  410.1 1.5 copy.48.offx_in
  411.6 71.8 %shard_map.280 = (bf16[2048,640]{1,0:T(8,128)(2,1)}, bf16[256,2048]{1,0:T(8,128)(2,1)}, bf16[8,64,1536]{2,1,0:T(8,128)(2,1)}, bf16[4,560,640]{2,1,0:T(8,128)(2,1)}) custom-call(bf16[2048,2048]{1,0:T(8,128)(2,1)} %get-tuple-element.95.refs_1_.grad_att, bf16[2048,320]{1,0:T(8,128)(2,1)} %get-tuple-element.74.weight.out_w, ...), custom_call_target="tpu_custom_call" | custom-call | flops 70000001024 | bytes 1048576 | tf_op jit(solution)/shard_map/pallas_call | solution.py:1593
  483.4 12.4 %shard_map.281 = bf16[4,560,640]{2,1,0:T(8,128)(2,1)} custom-call(bf16[4,560,640]{2,1,0:T(8,128)(2,1)} %get-tuple-element.109.filled, bf16[2048,2048]{1,0:T(8,128)(2,1)} %get-tuple-element.70.normed_in.a, bf16[2048,640]{1,0:T(8,128)(2,1)} %get-tuple-element.110.b.grads_in), custom_call_target="tpu_custom_call", output_to_operand_aliasing={{}: (0, {})} | custom-call | flops 5368709120 | bytes 11010048 | tf_op jit(solution)/shard_map/pallas_call | solution.py:1347
  495.8 1.6 reduce-scatter.6.cloned.1.call-done
  497.4 54.6 %shard_map.282 = (f32[256,2048]{1,0:T(8,128)}, f32[4,8,128]{2,1,0:T(8,128)}, bf16[8,64,768]{2,1,0:T(8,128)(2,1)}, f32[64,2560]{1,0:T(8,128)}) custom-call(bf16[2048,640]{1,0:T(8,128)(2,1)} %get-tuple-element.110.b.grads_in, bf16[2048,960]{1,0:T(8,128)(2,1)} %all-gather.4.cloned.1.call-done.mix_w_in.mixer_w, bf16[256,2048]{1,0:T(8,128)(2,1)} %bitcast.60, ...), custom_call_target="tpu_custom_call" | custom-call | flops 60000002048 | bytes 1048576 | tf_op jit(solution)/shard_map/pallas_call | solution.py:1645
  552.0 1.3 fusion.5
  553.3 0.3 copy-done.1
  553.6 0.2 fusion.4
  553.8 0.1 convert_bitcast_fusion
  553.9 1.3 copy.54
  555.2 0.1 convert_bitcast_fusion.1
  555.4 1.3 copy.53
  556.6 0.1 convert_bitcast_fusion.2
  556.8 1.3 copy.52
  558.1 0.8 slice_convert_fusion
  558.9 0.6 slice.128
  559.5 0.5 slice_bitcast_fusion
  560.0 0.6 slice.129
  560.6 0.1 fusion.6
  560.7 14.9 %shard_map.283 = (f32[64,2560]{1,0:T(8,128)}, f32[64,2560]{1,0:T(8,128)}, f32[8,128]{1,0:T(8,128)}) custom-call(bf16[560,640]{1,0:T(8,128)(2,1)} %reduce-scatter.8.cloned.1.call-done.summed, f32[4,8,128]{2,1,0:T(8,128)} %get-tuple-element.116.terms), custom_call_target="tpu_custom_call" | custom-call | flops 15000000512 | bytes 1048576 | tf_op jit(solution)/shard_map/pallas_call | solution.py:1674
  575.6 0.9 constant_dynamic-slice_fusion
  576.5 0.5 slice_bitcast_fusion.2
  577.0 0.7 pad_maximum_fusion.1
  577.7 1.0 copy.63
  578.7 1.3 copy.64
  580.0 0.2 copy-done.5
  580.2 0.8 copy.65
  581.0 0.8 copy.66
  581.9 0.8 copy.67
  (49 shorter events, 0.6 us)
Async XLA Ops:
  7.2 107.3 %all-gather.4.cloned.1.call-start = ((), (), s32[]{:S(2)}) async-start(), calls=%async_computation.3 | async-start | bytes 5242880 | tf_op jit(solution)/shard_map/all_gather | solution.py:1392
  34.8 216.8 %all-gather.6.cloned.1.call-start = ((), (), s32[]{:S(2)}) async-start(), calls=%async_computation.4 | async-start | bytes 7864320 | tf_op jit(solution)/shard_map/all_gather | solution.py:1392
  36.5 60.6 %copy-start.9 = (s32[2,4]{1,0:T(2,128)S(1)}, s32[2,4]{1,0:T(2,128)}, u32[]{:S(2)}) copy-start(s32[2,4]{1,0:T(2,128)} %param.18) | copy-start | bytes 100
  36.5 61.3 %copy-start.6 = (bf16[4,96,320]{2,1,0:T(8,128)(2,1)S(1)}, bf16[4,96,320]{2,1,0:T(8,128)(2,1)}, u32[]{:S(2)}) copy-start(bf16[4,96,320]{2,1,0:T(8,128)(2,1)} %get-tuple-element.72) | copy-start | bytes 737284
  97.0 198.2 %all-gather.8.cloned.1.call-start = ((), (), s32[]{:S(2)}) async-start(), calls=%async_computation.5 | async-start | bytes 3932160 | tf_op jit(solution)/shard_map/all_gather | solution.py:1392
  97.1 3.9 collective-permute-start
  101.3 67.0 %copy-start.7 = (s32[16,144,1]{1,0,2:T(8,128)}, s32[16,144,1]{1,0,2:T(8,128)S(1)}, u32[]{:S(2)}) copy-start(s32[16,144,1]{1,0,2:T(8,128)S(1)} %sub.40) | copy-start | bytes 27652
  168.4 243.1 %reduce-scatter.4.cloned.1.call-start = ((), (), s32[]{:S(2)}) async-start(), calls=%async_computation.6 | async-start | bytes 7864320 | tf_op jit(solution)/shard_map/reduce_scatter | solution.py:1396
  290.1 207.3 %reduce-scatter.6.cloned.1.call-start = ((), (), s32[]{:S(2)}) async-start(), calls=%async_computation.7 | async-start | bytes 5898240 | tf_op jit(solution)/shard_map/reduce_scatter | solution.py:1396
  409.4 0.7 copy-start.8
  409.4 148.7 %reduce-scatter.8.cloned.1.call-start = ((), (), s32[]{:S(2)}) async-start(), calls=%async_computation.8 | async-start | bytes 3584000 | tf_op jit(solution)/shard_map/reduce_scatter | solution.py:1396
  552.0 1.7 copy-start.1
  560.7 17.0 %copy-start.2 = (bf16[256,2048]{1,0:T(8,128)(2,1)S(1)}, bf16[256,2048]{1,0:T(8,128)(2,1)}, u32[]{:S(2)}) copy-start(bf16[256,2048]{1,0:T(8,128)(2,1)} %get-tuple-element.107) | copy-start | bytes 3145732
  575.6 3.1 copy-start
  578.7 1.5 copy-start.5
  578.7 2.4 copy-start.4
  580.2 1.7 copy-start.3
Sparse Core Ops, SparseCore 0:
  34.9 79.5 all-gather.3
  116.0 115.8 all-gather.5
  233.5 61.6 all-gather.7
  297.4 109.3 reduce-scatter.3
  409.5 87.8 reduce-scatter.5
  499.5 56.5 reduce-scatter.7

commit v6 on v5

--- a/solution.py
+++ b/solution.py
@@ -514,7 +514,8 @@
 
     def strip_copy(i):
         slot = lax.rem(i, 2)
-        return pltpu.make_async_copy(strip.at[slot], outer.at[block_rows(i, fill_tile), :], strip_sem.at[slot])
+        target = outer.at[block_rows(i, fill_tile), pl.ds(0, strip.shape[2])]
+        return pltpu.make_async_copy(strip.at[slot], target, strip_sem.at[slot])
 
     loads = load_columns(((w1, 0, v1), (w2, 0, v2)), load_sem)
     late = stage(((middle_in, middle), (cot_in, cot), (hidden_in, hidden)), stage_sem.at[pl.ds(2, 3)])
@@ -651,7 +652,10 @@
         copy.wait_recv()
     for k in range(line - 1):
         value = value + far[k]
-    gain_sum[...] = value
+    turned = value
+    for i in range(1, LANES // own_rows):
+        turned = jnp.where(lax.rem(t, LANES // own_rows) == i, pltpu.roll(value, LANES - i * own_rows, 1), turned)
+    gain_sum[...] = turned
     for copy in gains + out:
         copy.wait_send()
 
@@ -671,7 +675,8 @@
 
 
 def first_kernel(
-    line, branch, inner, out, gain, packed, mix_in, gains, arrived, mix, send_sem, recv_sem, local_sem
+    line, branch, inner, out, mixer_gain, mlp_gain, gate_w, conv_w, conv_b, gate_b, lru,
+    mix_in, gains, arrived, mix, gain, packed, send_sem, recv_sem, local_sem
 ):
     me = where_am_i()[0]
     t = number(me)
@@ -683,7 +688,24 @@
     def arrange():
         for i in range(plane):
             cols = slice(i * width, (i + 1) * width)
-            mix[i] = jnp.concatenate([branch[:, cols], inner[:, cols], out[:, cols]], axis=1)
+            rows = branch.shape[0]
+            if mix.shape[1] == rows:
+                mix[i] = jnp.concatenate([branch[:, cols], inner[:, cols], out[:, cols]], axis=1)
+            else:
+                mix[i, :rows] = jnp.concatenate([branch[:, cols], inner[:, cols]], axis=1)
+                mix[i, rows:] = jnp.concatenate([out[: rows // 2, cols], out[rows // 2 :, cols]], axis=1)
+        both = [mixer_gain[...].astype(F32), mlp_gain[...].astype(F32)]
+        spare = LANES - 2 * mixer_gain.shape[1]
+        if spare:
+            both.append(jnp.zeros((1, spare), F32))
+        gain[...] = jnp.broadcast_to(jnp.concatenate(both, axis=1), gain.shape)
+        minor = jnp.concatenate([ref[...].astype(F32) for ref in (conv_w, conv_b, gate_b, lru)], axis=0)
+        rows, cols = packed.shape
+        minor = jnp.concatenate([minor, jnp.zeros((8, cols - minor.shape[1]), F32)], axis=1)
+        pieces = [gate_w[...].astype(F32), minor]
+        if rows > gate_w.shape[0] + 8:
+            pieces.append(jnp.zeros((rows - gate_w.shape[0] - 8, cols), F32))
+        packed[...] = jnp.concatenate(pieces, axis=0).astype(BF16)
 
     index = me[0] * plane + t
     slice_of, chunk_of = index // line, lax.rem(index, line)
@@ -809,19 +831,21 @@
 
 def last_kernel(
     line, own_rows,
-    grads_in, mixer_w, tokens_in, grad_middle_in, gain, mlp_term, summed,
-    input_grad, gain_out, swapped, output_grad,
+    grads_in, mixer_w, tokens_in, grad_middle_in, gain, mlp_term, summed, swapped_in,
+    input_grad, gain_out, gate_grad, up_grad, down_grad, output_grad,
     *rest,
 ):
     bufs, rest = rest[:SUM_BUFS], rest[SUM_BUFS:]
-    held, mixer_term, land, send_sem, recv_sem, load_sem, grads, tokens, grad_middle, stage_sem = rest
+    held, mixer_term, land, send_sem, recv_sem, load_sem, grads, tokens, grad_middle, swapped, stage_sem = rest
     early = stage(((grads_in, grads),), stage_sem)
     spot = where_am_i()
     me = spot[0]
     t = number(me)
     plane = 8
     loads = load_columns(((mixer_w, 0, held),), load_sem)
-    late = stage(((tokens_in, tokens), (grad_middle_in, grad_middle)), stage_sem.at[pl.ds(1, 2)])
+    late = stage(
+        ((tokens_in, tokens), (grad_middle_in, grad_middle), (swapped_in, swapped)), stage_sem.at[pl.ds(1, 3)]
+    )
     peers = plane_peers(me)
     greet(peers)
     send = sender(send_sem, recv_sem)
@@ -842,6 +866,14 @@
         if cut < own_rows:
             rest = own_rows - cut
             swaps.append(swap_rows_start(summed, land, cut, rest, send, SUM_SEMS + 7, load_sem.at[2], me, peers))
+        fill(swapped, swapped.shape[2] // 3, 0)
+
+    hid = gate_grad.shape[1] // plane
+
+    def fill(src, size, low):
+        for k, dst in enumerate((gate_grad, up_grad, down_grad)):
+            for i in range(plane):
+                dst[:, i * hid + low : i * hid + low + size] = src[i, :, k * size : (k + 1) * size]
 
     opened, _ = plane_sum([(grads, held)], bufs, send, spot, body, after_sends=swap_now)
     per = plane * own_rows
@@ -854,10 +886,11 @@
         copy.wait_send()
     for swap in swaps:
         swap_end(swap)
-    size, width = swapped.shape[2], grads.shape[1] // 2
-    swapped[...] = land[:, :, :size]
+    width = grads.shape[1] // 2
+    size = land.shape[2] - -(-width // LANES) * LANES
+    fill(land, size // 3, swapped.shape[2] // 3)
     for i in range(0, plane, 2):
-        both = [land[i + j, :, size:].astype(F32) for j in range(2)]
+        both = [land[i + j, :, size : size + width].astype(F32) for j in range(2)]
         output_grad[:, i * width : (i + 2) * width] = jnp.concatenate(both, axis=1)
 
 
@@ -882,7 +915,7 @@
     line, groups, streams, span,
     normed_in, mix_w_in, off, wbd, vec, cot, gate, up, down,
     value_out, slope_out, inner, head_rows, conv_out, rate_out, keep_out, scale_out, decay_out, states_out, mixed, enter, ends, halo,
-    cot_all, ff_in, out_w,
+    cot_all, ff_in,
     normed, mix_w, stage_sem, branch, slope, conv, rate, keep, scale, decay, states, save_sem, driven, ext, tail_out, tail_in, chain_out, chain_in, send_sem, recv_sem, local_sem,
 ):
     spot = where_am_i()
@@ -918,7 +951,7 @@
     def project(q):
         loads[1 + order.index(q)].wait()
         rows = block_rows(q, place_rows)
-        both = jnp.dot(normed[rows, :], mix_w[:, : 2 * width], preferred_element_type=F32)
+        both = jnp.dot(normed[rows, :], mix_w[...], preferred_element_type=F32)
         branch[rows, :] = both[:, :width]
         part = both[:, width:].astype(BF16)
         inner[rows, :] = part
@@ -1013,7 +1046,6 @@
 
     lax.fori_loop(0, span, walk, split_lanes(enter[...]), unroll=4)
     save((states, states_out))
-    out_w[...] = mix_w[:, 2 * width :]
 
     @pl.loop(0, groups)
     def _(g):
@@ -1298,10 +1330,6 @@
 def outer_kernel(*refs):
     out, refs = refs[-1], refs[:-1]
     low = 0
-    if len(refs) % 2:
-        low = refs[0].shape[1]
-        out[:, :low] = refs[0][...]
-        refs = refs[1:]
     for a, b in zip(refs[::2], refs[1::2]):
         size = b.shape[1]
         part = lax.dot_general(a[...], b[...], rows_contract, preferred_element_type=F32)
@@ -1309,14 +1337,11 @@
         low += size
 
 
-def outer_call(*pairs, first=None):
+def outer_call(*pairs):
     count, d_model = pairs[0].shape
     tile = 256
     sizes = [b.shape[1] for b in pairs[1::2]]
-    specs, low = [], 0
-    if first is not None:
-        low = first.shape[1]
-        specs.append(pl.BlockSpec((tile, low), lambda i: (i, 0)))
+    specs = []
     for size in sizes:
         specs.append(pl.BlockSpec((count, tile), lambda i: (0, i)))
         specs.append(pl.BlockSpec((count, size), lambda i: (0, 0), pipeline_mode=pl.Buffered(1)))
@@ -1324,19 +1349,48 @@
         outer_kernel,
         grid=(d_model // tile,),
         in_specs=specs,
-        out_specs=pl.BlockSpec((tile, low + sum(sizes)), lambda i: (i, 0)),
-        out_shape=jax.ShapeDtypeStruct((d_model, low + sum(sizes)), BF16),
+        out_specs=pl.BlockSpec((tile, sum(sizes)), lambda i: (i, 0)),
+        out_shape=jax.ShapeDtypeStruct((d_model, sum(sizes)), BF16),
         compiler_params=pltpu.CompilerParams(vmem_limit_bytes=VMEM_LIMIT),
         cost_estimate=pl.CostEstimate(
             flops=2 * count * d_model * sum(sizes),
             bytes_accessed=2 * count * (d_model * len(sizes) + sum(sizes)),
             transcendentals=0,
         ),
-    )(*(() if first is None else (first,)), *pairs)
+    )(*pairs)
 
 
 def outer_into_kernel(filled, a, b, out):
     out[0] = lax.dot_general(a[...], b[...], rows_contract, preferred_element_type=F32).astype(BF16)
+
+
+def outer_beside_kernel(filled, a, b, out):
+    part = lax.dot_general(a[...], b[...], rows_contract, preferred_element_type=F32)
+    spare = out.shape[1] - part.shape[1]
+    if spare:
+        part = jnp.concatenate([part, jnp.zeros((part.shape[0], spare), F32)], axis=1)
+    out[...] = part.astype(BF16)
+
+
+def outer_beside(filled, a, b, cols):
+    count, d_model = a.shape
+    size, tile, place = b.shape[1], 256, filled.shape[1] // cols - 1
+    return pl.pallas_call(
+        outer_beside_kernel,
+        grid=(d_model // tile,),
+        in_specs=[
+            pl.BlockSpec(memory_space=pl.ANY),
+            pl.BlockSpec((count, tile), lambda i: (0, i)),
+            pl.BlockSpec((count, size), lambda i: (0, 0), pipeline_mode=pl.Buffered(1)),
+        ],
+        out_specs=pl.BlockSpec((tile, cols), lambda i: (i, place)),
+        out_shape=jax.ShapeDtypeStruct(filled.shape, BF16),
+        input_output_aliases={0: 0},
+        compiler_params=pltpu.CompilerParams(vmem_limit_bytes=VMEM_LIMIT),
+        cost_estimate=pl.CostEstimate(
+            flops=2 * count * d_model * size, bytes_accessed=2 * count * (d_model + size), transcendentals=0
+        ),
+    )(filled, a, b)
 
 
 def outer_into(filled, a, b):
@@ -1412,34 +1466,42 @@
     width, hid = rw // plane, ff // plane
     my_line = lax.axis_index("line")
 
-    gain_tile = jnp.concatenate([mixer_gain, mlp_gain]).astype(F32)
-    gain_tile = jnp.pad(gain_tile, (0, LANES - gain_tile.shape[0]))
-    gain_tile = jnp.broadcast_to(gain_tile[None], (8, LANES))
     chunk = gate_bias.shape[1]
-    minor = jnp.concatenate([conv_weight, conv_bias[None], gate_bias, lru_param[None]], axis=0)
-    extra = -(-8 * chunk // (2 * WIDTH))
-    spare = extra * 2 * WIDTH - 8 * chunk
-    minor = jnp.pad(minor.reshape(8 * chunk), (0, spare)).reshape(extra, 2 * WIDTH)
-    pack_rows = -(-(chunk + extra) // 16) * 16
-    packed = jnp.concatenate(
-        [gate_weight, minor, jnp.zeros((pack_rows - chunk - extra, 2 * WIDTH), BF16)], axis=0
-    )
+    pack_rows = -(-(chunk + 8) // 16) * 16
+    paired = own_rows % 32 == 0
+    mix_block = (plane, own_rows * 3 // 2, 2 * width) if paired else (plane, own_rows, 3 * width)
     mix_swapped, gains, arrived = comm_call(
         functools.partial(first_kernel, line),
         1,
-        [VMEM] * 3 + [ANY] * 2,
+        [VMEM] * 10,
         [
-            ((plane, own_rows, 3 * width), BF16, ANY),
+            (mix_block, BF16, ANY),
             ((line, plane, 8, LANES), F32, ANY),
             ((line, pack_rows, 2 * WIDTH), BF16, ANY),
         ],
-        [pltpu.VMEM((plane, own_rows, 3 * width), BF16)] + sems(13 + 2 * line) + [pltpu.SemaphoreType.DMA((3,))],
+        [
+            pltpu.VMEM(mix_block, BF16),
+            pltpu.VMEM((8, LANES), F32),
+            pltpu.VMEM((pack_rows, 2 * WIDTH), BF16),
+        ]
+        + sems(13 + 2 * line)
+        + [pltpu.SemaphoreType.DMA((3,))],
         15,
-    )(w_branch, w_input, w_output, gain_tile, packed)
+    )(
+        w_branch, w_input, w_output, mixer_gain[None], mlp_gain[None], gate_weight, conv_weight, conv_bias[None],
+        gate_bias, lru_param[None],
+    )
     gains = gains[:, :, 0]
     mixer_scale = gains[:, :, :own_rows].reshape(1, d_model)
     mlp_scale = gains[:, :, own_rows : 2 * own_rows].reshape(1, d_model)
-    mixer_w = line_gather(mix_swapped.reshape(plane * own_rows, 3 * width))
+    mixer_w = line_gather(mix_swapped.reshape(-1, mix_block[2]))
+    if paired:
+        mixer_w = mixer_w.reshape(line * plane, -1, 2 * width)
+        output_w = mixer_w[:, own_rows:].reshape(line * plane, own_rows // 2, 2, width)
+        output_w = output_w.transpose(0, 2, 1, 3).reshape(d_model, width)
+        mixer_w = mixer_w[:, :own_rows].reshape(d_model, 2 * width)
+    else:
+        mixer_w, output_w = mixer_w[:, : 2 * width], mixer_w[:, 2 * width :]
     x = tokens.reshape(own, d_model)
     cot = cotangent.reshape(own, d_model)
     tall = ((plane * own, d_model), BF16, ANY)
@@ -1457,8 +1519,7 @@
     )(x, mixer_scale, w_gate, w_up, w_down)
 
     heads_w = arrived[:, :chunk].reshape(width, 2 * WIDTH)
-    minor = arrived[:, chunk : chunk + extra].reshape(line, -1)[:, : 8 * chunk].reshape(line, 8, chunk)
-    minor = minor.transpose(1, 0, 2).reshape(8, width).astype(F32)
+    minor = arrived[:, chunk : chunk + 8, :chunk].transpose(1, 0, 2).reshape(8, width).astype(F32)
     taps, shift, bias, lru = minor[0:4], minor[4:5], minor[5:7], minor[7:8]
     vec = jnp.concatenate(
         [taps, shift, bias, jax.nn.softplus(lru), jax.nn.sigmoid(lru), jnp.zeros((7, width), F32)], axis=0
@@ -1496,7 +1557,7 @@
     edge = ((8 * streams, wide), F32)
     (
         value, slope, inner, head_rows, conv, rate, keep, scale, decay, states, mixed, enter, ends, halo, cot_all,
-        second_part, output_w,
+        second_part,
     ) = comm_call(
         functools.partial(mixer_forward_kernel, line, groups, streams, span),
         3,
@@ -1504,11 +1565,10 @@
         [full, full, short, short, full, full, full, full, tiled, tiled, short]
         + [((groups, wide), F32, VMEM)] * 2
         + [edge + (VMEM,), tall]
-        + swapped(FF_SECOND)
-        + [((d_model, width), BF16, VMEM)],
+        + swapped(FF_SECOND),
         [
             pltpu.VMEM((count, d_model), BF16),
-            pltpu.VMEM((d_model, 3 * width), BF16),
+            pltpu.VMEM((d_model, 2 * width), BF16),
             pltpu.SemaphoreType.DMA((1 + places,)),
         ]
         + [pltpu.VMEM((count, width), F32)] * 6
@@ -1557,7 +1617,7 @@
         grad_middle_kernel,
         5,
         [ANY] * 6 + [VMEM] + [ANY] * 3,
-        [own32, gain_rows, tall, ((d_model, 3 * FF_SECOND[1]), BF16, ANY)],
+        [own32, gain_rows, tall, ((d_model, 3 * FF_SECOND[1] + wide), BF16, ANY)],
         [pltpu.VMEM((own, d_model), BF16)]
         + sum_buffers(own, d_model)
         + sems(SUM_SEMS + GATHER_SEMS * PARTS)
@@ -1583,10 +1643,7 @@
     def by_owner(total_rows):
         return total_rows.reshape(plane, own_rows, -1)
 
-    def widen(pieces):
-        return jnp.concatenate(pieces, axis=2).transpose(1, 0, 2).reshape(own_rows, -1).astype(F32)
-
-    sums_out = outer_call(grad_att, mixed, first=sums_b)
+    sums_out = outer_beside(sums_b, grad_att, mixed, wide)
     grad_att, sums_out = lax.optimization_barrier((grad_att, sums_out))
     ff_sums.append(line_reduce(sums_out))
     pack_rows = -(-(chunk // 2 + 8) // 16) * 16
@@ -1642,21 +1699,23 @@
 
     gain_tiles = plane * own_rows // LANES
     deep = -(-2 * line // 8) * 8
-    input_grad, gain_terms, swapped_b, w_output_grad = comm_call(
+    input_grad, gain_terms, *ff_grads, w_output_grad = comm_call(
         functools.partial(last_kernel, line, own_rows),
         7,
-        [ANY] * 4 + [VMEM] * 2 + [ANY],
+        [ANY] * 4 + [VMEM] * 2 + [ANY] * 2,
         [
             own32,
             ((gain_tiles, deep, LANES), F32, VMEM),
-            ((plane, own_rows, 3 * FF_SECOND[1]), BF16, VMEM),
+            ((own_rows, ff), BF16, VMEM),
+            ((own_rows, ff), BF16, VMEM),
+            ((own_rows, ff), BF16, VMEM),
             ((own_rows, rw), F32, VMEM),
         ],
         sum_buffers(own, d_model)
         + [
             pltpu.VMEM((d_model, 2 * width), BF16),
             pltpu.VMEM((8, d_model), F32),
-            pltpu.VMEM((plane, own_rows, 3 * FF_SECOND[1] + width), BF16),
+            pltpu.VMEM((plane, own_rows, 3 * FF_SECOND[1] + wide), BF16),
         ]
         + sems(SUM_SEMS + 14)
         + [
@@ -1664,11 +1723,12 @@
             pltpu.VMEM((count, 2 * width), BF16),
             pltpu.VMEM((own, d_model), BF16),
             pltpu.VMEM((own, d_model), F32),
-            pltpu.SemaphoreType.DMA((3,)),
+            pltpu.VMEM((plane, own_rows, 3 * FF_FIRST[1]), BF16),
+            pltpu.SemaphoreType.DMA((4,)),
         ],
         60,
     )(
-        grads_mix, mixer_w, x, grad_middle, mixer_scale, mlp_gain_term, by_owner(ff_sums[1]),
+        grads_mix, mixer_w, x, grad_middle, mixer_scale, mlp_gain_term, by_owner(ff_sums[1]), swapped_a,
     )
     mix_summed = line_reduce(sums_mix.reshape(-1, 2 * width))
     w_branch_grad, w_input_grad, gain_sum = comm_call(
@@ -1687,17 +1747,12 @@
         15,
     )(mix_summed, gain_terms)
     small = mix_summed[plane * own_rows :].astype(F32)
-    third = FF_FIRST[1], FF_SECOND[1]
-    w_gate_grad, w_up_grad, w_down_grad = (
-        widen([swapped_a[:, :, k * third[0] : (k + 1) * third[0]], swapped_b[:, :, k * third[1] : (k + 1) * third[1]]])
-        for k in range(3)
-    )
+    w_gate_grad, w_up_grad, w_down_grad = (grad.astype(F32) for grad in ff_grads)
     input_grad = input_grad.reshape(streams_own, span, d_model)
     block_output = block_output.reshape(streams_own, span, d_model)
     gate_weight_grad = jnp.concatenate([small[: chunk // 2, :width], small[: chunk // 2, width:]], axis=0)
     minor_grad = small[chunk // 2 : chunk // 2 + 8, :chunk]
-    low = lax.rem((lax.axis_index("pair") * 2 + lax.axis_index("core")) * 2 + lax.axis_index("batch"), LANES // own_rows)
-    gain_grads = lax.dynamic_slice(gain_sum, (0, low * own_rows), (2, own_rows))
+    gain_grads = gain_sum[:2, :own_rows]
     return (
         block_output,
         input_grad,

time: 600 us -> 593 us (0.988)
  waiting for transfers between devices: 18.3 us -> 9.88 us
    pallas_call x2 -> x1, Pallas kernels: 31 us -> 19.2 us  [outer_call(): pl.pallas_call(outer_kernel, grid=(d_model // tile,), in_specs=specs, out...]
    pallas_call x1 -> x2, Pallas kernels: 23.7 us -> 33.3 us  [the longest x1 22.8 us: shards(): comm_call(functools.partial(first_kernel, line), 1, [VMEM] * 10, [(mix_bl...]
    all_gather x3, waiting for transfers between devices: 16.6 us -> 7.43 us  [line_gather(): return lax.all_gather(value, 'line', axis=0, tiled=True)]
  transfers between devices with their start and end apart: 7 -> 7, of which waited for: 3 -> 2; matrix products, arithmetic and copies ran while one was open for 2% -> 4% of each run, Pallas kernels for 83% -> 83%
where the time goes in v6:
time: 593 us; the launch traced here: 583 us
  Pallas kernels  525 us (89%)
  local copies, waits for them, and re-layouts  21.5 us (4%)
  between operations  14.6 us (2%)
  other arithmetic  9.97 us (2%)
  waiting for transfers between devices  9.88 us (2%)
    pallas_call x1, Pallas kernels, shards(): comm_call(grad_middle_kernel, 5, [ANY] * 6 + [VMEM] + [ANY] * 3, [own32,...  87.9 us
    pallas_call x1, Pallas kernels, shards(): comm_call(middle_kernel, 4, [VMEM] * 7 + [ANY] * 7, [own32, tall] + [full...  82.7 us
    pallas_call x1, Pallas kernels, shards(): comm_call(functools.partial(mixer_back_kernel, line, groups, streams, spa...  72 us
    pallas_call x1, Pallas kernels, shards(): comm_call(second_kernel, 2, [VMEM, VMEM, ANY, ANY, ANY], [tall] + swapped...  60.5 us
    pallas_call x1, Pallas kernels, shards(): comm_call(functools.partial(last_kernel, line, own_rows), 7, [ANY] * 4 +...  53.8 us
    pallas_call x1, Pallas kernels, shards(): comm_call(functools.partial(mixer_forward_kernel, line, groups, streams,...  53.7 us
    pallas_call x2, Pallas kernels, ff_call(): pl.pallas_call(ff_kernel, grid=(count // tile,), in_specs=[tokens, tokens...  33.4 us
    pallas_call x1, Pallas kernels, shards(): comm_call(functools.partial(first_kernel, line), 1, [VMEM] * 10, [(mix_bl...  22.8 us
  transfers between devices with their start and end apart: 7, of which 2 were waited for; matrix products, arithmetic and copies ran while one was open for 4% of the time, Pallas kernels for 83%

profile of v6, /device:TPU:0, one launch (start us, length us, event | category | flops | bytes accessed | tf_op | source)
XLA Modules:
  0.0 583.0 jit_solution(10948077901475630482)
XLA Ops:
  7.2 0.0 all-gather.4.cloned.1.call-start
  7.2 22.8 %shard_map.271 = (bf16[8,96,640]{2,1,0:T(8,128)(2,1)}, f32[4,8,8,128]{3,2,1,0:T(8,128)}, bf16[4,96,320]{2,1,0:T(8,128)(2,1)}) custom-call(bf16[64,2560]{1,0:T(8,128)(2,1)} %branch.1, bf16[64,2560]{1,0:T(8,128)(2,1)} %inner.1, bf16[64,2560]{1,0:T(8,128)(2,1)} %out.1, bf16[1,64]{1,0:T(2,128)(2,1)} %bitcast.56, bf16[1,64]{1,0:T(2,128)(2,1)} %bitcast.57, ...), custom_call_target="tpu_custom_call" | custom-call | flops 15000000512 | bytes 1048576 | tf_op jit(solution)/shard_map/pallas_call | solution.py:1473
  30.1 0.0 all-gather.4.cloned.1.call-update
  30.1 0.0 all-gather.6.cloned.1.call-start
  30.1 0.9 slice.82
  31.1 0.1 fusion.5
  31.1 0.7 reshape.218.gain
  31.8 60.5 %shard_map.272 = (bf16[2048,2048]{1,0:T(8,128)(2,1)}, bf16[8,64,1536]{2,1,0:T(8,128)(2,1)}) custom-call(bf16[256,2048]{1,0:T(8,128)(2,1)} %bitcast.53, f32[1,2048]{1,0:T(1,128)} %reshape.218.gain, bf16[64,6144]{1,0:T(8,128)(2,1)} %gate.3, bf16[64,6144]{1,0:T(8,128)(2,1)} %up.3, bf16[64,6144]{1,0:T(8,128)(2,1)} %down.3), custom_call_target="tpu_custom_call" | custom-call | flops 60000002048 | bytes 1048576 | tf_op jit(solution)/shard_map/pallas_call | solution.py:1512
  92.3 0.0 all-gather.6.cloned.1.call-update
  92.3 0.0 all-gather.8.cloned.1.call-start
  92.4 0.8 collective-permute-start
  93.3 0.1 slice.93
  93.4 0.1 slice.91
  93.4 0.7 reshape.227.gain
  94.1 0.1 pad.5.clone
  94.2 0.2 broadcast_select_fusion.3
  94.4 1.0 pad_maximum_fusion.wbd
  95.5 0.1 broadcast_add_fusion
  95.6 0.7 maximum_maximum_fusion.vec
  96.3 0.2 reduce_window_sum.11
  96.5 0.1 select_reduce_fusion
  96.6 0.1 slice.107
  96.7 1.4 copy.45.off.off_in
  98.1 7.4 %all-gather.4.cloned.1.call-done = bf16[3072,640]{1,0:T(8,128)(2,1)} async-done(((bf16[768,640]{1,0:T(8,128)(2,1)}), bf16[3072,640]{1,0:T(8,128)(2,1)}) %all-gather.4.cloned.1.call-update) | async-done | bytes 3932176 | tf_op jit(solution)/shard_map/all_gather | solution.py:1446
  105.5 1.4 slice.112
  106.9 3.5 slice.106
  110.3 1.3 reshape.225
  111.7 1.4 copy.46
  113.1 53.7 %shard_map.273 = (f32[2048,320]{1,0:T(8,128)}, f32[2048,320]{1,0:T(8,128)}, bf16[2048,320]{1,0:T(8,128)(2,1)}, bf16[2048,320]{1,0:T(8,128)(2,1)}, f32[2048,320]{...) custom-call(bf16[2048,2048]{1,0:T(8,128)(2,1)} %get-tuple-element.71, ...), custom_call_target="tpu_custom_call" | custom-call | flops 49999998976 | bytes 1048576 | tf_op jit(solution)/shard_map/pallas_call | solution.py:1561
  166.8 0.0 all-gather.8.cloned.1.call-update
  166.8 0.6 reduce-scatter.4.cloned.1.call-start
  167.4 82.7 %shard_map.274 = (f32[256,2048]{1,0:T(8,128)}, bf16[2048,2048]{1,0:T(8,128)(2,1)}, f32[2048,320]{1,0:T(8,128)}, f32[2048,320]{1,0:T(8,128)}, f32[2048,320]{1,0:T...) custom-call(bf16[2048,320]{1,0:T(8,128)(2,1)} %get-tuple-element.74.mixed.b, bf16[2048,320]{1,0:T(8,128)(2,1)} %bitcast.40, ...), custom_call_target="tpu_custom_call" | custom-call | flops 80000000000 | bytes 1048576 | tf_op jit(solution)/shard_map/pallas_call | solution.py:1592
  250.1 0.0 all-gather.6.cloned.1.call-done.gate_w.up_w.down_w.w1.part_a
  250.1 19.3 %shard_map.275 = (bf16[2048,1024]{1,0:T(8,128)(2,1)}, bf16[2048,512]{1,0:T(8,128)(2,1)}) custom-call(bf16[2048,2048]{1,0:T(8,128)(2,1)} %get-tuple-element.88.second.refs_0_, bf16[2048,2048]{1,0:T(8,128)(2,1)} %get-tuple-element.84.cot.refs_2_.cot_all, bf16[2048,1536]{1,0:T(8,128)(2,1)} %all-gather.6.cloned.1.call-done.gate_w.up_w.down_w.w1.part_a, ...), custom_call_target="tpu_custom_call" | custom-call | flops 12884901888 | bytes 16777216 | tf_op jit(solution)/shard_map/pallas_call | solution.py:1311
  269.4 19.2 %shard_map.276 = bf16[2048,1536]{1,0:T(8,128)(2,1)} custom-call(bf16[2048,2048]{1,0:T(8,128)(2,1)} %get-tuple-element.88.second.refs_0_, bf16[2048,1024]{1,0:T(8,128)(2,1)} %get-tuple-element.86.refs_1_.g1_in, bf16[2048,2048]{1,0:T(8,128)(2,1)} %get-tuple-element.84.cot.refs_2_.cot_all, bf16[2048,512]{1,0:T(8,128)(2,1)} %get-tuple-element.87.refs_3_.hidden_a_in), custom_call_target="tpu_custom_call" | custom-call | flops 12884901888 | bytes 23068672 | tf_op jit(solution)/shard_map/pallas_call | solution.py:1348
  288.6 0.2 reduce-scatter.6.cloned.1.call-start
  288.8 0.0 all-gather.8.cloned.1.call-done.gate_w.up_w.down_w.w2.part_b
  288.8 14.2 %shard_map.277 = (bf16[2048,512]{1,0:T(8,128)(2,1)}, bf16[2048,256]{1,0:T(8,128)(2,1)}) custom-call(bf16[2048,2048]{1,0:T(8,128)(2,1)} %get-tuple-element.88.second.refs_0_, bf16[2048,2048]{1,0:T(8,128)(2,1)} %get-tuple-element.84.cot.refs_2_.cot_all, bf16[2048,768]{1,0:T(8,128)(2,1)} %all-gather.8.cloned.1.call-done.gate_w.up_w.down_w.w2.part_b, ...), custom_call_target="tpu_custom_call" | custom-call | flops 6442450944 | bytes 16777216 | tf_op jit(solution)/shard_map/pallas_call | solution.py:1311
  303.0 87.9 %shard_map.278 = (f32[256,2048]{1,0:T(8,128)}, f32[8,2048]{1,0:T(8,128)}, bf16[2048,2048]{1,0:T(8,128)(2,1)}, bf16[2048,1152]{1,0:T(8,128)(2,1)}) custom-call(bf16[2048,1024]{1,0:T(8,128)(2,1)} %get-tuple-element.86.refs_1_.g1_in, bf16[2048,1536]{1,0:T(8,128)(2,1)} %all-gather.6.cloned.1.call-done.gate_w.up_w.down_w.w1.part_a, ...), custom_call_target="tpu_custom_call" | custom-call | flops 89999998976 | bytes 1048576 | tf_op jit(solution)/shard_map/pallas_call | solution.py:1616
  390.9 10.4 %shard_map.279 = bf16[2048,1152]{1,0:T(8,128)(2,1)} custom-call(bf16[2048,1152]{1,0:T(8,128)(2,1)} %get-tuple-element.94.filled, bf16[2048,2048]{1,0:T(8,128)(2,1)} %get-tuple-element.95.a.grad_att, bf16[2048,320]{1,0:T(8,128)(2,1)} %get-tuple-element.74.mixed.b), custom_call_target="tpu_custom_call", output_to_operand_aliasing={{}: (0, {})} | custom-call | flops 2684354560 | bytes 9699328 | tf_op jit(solution)/shard_map/pallas_call | solution.py:1378
  401.4 0.0 reduce-scatter.6.cloned.1.call-update
  401.4 0.3 reduce-scatter.8.cloned.1.call-start
  401.7 0.4 copy-done.8
  402.1 1.5 copy.49.offx_in
  403.6 72.0 %shard_map.280 = (bf16[2048,640]{1,0:T(8,128)(2,1)}, bf16[256,2048]{1,0:T(8,128)(2,1)}, bf16[8,64,1536]{2,1,0:T(8,128)(2,1)}, bf16[4,560,640]{2,1,0:T(8,128)(2,1)}) custom-call(bf16[2048,2048]{1,0:T(8,128)(2,1)} %get-tuple-element.95.a.grad_att, bf16[2048,320]{1,0:T(8,128)(2,1)} %bitcast.41, f32[2048,320]{1,0:T(8,128)} %get-tuple-element.96.value, ...), custom_call_target="tpu_custom_call" | custom-call | flops 70000001024 | bytes 1048576 | tf_op jit(solution)/shard_map/pallas_call | solution.py:1650
  475.6 12.2 %shard_map.281 = bf16[4,560,640]{2,1,0:T(8,128)(2,1)} custom-call(bf16[4,560,640]{2,1,0:T(8,128)(2,1)} %get-tuple-element.109.filled, bf16[2048,2048]{1,0:T(8,128)(2,1)} %get-tuple-element.71.normed_in.a, bf16[2048,640]{1,0:T(8,128)(2,1)} %get-tuple-element.110.b.grads_in), custom_call_target="tpu_custom_call", output_to_operand_aliasing={{}: (0, {})} | custom-call | flops 5368709120 | bytes 11010048 | tf_op jit(solution)/shard_map/pallas_call | solution.py:1401
  487.8 2.3 reduce-scatter.6.cloned.1.call-done
  490.2 53.8 %shard_map.282 = (f32[256,2048]{1,0:T(8,128)}, f32[4,8,128]{2,1,0:T(8,128)}, bf16[64,6144]{1,0:T(8,128)(2,1)}, bf16[64,6144]{1,0:T(8,128)(2,1)}, bf16[64,6144]{1,0:T(8,128)(2,1)}, /*index=5*/f32[64,2560]{1,0:T(8,128)}) custom-call(bf16[2048,640]{1,0:T(8,128)(2,1)} %get-tuple-element.110.b.grads_in, bf16[2048,640]{1,0:T(8,128)(2,1)} %bitcast.37, ...), custom_call_target="tpu_custom_call" | custom-call | flops 60000002048 | bytes 1048576 | tf_op jit(solution)/shard_map/pallas_call | solution.py:1702
  544.0 2.5 convert_element_type.21
  546.5 2.4 convert_element_type.22
  548.9 1.2 convert_element_type.23
  550.1 0.8 slice_convert_fusion
  551.0 0.6 slice.117
  551.5 0.5 slice_bitcast_fusion
  552.0 0.6 slice.118
  552.6 0.1 fusion.4
  552.7 16.3 %shard_map.283 = (f32[64,2560]{1,0:T(8,128)}, f32[64,2560]{1,0:T(8,128)}, f32[8,128]{1,0:T(8,128)}) custom-call(bf16[560,640]{1,0:T(8,128)(2,1)} %reduce-scatter.8.cloned.1.call-done.summed, f32[4,8,128]{2,1,0:T(8,128)} %get-tuple-element.117.terms), custom_call_target="tpu_custom_call" | custom-call | flops 15000000512 | bytes 1048576 | tf_op jit(solution)/shard_map/pallas_call | solution.py:1734
  569.0 1.4 slice_bitcast_fusion.2
  570.4 0.7 pad_maximum_fusion.1
  571.1 1.0 copy.57
  572.0 1.3 copy.58
  573.4 0.8 copy.59
  574.2 0.8 copy.60
  575.0 0.8 copy.61
  (38 shorter events, 0.2 us)
Async XLA Ops:
  7.2 98.3 %all-gather.4.cloned.1.call-start = ((), (), s32[]{:S(2)}) async-start(), calls=%async_computation.3 | async-start | bytes 4915200 | tf_op jit(solution)/shard_map/all_gather | solution.py:1446
  30.1 220.0 %all-gather.6.cloned.1.call-start = ((), (), s32[]{:S(2)}) async-start(), calls=%async_computation.4 | async-start | bytes 7864320 | tf_op jit(solution)/shard_map/all_gather | solution.py:1446
  31.8 60.6 %copy-start.9 = (s32[2,4]{1,0:T(2,128)S(1)}, s32[2,4]{1,0:T(2,128)}, u32[]{:S(2)}) copy-start(s32[2,4]{1,0:T(2,128)} %param.18) | copy-start | bytes 100
  31.8 61.4 %copy-start.6 = (bf16[4,96,320]{2,1,0:T(8,128)(2,1)S(1)}, bf16[4,96,320]{2,1,0:T(8,128)(2,1)}, u32[]{:S(2)}) copy-start(bf16[4,96,320]{2,1,0:T(8,128)(2,1)} %get-tuple-element.73) | copy-start | bytes 737284
  92.3 196.5 %all-gather.8.cloned.1.call-start = ((), (), s32[]{:S(2)}) async-start(), calls=%async_computation.5 | async-start | bytes 3932160 | tf_op jit(solution)/shard_map/all_gather | solution.py:1446
  92.4 3.9 collective-permute-start
  96.6 8.8 %copy-start.7 = (s32[16,144,1]{1,0,2:T(8,128)}, s32[16,144,1]{1,0,2:T(8,128)S(1)}, u32[]{:S(2)}) copy-start(s32[16,144,1]{1,0,2:T(8,128)S(1)} %sub.40) | copy-start | bytes 27652
  166.8 236.8 %reduce-scatter.4.cloned.1.call-start = ((), (), s32[]{:S(2)}) async-start(), calls=%async_computation.6 | async-start | bytes 7864320 | tf_op jit(solution)/shard_map/reduce_scatter | solution.py:1450
  288.6 201.6 %reduce-scatter.6.cloned.1.call-start = ((), (), s32[]{:S(2)}) async-start(), calls=%async_computation.7 | async-start | bytes 5898240 | tf_op jit(solution)/shard_map/reduce_scatter | solution.py:1450
  401.4 0.7 copy-start.8
  401.4 148.7 %reduce-scatter.8.cloned.1.call-start = ((), (), s32[]{:S(2)}) async-start(), calls=%async_computation.8 | async-start | bytes 3584000 | tf_op jit(solution)/shard_map/reduce_scatter | solution.py:1450
  544.0 4.9 copy-start.2
  552.7 18.4 %copy-start.1 = (bf16[256,2048]{1,0:T(8,128)(2,1)S(1)}, bf16[256,2048]{1,0:T(8,128)(2,1)}, u32[]{:S(2)}) copy-start(bf16[256,2048]{1,0:T(8,128)(2,1)} %get-tuple-element.107) | copy-start | bytes 3145732
  569.0 3.0 copy-start
  571.1 2.3 copy-start.5
  572.0 2.2 copy-start.4
  572.0 3.0 copy-start.3
Sparse Core Ops, SparseCore 0:
  30.2 75.1 all-gather.3
  107.0 116.9 all-gather.5
  225.6 61.6 all-gather.7
  289.4 110.1 reduce-scatter.3
  401.7 88.3 reduce-scatter.5
  492.3 56.5 reduce-scatter.7

commit v7 on v6

--- a/solution.py
+++ b/solution.py
@@ -1374,7 +1374,7 @@
 
 def outer_beside(filled, a, b, cols):
     count, d_model = a.shape
-    size, tile, place = b.shape[1], 256, filled.shape[1] // cols - 1
+    size, tile, place = b.shape[1], 512, filled.shape[1] // cols - 1
     return pl.pallas_call(
         outer_beside_kernel,
         grid=(d_model // tile,),
@@ -1396,7 +1396,7 @@
 def outer_into(filled, a, b):
     count, d_model = a.shape
     parts, size = filled.shape[0], b.shape[1]
-    tile = min(256, d_model // parts)
+    tile = min(512, d_model // parts)
     per = d_model // parts // tile
     return pl.pallas_call(
         outer_into_kernel,

time: 593 us -> 593 us (level)
  no operation moved by 1% of the time
where the time goes in v7:
time: 593 us; the launch traced here: 583 us
  Pallas kernels  521 us (88%)
  local copies, waits for them, and re-layouts  21.3 us (4%)
  between operations  14.5 us (2%)
  waiting for transfers between devices  13.3 us (2%)
  other arithmetic  9.98 us (2%)
    pallas_call x1, Pallas kernels, shards(): comm_call(grad_middle_kernel, 5, [ANY] * 6 + [VMEM] + [ANY] * 3, [own32,...  87.9 us
    pallas_call x1, Pallas kernels, shards(): comm_call(middle_kernel, 4, [VMEM] * 7 + [ANY] * 7, [own32, tall] + [full...  82.7 us
    pallas_call x1, Pallas kernels, shards(): comm_call(functools.partial(mixer_back_kernel, line, groups, streams, spa...  72 us
    pallas_call x1, Pallas kernels, shards(): comm_call(second_kernel, 2, [VMEM, VMEM, ANY, ANY, ANY], [tall] + swapped...  60.5 us
    pallas_call x1, Pallas kernels, shards(): comm_call(functools.partial(last_kernel, line, own_rows), 7, [ANY] * 4 +...  53.9 us
    pallas_call x1, Pallas kernels, shards(): comm_call(functools.partial(mixer_forward_kernel, line, groups, streams,...  53.7 us
    pallas_call x2, Pallas kernels, ff_call(): pl.pallas_call(ff_kernel, grid=(count // tile,), in_specs=[tokens, tokens...  33.5 us
    pallas_call x1, Pallas kernels, shards(): comm_call(functools.partial(first_kernel, line), 1, [VMEM] * 10, [(mix_bl...  22.8 us
  transfers between devices with their start and end apart: 7, of which 2 were waited for; matrix products, arithmetic and copies ran while one was open for 4% of the time, Pallas kernels for 83%

profile of v7, /device:TPU:0, one launch (start us, length us, event | category | flops | bytes accessed | tf_op | source)
XLA Modules:
  0.0 582.6 jit_solution(8486814863976326991)
XLA Ops:
  7.2 0.0 all-gather.4.cloned.1.call-start
  7.2 22.8 %shard_map.271 = (bf16[8,96,640]{2,1,0:T(8,128)(2,1)}, f32[4,8,8,128]{3,2,1,0:T(8,128)}, bf16[4,96,320]{2,1,0:T(8,128)(2,1)}) custom-call(bf16[64,2560]{1,0:T(8,128)(2,1)} %branch.1, bf16[64,2560]{1,0:T(8,128)(2,1)} %inner.1, bf16[64,2560]{1,0:T(8,128)(2,1)} %out.1, bf16[1,64]{1,0:T(2,128)(2,1)} %bitcast.56, bf16[1,64]{1,0:T(2,128)(2,1)} %bitcast.57, ...), custom_call_target="tpu_custom_call" | custom-call | flops 15000000512 | bytes 1048576 | tf_op jit(solution)/shard_map/pallas_call | solution.py:1473
  30.1 0.0 all-gather.4.cloned.1.call-update
  30.1 0.0 all-gather.6.cloned.1.call-start
  30.1 0.9 slice.82
  31.1 0.1 fusion.5
  31.1 0.7 reshape.218.gain
  31.8 60.5 %shard_map.272 = (bf16[2048,2048]{1,0:T(8,128)(2,1)}, bf16[8,64,1536]{2,1,0:T(8,128)(2,1)}) custom-call(bf16[256,2048]{1,0:T(8,128)(2,1)} %bitcast.53, f32[1,2048]{1,0:T(1,128)} %reshape.218.gain, bf16[64,6144]{1,0:T(8,128)(2,1)} %gate.3, bf16[64,6144]{1,0:T(8,128)(2,1)} %up.3, bf16[64,6144]{1,0:T(8,128)(2,1)} %down.3), custom_call_target="tpu_custom_call" | custom-call | flops 60000002048 | bytes 1048576 | tf_op jit(solution)/shard_map/pallas_call | solution.py:1512
  92.3 0.0 all-gather.6.cloned.1.call-update
  92.3 0.0 all-gather.8.cloned.1.call-start
  92.4 0.8 collective-permute-start
  93.3 0.1 slice.93
  93.4 0.1 slice.91
  93.4 0.7 reshape.227.gain
  94.1 0.1 pad.5.clone
  94.2 0.2 broadcast_select_fusion.3
  94.4 1.0 pad_maximum_fusion.wbd
  95.5 0.1 broadcast_add_fusion
  95.6 0.7 maximum_maximum_fusion.vec
  96.3 0.2 reduce_window_sum.11
  96.5 0.1 select_reduce_fusion
  96.6 0.1 slice.107
  96.7 1.4 copy.45.off.off_in
  98.1 7.4 %all-gather.4.cloned.1.call-done = bf16[3072,640]{1,0:T(8,128)(2,1)} async-done(((bf16[768,640]{1,0:T(8,128)(2,1)}), bf16[3072,640]{1,0:T(8,128)(2,1)}) %all-gather.4.cloned.1.call-update) | async-done | bytes 3932176 | tf_op jit(solution)/shard_map/all_gather | solution.py:1446
  105.5 1.4 slice.112
  106.9 3.5 slice.106
  110.3 1.3 reshape.225
  111.7 1.4 copy.46
  113.1 53.7 %shard_map.273 = (f32[2048,320]{1,0:T(8,128)}, f32[2048,320]{1,0:T(8,128)}, bf16[2048,320]{1,0:T(8,128)(2,1)}, bf16[2048,320]{1,0:T(8,128)(2,1)}, f32[2048,320]{...) custom-call(bf16[2048,2048]{1,0:T(8,128)(2,1)} %get-tuple-element.71, ...), custom_call_target="tpu_custom_call" | custom-call | flops 49999998976 | bytes 1048576 | tf_op jit(solution)/shard_map/pallas_call | solution.py:1561
  166.8 0.0 all-gather.8.cloned.1.call-update
  166.8 0.3 reduce-scatter.4.cloned.1.call-start
  167.0 82.7 %shard_map.274 = (f32[256,2048]{1,0:T(8,128)}, bf16[2048,2048]{1,0:T(8,128)(2,1)}, f32[2048,320]{1,0:T(8,128)}, f32[2048,320]{1,0:T(8,128)}, f32[2048,320]{1,0:T...) custom-call(bf16[2048,320]{1,0:T(8,128)(2,1)} %get-tuple-element.74.mixed.b, bf16[2048,320]{1,0:T(8,128)(2,1)} %bitcast.40, ...), custom_call_target="tpu_custom_call" | custom-call | flops 80000000000 | bytes 1048576 | tf_op jit(solution)/shard_map/pallas_call | solution.py:1592
  249.8 0.0 all-gather.6.cloned.1.call-done.gate_w.up_w.down_w.w1.part_a
  249.8 19.3 %shard_map.275 = (bf16[2048,1024]{1,0:T(8,128)(2,1)}, bf16[2048,512]{1,0:T(8,128)(2,1)}) custom-call(bf16[2048,2048]{1,0:T(8,128)(2,1)} %get-tuple-element.88.second.refs_0_, bf16[2048,2048]{1,0:T(8,128)(2,1)} %get-tuple-element.84.cot.refs_2_.cot_all, bf16[2048,1536]{1,0:T(8,128)(2,1)} %all-gather.6.cloned.1.call-done.gate_w.up_w.down_w.w1.part_a, ...), custom_call_target="tpu_custom_call" | custom-call | flops 12884901888 | bytes 16777216 | tf_op jit(solution)/shard_map/pallas_call | solution.py:1311
  269.1 19.2 %shard_map.276 = bf16[2048,1536]{1,0:T(8,128)(2,1)} custom-call(bf16[2048,2048]{1,0:T(8,128)(2,1)} %get-tuple-element.88.second.refs_0_, bf16[2048,1024]{1,0:T(8,128)(2,1)} %get-tuple-element.86.refs_1_.g1_in, bf16[2048,2048]{1,0:T(8,128)(2,1)} %get-tuple-element.84.cot.refs_2_.cot_all, bf16[2048,512]{1,0:T(8,128)(2,1)} %get-tuple-element.87.refs_3_.hidden_a_in), custom_call_target="tpu_custom_call" | custom-call | flops 12884901888 | bytes 23068672 | tf_op jit(solution)/shard_map/pallas_call | solution.py:1348
  288.2 0.0 reduce-scatter.4.cloned.1.call-update
  288.3 0.3 reduce-scatter.6.cloned.1.call-start
  288.6 0.0 all-gather.8.cloned.1.call-done.gate_w.up_w.down_w.w2.part_b
  288.6 14.2 %shard_map.277 = (bf16[2048,512]{1,0:T(8,128)(2,1)}, bf16[2048,256]{1,0:T(8,128)(2,1)}) custom-call(bf16[2048,2048]{1,0:T(8,128)(2,1)} %get-tuple-element.88.second.refs_0_, bf16[2048,2048]{1,0:T(8,128)(2,1)} %get-tuple-element.84.cot.refs_2_.cot_all, bf16[2048,768]{1,0:T(8,128)(2,1)} %all-gather.8.cloned.1.call-done.gate_w.up_w.down_w.w2.part_b, ...), custom_call_target="tpu_custom_call" | custom-call | flops 6442450944 | bytes 16777216 | tf_op jit(solution)/shard_map/pallas_call | solution.py:1311
  302.8 87.9 %shard_map.278 = (f32[256,2048]{1,0:T(8,128)}, f32[8,2048]{1,0:T(8,128)}, bf16[2048,2048]{1,0:T(8,128)(2,1)}, bf16[2048,1152]{1,0:T(8,128)(2,1)}) custom-call(bf16[2048,1024]{1,0:T(8,128)(2,1)} %get-tuple-element.86.refs_1_.g1_in, bf16[2048,1536]{1,0:T(8,128)(2,1)} %all-gather.6.cloned.1.call-done.gate_w.up_w.down_w.w1.part_a, ...), custom_call_target="tpu_custom_call" | custom-call | flops 89999998976 | bytes 1048576 | tf_op jit(solution)/shard_map/pallas_call | solution.py:1616
  390.7 8.6 %shard_map.279 = bf16[2048,1152]{1,0:T(8,128)(2,1)} custom-call(bf16[2048,1152]{1,0:T(8,128)(2,1)} %get-tuple-element.94.filled, bf16[2048,2048]{1,0:T(8,128)(2,1)} %get-tuple-element.95.a.grad_att, bf16[2048,320]{1,0:T(8,128)(2,1)} %get-tuple-element.74.mixed.b), custom_call_target="tpu_custom_call", output_to_operand_aliasing={{}: (0, {})} | custom-call | flops 2684354560 | bytes 9699328 | tf_op jit(solution)/shard_map/pallas_call | solution.py:1378
  399.3 0.5 reduce-scatter.8.cloned.1.call-start
  399.8 0.2 copy-done.8
  400.0 1.5 copy.49.offx_in
  401.4 72.0 %shard_map.280 = (bf16[2048,640]{1,0:T(8,128)(2,1)}, bf16[256,2048]{1,0:T(8,128)(2,1)}, bf16[8,64,1536]{2,1,0:T(8,128)(2,1)}, bf16[4,560,640]{2,1,0:T(8,128)(2,1)}) custom-call(bf16[2048,2048]{1,0:T(8,128)(2,1)} %get-tuple-element.95.a.grad_att, bf16[2048,320]{1,0:T(8,128)(2,1)} %bitcast.41, f32[2048,320]{1,0:T(8,128)} %get-tuple-element.96.value, ...), custom_call_target="tpu_custom_call" | custom-call | flops 70000001024 | bytes 1048576 | tf_op jit(solution)/shard_map/pallas_call | solution.py:1650
  473.5 10.6 %shard_map.281 = bf16[4,560,640]{2,1,0:T(8,128)(2,1)} custom-call(bf16[4,560,640]{2,1,0:T(8,128)(2,1)} %get-tuple-element.109.filled, bf16[2048,2048]{1,0:T(8,128)(2,1)} %get-tuple-element.71.normed_in.a, bf16[2048,640]{1,0:T(8,128)(2,1)} %get-tuple-element.110.b.grads_in), custom_call_target="tpu_custom_call", output_to_operand_aliasing={{}: (0, {})} | custom-call | flops 5368709120 | bytes 11010048 | tf_op jit(solution)/shard_map/pallas_call | solution.py:1401
  484.1 5.8 reduce-scatter.6.cloned.1.call-done
  489.9 53.9 %shard_map.282 = (f32[256,2048]{1,0:T(8,128)}, f32[4,8,128]{2,1,0:T(8,128)}, bf16[64,6144]{1,0:T(8,128)(2,1)}, bf16[64,6144]{1,0:T(8,128)(2,1)}, bf16[64,6144]{1,0:T(8,128)(2,1)}, /*index=5*/f32[64,2560]{1,0:T(8,128)}) custom-call(bf16[2048,640]{1,0:T(8,128)(2,1)} %get-tuple-element.110.b.grads_in, bf16[2048,640]{1,0:T(8,128)(2,1)} %bitcast.37, ...), custom_call_target="tpu_custom_call" | custom-call | flops 60000002048 | bytes 1048576 | tf_op jit(solution)/shard_map/pallas_call | solution.py:1702
  543.7 2.5 convert_element_type.21
  546.2 2.4 convert_element_type.22
  548.6 1.2 convert_element_type.23
  549.8 0.8 slice_convert_fusion
  550.7 0.6 slice.117
  551.3 0.5 slice_bitcast_fusion
  551.8 0.6 slice.118
  552.4 0.1 fusion.4
  552.4 16.3 %shard_map.283 = (f32[64,2560]{1,0:T(8,128)}, f32[64,2560]{1,0:T(8,128)}, f32[8,128]{1,0:T(8,128)}) custom-call(bf16[560,640]{1,0:T(8,128)(2,1)} %reduce-scatter.8.cloned.1.call-done.summed, f32[4,8,128]{2,1,0:T(8,128)} %get-tuple-element.117.terms), custom_call_target="tpu_custom_call" | custom-call | flops 15000000512 | bytes 1048576 | tf_op jit(solution)/shard_map/pallas_call | solution.py:1734
  568.7 1.4 slice_bitcast_fusion.2
  570.1 0.7 pad_maximum_fusion.1
  570.7 1.0 copy.57
  571.7 1.3 copy.58
  573.0 0.8 copy.59
  573.9 0.8 copy.60
  574.7 0.8 copy.61
  (38 shorter events, 0.2 us)
Async XLA Ops:
  7.2 98.3 %all-gather.4.cloned.1.call-start = ((), (), s32[]{:S(2)}) async-start(), calls=%async_computation.3 | async-start | bytes 4915200 | tf_op jit(solution)/shard_map/all_gather | solution.py:1446
  30.1 219.7 %all-gather.6.cloned.1.call-start = ((), (), s32[]{:S(2)}) async-start(), calls=%async_computation.4 | async-start | bytes 7864320 | tf_op jit(solution)/shard_map/all_gather | solution.py:1446
  31.8 60.6 %copy-start.9 = (s32[2,4]{1,0:T(2,128)S(1)}, s32[2,4]{1,0:T(2,128)}, u32[]{:S(2)}) copy-start(s32[2,4]{1,0:T(2,128)} %param.18) | copy-start | bytes 100
  31.8 61.4 %copy-start.6 = (bf16[4,96,320]{2,1,0:T(8,128)(2,1)S(1)}, bf16[4,96,320]{2,1,0:T(8,128)(2,1)}, u32[]{:S(2)}) copy-start(bf16[4,96,320]{2,1,0:T(8,128)(2,1)} %get-tuple-element.73) | copy-start | bytes 737284
  92.3 196.3 %all-gather.8.cloned.1.call-start = ((), (), s32[]{:S(2)}) async-start(), calls=%async_computation.5 | async-start | bytes 3932160 | tf_op jit(solution)/shard_map/all_gather | solution.py:1446
  92.4 3.9 collective-permute-start
  96.6 8.8 %copy-start.7 = (s32[16,144,1]{1,0,2:T(8,128)}, s32[16,144,1]{1,0,2:T(8,128)S(1)}, u32[]{:S(2)}) copy-start(s32[16,144,1]{1,0,2:T(8,128)S(1)} %sub.40) | copy-start | bytes 27652
  166.8 234.7 %reduce-scatter.4.cloned.1.call-start = ((), (), s32[]{:S(2)}) async-start(), calls=%async_computation.6 | async-start | bytes 7864320 | tf_op jit(solution)/shard_map/reduce_scatter | solution.py:1450
  288.3 201.6 %reduce-scatter.6.cloned.1.call-start = ((), (), s32[]{:S(2)}) async-start(), calls=%async_computation.7 | async-start | bytes 5898240 | tf_op jit(solution)/shard_map/reduce_scatter | solution.py:1450
  399.3 0.7 copy-start.8
  399.3 150.6 %reduce-scatter.8.cloned.1.call-start = ((), (), s32[]{:S(2)}) async-start(), calls=%async_computation.8 | async-start | bytes 3584000 | tf_op jit(solution)/shard_map/reduce_scatter | solution.py:1450
  543.7 4.9 copy-start.2
  552.4 18.3 %copy-start.1 = (bf16[256,2048]{1,0:T(8,128)(2,1)S(1)}, bf16[256,2048]{1,0:T(8,128)(2,1)}, u32[]{:S(2)}) copy-start(bf16[256,2048]{1,0:T(8,128)(2,1)} %get-tuple-element.107) | copy-start | bytes 3145732
  568.7 3.0 copy-start
  570.7 2.3 copy-start.5
  571.7 2.2 copy-start.4
  571.7 3.0 copy-start.3
Sparse Core Ops, SparseCore 0:
  30.2 75.1 all-gather.3
  107.0 116.9 all-gather.5
  225.6 61.6 all-gather.7
  289.4 109.8 reduce-scatter.3
  401.5 88.3 reduce-scatter.5
  492.0 56.5 reduce-scatter.7
